TPU v7x, 32 devices: a whole 2x2x4 slice. The times are simulated.
32 devices in a mesh: fsdp: 4 (over y, x), ctx: 2 (over core), tp: 4 (over z).
Axes of the slice: x: 2, y: 2, z: 4, core: 2. Of those that a mesh axis runs over, the one named last changes fastest.
Arguments:
- tokens: bfloat16 [8192, 768], P(('fsdp', 'ctx')), may hold values from -6 to 6
- grad_out: bfloat16 [8192, 768], P(('fsdp', 'ctx')), may hold values from -6 to 6
- w_qkv: bfloat16 [768, 3, 768], P(('fsdp', 'ctx'), None, 'tp'), may hold values from -0.21875 to 0.21875
- w_attn_out: bfloat16 [768, 768], P(('fsdp', 'ctx'), 'tp'), may hold values from -1.75 to 1.75
- rel_bias: float32 [32, 12], P(None, 'tp'), may hold values from -4 to 4
- gain_attn: bfloat16 [768], P(('fsdp', 'ctx')), may hold values from 0.099609375 to 1.8984375
- gain_ffn: bfloat16 [768], P(('fsdp', 'ctx')), may hold values from 0.099609375 to 1.8984375
- w_router: bfloat16 [768, 4], P(('fsdp', 'ctx')), may hold values from -0.15625 to 0.15625
- w_in: bfloat16 [4, 768, 3072], P('fsdp', None, 'tp'), may hold values from -0.21875 to 0.21875
- w_down: bfloat16 [4, 768, 3072], P('fsdp', None, 'tp'), may hold values from -0.4375 to 0.4375
- expert_ids: int32 [8192, 1], P(('fsdp', 'ctx')), may hold values from 0 to 3; in each aligned block of 1024 rows (0 to 1023, 1024 to 2047, ...) at most 512 rows name the same one
- doc_ids: int32 [8192], P('fsdp'), may hold values from 0 to 3, as said below
Outputs:
- out: bfloat16 [8192, 768], P(('fsdp', 'ctx'), 'tp')
- grad_tokens: float32 [8192, 768], P(('fsdp', 'ctx'), 'tp')
- grad_w_qkv: float32 [768, 3, 768], P(('fsdp', 'ctx'), None, 'tp')
- grad_w_attn_out: float32 [768, 768], P(('fsdp', 'ctx'), 'tp')
- grad_rel_bias: float32 [32, 12], P(('fsdp', 'ctx'), 'tp')
- grad_gain_attn: float32 [768], P(('fsdp', 'ctx'))
- grad_gain_ffn: float32 [768], P(('fsdp', 'ctx'))
- grad_w_router: float32 [768, 4], P(('fsdp', 'ctx'))
- grad_w_in: float32 [4, 768, 3072], P('fsdp', 'ctx', 'tp')
- grad_w_down: float32 [4, 768, 3072], P('fsdp', 'ctx', 'tp')
Inputs may be any that keep to these rules, and one draw needn't show every extreme that they name: `expert_ids`: in each aligned block of 1024 rows no expert is named more than 512 times, and in every draw some block names some expert exactly 512 times. `doc_ids`: within each packed sequence of 2048 tokens the ids start at 0, never fall, and end at 3.
All inputs are finite; a program needn't handle non-finite values.
Results may differ from a plain program's by a relative error of at most 0.02.
Values may be sent and summed in bfloat16 or wider, within the bound.
No kernel may reach another device: no remote copies, remote signals or barrier semaphores. Data moves between devices by JAX's collectives and lax.ppermute only.
A program may use at most 192 MiB of HBM per device.

v0:
```python
from functools import partial

import jax
import jax.numpy as jnp
from jax import lax
from jax.sharding import PartitionSpec as P

norm_eps = 1e-06
masked_score = -1e30
bucket_edges = (12, 16, 23, 32, 46, 64, 91)


def relative_bucket(offset):
    distance = jnp.abs(offset)
    far_bucket = jnp.zeros_like(distance) + 8
    for edge in bucket_edges:
        far_bucket = far_bucket + (distance >= edge).astype(jnp.int32)
    result = jnp.where(distance < 8, distance, far_bucket)
    return result + jnp.where(offset > 0, 16, 0)


def toeplitz_rows(vector, height, length):
    heads_here, span = vector.shape
    shifted = jnp.roll(vector, -(height - 1), axis=1)
    tiled = jnp.broadcast_to(shifted[:, None, :], (heads_here, height, span)).reshape(
        heads_here, height * span
    )
    tiled = tiled[:, : height * (span - 1)]
    return tiled.reshape(heads_here, height, span - 1)[:, :, :length]


def diagonal_sums(matrix):
    heads_here, height, length = matrix.shape
    span = height + length - 1
    padded = jnp.pad(matrix, ((0, 0), (0, 0), (0, span - 1 - length)))
    flat_rows = jnp.pad(padded.reshape(heads_here, height * (span - 1)), ((0, 0), (0, height)))
    sums = jnp.sum(flat_rows.reshape(heads_here, height, span), axis=1, dtype=jnp.float32)
    return jnp.roll(sums, height - 1, axis=1)


def block_scores(query_heads, key_heads, table, query_first, query_docs, key_docs, score_scale):
    height = query_heads.shape[0]
    length = key_heads.shape[0]
    raw = jnp.einsum("qhe,khe->hqk", query_heads, key_heads, preferred_element_type=jnp.float32)
    offsets = jnp.arange(height + length - 1, dtype=jnp.int32) - (height - 1) - query_first
    bucket_ids = jnp.arange(table.shape[0], dtype=jnp.int32)
    selector = (relative_bucket(offsets)[:, None] == bucket_ids[None, :]).astype(jnp.float32)
    vector = jnp.dot(selector, table, precision=lax.Precision.HIGHEST).T
    scores = raw * score_scale + toeplitz_rows(vector, height, length)
    allowed = (query_docs[:, None] == key_docs[None, :])[None]
    return (scores, allowed, selector)


def shards(
    tokens,
    grad_out,
    w_qkv,
    w_attn_out,
    rel_bias,
    gain_attn,
    gain_ffn,
    w_router,
    w_in,
    w_down,
    expert_ids,
    doc_ids,
):
    qkv_full, out_full, router_full, gain_one, gain_two = (
        lax.all_gather(w_qkv, ("fsdp", "ctx"), axis=0, tiled=True),
        lax.all_gather(w_attn_out, ("fsdp", "ctx"), axis=0, tiled=True),
        lax.all_gather(w_router, ("fsdp", "ctx"), axis=0, tiled=True),
        lax.all_gather(gain_attn, ("fsdp", "ctx"), axis=0, tiled=True),
        lax.all_gather(gain_ffn, ("fsdp", "ctx"), axis=0, tiled=True),
    )
    rows_dev, model_width = tokens.shape
    heads_here = rel_bias.shape[1]
    head_width = w_qkv.shape[2]
    head_size = head_width // heads_here
    score_scale = head_size ** (-0.5)
    expert_count = w_router.shape[1]
    capacity = 2 * rows_dev // expert_count
    tp_share = model_width // lax.axis_size("tp")
    column_start = lax.axis_index("tp") * tp_share
    block_rows = min(512, rows_dev)
    block_total = rows_dev // block_rows
    gain_one_f = gain_one.astype(jnp.float32)
    gain_two_f = gain_two.astype(jnp.float32)
    tokens_f = tokens.astype(jnp.float32)
    scale_one = lax.rsqrt(jnp.mean(tokens_f * tokens_f, axis=-1, keepdims=True) + norm_eps)
    hat_one = tokens_f * scale_one
    normed_one = (hat_one * gain_one_f).astype(jnp.bfloat16)
    qkv_local = jnp.einsum(
        "td,dch->tch", normed_one, qkv_full, preferred_element_type=jnp.float32
    ).astype(jnp.bfloat16)
    kv_all = lax.all_gather(qkv_local[:, 1:], "ctx", axis=0, tiled=True)
    seq_len = kv_all.shape[0]
    key_heads = kv_all[:, 0].reshape(seq_len, heads_here, head_size)
    value_heads = kv_all[:, 1].reshape(seq_len, heads_here, head_size)
    ctx_start = lax.axis_index("ctx") * rows_dev
    query_docs = lax.dynamic_slice_in_dim(doc_ids, ctx_start, rows_dev)
    mixed_list = []
    log_totals = []
    for block_index in range(block_total):
        first_row = block_index * block_rows
        query_heads = qkv_local[first_row : first_row + block_rows, 0].reshape(
            block_rows, heads_here, head_size
        )
        scores, allowed, selector = block_scores(
            query_heads,
            key_heads,
            rel_bias,
            ctx_start + first_row,
            query_docs[first_row : first_row + block_rows],
            doc_ids,
            score_scale,
        )
        row_peak = jnp.max(jnp.where(allowed, scores, masked_score), axis=-1, keepdims=True)
        weights = jnp.where(allowed, jnp.exp(scores - row_peak), 0.0)
        row_total = jnp.sum(weights, axis=-1, keepdims=True)
        attn_probs = (weights / row_total).astype(jnp.bfloat16)
        mixed_block = jnp.einsum(
            "hqk,khe->qhe", attn_probs, value_heads, preferred_element_type=jnp.float32
        )
        mixed_list.append(mixed_block.reshape(block_rows, head_width).astype(jnp.bfloat16))
        log_totals.append(row_peak + jnp.log(row_total))
    mixed_rows = jnp.concatenate(mixed_list, axis=0)
    attn_terms = jnp.einsum("te,de->td", mixed_rows, out_full, preferred_element_type=jnp.float32)
    hidden = tokens_f + lax.psum(attn_terms, "tp")
    scale_two = lax.rsqrt(jnp.mean(hidden * hidden, axis=-1, keepdims=True) + norm_eps)
    hat_two = hidden * scale_two
    normed_two = (hat_two * gain_two_f).astype(jnp.bfloat16)
    logits = jnp.dot(normed_two, router_full, preferred_element_type=jnp.float32)
    route = jax.nn.softmax(logits, axis=-1)
    chosen = expert_ids[:, 0]
    one_hot = (chosen[:, None] == jnp.arange(expert_count, dtype=jnp.int32)[None, :]).astype(
        jnp.int32
    )
    one_hot_f = one_hot.astype(jnp.float32)
    gate_value = jnp.sum(route * one_hot_f, axis=-1)
    earlier = jnp.cumsum(one_hot, axis=0) - one_hot
    slot_index = jnp.sum(earlier * one_hot, axis=-1)
    target = chosen * capacity + slot_index
    buffer = (
        jnp.zeros((expert_count * capacity, model_width), jnp.bfloat16).at[target].set(normed_two)
    )
    received = lax.all_to_all(
        buffer.reshape(expert_count, capacity, model_width),
        "fsdp",
        split_axis=0,
        concat_axis=1,
        tiled=True,
    )
    expert_inner = jnp.einsum("erd,edf->erf", received, w_in, preferred_element_type=jnp.float32)
    gelu_value, gelu_pull = jax.vjp(partial(jax.nn.gelu, approximate=False), expert_inner)
    active = gelu_value.astype(jnp.bfloat16)
    expert_terms = jnp.einsum("erf,edf->erd", active, w_down, preferred_element_type=jnp.float32)
    sent_back = lax.all_to_all(expert_terms, "fsdp", split_axis=1, concat_axis=0, tiled=True)
    token_terms = sent_back.reshape(expert_count * capacity, model_width)[target]
    returned = lax.psum_scatter(token_terms, "tp", scatter_dimension=1, tiled=True).astype(
        jnp.bfloat16
    )
    returned_f = returned.astype(jnp.float32)
    hidden_share = lax.dynamic_slice_in_dim(hidden, column_start, tp_share, 1)
    out_share = (hidden_share + gate_value[:, None] * returned_f).astype(jnp.bfloat16)
    cotangent = grad_out.astype(jnp.float32)
    cot_share = lax.dynamic_slice_in_dim(cotangent, column_start, tp_share, 1)
    gate_terms = jnp.sum(cot_share * returned_f, axis=-1)
    d_expert = (gate_value[:, None] * cotangent).astype(jnp.bfloat16)
    d_buffer = (
        jnp.zeros((expert_count * capacity, model_width), jnp.bfloat16).at[target].set(d_expert)
    )
    d_received = lax.all_to_all(
        d_buffer.reshape(expert_count, capacity, model_width),
        "fsdp",
        split_axis=0,
        concat_axis=1,
        tiled=True,
    )
    d_active = jnp.einsum("erd,edf->erf", d_received, w_down, preferred_element_type=jnp.float32)
    grad_down = jnp.einsum("erd,erf->edf", d_received, active, preferred_element_type=jnp.float32)
    d_inner = gelu_pull(d_active)[0].astype(jnp.bfloat16)
    grad_in = jnp.einsum("erd,erf->edf", received, d_inner, preferred_element_type=jnp.float32)
    d_rows = jnp.einsum("erf,edf->erd", d_inner, w_in, preferred_element_type=jnp.float32)
    rows_back = lax.all_to_all(d_rows, "fsdp", split_axis=1, concat_axis=0, tiled=True)
    token_grads = rows_back.reshape(expert_count * capacity, model_width)[target]
    d_normed_two, d_gate = lax.psum((token_grads, gate_terms), "tp")
    d_logits = (d_gate * gate_value)[:, None] * (one_hot_f - route)
    grad_router = jnp.dot(
        normed_two.T, d_logits, precision=lax.Precision.HIGHEST, preferred_element_type=jnp.float32
    )
    d_normed_two = d_normed_two + jnp.dot(
        d_logits, router_full.T, precision=lax.Precision.HIGHEST, preferred_element_type=jnp.float32
    )
    grad_gain_two = jnp.sum(d_normed_two * hat_two, axis=0)
    d_hat_two = d_normed_two * gain_two_f
    d_hidden = cotangent + scale_two * (
        d_hat_two - hat_two * jnp.mean(d_hat_two * hat_two, axis=-1, keepdims=True)
    )
    d_attn = d_hidden.astype(jnp.bfloat16)
    grad_attn_out = jnp.einsum("td,te->de", d_attn, mixed_rows, preferred_element_type=jnp.float32)
    d_mixed = jnp.einsum("td,de->te", d_attn, out_full, preferred_element_type=jnp.float32).astype(
        jnp.bfloat16
    )
    d_key_acc = jnp.zeros((seq_len, heads_here, head_size), jnp.float32)
    d_value_acc = jnp.zeros((seq_len, heads_here, head_size), jnp.float32)
    d_table = jnp.zeros((heads_here, rel_bias.shape[0]), jnp.float32)
    d_query_list = []
    for block_index in range(block_total):
        first_row = block_index * block_rows
        query_heads = qkv_local[first_row : first_row + block_rows, 0].reshape(
            block_rows, heads_here, head_size
        )
        scores, allowed, selector = block_scores(
            query_heads,
            key_heads,
            rel_bias,
            ctx_start + first_row,
            query_docs[first_row : first_row + block_rows],
            doc_ids,
            score_scale,
        )
        probs_full = jnp.where(allowed, jnp.exp(scores - log_totals[block_index]), 0.0)
        d_mixed_heads = d_mixed[first_row : first_row + block_rows].reshape(
            block_rows, heads_here, head_size
        )
        d_probs = jnp.einsum(
            "qhe,khe->hqk", d_mixed_heads, value_heads, preferred_element_type=jnp.float32
        )
        row_delta = jnp.sum(probs_full * d_probs, axis=-1, keepdims=True)
        d_scores = (probs_full * (d_probs - row_delta)).astype(jnp.bfloat16)
        d_query_block = (
            jnp.einsum("hqk,khe->qhe", d_scores, key_heads, preferred_element_type=jnp.float32)
            * score_scale
        )
        d_query_list.append(d_query_block.reshape(block_rows, head_width))
        d_key_acc = (
            d_key_acc
            + jnp.einsum("hqk,qhe->khe", d_scores, query_heads, preferred_element_type=jnp.float32)
            * score_scale
        )
        d_value_acc = d_value_acc + jnp.einsum(
            "hqk,qhe->khe",
            probs_full.astype(jnp.bfloat16),
            d_mixed_heads,
            preferred_element_type=jnp.float32,
        )
        d_table = d_table + jnp.dot(
            diagonal_sums(d_scores), selector, precision=lax.Precision.HIGHEST
        )
    d_query = jnp.concatenate(d_query_list, axis=0)
    d_key_values = jnp.stack(
        (d_key_acc.reshape(seq_len, head_width), d_value_acc.reshape(seq_len, head_width)), axis=1
    )
    d_kv_mine, grad_in_share, grad_down_share = (
        lax.psum_scatter(
            d_key_values.astype(jnp.bfloat16), "ctx", scatter_dimension=0, tiled=True
        ).astype(jnp.float32),
        lax.psum_scatter(
            grad_in.astype(jnp.bfloat16), "ctx", scatter_dimension=1, tiled=True
        ).astype(jnp.float32),
        lax.psum_scatter(
            grad_down.astype(jnp.bfloat16), "ctx", scatter_dimension=1, tiled=True
        ).astype(jnp.float32),
    )
    d_qkv = jnp.concatenate((d_query[:, None, :], d_kv_mine), axis=1).astype(jnp.bfloat16)
    grad_qkv = jnp.einsum("td,tch->dch", normed_one, d_qkv, preferred_element_type=jnp.float32)
    qkv_terms = jnp.einsum("tch,dch->td", d_qkv, qkv_full, preferred_element_type=jnp.float32)
    d_normed_one = lax.psum(qkv_terms.astype(jnp.bfloat16), "tp").astype(jnp.float32)
    grad_gain_one = jnp.sum(d_normed_one * hat_one, axis=0)
    d_hat_one = d_normed_one * gain_one_f
    d_tokens = d_hidden + scale_one * (
        d_hat_one - hat_one * jnp.mean(d_hat_one * hat_one, axis=-1, keepdims=True)
    )
    d_share = lax.dynamic_slice_in_dim(d_tokens, column_start, tp_share, 1)
    grad_qkv_s, grad_out_s, grad_table_s, grad_one_s, grad_two_s, grad_router_s = (
        lax.psum_scatter(grad_qkv, ("fsdp", "ctx"), scatter_dimension=0, tiled=True),
        lax.psum_scatter(grad_attn_out, ("fsdp", "ctx"), scatter_dimension=0, tiled=True),
        lax.psum_scatter(d_table.T, ("fsdp", "ctx"), scatter_dimension=0, tiled=True),
        lax.psum_scatter(grad_gain_one, ("fsdp", "ctx"), scatter_dimension=0, tiled=True),
        lax.psum_scatter(grad_gain_two, ("fsdp", "ctx"), scatter_dimension=0, tiled=True),
        lax.psum_scatter(grad_router, ("fsdp", "ctx"), scatter_dimension=0, tiled=True),
    )
    return (
        out_share,
        d_share,
        grad_qkv_s,
        grad_out_s,
        grad_table_s,
        grad_one_s,
        grad_two_s,
        grad_router_s,
        grad_in_share,
        grad_down_share,
    )


def solution(mesh):
    placed = (
        P(("fsdp", "ctx"), None),
        P(("fsdp", "ctx"), None),
        P(("fsdp", "ctx"), None, "tp"),
        P(("fsdp", "ctx"), "tp"),
        P(None, "tp"),
        P(("fsdp", "ctx")),
        P(("fsdp", "ctx")),
        P(("fsdp", "ctx"), None),
        P("fsdp", None, "tp"),
        P("fsdp", None, "tp"),
        P(("fsdp", "ctx"), None),
        P("fsdp"),
    )
    return jax.shard_map(
        shards,
        mesh=mesh,
        in_specs=placed,
        out_specs=(
            P(("fsdp", "ctx"), "tp"),
            P(("fsdp", "ctx"), "tp"),
            P(("fsdp", "ctx"), None, "tp"),
            P(("fsdp", "ctx"), "tp"),
            P(("fsdp", "ctx"), "tp"),
            P(("fsdp", "ctx")),
            P(("fsdp", "ctx")),
            P(("fsdp", "ctx"), None),
            P("fsdp", "ctx", "tp"),
            P("fsdp", "ctx", "tp"),
        ),
        check_vma=False,
    )
```

profile of v0, /device:TPU:0, one launch (start us, length us, event | category | flops | bytes accessed | tf_op | source)
XLA Modules:
  0.0 1398.3 jit_solution(13523432368881739372)
XLA Ops:
  10.9 15.7 %all-reduce.10 = (bf16[768]{0:T(1024)(128)(2,1)S(1)}, bf16[768]{0:T(1024)(128)(2,1)}) all-reduce(bf16[768]{0:T(1024)(128)(2,1)S(1)} %dynamic-update-slice, bf16[768]{0:T(1024)(128)(2,1)S(1)} %dynamic-update-slice.1), channel_id=1, replica_groups=mesh['fsdp'=4,'ctx'=2,'tp'=4] {'fsdp','ctx'}, use_global_device_ids=true, to_apply=%add.4 | all-reduce | flops 1536 | bytes 6144
  29.5 12.2 all_gather.19
  51.6 7.9 broadcast_in_dim.54
  59.5 23.5 %reshape.475 = f32[3930624]{0:T(1024)} reshape(f32[3,512,2559]{2,1,0:T(8,128)} %broadcast_in_dim.54) | data formatting | bytes 31444992
  83.0 22.6 %reshape.388 = f32[3,1310208]{1,0:T(4,128)} reshape(f32[3930624]{0:T(1024)} %reshape.475) | data formatting | bytes 31444992 | tf_op jit(solution)/shard_map/reshape | solution.py:25
  105.6 18.5 %slice.118 = f32[3,1309696]{1,0:T(4,128)} slice(f32[3,1310208]{1,0:T(4,128)} %reshape.388), slice={[0:3], [0:1309696]} | slice | bytes 31432704 | tf_op jit(solution)/shard_map/slice | solution.py:28
  124.1 44.6 %reshape.477 = f32[3929088]{0:T(1024)} reshape(f32[3,1309696]{1,0:T(4,128)} %slice.118) | data formatting | bytes 31432704
  168.7 24.7 %reshape.389 = f32[3,512,2558]{2,1,0:T(8,128)} reshape(f32[3929088]{0:T(1024)} %reshape.477) | data formatting | bytes 31432704 | tf_op jit(solution)/shard_map/reshape | solution.py:29
  193.4 7.5 broadcast_in_dim.58
  200.9 23.7 %reshape.471 = f32[3930624]{0:T(1024)} reshape(f32[3,512,2559]{2,1,0:T(8,128)} %broadcast_in_dim.58) | data formatting | bytes 31444992
  224.6 22.6 %reshape.390 = f32[3,1310208]{1,0:T(4,128)} reshape(f32[3930624]{0:T(1024)} %reshape.471) | data formatting | bytes 31444992 | tf_op jit(solution)/shard_map/reshape | solution.py:25
  247.1 18.2 %slice.123 = f32[3,1309696]{1,0:T(4,128)} slice(f32[3,1310208]{1,0:T(4,128)} %reshape.390), slice={[0:3], [0:1309696]} | slice | bytes 31432704 | tf_op jit(solution)/shard_map/slice | solution.py:28
  265.3 44.8 %reshape.473 = f32[3929088]{0:T(1024)} reshape(f32[3,1309696]{1,0:T(4,128)} %slice.123) | data formatting | bytes 31432704
  310.1 24.9 %reshape.391 = f32[3,512,2558]{2,1,0:T(8,128)} reshape(f32[3929088]{0:T(1024)} %reshape.473) | data formatting | bytes 31432704 | tf_op jit(solution)/shard_map/reshape | solution.py:29
  335.0 9.8 all_gather.21
  349.2 9.6 select_reduce_fusion.1
  358.8 7.6 fusion
  366.4 6.6 fusion.55
  375.6 6.3 select_reduce_fusion
  381.9 7.5 fusion.1
  389.5 6.6 fusion.54
  400.2 119.8 %all-reduce.15.cloned.1.call-done = f32[1024,768]{1,0:T(8,128)} async-done(((f32[1024,768]{1,0:T(8,128)}), f32[1024,768]{1,0:T(8,128)}) %all-reduce.15.cloned.1.call-update) | async-done | bytes 3145744 | tf_op jit(solution)/shard_map/psum | solution.py:128
  520.0 4.4 multiply_reduce_fusion.5
  524.4 8.6 scatter_custom_fusion
  533.0 40.7 %all_to_all.16 = bf16[4,512,768]{2,1,0:T(8,128)(2,1)S(1)} all-to-all(bf16[4,512,768]{2,1,0:T(8,128)(2,1)} %bitcast.148), channel_id=1, replica_groups=mesh['fsdp'=4,'ctx'=2,'tp'=4] {'fsdp'}, dimensions={0} | all-to-all | bytes 6291456 | tf_op jit(solution)/shard_map/all_to_all | solution.py:146
  573.7 18.1 %multiply_convert_fusion.2 = (bf16[2048,768]{1,0:T(8,128)(2,1)S(1)}, f32[2048,768]{1,0:T(8,128)}, f32[2048,768]{1,0:T(8,128)}) fusion(bf16[2048,768]{1,0:T(8,128)(2,1)S(1)} %bitcast.154, bf16[1,768,768]{2,1,0:T(8,128)(2,1)S(1)} %copy-done), kind=kOutput, calls=%fused_computation.33 | convolution fusion | flops 2518155264 | bytes 20054016 | tf_op jit(solution)/shard_map/erd,edf->erf/dot_general | solution.py:153
  594.5 35.0 %copy.40 = f32[1,2048,768]{2,0,1:T(1,128)} copy(f32[1,2048,768]{2,1,0:T(8,128)S(1)} %convolution_bitcast_fusion.1) | data formatting | bytes 12582912 | tf_op jit(solution)/shard_map/erf,edf->erd/dot_general | solution.py:156
  629.6 5.4 all-to-all-start.1
  635.0 71.0 %all-gather = bf16[8,96,4]{1,2,0:T(4,128)(2,1)S(1)} all-gather(bf16[1,96,4]{1,2,0:T(4,128)(2,1)S(1)} %bitcast.184), channel_id=1, replica_groups=mesh['fsdp'=4,'ctx'=2,'tp'=4] {'fsdp','ctx'}, dimensions={0}, use_global_device_ids=true | all-gather | bytes 6912 | tf_op jit(solution)/shard_map/all_gather | solution.py:71
  710.2 8.6 scatter_custom_fusion.1
  718.8 4.7 all-to-all-start.2
  723.6 5.8 copy.64
  729.3 8.7 gather_fusion
  741.6 19.2 %all-to-all-done.2 = bf16[4,512,768]{2,1,0:T(8,128)(2,1)} async-done(((bf16[4,512,768]{2,1,0:T(8,128)(2,1)}), bf16[4,512,768]{2,1,0:T(8,128)(2,1)}, u32[]{:S(2)}, u32[]{:S(2)}) %all-to-all-start.2) | async-done | bytes 3145760 | tf_op jit(solution)/shard_map/all_to_all | solution.py:172
  760.8 10.1 add_convert_fusion
  773.6 35.1 %copy.41 = f32[1,2048,768]{2,0,1:T(1,128)S(1)} copy(f32[1,2048,768]{2,1,0:T(8,128)S(1)} %convolution_bitcast_fusion) | data formatting | bytes 12582912 | tf_op jit(solution)/shard_map/erf,edf->erd/dot_general | solution.py:183
  808.7 73.3 %all_to_all.17 = f32[1,2048,768]{2,0,1:T(1,128)S(1)} all-to-all(f32[1,2048,768]{2,0,1:T(1,128)S(1)} %copy.41), channel_id=1, replica_groups=mesh['fsdp'=4,'ctx'=2,'tp'=4] {'fsdp'}, dimensions={1} | all-to-all | bytes 12582912 | tf_op jit(solution)/shard_map/all_to_all | solution.py:184
  885.0 8.7 gather_fusion.1
  901.9 10.3 psum.30
  912.2 100.5 %all-reduce.17.cloned.1.call-done = f32[1024,768]{1,0:T(8,128)} async-done(((f32[1024,768]{1,0:T(8,128)}), f32[1024,768]{1,0:T(8,128)}) %all-reduce.17.cloned.1.call-update) | async-done | bytes 3145744 | tf_op jit(solution)/shard_map/psum | solution.py:186
  1012.8 6.3 multiply_reduce_fusion.2
  1026.9 10.5 multiply_reduce_fusion
  1037.4 7.2 multiply_reduce_fusion.1
  1047.3 17.7 %multiply_convert_fusion = (bf16[3,512,2048]{2,1,0:T(8,128)(2,1)}, bf16[3,512,2048]{2,1,0:T(8,128)(2,1)}) fusion(f32[3,512,2048]{2,1,0:T(8,128)} %get-tuple-element.80, f32[3,512,2048]{2,1,0:T(8,128)} %get-tuple-element.70, f32[3,512]{1,0:T(4,128)S(1)} %get-tuple-element.79, f32[3,512]{1,0:T(4,128)S(1)} %log_add_fusion, ...), kind=kLoop, calls=%fused_computation.6 | loop fusion | flops 31457280 | bytes 65036288 | tf_op jit(solution)/shard_map/convert_element_type | solution.py:230
  1065.0 4.2 fusion.133
  1072.4 6.5 fusion.41
  1079.0 6.8 fusion.40
  1088.4 5.3 fusion.53
  1093.7 4.8 fusion.52
  1108.6 6.6 pad.16
  1115.2 15.6 %reshape.479 = bf16[3929088]{0:T(1024)(128)(2,1)} reshape(bf16[3,512,2558]{2,1,0:T(8,128)(2,1)} %pad.16) | data formatting | bytes 15716352
  1130.8 10.4 reshape.406
  1144.9 11.9 pad_convert_fusion
  1156.8 6.7 pad.14
  1163.5 15.6 %reshape.483 = bf16[3929088]{0:T(1024)(128)(2,1)} reshape(bf16[3,512,2558]{2,1,0:T(8,128)(2,1)} %pad.14) | data formatting | bytes 15716352
  1179.1 10.6 reshape.405
  1192.8 12.2 pad_convert_fusion.1
  1205.0 45.2 %reshape.481 = f32[3930624]{0:T(1024)} reshape(f32[3,1310208]{1,0:T(4,128)} %pad_convert_fusion) | data formatting | bytes 31444992
  1250.2 23.6 %reshape.408 = f32[3,512,2559]{2,1,0:T(8,128)} reshape(f32[3930624]{0:T(1024)} %reshape.481) | data formatting | bytes 31444992 | tf_op jit(solution)/shard_map/convert_element_type | solution.py:37
  1273.8 6.3 reduce_sum.160
  1280.1 44.7 %reshape.485 = f32[3930624]{0:T(1024)} reshape(f32[3,1310208]{1,0:T(4,128)} %pad_convert_fusion.1) | data formatting | bytes 31444992
  1324.9 23.3 %reshape.407 = f32[3,512,2559]{2,1,0:T(8,128)} reshape(f32[3930624]{0:T(1024)} %reshape.485) | data formatting | bytes 31444992 | tf_op jit(solution)/shard_map/convert_element_type | solution.py:37
  1348.3 6.4 reduce_sum.159
  1365.2 24.2 %all-reduce.9 = (f32[32,3]{0,1:T(4,128)S(1)}, f32[768]{0:T(1024)S(1)}, f32[768]{0:T(1024)S(1)}) all-reduce(f32[32,3]{0,1:T(4,128)S(1)} %fusion.56, f32[768]{0:T(1024)S(1)} %get-tuple-element.42, f32[768]{0:T(1024)S(1)} %copy-done.35), channel_id=6, replica_groups=mesh['fsdp'=4,'ctx'=2,'tp'=4] {'fsdp','ctx'}, use_global_device_ids=true, to_apply=%region_29.30.clone | all-reduce | flops 1632 | bytes 13056
  (242 shorter events, 95.0 us)
Async XLA Ops:
  7.2 566.5 %copy-start = (bf16[1,768,768]{2,1,0:T(8,128)(2,1)S(1)}, bf16[1,768,768]{2,1,0:T(8,128)(2,1)}, u32[]{:S(2)}) copy-start(bf16[1,768,768]{2,1,0:T(8,128)(2,1)} %param.20) | copy-start | bytes 3538948
  7.2 340.0 %all-gather.3.cloned.1.call-start = ((), (), s32[]{:S(2)}) async-start(), calls=%async_computation.11 | async-start | bytes 2359296 | tf_op jit(solution)/shard_map/all_gather | solution.py:95
  26.6 20.0 %copy-start.36 = (f32[768]{0:T(1024)}, f32[768]{0:T(1024)S(1)}, u32[]{:S(2)}) copy-start(f32[768]{0:T(1024)S(1)} %convert_element_type.255) | copy-start | bytes 9220
  28.4 18.2 %copy-start.30 = (f32[1024]{0:T(1024)}, f32[1024]{0:T(1024)S(1)}, u32[]{:S(2)}) copy-start(f32[1024]{0:T(1024)S(1)} %add_rsqrt_fusion.1) | copy-start | bytes 12292
  43.8 4.1 copy-start.46
  47.8 472.2 %all-reduce.15.cloned.1.call-start = ((), (), s32[]{:S(2)}) async-start(), calls=%async_computation.12 | async-start | bytes 6291456 | tf_op jit(solution)/shard_map/psum | solution.py:128
  51.5 8.0 copy-start.29
  168.7 24.7 %slice-start.12 = ((f32[3,2559]{1,0:T(4,128)}), f32[3,511]{1,0:T(4,128)S(1)}, s32[]{:S(2)}) async-start(f32[3,2559]{1,0:T(4,128)} %copy-done.29), calls=%async_computation.34 | async-start | bytes 16384 | tf_op jit(solution)/shard_map/jit(_roll_static)/slice | solution.py:24
  310.1 24.9 %copy-start.34 = (s32[2048]{0:T(1024)S(1)}, s32[2048]{0:T(1024)}, u32[]{:S(2)}) copy-start(s32[2048]{0:T(1024)} %param.23) | copy-start | bytes 24580
  310.1 24.9 %copy-start.28 = (bf16[96,192]{1,0:T(8,128)(2,1)S(1)}, bf16[96,192]{1,0:T(8,128)(2,1)}, u32[]{:S(2)}) copy-start(bf16[96,192]{1,0:T(8,128)(2,1)} %param.15) | copy-start | bytes 110596
  345.5 27.5 %copy-start.16 = (bf16[512,1,192]{0,2,1:T(8,128)(2,1)}, bf16[512,1,192]{0,2,1:T(8,128)(2,1)S(1)}, u32[]{:S(2)}) copy-start(bf16[512,1,192]{0,2,1:T(8,128)(2,1)S(1)} %get-tuple-element.58) | copy-start | bytes 589828
  347.2 19.2 %copy-start.3 = (pred[512,2048]{1,0:T(8,128)(4,1)}, pred[512,2048]{1,0:T(8,128)(4,1)S(1)}, u32[]{:S(2)}) copy-start(pred[512,2048]{1,0:T(8,128)(4,1)S(1)} %get-tuple-element.63) | copy-start | bytes 3145732
  349.1 23.9 %copy-start.6 = (bf16[2048,1,192]{0,2,1:T(8,128)(2,1)}, bf16[2048,1,192]{0,2,1:T(8,128)(2,1)S(1)}, u32[]{:S(2)}) copy-start(bf16[2048,1,192]{0,2,1:T(8,128)(2,1)S(1)} %get-tuple-element.55) | copy-start | bytes 2359300
  349.1 40.3 %copy-start.11 = (bf16[2048,1,192]{0,2,1:T(8,128)(2,1)}, bf16[2048,1,192]{0,2,1:T(8,128)(2,1)S(1)}, u32[]{:S(2)}) copy-start(bf16[2048,1,192]{0,2,1:T(8,128)(2,1)S(1)} %get-tuple-element.56) | copy-start | bytes 2359300
  358.8 7.6 copy-start.26
  366.3 6.7 copy-start.32
  366.3 6.7 slice-start.6
  366.4 7.1 slice-start.7
  366.4 8.3 slice-start.8
  366.4 9.2 slice-start.9
  373.0 23.1 %copy-start.20 = (bf16[3,64,512]{2,1,0:T(8,128)(2,1)}, bf16[3,64,512]{2,1,0:T(8,128)(2,1)S(1)}, u32[]{:S(2)}) copy-start(bf16[3,64,512]{2,1,0:T(8,128)(2,1)S(1)} %fusion.55) | copy-start | bytes 589828
  389.5 6.7 copy-start.13
  396.1 128.3 %copy-start.22 = (bf16[3,64,512]{2,1,0:T(8,128)(2,1)}, bf16[3,64,512]{2,1,0:T(8,128)(2,1)S(1)}, u32[]{:S(2)}) copy-start(bf16[3,64,512]{2,1,0:T(8,128)(2,1)S(1)} %fusion.54) | copy-start | bytes 589828
  573.7 18.2 %copy-start.14 = (bf16[4,512,768]{2,1,0:T(8,128)(2,1)}, bf16[4,512,768]{2,1,0:T(8,128)(2,1)S(1)}, u32[]{:S(2)}) copy-start(bf16[4,512,768]{2,1,0:T(8,128)(2,1)S(1)} %all_to_all.16) | copy-start | bytes 9437188
  573.7 18.2 %copy-start.44 = (bf16[1,768,768]{2,1,0:T(8,128)(2,1)S(1)}, bf16[1,768,768]{2,1,0:T(8,128)(2,1)}, u32[]{:S(2)}) copy-start(bf16[1,768,768]{2,1,0:T(8,128)(2,1)} %param.21) | copy-start | bytes 3538948
  629.6 5.5 copy-start.43
  629.6 89.2 %all-to-all-start.1 = ((f32[1,2048,768]{2,0,1:T(1,128)}), f32[1,2048,768]{2,0,1:T(1,128)}, u32[]{:S(2)}, u32[]{:S(2)}) async-start(f32[1,2048,768]{2,0,1:T(1,128)} %copy.40), calls=%async_computation.1 | async-start | bytes 12582912 | tf_op jit(solution)/shard_map/all_to_all | solution.py:157
  718.8 42.0 %all-to-all-start.2 = ((bf16[4,512,768]{2,1,0:T(8,128)(2,1)}), bf16[4,512,768]{2,1,0:T(8,128)(2,1)}, u32[]{:S(2)}, u32[]{:S(2)}) async-start(bf16[4,512,768]{2,1,0:T(8,128)(2,1)} %bitcast.147), calls=%async_computation.2 | async-start | bytes 6291456 | tf_op jit(solution)/shard_map/all_to_all | solution.py:172
  723.5 173.6 %reduce-scatter.23.cloned.1.call-start = ((), (), s32[]{:S(2)}) async-start(), calls=%async_computation.20 | async-start | bytes 3932160
  741.5 271.2 %all-reduce.17.cloned.1.call-start = ((), (), s32[]{:S(2)}) async-start(), calls=%async_computation.13 | async-start | bytes 6291456 | tf_op jit(solution)/shard_map/psum | solution.py:186
  893.7 205.0 %reduce-scatter.13.cloned.1.call-start = ((), (), s32[]{:S(2)}) async-start(), calls=%async_computation.14 | async-start | bytes 2359296 | tf_op jit(solution)/shard_map/reduce_scatter | solution.py:255
  1012.8 11.4 slice-start.3
  1012.8 11.4 slice-start.4
  1019.1 5.1 slice-start.5
  1024.2 13.2 slice-start
  1026.8 10.6 slice-start.1
  1026.8 10.6 slice-start.2
  1026.8 10.6 copy-start.4
  1047.3 17.7 %copy-start.18 = (bf16[512,1,192]{0,2,1:T(8,128)(2,1)S(1)}, bf16[512,1,192]{0,2,1:T(8,128)(2,1)}, u32[]{:S(2)}) copy-start(bf16[512,1,192]{0,2,1:T(8,128)(2,1)} %get-tuple-element.57) | copy-start | bytes 589828
  1065.0 4.6 copy-start.2
  1065.0 4.6 copy-start.17
  1072.1 32.1 %reduce-scatter.21.cloned.1.call-start = ((), (), s32[]{:S(2)}) async-start(), calls=%async_computation.19 | async-start | bytes 1769472 | tf_op jit(solution)/shard_map/reduce_scatter | solution.py:261
  1079.0 7.0 copy-start.10
  1079.0 9.4 copy-start.7
  1079.0 27.4 %reduce-scatter.19.cloned.1.call-start = ((), (), s32[]{:S(2)}) async-start(), calls=%async_computation.18 | async-start | bytes 1769472 | tf_op jit(solution)/shard_map/reduce_scatter | solution.py:258
  1085.9 271.2 %reduce-scatter.25.cloned.1.call-start = ((), (), s32[]{:S(2)}) async-start(), calls=%async_computation.21 | async-start | bytes 442368
  1088.4 10.3 copy-start.19
  1098.6 260.1 %all-reduce.19.cloned.1.call-start = ((), (), s32[]{:S(2)}) async-start(), calls=%async_computation.15 | async-start | bytes 3145728 | tf_op jit(solution)/shard_map/psum | solution.py:268
  1102.4 288.9 %reduce-scatter.17.cloned.1.call-start = ((), (), s32[]{:S(2)}) async-start(), calls=%async_computation.17 | async-start | bytes 884736 | tf_op jit(solution)/shard_map/reduce_scatter | solution.py:277
  1130.8 10.4 copy-start.21
  1130.8 10.4 copy-start.23
  1144.6 246.7 %reduce-scatter.15.cloned.1.call-start = ((), (), s32[]{:S(2)}) async-start(), calls=%async_computation.16 | async-start | bytes 2654208 | tf_op jit(solution)/shard_map/reduce_scatter | solution.py:276
  1179.1 10.6 copy-start.8
  1179.1 10.6 copy-start.31
  1179.1 10.6 copy-start.37
  1179.1 10.6 copy-start.45
  1280.1 44.7 %copy-start.24 = (f32[3,2559]{1,0:T(4,128)}, f32[3,2559]{1,0:T(4,128)S(1)}, u32[]{:S(2)}) copy-start(f32[3,2559]{1,0:T(4,128)S(1)} %reduce_sum.160) | copy-start | bytes 92128
  1348.2 6.5 copy-start.15
  1348.2 7.4 slice-start.10
  1348.2 7.4 slice-start.11
  1348.2 7.4 copy-start.41
  1348.2 8.1 copy-start.39
  1357.1 34.3 %copy-start.1 = (bf16[1,768,768]{2,1,0:T(8,128)(2,1)S(1)}, bf16[1,768,768]{2,1,0:T(8,128)(2,1)}, u32[]{:S(2)}) copy-start(bf16[1,768,768]{2,1,0:T(8,128)(2,1)} %param.20) | copy-start | bytes 3538948
  1358.6 6.6 copy-start.35
  (11 other events, 25.8 us)
Sparse Core Ops, SparseCore 0:
  47.9 10.0 all-gather.2
  398.6 121.3 all-reduce.14
  741.7 59.9 reduce-scatter.22
  893.8 118.9 all-reduce.16
  1072.2 8.0 reduce-scatter.12
  1083.1 9.8 reduce-scatter.20
  1095.8 9.8 reduce-scatter.18
  1109.6 35.0 reduce-scatter.24
  1147.2 69.0 all-reduce.18
  1220.2 34.0 reduce-scatter.16
  1258.6 42.4 reduce-scatter.14
where the time goes:
time: 1410 us; the launch traced here: 1400 us
  local copies, waits for them, and re-layouts  608 us (43%)
  blocking collectives  257 us (18%)
  waiting for transfers between devices  240 us (17%)
  matrix products  145 us (10%)
  other arithmetic  120 us (9%)
  between operations  17.3 us (1%)
    unnamed x144, local copies, waits for them, and re-layouts  286 us
    psum x1, waiting for transfers between devices, shards(): hidden = tokens_f + lax.psum(attn_terms, 'tp')  120 us
    psum x1, waiting for transfers between devices, shards(): d_normed_two, d_gate = lax.psum((token_grads, gate_terms), 'tp')  101 us
    all_to_all x1, blocking collectives, shards(): lax.all_to_all(d_rows, 'fsdp', split_axis=1, concat_axis=0, tiled=True)  73.3 us
    all_gather x1, blocking collectives, shards(): lax.all_gather(w_router, ('fsdp', 'ctx'), axis=0, tiled=True)  71 us
    reshape x2, local copies, waits for them, and re-layouts, toeplitz_rows(): return tiled.reshape(heads_here, height, span - 1)[:, :, :length]  49.6 us
    convert_element_type x2, local copies, waits for them, and re-layouts, diagonal_sums(): jnp.sum(flat_rows.reshape(heads_here, height, span), axis=1, dtype=jnp.fl...  46.9 us
    reshape x2, local copies, waits for them, and re-layouts, toeplitz_rows(): jnp.broadcast_to(shifted[:, None, :], (heads_here, height, span))  45.1 us
  transfers between devices with their start and end apart: 13, of which 3 were waited for; matrix products, arithmetic and copies ran while one was open for 49% of the time, Pallas kernels for 0%

commit v1 on v0

v1 whole, which is shorter than its diff:
```python
from functools import partial

import jax
import jax.numpy as jnp
from jax import lax
from jax.experimental import pallas as pl
from jax.experimental.pallas import tpu as pltpu
from jax.sharding import PartitionSpec as P

norm_eps = 1e-06
bucket_edges = (12, 16, 23, 32, 46, 64, 91)
LANES = 128
TILE = 128
MIB = 1024 * 1024
NT = (((1,), (1,)), ((), ()))
TN = (((0,), (0,)), ((), ()))


BQ = 256
BK = 256
HD = 64
NEG = -1e30
FLOOR = -1e28
F32 = jnp.float32
BF = jnp.bfloat16


def call(kernel, grid, in_specs, out_specs, out_shape, scratch=(), prefetch=0, vmem=48, name=None):
    return pl.pallas_call(
        kernel,
        grid_spec=pltpu.PrefetchScalarGridSpec(
            num_scalar_prefetch=prefetch,
            grid=grid,
            in_specs=in_specs,
            out_specs=out_specs,
            scratch_shapes=list(scratch),
        ),
        out_shape=out_shape,
        compiler_params=pltpu.CompilerParams(
            dimension_semantics=("arbitrary",) * len(grid), vmem_limit_bytes=vmem * MIB
        ),
        name=name,
    )


def whole(*shape):
    return pl.BlockSpec(shape, lambda *_: (0,) * len(shape))


def shaped(shape, dtype):
    return jax.ShapeDtypeStruct(shape, dtype)


def relative_bucket(offset):
    distance = jnp.abs(offset)
    far_bucket = jnp.zeros_like(distance) + 8
    for edge in bucket_edges:
        far_bucket = far_bucket + (distance >= edge).astype(jnp.int32)
    result = jnp.where(distance < 8, distance, far_bucket)
    return result + jnp.where(offset > 0, 16, 0)


def dot(a, b, dims=None):
    if dims is None:
        return jnp.dot(a, b, preferred_element_type=F32)
    return lax.dot_general(a, b, dims, preferred_element_type=F32)


def to_row(column):
    n = column.shape[0]
    return jnp.broadcast_to(column, (n, LANES)).T[0:1, :]


def to_column(row):
    n = row.shape[1]
    return jnp.broadcast_to(row, (LANES, n)).T[:, 0:1]


def split3(x):
    hi = x.astype(BF)
    rest = x - hi.astype(F32)
    mid = rest.astype(BF)
    low = (rest - mid.astype(F32)).astype(BF)
    return hi, mid, low


def key_side(docs_col, rows):
    lane = lax.broadcasted_iota(jnp.int32, (rows, HD), 1)
    same = (docs_col == lane).astype(F32)
    ones = jnp.where((lane >= 4) & (lane < 7), 1.0, 0.0)
    return jnp.where(lane < 4, same, ones)


def query_side(docs_row, cols, tail):
    row = lax.broadcasted_iota(jnp.int32, (HD, cols), 0)
    other = jnp.where((row < 4) & (docs_row != row), NEG, 0.0)
    if tail is None:
        return other.astype(BF)
    hi, mid, low = (t.astype(F32) for t in split3(tail))
    part = jnp.where(row == 4, hi, jnp.where(row == 5, mid, jnp.where(row == 6, low, 0.0)))
    return jnp.where(row < 4, other, part).astype(BF)


def shifted(x, by):
    return x if by == 0 else pltpu.roll(x, x.shape[1] - by, 1)


def diagonal_sums(tile):
    total = jnp.zeros((8, 2 * BQ), F32)
    for first in range(0, BK, 8):
        strip = tile[first : first + 8, :]
        total = total + shifted(jnp.concatenate([strip, jnp.zeros((8, BQ), F32)], axis=1), first)
    result = jnp.zeros((1, 2 * BQ), F32)
    for r in range(8):
        result = result + shifted(total, r)[r : r + 1, :]
    return result


def ones_rows(cols):
    return jnp.where(lax.broadcasted_iota(jnp.int32, (16, cols), 0) == 0, 1.0, 0.0).astype(BF)


def fwd_kernel(heads, info, far, qkv_all, q_ref, dcol, drow, band, mixed_ref, low_ref, lse_ref, k_aug, v_t):
    i = pl.program_id(0)
    seq = qkv_all.shape[0]
    width = heads * HD

    @pl.when(i == 0)
    def _():
        for r in range(seq // BK):
            rows = pl.ds(r * BK, BK)
            side = key_side(dcol[rows, :], BK).astype(BF)
            vt = qkv_all[rows, 2 * width : 3 * width].astype(F32).T.astype(BF)
            for h in range(heads):
                k = qkv_all[rows, width + h * HD : width + (h + 1) * HD]
                k_aug[h, rows, :] = jnp.concatenate([k, side], axis=1)
                v_t[h, 0:HD, rows] = vt[h * HD : (h + 1) * HD, :]
                v_t[h, HD : HD + 16, rows] = ones_rows(BK)

    qb = info[0] + i
    lo = info[1 + i]
    hi = info[1 + pl.num_programs(0) + i]
    qt = (q_ref[...].astype(F32) * (HD**-0.5)).T.astype(BF)
    side = query_side(drow[...], BQ, None)
    q_aug = [jnp.concatenate([qt[h * HD : (h + 1) * HD, :], side], axis=0) for h in range(heads)]

    def step(kb, carry, bias_of):
        rows = pl.ds(pl.multiple_of(kb * BK, BK), BK)
        out = []
        for h in range(heads):
            peak, acc = carry[h]
            s = jnp.dot(k_aug[h, rows, :], q_aug[h], preferred_element_type=F32)
            s = s + bias_of(h, kb)
            new = jnp.maximum(peak, jnp.max(s, axis=0, keepdims=True))
            p = jnp.exp(s - new).astype(BF)
            acc = acc * jnp.exp(peak - new) + jnp.dot(v_t[h, :, rows], p, preferred_element_type=F32)
            out.append((new, acc))
        return tuple(out)

    carry = tuple(
        (jnp.full((1, BQ), FLOOR, F32), jnp.zeros((HD + 16, BQ), F32)) for _ in range(heads)
    )
    carry = lax.fori_loop(lo, jnp.minimum(hi, qb - 1), lambda kb, c: step(kb, c, lambda h, _: far[0, h]), carry)
    carry = lax.fori_loop(
        jnp.maximum(lo, qb - 1),
        jnp.minimum(hi, qb + 2),
        lambda kb, c: step(kb, c, lambda h, t: band[h, t - qb + 1]),
        carry,
    )
    carry = lax.fori_loop(jnp.maximum(lo, qb + 2), hi, lambda kb, c: step(kb, c, lambda h, _: far[1, h]), carry)
    for h in range(heads):
        peak, acc = carry[h]
        total = acc[HD : HD + 1, :]
        mixed = acc[0:HD, :] / total
        mixed_ref[h * HD : (h + 1) * HD, :] = mixed
        low_ref[h * HD : (h + 1) * HD, :] = mixed.astype(BF)
        lse_ref[h : h + 1, :] = peak + jnp.log(total)


def attention_fwd(info, far, qkv_all, dcol, drow, band, rows):
    seq, cols = qkv_all.shape
    width = cols // 3
    heads = width // HD
    steps = rows // BQ
    full = lambda shape: pl.BlockSpec(shape, lambda i, info: (0,) * len(shape))
    return pl.pallas_call(
        partial(fwd_kernel, heads),
        grid_spec=pltpu.PrefetchScalarGridSpec(
            num_scalar_prefetch=1,
            grid=(steps,),
            in_specs=[
                pl.BlockSpec(memory_space=pltpu.SMEM),
                full((seq, cols)),
                pl.BlockSpec((BQ, width), lambda i, info: (info[0] + i, 0)),
                full((seq, 1)),
                pl.BlockSpec((1, BQ), lambda i, info: (0, info[0] + i)),
                full((heads, 3, BK, BQ)),
            ],
            out_specs=[
                pl.BlockSpec((width, BQ), lambda i, info: (0, i)),
                pl.BlockSpec((width, BQ), lambda i, info: (0, i)),
                pl.BlockSpec((heads, BQ), lambda i, info: (0, i)),
            ],
            scratch_shapes=[
                pltpu.VMEM((heads, seq, 2 * HD), BF),
                pltpu.VMEM((heads, HD + 16, seq), BF),
            ],
        ),
        out_shape=[
            jax.ShapeDtypeStruct((width, rows), F32),
            jax.ShapeDtypeStruct((width, rows), BF),
            jax.ShapeDtypeStruct((heads, rows), F32),
        ],
        compiler_params=pltpu.CompilerParams(
            dimension_semantics=("arbitrary",), vmem_limit_bytes=40 * 1024 * 1024
        ),
        name="attention_fwd",
    )(info, far, qkv_all, qkv_all[:, 0:width], dcol, drow, band)


def bwd_kernel(
    heads, info, far, qkv_all, q_ref, dcol, drow, band, mixed_ref, lse_ref, dmix_ref,
    dq_ref, dkv_ref, skew_ref, side_ref, k_aug, v_aug, k_t, near_acc, dkv_acc,
):
    i = pl.program_id(0)
    seq = qkv_all.shape[0]
    width = heads * HD

    @pl.when(i == 0)
    def _():
        near_acc[...] = jnp.zeros_like(near_acc)
        dkv_acc[...] = jnp.zeros_like(dkv_acc)
        side_ref[...] = jnp.zeros_like(side_ref)
        for r in range(seq // BK):
            rows = pl.ds(r * BK, BK)
            side = key_side(dcol[rows, :], BK).astype(BF)
            lane = lax.broadcasted_iota(jnp.int32, (BK, HD), 1)
            ones = jnp.where(lane < 3, 1.0, 0.0).astype(BF)
            kt = qkv_all[rows, width : 2 * width].astype(F32).T.astype(BF)
            for h in range(heads):
                k = qkv_all[rows, width + h * HD : width + (h + 1) * HD]
                v = qkv_all[rows, 2 * width + h * HD : 2 * width + (h + 1) * HD]
                k_aug[h, rows, :] = jnp.concatenate([k, side], axis=1)
                v_aug[h, rows, :] = jnp.concatenate([v, ones], axis=1)
                k_t[h, 0:HD, rows] = kt[h * HD : (h + 1) * HD, :]
                k_t[h, HD : HD + 16, rows] = ones_rows(BK)

    qb = info[0] + i
    lo = info[1 + i]
    hi = info[1 + pl.num_programs(0) + i]
    q_scaled = q_ref[...].astype(F32) * (HD**-0.5)
    qt = q_scaled.T.astype(BF)
    q_rows = q_scaled.astype(BF)
    dmix_t = dmix_ref[...].astype(F32)
    dmix_rows = dmix_t.T.astype(BF)
    zero = jnp.zeros((BQ, HD), BF)
    row = lax.broadcasted_iota(jnp.int32, (HD, BQ), 0)
    q_aug, d_aug, rhs = [], [], []
    for h in range(heads):
        cols = slice(h * HD, (h + 1) * HD)
        lse = lse_ref[h : h + 1, :]
        kinds = []
        for tail in (far[0, h] - lse, -lse, far[1, h] - lse):
            kinds.append(jnp.concatenate([qt[cols, :], query_side(drow[...], BQ, tail)], axis=0))
        q_aug.append(kinds)
        delta = -jnp.sum(dmix_t[cols, :] * mixed_ref[cols, :], axis=0, keepdims=True)
        a, b, c = (t.astype(F32) for t in split3(delta))
        part = jnp.where(row == 0, a, jnp.where(row == 1, b, jnp.where(row == 2, c, 0.0)))
        d_aug.append(jnp.concatenate([dmix_t[cols, :].astype(BF), part.astype(BF)], axis=0))
        top = jnp.concatenate([dmix_rows[:, cols], zero], axis=1)
        low = jnp.concatenate([zero, q_rows[:, cols]], axis=1)
        rhs.append(jnp.concatenate([top, low], axis=0))

    def step(kb, carry, kind):
        rows = pl.ds(pl.multiple_of(kb * BK, BK), BK)
        out = []
        for h in range(heads):
            s = jnp.dot(k_aug[h, rows, :], q_aug[h][kind], preferred_element_type=F32)
            if kind == 1:
                s = s + band[h, kb - qb + 1]
            p = jnp.exp(s)
            dp = jnp.dot(v_aug[h, rows, :], d_aug[h], preferred_element_type=F32)
            ds = p * dp
            ds_low = ds.astype(BF)
            if kind == 1:
                near_acc[h, kb - qb + 1] = near_acc[h, kb - qb + 1] + ds_low.astype(F32)
            both = jnp.concatenate([p.astype(BF), ds_low], axis=1)
            dkv_acc[h, rows, :] += jnp.dot(both, rhs[h], preferred_element_type=F32)
            out.append(carry[h] + jnp.dot(k_t[h, :, rows], ds_low, preferred_element_type=F32))
        return tuple(out)

    zero_dq = jnp.zeros((HD + 16, BQ), F32)
    left = lax.fori_loop(lo, jnp.minimum(hi, qb - 1), lambda kb, c: step(kb, c, 0), (zero_dq,) * heads)
    near = lax.fori_loop(
        jnp.maximum(lo, qb - 1), jnp.minimum(hi, qb + 2), lambda kb, c: step(kb, c, 1), left
    )
    last = lax.fori_loop(jnp.maximum(lo, qb + 2), hi, lambda kb, c: step(kb, c, 2), near)
    for h in range(heads):
        dq_ref[h * HD : (h + 1) * HD, :] = (last[h][0:HD, :] * (HD**-0.5)).astype(BF)
        side_ref[2 * h : 2 * h + 1, :] += left[h][HD : HD + 1, :]
        side_ref[2 * h + 1 : 2 * h + 2, :] += last[h][HD : HD + 1, :] - near[h][HD : HD + 1, :]

    @pl.when(i == pl.num_programs(0) - 1)
    def _():
        for h in range(heads):
            for t in range(3):
                skew_ref[3 * h + t : 3 * h + t + 1, :] = diagonal_sums(near_acc.at[h, t])
        for r in range(seq // BK):
            rows = pl.ds(r * BK, BK)
            acc = [dkv_acc[h, rows, :] for h in range(heads)]
            dk = [a[:, HD : 2 * HD] for a in acc]
            dv = [a[:, 0:HD] for a in acc]
            dkv_ref[rows, :] = jnp.concatenate(dk + dv, axis=1).astype(BF)


def attention_bwd(info, far, qkv_all, dcol, drow, band, mixed, lse, dmix, rows):
    seq, cols = qkv_all.shape
    width = cols // 3
    heads = width // HD
    steps = rows // BQ
    full = lambda shape: pl.BlockSpec(shape, lambda i, info: (0,) * len(shape))
    return pl.pallas_call(
        partial(bwd_kernel, heads),
        grid_spec=pltpu.PrefetchScalarGridSpec(
            num_scalar_prefetch=1,
            grid=(steps,),
            in_specs=[
                pl.BlockSpec(memory_space=pltpu.SMEM),
                full((seq, cols)),
                pl.BlockSpec((BQ, width), lambda i, info: (info[0] + i, 0)),
                full((seq, 1)),
                pl.BlockSpec((1, BQ), lambda i, info: (0, info[0] + i)),
                full((heads, 3, BK, BQ)),
                pl.BlockSpec((width, BQ), lambda i, info: (0, i)),
                pl.BlockSpec((heads, BQ), lambda i, info: (0, i)),
                pl.BlockSpec((None, width, BQ), lambda i, info: (i, 0, 0)),
            ],
            out_specs=[
                pl.BlockSpec((width, BQ), lambda i, info: (0, i)),
                full((seq, 2 * width)),
                full((16, 2 * BK)),
                full((8, BQ)),
            ],
            scratch_shapes=[
                pltpu.VMEM((heads, seq, 2 * HD), BF),
                pltpu.VMEM((heads, seq, 2 * HD), BF),
                pltpu.VMEM((heads, HD + 16, seq), BF),
                pltpu.VMEM((heads, 3, BK, BQ), F32),
                pltpu.VMEM((heads, seq, 2 * HD), F32),
            ],
        ),
        out_shape=[
            jax.ShapeDtypeStruct((width, rows), BF),
            jax.ShapeDtypeStruct((seq, 2 * width), BF),
            jax.ShapeDtypeStruct((16, 2 * BK), F32),
            jax.ShapeDtypeStruct((8, BQ), F32),
        ],
        compiler_params=pltpu.CompilerParams(
            dimension_semantics=("arbitrary",), vmem_limit_bytes=56 * 1024 * 1024
        ),
        name="attention_bwd",
    )(info, far, qkv_all, qkv_all[:, 0:width], dcol, drow, band, mixed, lse, dmix)


def band_kernel(vec_ref, band_ref):
    heads = band_ref.shape[0]
    for h in range(heads):
        for t in range(3):
            wide = jnp.broadcast_to(vec_ref[3 * h + t : 3 * h + t + 1, :], (BK, 2 * BQ))
            band_ref[h, t] = pltpu.roll(wide, 0, 1, stride=1, stride_axis=0)[:, 0:BQ]


def qkv_kernel(tok_ref, gain_ref, w_ref, qkv_ref, norm_ref, scale_ref):
    x = tok_ref[...].astype(F32)
    scale = lax.rsqrt(jnp.mean(x * x, axis=-1, keepdims=True) + norm_eps)
    normed = (x * scale * gain_ref[...].astype(F32)).astype(BF)
    norm_ref[...] = normed
    scale_ref[...] = scale
    qkv_ref[...] = dot(normed, w_ref[...]).astype(BF)


def router_parts(hidden, gain, router, chosen, experts):
    scale = lax.rsqrt(jnp.mean(hidden * hidden, axis=-1, keepdims=True) + norm_eps)
    hat = hidden * scale
    normed = (hat * gain).astype(BF)
    lane = lax.broadcasted_iota(jnp.int32, (hidden.shape[0], LANES), 1)
    logits = jnp.where(lane < experts, dot(normed, router), NEG)
    weights = jnp.exp(logits - jnp.max(logits, axis=-1, keepdims=True))
    route = weights / jnp.sum(weights, axis=-1, keepdims=True)
    one_hot = jnp.where(lane == chosen, 1.0, 0.0)
    gate = jnp.sum(route * one_hot, axis=-1, keepdims=True)
    return scale, hat, normed, route, one_hot, gate


def hidden_kernel(
    experts, tok_ref, mixed_ref, wout_ref, gain_ref, router_ref, chosen_ref,
    hidden_ref, norm_ref, gate_ref,
):
    attn = dot(mixed_ref[...], wout_ref[...], TN)
    hidden = tok_ref[...].astype(F32) + attn
    parts = router_parts(hidden, gain_ref[...].astype(F32), router_ref[...], chosen_ref[...], experts)
    hidden_ref[...] = hidden
    norm_ref[...] = parts[2]
    gate_ref[...] = to_row(parts[5])


def expert_kernel(
    groups, owner, pos_row, pos_col, norm_ref, cot_ref, gate_ref, w_ref,
    back_ref, eo_ref, x_ref, de_ref, act_ref, di_ref, eo_s, dr_s,
):
    i = pl.program_id(0)
    rows = norm_ref.shape[0]
    width = norm_ref.shape[1]
    ff = w_ref.shape[1] // 2
    place = lax.broadcasted_iota(jnp.int32, (TILE, rows), 0) + i * TILE
    hit = pos_row[...] == place
    pick = jnp.where(hit, 1.0, 0.0).astype(BF)
    x = dot(pick, norm_ref[...]).astype(BF)
    cot = dot(pick, cot_ref[...])
    gate = jnp.sum(jnp.where(hit, gate_ref[...], 0.0), axis=1, keepdims=True)
    d_e = (gate * cot).astype(BF)
    w_in = w_ref[:, 0:ff]
    w_down = w_ref[:, ff : 2 * ff]
    inner = dot(x, w_in)
    half = 0.5 * (1.0 + lax.erf(inner * (0.5**0.5)))
    active = (inner * half).astype(BF)
    slope = half + inner * (jnp.exp(-0.5 * inner * inner) * 0.3989422804014327)
    d_inner = (dot(d_e, w_down) * slope).astype(BF)
    terms = dot(active, w_down, NT)
    d_rows = dot(d_inner, w_in, NT)
    d_gate = jnp.sum(cot * terms, axis=1, keepdims=True)
    lane = lax.broadcasted_iota(jnp.int32, (TILE, LANES), 1)
    hi, mid, low = (t.astype(F32) for t in split3(d_gate))
    extra = jnp.where(lane == 0, hi, jnp.where(lane == 1, mid, jnp.where(lane == 2, low, 0.0)))
    here = pl.ds(pl.multiple_of(i * TILE, TILE), TILE)
    eo_s[here, :] = terms.astype(BF)
    dr_s[here, :] = jnp.concatenate([d_rows.astype(BF), extra.astype(BF)], axis=1)
    x_ref[...] = x
    de_ref[...] = d_e
    act_ref[...] = active
    di_ref[...] = d_inner

    @pl.when(i == pl.num_programs(0) - 1)
    def _():
        total = dr_s.shape[0]
        part = rows // groups
        for g in range(groups):
            mine = pl.ds(g * part, part)
            place = lax.broadcasted_iota(jnp.int32, (part, total), 1)
            pick = jnp.where(pos_col[mine, :] == place, 1.0, 0.0).astype(BF)
            back = dot(pick, dr_s[...])
            back_ref[g, 0:part, :] = back[:, 0:width].astype(BF)
            tail = back[:, width : width + LANES].T
            d_gate = tail[0:1, :] + tail[1:2, :] + tail[2:3, :]
            row = lax.broadcasted_iota(jnp.int32, (16, part), 0)
            strip = jnp.where(row == 0, jnp.broadcast_to(d_gate, (16, part)), 0.0)
            fill = jnp.zeros((16, width - part), F32)
            back_ref[g, part : part + 16, :] = jnp.concatenate([strip, fill], axis=1).astype(BF)
            eo_ref[:, mine] = dot(pick, eo_s[...]).T.astype(BF)


def weight_grad_kernel(owner, x_ref, di_ref, de_ref, act_ref, out_ref, acc):
    i = pl.program_id(0)
    last = pl.num_programs(0) - 1
    me = owner[i]
    before = owner[jnp.maximum(i - 1, 0)]
    after = owner[jnp.minimum(i + 1, last)]
    ff = di_ref.shape[1]

    @pl.when((i == 0) | (before != me))
    def _():
        acc[...] = jnp.zeros_like(acc)

    acc[:, 0:ff] += dot(x_ref[...], di_ref[...], TN)
    acc[:, ff : 2 * ff] += dot(de_ref[...], act_ref[...], TN)

    @pl.when((i == last) | (after != me))
    def _():
        out_ref[...] = acc[...].astype(BF)


def hidden_back_kernel(
    experts, info, back_ref, hidden_ref, cot_ref, gain_ref, router_ref, chosen_ref, wout_ref, mixed_ref,
    dh_ref, dmix_ref, small_ref, gout_ref,
):
    part = hidden_ref.shape[0]
    gain = gain_ref[...].astype(F32)
    scale, hat, normed, route, one_hot, gate = router_parts(
        hidden_ref[...], gain, router_ref[...], chosen_ref[...], experts
    )
    d_gate = to_column(back_ref[part : part + 16, 0:part].astype(F32)[0:1, :])
    d_logits = (d_gate * gate) * (one_hot - route)
    parts = split3(d_logits)
    d_normed = back_ref[0:part, :].astype(F32)
    for p in parts:
        d_normed = d_normed + dot(p, router_ref[...], NT)
    g_router = jnp.zeros((LANES, hat.shape[1]), F32)
    for p in parts:
        g_router = g_router + dot(p, normed, TN)
    small_ref[0:experts, :] = g_router[0:experts, :]
    small_ref[experts : experts + 1, :] = jnp.sum(d_normed * hat, axis=0, keepdims=True)
    if small_ref.shape[0] > experts + 1:
        small_ref[experts + 1 :, :] = jnp.zeros(
            (small_ref.shape[0] - experts - 1, hat.shape[1]), F32
        )
    d_hat = d_normed * gain
    d_hidden = cot_ref[...].astype(F32) + scale * (
        d_hat - hat * jnp.mean(d_hat * hat, axis=-1, keepdims=True)
    )
    d_attn = d_hidden.astype(BF)
    dmix_ref[...] = dot(wout_ref[...], d_attn, NT).astype(BF)
    dh_ref[...] = d_hidden.T.astype(BF)
    gout_ref[...] = dot(mixed_ref[...], d_attn).astype(BF)


def qkv_back_kernel(
    groups, info, dq_ref, dkv_ref, got_ref, norm_ref, tok_ref, scale_ref, gain_ref, w_ref,
    terms_ref, gw_ref, gain_out_ref, acc,
):
    i = pl.program_id(0)
    width = dq_ref.shape[0]
    dkv = dkv_ref[...].astype(F32) + got_ref[...].astype(F32)
    d_qkv = jnp.concatenate([dq_ref[...].astype(F32).T, dkv], axis=1).astype(BF)
    hat = tok_ref[...].astype(F32) * scale_ref[...]
    terms = dot(d_qkv, w_ref[...], NT)
    weighted = terms * hat
    mean = jnp.mean(weighted * gain_ref[...].astype(F32), axis=-1, keepdims=True)

    @pl.when(i == 0)
    def _():
        acc[...] = jnp.zeros_like(acc)
        gain_out_ref[...] = jnp.zeros_like(gain_out_ref)

    gain_out_ref[0:1, :] += jnp.sum(weighted, axis=0, keepdims=True)
    acc[...] += dot(norm_ref[...], d_qkv, TN)
    flat = terms.T.astype(BF)
    mean_row = to_row(mean)
    hi, mid, low = (t.astype(F32) for t in split3(mean_row))
    row = lax.broadcasted_iota(jnp.int32, (16, mean_row.shape[1]), 0)
    strip = jnp.where(row == 0, hi, jnp.where(row == 1, mid, jnp.where(row == 2, low, 0.0))).astype(BF)
    for g in range(groups):
        terms_ref[g, 0:width, :] = flat[g * width : (g + 1) * width, :]
        terms_ref[g, width : width + 16, :] = strip

    @pl.when(i == pl.num_programs(0) - 1)
    def _():
        gw_ref[...] = acc[...].astype(gw_ref.dtype)


def token_grad_kernel(info, sum_ref, dh_ref, tok_ref, scale_ref, gain_ref, out_ref):
    width = dh_ref.shape[0]
    mean = jnp.sum(sum_ref[width : width + 16, :].astype(F32), axis=0, keepdims=True)
    terms = sum_ref[0:width, :].astype(F32)
    d_hat = terms.T * gain_ref[...].astype(F32)
    scale = scale_ref[...]
    hat = tok_ref[...].astype(F32) * scale
    out_ref[...] = dh_ref[...].astype(F32).T + scale * (d_hat - hat * to_column(mean))


def out_kernel(eo_ref, hidden_ref, gate_ref, out_ref):
    out_ref[...] = (hidden_ref[...] + (eo_ref[...].astype(F32) * gate_ref[...]).T).astype(BF)


def placement(chosen, experts, tiles):
    rows = chosen.shape[0]
    ids = jnp.arange(experts, dtype=jnp.int32)
    one_hot = chosen[:, None] == ids[None, :]
    below = jnp.arange(rows)[:, None] > jnp.arange(rows)[None, :]
    earlier = dot(below.astype(BF), one_hot.astype(BF)).astype(jnp.int32)
    count = jnp.sum(one_hot.astype(jnp.int32), axis=0)
    used = jnp.maximum((count + TILE - 1) // TILE, 1)
    ends = jnp.sum(jnp.where(ids[None, :] <= ids[:, None], used[None, :], 0), axis=1)
    first = (ends - used) * TILE
    pos = jnp.sum(jnp.where(one_hot, earlier + first[None, :], 0), axis=1).astype(jnp.int32)
    tile_ids = jnp.arange(tiles, dtype=jnp.int32)
    owner = jnp.sum((ends[None, :] <= tile_ids[:, None]).astype(jnp.int32), axis=1)
    return pos, jnp.minimum(owner, experts - 1).astype(jnp.int32)


def shards(
    tokens,
    grad_out,
    w_qkv,
    w_attn_out,
    rel_bias,
    gain_attn,
    gain_ffn,
    w_router,
    w_in,
    w_down,
    expert_ids,
    doc_ids,
):
    rows, model = tokens.shape
    heads = rel_bias.shape[1]
    width = w_qkv.shape[2]
    own = w_qkv.shape[0]
    experts = w_router.shape[1]
    ff = w_in.shape[2]
    seq = doc_ids.shape[0]
    ctx_n = lax.axis_size("ctx")
    tp_n = lax.axis_size("tp")
    ctx_at = lax.axis_index("ctx")
    tp_at = lax.axis_index("tp")
    dense_at = lax.axis_index("fsdp") * ctx_n + ctx_at
    part = rows // tp_n
    share = model // tp_n
    blocks = rows // BQ
    dense = ("fsdp", "ctx")

    small = jnp.concatenate(
        (
            w_qkv.reshape(own, 3 * width),
            w_attn_out,
            w_router,
            gain_attn[:, None],
            gain_ffn[:, None],
            jnp.zeros((own, LANES - experts - 2), BF),
        ),
        axis=1,
    )
    small_all = lax.all_gather(small, dense, axis=0, tiled=True)
    tokens_all = lax.all_gather(tokens, "ctx", axis=0, tiled=True)
    half = model // ctx_n
    w_both = jnp.concatenate((w_in.reshape(-1, ff), w_down.reshape(-1, ff)), axis=1)
    w_half = lax.dynamic_slice_in_dim(w_both, ctx_at * half, half, 0)
    w_experts = lax.all_gather(w_half, dense, axis=0, tiled=True)
    qkv_full = small_all[:, 0 : 3 * width]
    out_mine = small_all[:, 3 * width : 4 * width]
    tail = small_all[:, 4 * width :]
    gain_one = tail[:, experts][None, :]
    gain_two = tail[:, experts + 1][None, :]
    router = jnp.where(jnp.arange(LANES)[None, :] < experts, tail, jnp.zeros_like(tail))
    out_t = lax.all_gather(out_mine.T, "tp", axis=0, tiled=True)

    chosen = expert_ids[:, 0]
    tiles = rows // TILE + experts - 1
    pos, owner = placement(chosen, experts, tiles)
    docs_row = doc_ids[None, :]
    docs_col = doc_ids[:, None]
    firsts = lax.dynamic_slice_in_dim(doc_ids.reshape(-1, BQ)[:, 0], ctx_at * blocks, blocks)
    lasts = lax.dynamic_slice_in_dim(doc_ids.reshape(-1, BQ)[:, BQ - 1], ctx_at * blocks, blocks)
    low = jnp.sum((docs_row < firsts[:, None]).astype(jnp.int32), axis=1) // BK
    high = (jnp.sum((docs_row <= lasts[:, None]).astype(jnp.int32), axis=1) + BK - 1) // BK
    info = jnp.concatenate(((ctx_at * blocks)[None], low, high)).astype(jnp.int32)
    wrapped = jnp.arange(2 * BQ, dtype=jnp.int32)
    wrapped = jnp.where(wrapped < BQ, wrapped, wrapped - 2 * BQ)
    offsets = (jnp.arange(3, dtype=jnp.int32)[:, None] - 1) * BK - wrapped[None, :]
    selector = relative_bucket(offsets)[:, :, None] == jnp.arange(rel_bias.shape[0])[None, None, :]
    selector = selector.astype(F32)
    vectors = jnp.einsum("tcb,bh->htc", selector, rel_bias, precision=lax.Precision.HIGHEST)
    far = jnp.stack((rel_bias[15], rel_bias[31]))
    band = call(
        band_kernel,
        (1,),
        [whole(3 * heads, 2 * BQ)],
        whole(heads, 3, BK, BQ),
        shaped((heads, 3, BK, BQ), F32),
        name="bias_band",
    )(vectors.reshape(3 * heads, 2 * BQ))

    qkv_all, normed_one, scale_one = call(
        qkv_kernel,
        (seq // BQ,),
        [pl.BlockSpec((BQ, model), lambda i: (i, 0)), whole(1, model), whole(model, 3 * width)],
        [
            pl.BlockSpec((BQ, 3 * width), lambda i: (i, 0)),
            pl.BlockSpec((BQ, model), lambda i: (i, 0)),
            pl.BlockSpec((BQ, 1), lambda i: (i, 0)),
        ],
        [shaped((seq, 3 * width), BF), shaped((seq, model), BF), shaped((seq, 1), F32)],
        name="norm_qkv",
    )(tokens_all, gain_one, qkv_full)
    mixed, mixed_low, lse = attention_fwd(info, far, qkv_all, docs_col, docs_row, band, rows)
    mixed_all = lax.all_gather(mixed_low, "tp", axis=0, tiled=True)

    chosen_col = expert_ids
    hidden, normed_two, gate_row = call(
        partial(hidden_kernel, experts),
        (blocks,),
        [
            pl.BlockSpec((BQ, model), lambda i: (i, 0)),
            pl.BlockSpec((model, BQ), lambda i: (0, i)),
            whole(model, model),
            whole(1, model),
            whole(model, LANES),
            pl.BlockSpec((BQ, 1), lambda i: (i, 0)),
        ],
        [
            pl.BlockSpec((BQ, model), lambda i: (i, 0)),
            pl.BlockSpec((BQ, model), lambda i: (i, 0)),
            pl.BlockSpec((1, BQ), lambda i: (0, i)),
        ],
        [shaped((rows, model), F32), shaped((rows, model), BF), shaped((1, rows), F32)],
        name="hidden_router",
    )(tokens, mixed_all, out_t, gain_two, router, chosen_col)
    sorted_rows = tiles * TILE
    sorted_spec = lambda cols: pl.BlockSpec((TILE, cols), lambda i, owner: (i, 0))
    back, eo_t, x_sorted, d_expert, active, d_inner = call(
        partial(expert_kernel, tp_n),
        (tiles,),
        [
            whole(1, rows),
            whole(rows, 1),
            whole(rows, model),
            whole(rows, model),
            whole(1, rows),
            pl.BlockSpec((model, 2 * ff), lambda i, owner: (owner[i], 0)),
        ],
        [
            whole(tp_n, part + 16, model),
            whole(model, rows),
            sorted_spec(model),
            sorted_spec(model),
            sorted_spec(ff),
            sorted_spec(ff),
        ],
        [
            shaped((tp_n, part + 16, model), BF),
            shaped((model, rows), BF),
            shaped((sorted_rows, model), BF),
            shaped((sorted_rows, model), BF),
            shaped((sorted_rows, ff), BF),
            shaped((sorted_rows, ff), BF),
        ],
        scratch=[pltpu.VMEM((sorted_rows, model), BF), pltpu.VMEM((sorted_rows, model + LANES), BF)],
        prefetch=1,
        name="experts",
    )(owner, pos[None, :], pos[:, None], normed_two, grad_out, gate_row, w_experts)
    back_mine = lax.psum_scatter(
        back.reshape(tp_n * (part + 16), model), "tp", scatter_dimension=0, tiled=True
    )
    grad_experts = call(
        weight_grad_kernel,
        (tiles,),
        [sorted_spec(model), sorted_spec(ff), sorted_spec(model), sorted_spec(ff)],
        pl.BlockSpec((model, 2 * ff), lambda i, owner: (owner[i], 0)),
        shaped((experts * model, 2 * ff), BF),
        scratch=[pltpu.VMEM((model, 2 * ff), F32)],
        prefetch=1,
        name="expert_weight_grads",
    )(owner, x_sorted, d_inner, d_expert, active)

    at = jnp.stack((tp_at, ctx_at * blocks)).astype(jnp.int32)
    small_rows = -(-(experts + 1) // 8) * 8
    row_block = pl.BlockSpec((part, model), lambda i, at: (at[0], 0))
    dh_t, dmix_t, small_grads, grad_out_t = call(
        partial(hidden_back_kernel, experts),
        (1,),
        [
            whole(part + 16, model),
            row_block,
            row_block,
            whole(1, model),
            whole(model, LANES),
            pl.BlockSpec((part, 1), lambda i, at: (at[0], 0)),
            whole(model, model),
            pl.BlockSpec((model, part), lambda i, at: (0, at[0])),
        ],
        [whole(model, part), whole(model, part), whole(small_rows, model), whole(model, model)],
        [
            shaped((model, part), BF),
            shaped((model, part), BF),
            shaped((small_rows, model), F32),
            shaped((model, model), BF),
        ],
        prefetch=1,
        name="hidden_back",
    )(at, back_mine, hidden, grad_out, gain_two, router, chosen_col, out_t, mixed_all)
    dmix = lax.all_to_all(dmix_t.reshape(tp_n, width, part), "tp", 0, 0)
    dh = lax.all_to_all(dh_t.reshape(tp_n, width, part), "tp", 0, 0)
    grad_experts_mine = lax.psum_scatter(grad_experts, dense, scatter_dimension=0, tiled=True)
    eo_mine = lax.psum_scatter(eo_t, "tp", scatter_dimension=0, tiled=True)
    grad_out_tp = lax.psum_scatter(grad_out_t, "tp", scatter_dimension=0, tiled=True)
    small_sums = lax.psum(small_grads, ("fsdp", "ctx", "tp"))

    dq_t, dkv, skew, sides = attention_bwd(
        info, far, qkv_all, docs_col, docs_row, band, mixed, lse, dmix, rows
    )
    if ctx_n == 2:
        other = lax.dynamic_slice_in_dim(dkv, (1 - ctx_at) * rows, rows)
        got = lax.ppermute(other, "ctx", [(0, 1), (1, 0)])
        mine = lax.dynamic_slice_in_dim(dkv, ctx_at * rows, rows)
    else:
        mine = lax.psum_scatter(dkv, "ctx", scatter_dimension=0, tiled=True)
        got = jnp.zeros_like(mine)
    terms, grad_qkv, gain_sum = call(
        partial(qkv_back_kernel, tp_n),
        (blocks,),
        [
            pl.BlockSpec((width, BQ), lambda i, at: (0, i)),
            pl.BlockSpec((BQ, 2 * width), lambda i, at: (i, 0)),
            pl.BlockSpec((BQ, 2 * width), lambda i, at: (i, 0)),
            pl.BlockSpec((BQ, model), lambda i, at: (at[1] + i, 0)),
            pl.BlockSpec((BQ, model), lambda i, at: (i, 0)),
            pl.BlockSpec((BQ, 1), lambda i, at: (at[1] + i, 0)),
            whole(1, model),
            whole(model, 3 * width),
        ],
        [
            pl.BlockSpec((tp_n, width + 16, BQ), lambda i, at: (0, 0, i)),
            whole(model, 3 * width),
            whole(8, model),
        ],
        [
            shaped((tp_n, width + 16, rows), BF),
            shaped((model, 3 * width), BF),
            shaped((8, model), F32),
        ],
        scratch=[pltpu.VMEM((model, 3 * width), F32)],
        prefetch=1,
        name="qkv_back",
    )(at, dq_t, mine, got, normed_one, tokens, scale_one, gain_one, qkv_full)
    terms_mine = lax.psum_scatter(
        terms.reshape(tp_n * (width + 16), rows), "tp", scatter_dimension=0, tiled=True
    )
    grad_dense = lax.psum_scatter(
        jnp.concatenate((grad_qkv, grad_out_tp.T), axis=1), dense, scatter_dimension=0, tiled=True
    ).astype(F32)

    diagonals = skew[0 : 3 * heads].reshape(heads, 3, 2 * BQ)
    table = jnp.einsum("htc,tcb->bh", diagonals, selector, precision=lax.Precision.HIGHEST)
    side = jnp.sum(sides[0 : 2 * heads], axis=1).reshape(heads, 2)
    bucket_ids = jnp.arange(rel_bias.shape[0])[:, None]
    table = table + jnp.where(bucket_ids == 15, side[None, :, 0], 0.0)
    table = table + jnp.where(bucket_ids == 31, side[None, :, 1], 0.0)
    slots = jnp.where(jnp.arange(tp_n)[:, None] == tp_at, table.reshape(1, -1), 0.0)
    late = jnp.concatenate((gain_sum[0], slots.reshape(-1)))
    late_sums = lax.psum(late, ("fsdp", "ctx", "tp"))
    table_all = late_sums[model:].reshape(tp_n, rel_bias.shape[0], heads)
    table_mine = lax.dynamic_index_in_dim(table_all, tp_at, 0, keepdims=False)
    table_rows = rel_bias.shape[0] // (lax.axis_size("fsdp") * ctx_n)
    grad_table = lax.dynamic_slice_in_dim(table_mine, dense_at * table_rows, table_rows)
    grad_gain_one = lax.dynamic_slice_in_dim(late_sums[:model], dense_at * own, own)
    small_mine = lax.dynamic_slice_in_dim(small_sums, dense_at * own, own, 1)
    grad_router = small_mine[0:experts].T
    grad_gain_two = small_mine[experts]

    columns = tp_at * share
    hidden_share = lax.dynamic_slice_in_dim(hidden, columns, share, 1)
    tokens_share = lax.dynamic_slice_in_dim(tokens, columns, share, 1)
    gain_share = lax.dynamic_slice_in_dim(gain_one, columns, share, 1)
    out_share = call(
        out_kernel,
        (blocks,),
        [
            pl.BlockSpec((share, BQ), lambda i: (0, i)),
            pl.BlockSpec((BQ, share), lambda i: (i, 0)),
            pl.BlockSpec((1, BQ), lambda i: (0, i)),
        ],
        pl.BlockSpec((BQ, share), lambda i: (i, 0)),
        shaped((rows, share), BF),
        name="layer_output",
    )(eo_mine, hidden_share, gate_row)
    grad_tokens = call(
        token_grad_kernel,
        (tp_n,),
        [
            pl.BlockSpec((width + 16, part), lambda i, at: (0, i)),
            pl.BlockSpec((None, width, part), lambda i, at: (i, 0, 0)),
            pl.BlockSpec((part, share), lambda i, at: (i, 0)),
            pl.BlockSpec((part, 1), lambda i, at: (at[0] + i, 0)),
            whole(1, share),
        ],
        pl.BlockSpec((part, share), lambda i, at: (i, 0)),
        shaped((rows, share), F32),
        prefetch=1,
        name="token_grads",
    )((ctx_at * tp_n)[None].astype(jnp.int32), terms_mine, dh, tokens_share, scale_one, gain_share)
    grad_experts_f = grad_experts_mine.astype(F32)
    return (
        out_share,
        grad_tokens,
        grad_dense[:, 0 : 3 * width].reshape(own, 3, width),
        grad_dense[:, 3 * width :],
        grad_table,
        grad_gain_one,
        grad_gain_two,
        grad_router,
        grad_experts_f[None, :, 0:ff],
        grad_experts_f[None, :, ff:],
    )


def solution(mesh):
    placed = (
        P(("fsdp", "ctx"), None),
        P(("fsdp", "ctx"), None),
        P(("fsdp", "ctx"), None, "tp"),
        P(("fsdp", "ctx"), "tp"),
        P(None, "tp"),
        P(("fsdp", "ctx")),
        P(("fsdp", "ctx")),
        P(("fsdp", "ctx"), None),
        P("fsdp", None, "tp"),
        P("fsdp", None, "tp"),
        P(("fsdp", "ctx"), None),
        P("fsdp"),
    )
    return jax.shard_map(
        shards,
        mesh=mesh,
        in_specs=placed,
        out_specs=(
            P(("fsdp", "ctx"), "tp"),
            P(("fsdp", "ctx"), "tp"),
            P(("fsdp", "ctx"), None, "tp"),
            P(("fsdp", "ctx"), "tp"),
            P(("fsdp", "ctx"), "tp"),
            P(("fsdp", "ctx")),
            P(("fsdp", "ctx")),
            P(("fsdp", "ctx"), None),
            P("fsdp", "ctx", "tp"),
            P("fsdp", "ctx", "tp"),
        ),
        check_vma=False,
    )
```

time: 1410 us -> 506 us (0.36)
  local copies, waits for them, and re-layouts: 608 us -> 50.8 us
  blocking collectives: 257 us -> 44.9 us
  matrix products: 145 us -> 0.85 us
  Pallas kernels: 0 us -> 119 us
  other arithmetic: 120 us -> 7.14 us
  waiting for transfers between devices: 240 us -> 259 us
    unnamed x144 -> x83, local copies, waits for them, and re-layouts: 286 us -> 26.9 us
    psum x3 -> x0, waiting for transfers between devices: 220 us -> none  [the longest x1 120 us: shards(): hidden = tokens_f + lax.psum(attn_terms, 'tp')]
    dot_general x29 -> x3, matrix products: 139 us -> 0.85 us  [the longest x1 0.48 us: dot(): return jnp.dot(a, b, preferred_element_type=F32)]
    pallas_call x0 -> x11, Pallas kernels: none -> 119 us  [the longest x1 29.1 us: shards(): call(partial(expert_kernel, tp_n), (tiles,), [whole(1, rows), whole(rows,...]
    all_gather x1 -> x5, waiting for transfers between devices: 0.02 us -> 117 us  [the longest x1 50.2 us: shards(): w_experts = lax.all_gather(w_half, dense, axis=0, tiled=True)]
    reduce_scatter x5, waiting for transfers between devices: 0.04 us -> 117 us  [the longest x1 76.1 us: shards(): lax.psum_scatter(grad_experts, dense, scatter_dimension=0, tiled=True)]
    reshape x6, local copies, waits for them, and re-layouts: 116 us -> 0.47 us  [the longest x1 0.2 us: shards(): table_all = late_sums[model:].reshape(tp_n, rel_bias.shape[0], heads)]
    all_to_all x2 -> x0, blocking collectives: 114 us -> none  [the longest x1 73.3 us: shards(): lax.all_to_all(d_rows, 'fsdp', split_axis=1, concat_axis=0, tiled=True)]
  transfers between devices with their start and end apart: 13 -> 14, of which waited for: 3 -> 9; matrix products, arithmetic and copies ran while one was open for 49% -> 6% of each run, Pallas kernels for 0% -> 17%
where the time goes in v1:
time: 506 us; the launch traced here: 505 us
  waiting for transfers between devices  259 us (51%)
  Pallas kernels  119 us (24%)
  local copies, waits for them, and re-layouts  50.8 us (10%)
  blocking collectives  44.9 us (9%)
  between operations  14.4 us (3%)
  starting transfers between devices  7.85 us (2%)
  other arithmetic  7.14 us (1%)
    reduce_scatter x1, waiting for transfers between devices, shards(): lax.psum_scatter(grad_experts, dense, scatter_dimension=0, tiled=True)  76.1 us
    all_gather x1, waiting for transfers between devices, shards(): w_experts = lax.all_gather(w_half, dense, axis=0, tiled=True)  50.2 us
    psum x1, blocking collectives, shards(): late_sums = lax.psum(late, ('fsdp', 'ctx', 'tp'))  44.9 us
    reduce_scatter x1, waiting for transfers between devices, shards(): lax.psum_scatter(back.reshape(tp_n * (part + 16), model), 'tp', scatter_d...  36.9 us
    all_gather x1, waiting for transfers between devices, shards(): mixed_all = lax.all_gather(mixed_low, 'tp', axis=0, tiled=True)  34.9 us
    pallas_call x1, Pallas kernels, shards(): call(partial(expert_kernel, tp_n), (tiles,), [whole(1, rows), whole(rows,...  29.1 us
    unnamed x83, local copies, waits for them, and re-layouts  26.9 us
    all_gather x1, waiting for transfers between devices, shards(): small_all = lax.all_gather(small, dense, axis=0, tiled=True)  26.6 us
  transfers between devices with their start and end apart: 14, of which 9 were waited for; matrix products, arithmetic and copies ran while one was open for 6% of the time, Pallas kernels for 17%

profile of v1, /device:TPU:0, one launch (start us, length us, event | category | flops | bytes accessed | tf_op | source)
XLA Modules:
  0.0 504.6 jit_solution(8286551254771828609)
XLA Ops:
  7.2 1.1 copy.106
  8.5 0.8 copy.108
  9.3 0.8 copy.109
  10.0 0.8 copy.110
  10.8 1.6 concatenate.16
  13.6 26.6 %all-gather.8.cloned.1.call-done = bf16[768,896]{1,0:T(8,128)(2,1)} async-done(((bf16[96,896]{1,0:T(8,128)(2,1)}), bf16[768,896]{1,0:T(8,128)(2,1)}) %all-gather.8.cloned.1.call-update) | async-done | bytes 1376272 | tf_op jit(solution)/shard_map/all_gather | solution.py:622
  40.2 1.2 slice_bitcast_fusion.2
  41.4 0.9 copy.113
  44.4 2.0 slice_reduce_fusion
  46.4 2.3 slice.106.w_ref
  48.7 5.2 %all-gather.6.cloned.1.call-done.tok_ref = bf16[2048,768]{1,0:T(8,128)(2,1)} async-done(((bf16[1024,768]{1,0:T(8,128)(2,1)}), bf16[2048,768]{1,0:T(8,128)(2,1)}) %all-gather.6.cloned.1.call-update) | async-done | bytes 3145744 | tf_op jit(solution)/shard_map/all_gather | solution.py:623
  53.9 1.2 copy-done.5
  55.1 7.4 %norm_qkv.1 = (bf16[2048,576]{1,0:T(8,128)(2,1)S(1)}, bf16[2048,768]{1,0:T(8,128)(2,1)}, f32[2048,1]{1,0:T(8,128)S(1)}) custom-call(bf16[2048,768]{1,0:T(8,128)(2,1)} %all-gather.6.cloned.1.call-done.tok_ref, bf16[1,768]{1,0:T(2,128)(2,1)S(1)} %broadcast_in_dim_squeeze.8.gain_ref, bf16[768,576]{1,0:T(8,128)(2,1)S(1)} %copy-done.5), custom_call_target="tpu_custom_call" | custom-call | tf_op jit(solution)/shard_map/norm_qkv/pallas_call | solution.py:662
  62.6 19.6 %attention_fwd.1 = (f32[192,1024]{1,0:T(8,128)S(1)}, bf16[192,1024]{1,0:T(8,128)(2,1)S(1)}, f32[3,1024]{1,0:T(4,128)S(1)}) custom-call(s32[9]{0:T(128)S(1)} %pad_add_fusion.info, f32[2,3]{1,0:T(2,128)S(1)} %pad_maximum_fusion.2.far, bf16[2048,576]{1,0:T(8,128)(2,1)S(1)} %get-tuple-element.36.qkv_all, bf16[2048,192]{1,0:T(8,128)(2,1)S(1)} %slice.86.q_ref, ...), custom_call_target="tpu_custom_call" | custom-call | tf_op jit(solution)/shard_map/attention_fwd/pallas_call | solution.py:186
  82.2 0.9 copy-done.21
  83.1 0.7 copy-done.24
  84.5 2.3 fusion.1
  87.2 1.0 copy.114.chosen_ref
  88.9 1.0 copy.115.pos_col
  90.1 0.9 slice_select_fusion.router_ref
  91.1 34.9 %all-gather.10.cloned.1.call-done.mixed_ref = bf16[768,1024]{1,0:T(8,128)(2,1)} async-done(((bf16[192,1024]{1,0:T(8,128)(2,1)}), bf16[768,1024]{1,0:T(8,128)(2,1)}) %all-gather.10.cloned.1.call-update) | async-done | bytes 1572880 | tf_op jit(solution)/shard_map/all_gather | solution.py:675
  125.9 1.3 copy-done.8
  127.2 1.0 copy-done.10
  128.2 6.3 %hidden_router.1 = (f32[1024,768]{1,0:T(8,128)}, bf16[1024,768]{1,0:T(8,128)(2,1)S(1)}, f32[1,1024]{1,0:T(1,128)S(1)}) custom-call(bf16[1024,768]{1,0:T(8,128)(2,1)S(1)} %copy-done.1, bf16[768,1024]{1,0:T(8,128)(2,1)} %all-gather.10.cloned.1.call-done.mixed_ref, bf16[768,768]{1,0:T(8,128)(2,1)S(1)} %copy-done.8, ...), custom_call_target="tpu_custom_call" | custom-call | tf_op jit(solution)/shard_map/hidden_router/pallas_call | solution.py:678
  134.6 1.2 copy-done.18
  135.7 50.2 %all-gather.14.cloned.1.call-done.w_ref = bf16[3072,1536]{1,0:T(8,128)(2,1)} async-done(((bf16[384,1536]{1,0:T(8,128)(2,1)}), bf16[3072,1536]{1,0:T(8,128)(2,1)}) %all-gather.14.cloned.1.call-update) | async-done | bytes 9437200 | tf_op jit(solution)/shard_map/all_gather | solution.py:627
  186.0 1.0 copy-done.16
  187.0 1.4 copy-done.19
  188.4 29.1 %experts.1 = (bf16[4,272,768]{2,1,0:T(8,128)(2,1)}, bf16[768,1024]{1,0:T(8,128)(2,1)S(1)}, bf16[1408,768]{1,0:T(8,128)(2,1)}, bf16[1408,768]{1,0:T(8,128)(2,1)},...) custom-call(s32[11]{0:T(128)S(1)} %broadcast_minimum_fusion.owner, s32[1,1024]{1,0:T(1,128)S(1)} %bitcast.47, ...), custom_call_target="tpu_custom_call" | custom-call | tf_op jit(solution)/shard_map/experts/pallas_call | solution.py:699
  217.6 1.2 copy-done.17
  218.9 36.9 %reduce-scatter.11.cloned.1.call-done.back_ref = bf16[272,768]{1,0:T(8,128)(2,1)} async-done(((bf16[1088,768]{1,0:T(8,128)(2,1)}), bf16[272,768]{1,0:T(8,128)(2,1)}) %reduce-scatter.11.cloned.1.call-update) | async-done | bytes 417808 | tf_op jit(solution)/shard_map/reduce_scatter | solution.py:730
  255.8 1.0 copy-done.11
  256.8 1.0 copy-done.23
  257.8 4.9 hidden_back.1
  262.7 1.0 copy-done.20
  264.5 3.5 all-to-all-start
  268.3 21.3 %all-to-all-done.dmix_ref = bf16[4,192,256]{2,1,0:T(8,128)(2,1)S(1)} async-done(((bf16[4,192,256]{2,1,0:T(8,128)(2,1)}), bf16[4,192,256]{2,1,0:T(8,128)(2,1)S(1)}, u32[]{:S(2)}, u32[]{:S(2)}) %all-to-all-start) | async-done | bytes 393248 | tf_op jit(solution)/shard_map/all_to_all | solution.py:770
  289.6 0.7 copy-done.31
  290.3 25.2 %attention_bwd.1 = (bf16[192,1024]{1,0:T(8,128)(2,1)}, bf16[2048,384]{1,0:T(8,128)(2,1)}, f32[16,512]{1,0:T(8,128)}, f32[8,256]{1,0:T(8,128)}) custom-call(s32[9]{0:T(128)} %copy-done.30, f32[2,3]{1,0:T(2,128)} %copy-done.29, bf16[2048,576]{1,0:T(8,128)(2,1)} %copy-done.2, bf16[2048,192]{1,0:T(8,128)(2,1)} %copy-done.4, s32[2048,1]{1,0:T(8,128)} %copy-done.3, ...), custom_call_target="tpu_custom_call" | custom-call | tf_op jit(solution)/shard_map/attention_bwd/pallas_call | solution.py:322
  315.5 1.7 constant_dynamic-slice_fusion.3
  317.3 2.3 collective-permute-done.got_ref
  319.6 8.3 %qkv_back.1 = (bf16[4,208,1024]{2,1,0:T(8,128)(2,1)}, bf16[768,576]{1,0:T(8,128)(2,1)S(1)}, f32[8,768]{1,0:T(8,128)S(1)}) custom-call(s32[2]{0:T(128)S(1)} %pad_add_fusion.1.info, bf16[192,1024]{1,0:T(8,128)(2,1)S(1)} %copy-done.26, bf16[1024,384]{1,0:T(8,128)(2,1)S(1)} %get-tuple-element.123.dkv_ref, bf16[1024,384]{1,0:T(8,128)(2,1)S(1)} %collective-permute-done.got_ref, ...), custom_call_target="tpu_custom_call" | custom-call | tf_op jit(solution)/shard_map/qkv_back/pallas_call | solution.py:787
  327.9 1.1 copy.126
  329.0 1.2 pad_maximum_fusion
  330.9 1.6 copy-done.14
  332.5 1.6 copy-done.15
  334.2 15.7 %expert_weight_grads.1 = bf16[3072,1536]{1,0:T(8,128)(2,1)} custom-call(s32[11]{0:T(128)S(1)} %broadcast_minimum_fusion.owner, bf16[1408,768]{1,0:T(8,128)(2,1)S(1)} %copy-done.14, bf16[1408,768]{1,0:T(8,128)(2,1)S(1)} %copy-done.15, bf16[1408,768]{1,0:T(8,128)(2,1)} %get-tuple-element.60.de_ref, bf16[1408,768]{1,0:T(8,128)(2,1)} %get-tuple-element.61.act_ref), custom_call_target="tpu_custom_call" | custom-call | tf_op jit(solution)/shard_map/expert_weight_grads/pallas_call | solution.py:733
  350.0 1.4 constant_dynamic-slice_fusion.2.tok_ref
  351.4 0.9 dynamic-slice_reduce_fusion
  352.3 1.7 constant_dynamic-slice_fusion.5.hidden_ref
  354.1 1.0 copy-done.25
  355.7 0.9 copy.122
  356.7 3.5 all-to-all-start.1
  361.2 44.9 %all-reduce = (f32[1152]{0:T(1024)S(1)}, f32[8,768]{1,0:T(8,128)S(1)}) all-reduce(f32[1152]{0:T(1024)S(1)} %pad_maximum_fusion.1, f32[8,768]{1,0:T(8,128)S(1)} %get-tuple-element.57), channel_id=1, replica_groups=mesh['fsdp'=4,'ctx'=2,'tp'=4] {'fsdp','ctx','tp'}, use_global_device_ids=true, to_apply=%region_12.13 | all-reduce | flops 7296 | bytes 58368 | tf_op jit(solution)/shard_map/psum | solution.py:829
  408.7 1.0 slice.110
  409.8 0.9 copy.124
  410.7 0.7 slice.111
  411.5 3.9 reduce-scatter.13.cloned.1.call-done.sum_ref
  415.3 1.0 copy-done.22
  416.3 1.2 token_grads.1
  417.6 1.2 copy.123
  418.8 76.1 %reduce-scatter.17.cloned.1.call-done = bf16[384,1536]{1,0:T(8,128)(2,1)} async-done(((bf16[3072,1536]{1,0:T(8,128)(2,1)}), bf16[384,1536]{1,0:T(8,128)(2,1)}) %reduce-scatter.17.cloned.1.call-update) | async-done | bytes 1179664 | tf_op jit(solution)/shard_map/reduce_scatter | solution.py:772
  494.9 1.5 convert_element_type.100
  496.5 1.6 slice_bitcast_fusion
  (142 shorter events, 11.4 us)
Async XLA Ops:
  7.2 6.1 %copy-start.27 = (s32[2048]{0:T(1024)S(1)}, s32[2048]{0:T(1024)}, u32[]{:S(2)}) copy-start(s32[2048]{0:T(1024)} %param.23) | copy-start | bytes 24580
  7.2 6.1 %copy-start.36 = (f32[32,3]{0,1:T(4,128)S(1)}, f32[32,3]{0,1:T(4,128)}, u32[]{:S(2)}) copy-start(f32[32,3]{0,1:T(4,128)} %param.16) | copy-start | bytes 1156
  7.2 33.0 %all-gather.8.cloned.1.call-start = ((), (), s32[]{:S(2)}) async-start(), calls=%async_computation.9 | async-start | bytes 1548288 | tf_op jit(solution)/shard_map/all_gather | solution.py:622
  12.5 41.4 %all-gather.6.cloned.1.call-start = ((), (), s32[]{:S(2)}) async-start(), calls=%async_computation.8 | async-start | bytes 4718592 | tf_op jit(solution)/shard_map/all_gather | solution.py:623
  13.2 77.9 %all-gather.12.cloned.1.call-start = ((), (), s32[]{:S(2)}) async-start(), calls=%async_computation.11 | async-start | bytes 1474560 | tf_op jit(solution)/shard_map/all_gather | solution.py:634
  42.3 83.6 %all-gather.10.cloned.1.call-start = ((), (), s32[]{:S(2)}) async-start(), calls=%async_computation.10 | async-start | bytes 1966080 | tf_op jit(solution)/shard_map/all_gather | solution.py:675
  43.4 19.2 %copy-start = (f32[3,3,256,256]{3,2,1,0:T(8,128)}, f32[3,3,256,256]{3,2,1,0:T(8,128)S(1)}, u32[]{:S(2)}) copy-start(f32[3,3,256,256]{3,2,1,0:T(8,128)S(1)} %bias_band.1.band) | copy-start | bytes 7077892
  43.8 18.8 %copy-start.3 = (s32[2048,1]{1,0:T(8,128)}, s32[2048,1]{1,0:T(8,128)S(1)}, u32[]{:S(2)}) copy-start(s32[2048,1]{1,0:T(8,128)S(1)} %copy.112.dcol) | copy-start | bytes 24580
  44.3 18.2 %copy-start.30 = (s32[9]{0:T(128)}, s32[9]{0:T(128)S(1)}, u32[]{:S(2)}) copy-start(s32[9]{0:T(128)S(1)} %pad_add_fusion.info) | copy-start | bytes 112
  44.3 18.2 %copy-start.29 = (f32[2,3]{1,0:T(2,128)}, f32[2,3]{1,0:T(2,128)S(1)}, u32[]{:S(2)}) copy-start(f32[2,3]{1,0:T(2,128)S(1)} %pad_maximum_fusion.2.far) | copy-start | bytes 76
  53.9 1.2 copy-start.5
  62.5 19.8 %copy-start.2 = (bf16[2048,576]{1,0:T(8,128)(2,1)}, bf16[2048,576]{1,0:T(8,128)(2,1)S(1)}, u32[]{:S(2)}) copy-start(bf16[2048,576]{1,0:T(8,128)(2,1)S(1)} %get-tuple-element.36.qkv_all) | copy-start | bytes 7077892
  62.5 19.8 %copy-start.12 = (f32[2048,1]{1,0:T(8,128)}, f32[2048,1]{1,0:T(8,128)S(1)}, u32[]{:S(2)}) copy-start(f32[2048,1]{1,0:T(8,128)S(1)} %get-tuple-element.49.scale_ref) | copy-start | bytes 24580
  62.5 19.7 %copy-start.4 = (bf16[2048,192]{1,0:T(8,128)(2,1)}, bf16[2048,192]{1,0:T(8,128)(2,1)S(1)}, u32[]{:S(2)}) copy-start(bf16[2048,192]{1,0:T(8,128)(2,1)S(1)} %slice.86.q_ref) | copy-start | bytes 2359300
  82.2 0.9 copy-start.21
  83.1 0.7 copy-start.24
  83.9 0.6 copy-start.28
  84.5 101.5 %all-gather.14.cloned.1.call-start = ((), (), s32[]{:S(2)}) async-start(), calls=%async_computation.12 | async-start | bytes 10616832 | tf_op jit(solution)/shard_map/all_gather | solution.py:627
  84.5 2.6 copy-start.34
  86.9 39.0 %copy-start.1 = (bf16[1024,768]{1,0:T(8,128)(2,1)S(1)}, bf16[1024,768]{1,0:T(8,128)(2,1)}, u32[]{:S(2)}) copy-start(bf16[1024,768]{1,0:T(8,128)(2,1)} %tok_ref.3) | copy-start | bytes 4718596
  86.9 168.8 %reduce-scatter.11.cloned.1.call-start = ((), (), s32[]{:S(2)}) async-start(), calls=%async_computation.14 | async-start | bytes 2088960 | tf_op jit(solution)/shard_map/reduce_scatter | solution.py:730
  91.0 94.9 %copy-start.7 = (bf16[1024,768]{1,0:T(8,128)(2,1)S(1)}, bf16[1024,768]{1,0:T(8,128)(2,1)}, u32[]{:S(2)}) copy-start(bf16[1024,768]{1,0:T(8,128)(2,1)} %cot_ref.3) | copy-start | bytes 4718596
  125.9 1.3 copy-start.8
  127.2 1.0 copy-start.10
  134.6 1.2 copy-start.18
  186.0 1.0 copy-start.16
  187.0 1.4 copy-start.19
  217.6 1.2 copy-start.17
  218.7 37.0 %copy-start.9 = (bf16[768,768]{1,0:T(8,128)(2,1)S(1)}, bf16[768,768]{1,0:T(8,128)(2,1)}, u32[]{:S(2)}) copy-start(bf16[768,768]{1,0:T(8,128)(2,1)} %all-gather.12.cloned.1.call-done.wout_ref) | copy-start | bytes 3538948
  218.8 109.1 %reduce-scatter.19.cloned.1.call-start = ((), (), s32[]{:S(2)}) async-start(), calls=%async_computation.18 | async-start | bytes 1474560
  255.8 1.0 copy-start.11
  256.8 1.0 copy-start.23
  262.7 1.0 copy-start.20
  263.8 90.3 %reduce-scatter.9.cloned.1.call-start = ((), (), s32[]{:S(2)}) async-start(), calls=%async_computation.13 | async-start | bytes 1966080 | tf_op jit(solution)/shard_map/reduce_scatter | solution.py:773
  264.5 25.0 %all-to-all-start = ((bf16[4,192,256]{2,1,0:T(8,128)(2,1)}), bf16[4,192,256]{2,1,0:T(8,128)(2,1)S(1)}, u32[]{:S(2)}, u32[]{:S(2)}) async-start(bf16[4,192,256]{2,1,0:T(8,128)(2,1)} %bitcast.16), calls=%async_computation.2 | async-start | bytes 786432 | tf_op jit(solution)/shard_map/all_to_all | solution.py:770
  268.0 140.7 %reduce-scatter.15.cloned.1.call-start = ((), (), s32[]{:S(2)}) async-start(), calls=%async_computation.16 | async-start | bytes 1327104 | tf_op jit(solution)/shard_map/reduce_scatter | solution.py:817
  289.6 0.7 copy-start.31
  315.5 4.1 copy-start.6
  315.5 4.1 copy-start.13
  315.5 4.1 copy-start.26
  317.2 2.4 collective-permute-start
  330.3 85.1 %reduce-scatter.13.cloned.1.call-start = ((), (), s32[]{:S(2)}) async-start(), calls=%async_computation.15 | async-start | bytes 2129920 | tf_op jit(solution)/shard_map/reduce_scatter | solution.py:814
  330.9 164.0 %reduce-scatter.17.cloned.1.call-start = ((), (), s32[]{:S(2)}) async-start(), calls=%async_computation.17 | async-start | bytes 10616832 | tf_op jit(solution)/shard_map/reduce_scatter | solution.py:772
  330.9 1.6 copy-start.14
  332.5 1.7 copy-start.15
  354.1 1.0 copy-start.25
  355.1 5.1 %copy-start.33 = (f32[16,512]{1,0:T(8,128)S(1)}, f32[16,512]{1,0:T(8,128)}, u32[]{:S(2)}) copy-start(f32[16,512]{1,0:T(8,128)} %get-tuple-element.55) | copy-start | bytes 98308
  355.1 5.1 %copy-start.35 = (f32[8,256]{1,0:T(8,128)S(1)}, f32[8,256]{1,0:T(8,128)}, u32[]{:S(2)}) copy-start(f32[8,256]{1,0:T(8,128)} %get-tuple-element.56) | copy-start | bytes 24580
  356.7 54.8 %all-to-all-start.1 = ((bf16[4,192,256]{2,1,0:T(8,128)(2,1)}), bf16[4,192,256]{2,1,0:T(8,128)(2,1)S(1)}, u32[]{:S(2)}, u32[]{:S(2)}) async-start(bf16[4,192,256]{2,1,0:T(8,128)(2,1)} %bitcast.18), calls=%async_computation.4 | async-start | bytes 786432 | tf_op jit(solution)/shard_map/all_to_all | solution.py:771
  408.7 2.0 copy-start.32
  415.3 1.0 copy-start.22
Sparse Core Ops, SparseCore 0:
  12.6 27.5 all-gather.7
  41.7 12.1 all-gather.5
  56.0 31.6 all-gather.11
  89.7 36.1 all-gather.9
  128.2 57.6 all-gather.13
  218.9 36.8 reduce-scatter.10
  263.9 34.2 reduce-scatter.18
  300.5 34.8 reduce-scatter.8
  339.3 35.9 reduce-scatter.14
  377.5 37.7 reduce-scatter.12
  419.2 75.6 reduce-scatter.16

commit v2 on v1

v2 whole, which is shorter than its diff:
```python
from functools import partial

import jax
import jax.numpy as jnp
from jax import lax
from jax.experimental import pallas as pl
from jax.experimental.pallas import tpu as pltpu
from jax.sharding import PartitionSpec as P

norm_eps = 1e-06
bucket_edges = (12, 16, 23, 32, 46, 64, 91)
LANES = 128
TILE = 128
MIB = 1024 * 1024
NT = (((1,), (1,)), ((), ()))
TN = (((0,), (0,)), ((), ()))


BQ = 256
BK = 256
HD = 64
NEG = -1e30
FLOOR = -1e28
F32 = jnp.float32
BF = jnp.bfloat16


def call(kernel, grid, in_specs, out_specs, out_shape, scratch=(), prefetch=0, vmem=58, name=None, us=1):
    return pl.pallas_call(
        kernel,
        grid_spec=pltpu.PrefetchScalarGridSpec(
            num_scalar_prefetch=prefetch,
            grid=grid,
            in_specs=in_specs,
            out_specs=out_specs,
            scratch_shapes=list(scratch),
        ),
        out_shape=out_shape,
        compiler_params=pltpu.CompilerParams(
            dimension_semantics=("arbitrary",) * len(grid), vmem_limit_bytes=vmem * MIB
        ),
        cost_estimate=pl.CostEstimate(
            flops=int(us * 1e9), bytes_accessed=int(us * 3e6), transcendentals=0
        ),
        name=name,
    )


def whole(*shape):
    return pl.BlockSpec(shape, lambda *_: (0,) * len(shape))


def shaped(shape, dtype):
    return jax.ShapeDtypeStruct(shape, dtype)


def relative_bucket(offset):
    distance = jnp.abs(offset)
    far_bucket = jnp.zeros_like(distance) + 8
    for edge in bucket_edges:
        far_bucket = far_bucket + (distance >= edge).astype(jnp.int32)
    result = jnp.where(distance < 8, distance, far_bucket)
    return result + jnp.where(offset > 0, 16, 0)


def dot(a, b, dims=None):
    if dims is None:
        return jnp.dot(a, b, preferred_element_type=F32)
    return lax.dot_general(a, b, dims, preferred_element_type=F32)


def to_row(column):
    n = column.shape[0]
    return jnp.broadcast_to(column, (n, LANES)).T[0:1, :]


def to_column(row):
    n = row.shape[1]
    return jnp.broadcast_to(row, (LANES, n)).T[:, 0:1]


def split3(x):
    hi = x.astype(BF)
    rest = x - hi.astype(F32)
    mid = rest.astype(BF)
    low = (rest - mid.astype(F32)).astype(BF)
    return hi, mid, low


def key_side(docs_col, rows):
    lane = lax.broadcasted_iota(jnp.int32, (rows, HD), 1)
    same = (docs_col == lane.astype(F32)).astype(F32)
    ones = jnp.where((lane >= 4) & (lane < 7), 1.0, 0.0)
    return jnp.where(lane < 4, same, ones)


def query_side(docs_row, cols, tail):
    row = lax.broadcasted_iota(jnp.int32, (HD, cols), 0)
    other = jnp.where((row < 4) & (docs_row != row.astype(F32)), NEG, 0.0)
    if tail is None:
        return other.astype(BF)
    hi, mid, low = (t.astype(F32) for t in split3(tail))
    part = jnp.where(row == 4, hi, jnp.where(row == 5, mid, jnp.where(row == 6, low, 0.0)))
    return jnp.where(row < 4, other, part).astype(BF)


def shifted(x, by):
    return x if by == 0 else pltpu.roll(x, x.shape[1] - by, 1)


def diagonal_sums(tile):
    total = jnp.zeros((8, 2 * BQ), F32)
    for first in range(0, BK, 8):
        strip = tile[first : first + 8, :]
        total = total + shifted(jnp.concatenate([strip, jnp.zeros((8, BQ), F32)], axis=1), first)
    result = jnp.zeros((1, 2 * BQ), F32)
    for r in range(8):
        result = result + shifted(total, r)[r : r + 1, :]
    return result


def ones_rows(cols):
    return jnp.where(lax.broadcasted_iota(jnp.int32, (16, cols), 0) == 0, 1.0, 0.0).astype(BF)


def fwd_kernel(heads, info, far, qkv_all, dcol, drow, band, mixed_ref, low_ref, lse_ref, k_aug, v_t):
    i = pl.program_id(0)
    seq = qkv_all.shape[0]
    width = heads * HD

    @pl.when(i == 0)
    def _():
        for r in range(seq // BK):
            rows = pl.ds(r * BK, BK)
            side = key_side(to_column(dcol[:, r * BK : (r + 1) * BK]), BK).astype(BF)
            vt = qkv_all[rows, 2 * width : 3 * width].astype(F32).T.astype(BF)
            for h in range(heads):
                k = qkv_all[rows, width + h * HD : width + (h + 1) * HD]
                k_aug[h, rows, :] = jnp.concatenate([k, side], axis=1)
                v_t[h, 0:HD, rows] = vt[h * HD : (h + 1) * HD, :]
                v_t[h, HD : HD + 16, rows] = ones_rows(BK)

    qb = info[0] + i
    lo = info[1 + i]
    hi = info[1 + pl.num_programs(0) + i]
    qt = (qkv_all[pl.ds(pl.multiple_of(qb * BQ, BQ), BQ), 0:width].astype(F32) * (HD**-0.5)).T.astype(BF)
    side = query_side(drow[...], BQ, None)
    q_aug = [jnp.concatenate([qt[h * HD : (h + 1) * HD, :], side], axis=0) for h in range(heads)]

    def step(kb, carry, bias_of):
        rows = pl.ds(pl.multiple_of(kb * BK, BK), BK)
        out = []
        for h in range(heads):
            peak, acc = carry[h]
            s = jnp.dot(k_aug[h, rows, :], q_aug[h], preferred_element_type=F32)
            s = s + bias_of(h, kb)
            new = jnp.maximum(peak, jnp.max(s, axis=0, keepdims=True))
            p = jnp.exp(s - new).astype(BF)
            acc = acc * jnp.exp(peak - new) + jnp.dot(v_t[h, :, rows], p, preferred_element_type=F32)
            out.append((new, acc))
        return tuple(out)

    carry = tuple(
        (jnp.full((1, BQ), FLOOR, F32), jnp.zeros((HD + 16, BQ), F32)) for _ in range(heads)
    )
    carry = lax.fori_loop(lo, jnp.minimum(hi, qb - 1), lambda kb, c: step(kb, c, lambda h, _: far[0, h]), carry)
    carry = lax.fori_loop(
        jnp.maximum(lo, qb - 1),
        jnp.minimum(hi, qb + 2),
        lambda kb, c: step(kb, c, lambda h, t: band[h, t - qb + 1]),
        carry,
    )
    carry = lax.fori_loop(jnp.maximum(lo, qb + 2), hi, lambda kb, c: step(kb, c, lambda h, _: far[1, h]), carry)
    for h in range(heads):
        peak, acc = carry[h]
        total = acc[HD : HD + 1, :]
        mixed = acc[0:HD, :] / total
        mixed_ref[h * HD : (h + 1) * HD, :] = mixed
        low_ref[h * HD : (h + 1) * HD, :] = mixed.astype(BF)
        lse_ref[h : h + 1, :] = peak + jnp.log(total)


def attention_fwd(info, far, qkv_all, dcol, drow, band, rows):
    seq, cols = qkv_all.shape
    width = cols // 3
    heads = width // HD
    steps = rows // BQ
    full = lambda shape: pl.BlockSpec(shape, lambda i, info: (0,) * len(shape))
    return pl.pallas_call(
        partial(fwd_kernel, heads),
        grid_spec=pltpu.PrefetchScalarGridSpec(
            num_scalar_prefetch=1,
            grid=(steps,),
            in_specs=[
                pl.BlockSpec(memory_space=pltpu.SMEM),
                full((seq, cols)),
                full((1, seq)),
                pl.BlockSpec((1, BQ), lambda i, info: (0, info[0] + i)),
                full((heads, 3, BK, BQ)),
            ],
            out_specs=[
                pl.BlockSpec((width, BQ), lambda i, info: (0, i)),
                pl.BlockSpec((width, BQ), lambda i, info: (0, i)),
                pl.BlockSpec((heads, BQ), lambda i, info: (0, i)),
            ],
            scratch_shapes=[
                pltpu.VMEM((heads, seq, 2 * HD), BF),
                pltpu.VMEM((heads, HD + 16, seq), BF),
            ],
        ),
        out_shape=[
            jax.ShapeDtypeStruct((width, rows), F32),
            jax.ShapeDtypeStruct((width, rows), BF),
            jax.ShapeDtypeStruct((heads, rows), F32),
        ],
        compiler_params=pltpu.CompilerParams(
            dimension_semantics=("arbitrary",), vmem_limit_bytes=58 * 1024 * 1024
        ),
        cost_estimate=pl.CostEstimate(
            flops=int(19 * 1e9), bytes_accessed=int(19 * 3e6), transcendentals=0
        ),
        name="attention_fwd",
    )(info, far, qkv_all, dcol, drow, band)


def bwd_kernel(
    heads, info, far, qkv_all, dcol, drow, band, mixed_ref, lse_ref, m0, m1, m2, m3,
    dq_ref, dkv_ref, skew_ref, side_ref, k_aug, v_aug, k_t, near_acc, dkv_acc,
):
    i = pl.program_id(0)
    seq = qkv_all.shape[0]
    width = heads * HD

    @pl.when(i == 0)
    def _():
        near_acc[...] = jnp.zeros_like(near_acc)
        dkv_acc[...] = jnp.zeros_like(dkv_acc)
        side_ref[...] = jnp.zeros_like(side_ref)
        for r in range(seq // BK):
            rows = pl.ds(r * BK, BK)
            side = key_side(to_column(dcol[:, r * BK : (r + 1) * BK]), BK).astype(BF)
            lane = lax.broadcasted_iota(jnp.int32, (BK, HD), 1)
            ones = jnp.where(lane < 3, 1.0, 0.0).astype(BF)
            kt = qkv_all[rows, width : 2 * width].astype(F32).T.astype(BF)
            for h in range(heads):
                k = qkv_all[rows, width + h * HD : width + (h + 1) * HD]
                v = qkv_all[rows, 2 * width + h * HD : 2 * width + (h + 1) * HD]
                k_aug[h, rows, :] = jnp.concatenate([k, side], axis=1)
                v_aug[h, rows, :] = jnp.concatenate([v, ones], axis=1)
                k_t[h, 0:HD, rows] = kt[h * HD : (h + 1) * HD, :]
                k_t[h, HD : HD + 16, rows] = ones_rows(BK)

    steps = pl.num_programs(0)
    block = lax.rem(info[1 + 2 * steps] + steps - i, steps)
    qb = info[0] + block
    lo = info[1 + block]
    hi = info[1 + steps + block]
    dmix = m0[...]
    for s, ref in ((1, m1), (2, m2), (3, m3)):
        dmix = jnp.where(i == s, ref[...], dmix)
    q_scaled = qkv_all[pl.ds(pl.multiple_of(qb * BQ, BQ), BQ), 0:width].astype(F32) * (HD**-0.5)
    qt = q_scaled.T.astype(BF)
    q_rows = q_scaled.astype(BF)
    dmix_t = dmix.astype(F32)
    dmix_rows = dmix_t.T.astype(BF)
    zero = jnp.zeros((BQ, HD), BF)
    row = lax.broadcasted_iota(jnp.int32, (HD, BQ), 0)
    q_aug, d_aug, rhs = [], [], []
    for h in range(heads):
        cols = slice(h * HD, (h + 1) * HD)
        lse = lse_ref[h : h + 1, :]
        kinds = []
        for tail in (far[0, h] - lse, -lse, far[1, h] - lse):
            kinds.append(jnp.concatenate([qt[cols, :], query_side(drow[...], BQ, tail)], axis=0))
        q_aug.append(kinds)
        delta = -jnp.sum(dmix_t[cols, :] * mixed_ref[cols, :], axis=0, keepdims=True)
        a, b, c = (t.astype(F32) for t in split3(delta))
        part = jnp.where(row == 0, a, jnp.where(row == 1, b, jnp.where(row == 2, c, 0.0)))
        d_aug.append(jnp.concatenate([dmix_t[cols, :].astype(BF), part.astype(BF)], axis=0))
        top = jnp.concatenate([dmix_rows[:, cols], zero], axis=1)
        low = jnp.concatenate([zero, q_rows[:, cols]], axis=1)
        rhs.append(jnp.concatenate([top, low], axis=0))

    def step(kb, carry, kind):
        rows = pl.ds(pl.multiple_of(kb * BK, BK), BK)
        out = []
        for h in range(heads):
            s = jnp.dot(k_aug[h, rows, :], q_aug[h][kind], preferred_element_type=F32)
            if kind == 1:
                s = s + band[h, kb - qb + 1]
            p = jnp.exp(s)
            dp = jnp.dot(v_aug[h, rows, :], d_aug[h], preferred_element_type=F32)
            ds = p * dp
            ds_low = ds.astype(BF)
            if kind == 1:
                near_acc[h, kb - qb + 1] = near_acc[h, kb - qb + 1] + ds_low.astype(F32)
            both = jnp.concatenate([p.astype(BF), ds_low], axis=1)
            dkv_acc[h, rows, :] += jnp.dot(both, rhs[h], preferred_element_type=F32)
            out.append(carry[h] + jnp.dot(k_t[h, :, rows], ds_low, preferred_element_type=F32))
        return tuple(out)

    zero_dq = jnp.zeros((HD + 16, BQ), F32)
    left = lax.fori_loop(lo, jnp.minimum(hi, qb - 1), lambda kb, c: step(kb, c, 0), (zero_dq,) * heads)
    near = lax.fori_loop(
        jnp.maximum(lo, qb - 1), jnp.minimum(hi, qb + 2), lambda kb, c: step(kb, c, 1), left
    )
    last = lax.fori_loop(jnp.maximum(lo, qb + 2), hi, lambda kb, c: step(kb, c, 2), near)
    for h in range(heads):
        dq_ref[h * HD : (h + 1) * HD, :] = (last[h][0:HD, :] * (HD**-0.5)).astype(BF)
        side_ref[2 * h : 2 * h + 1, :] += left[h][HD : HD + 1, :]
        side_ref[2 * h + 1 : 2 * h + 2, :] += last[h][HD : HD + 1, :] - near[h][HD : HD + 1, :]

    @pl.when(i == pl.num_programs(0) - 1)
    def _():
        for h in range(heads):
            for t in range(3):
                skew_ref[3 * h + t : 3 * h + t + 1, :] = diagonal_sums(near_acc.at[h, t])
        for r in range(seq // BK):
            rows = pl.ds(r * BK, BK)
            acc = [dkv_acc[h, rows, :] for h in range(heads)]
            dk = [a[:, HD : 2 * HD] for a in acc]
            dv = [a[:, 0:HD] for a in acc]
            dkv_ref[rows, :] = jnp.concatenate(dk + dv, axis=1).astype(BF)


def attention_bwd(info, far, qkv_all, dcol, drow, band, mixed, lse, dmix, rows):
    seq, cols = qkv_all.shape
    width = cols // 3
    heads = width // HD
    steps = rows // BQ
    full = lambda shape: pl.BlockSpec(shape, lambda i, info: (0,) * len(shape))
    block = lambda i, info: lax.rem(info[1 + 2 * steps] + steps - i, steps)
    return pl.pallas_call(
        partial(bwd_kernel, heads),
        grid_spec=pltpu.PrefetchScalarGridSpec(
            num_scalar_prefetch=1,
            grid=(steps,),
            in_specs=[
                pl.BlockSpec(memory_space=pltpu.SMEM),
                full((seq, cols)),
                full((1, seq)),
                pl.BlockSpec((1, BQ), lambda i, info: (0, info[0] + block(i, info))),
                full((heads, 3, BK, BQ)),
                pl.BlockSpec((width, BQ), lambda i, info: (0, block(i, info))),
                pl.BlockSpec((heads, BQ), lambda i, info: (0, block(i, info))),
                *[full((width, BQ))] * 4,
            ],
            out_specs=[
                pl.BlockSpec((width, BQ), lambda i, info: (0, block(i, info))),
                full((seq, 2 * width)),
                full((16, 2 * BK)),
                full((8, BQ)),
            ],
            scratch_shapes=[
                pltpu.VMEM((heads, seq, 2 * HD), BF),
                pltpu.VMEM((heads, seq, 2 * HD), BF),
                pltpu.VMEM((heads, HD + 16, seq), BF),
                pltpu.VMEM((heads, 3, BK, BQ), F32),
                pltpu.VMEM((heads, seq, 2 * HD), F32),
            ],
        ),
        out_shape=[
            jax.ShapeDtypeStruct((width, rows), BF),
            jax.ShapeDtypeStruct((seq, 2 * width), BF),
            jax.ShapeDtypeStruct((16, 2 * BK), F32),
            jax.ShapeDtypeStruct((8, BQ), F32),
        ],
        compiler_params=pltpu.CompilerParams(
            dimension_semantics=("arbitrary",), vmem_limit_bytes=58 * 1024 * 1024
        ),
        cost_estimate=pl.CostEstimate(
            flops=int(24 * 1e9), bytes_accessed=int(24 * 3e6), transcendentals=0
        ),
        name="attention_bwd",
    )(info, far, qkv_all, dcol, drow, band, mixed, lse, *dmix)


def band_kernel(vec_ref, band_ref):
    heads = band_ref.shape[0]
    for h in range(heads):
        for t in range(3):
            wide = jnp.broadcast_to(vec_ref[3 * h + t : 3 * h + t + 1, :], (BK, 2 * BQ))
            band_ref[h, t] = pltpu.roll(wide, 0, 1, stride=1, stride_axis=0)[:, 0:BQ]


def pack_kernel(qkv_ref, router_ref, one_ref, two_ref, out_ref):
    experts, rows = router_ref.shape
    fill = jnp.zeros((LANES - experts - 2, rows), F32)
    tail = [r[...].astype(F32) for r in (router_ref, one_ref, two_ref)]
    tail = jnp.concatenate([*tail, fill], axis=0).T.astype(BF)
    out_ref[...] = jnp.concatenate([*(qkv_ref[c] for c in range(3)), tail], axis=1)


def qkv_kernel(
    cols, experts, count, at, own_ref, other_ref, *refs
):
    pieces = refs[:count]
    qkv_ref, norm_ref, scale_ref, small_ref, gains_ref = refs[count:]
    i = pl.program_id(0)

    @pl.when(i == 0)
    def _():
        slot = 0
        for piece in pieces:
            for s in range(piece.shape[0]):
                first = pl.multiple_of(at[slot], 16)
                small_ref[pl.ds(first, piece.shape[1]), :] = piece[s]
                slot += 1
        tail = small_ref[:, cols:].astype(F32).T
        gains_ref[...] = tail[experts : experts + 8, :]

    x = jnp.where(i < pl.num_programs(0) // 2, own_ref[...], other_ref[...]).astype(F32)
    scale = lax.rsqrt(jnp.mean(x * x, axis=-1, keepdims=True) + norm_eps)
    normed = (x * scale * gains_ref[0:1, :]).astype(BF)
    norm_ref[...] = normed
    scale_ref[...] = to_row(scale)
    qkv_ref[...] = dot(normed, small_ref[:, 0:cols]).astype(BF)


def router_parts(hidden, gain, router, chosen, experts):
    scale = lax.rsqrt(jnp.mean(hidden * hidden, axis=-1, keepdims=True) + norm_eps)
    hat = hidden * scale
    normed = (hat * gain).astype(BF)
    lane = lax.broadcasted_iota(jnp.int32, (hidden.shape[0], LANES), 1)
    logits = jnp.where(lane < experts, dot(normed, router), NEG)
    weights = jnp.exp(logits - jnp.max(logits, axis=-1, keepdims=True))
    route = weights / jnp.sum(weights, axis=-1, keepdims=True)
    one_hot = jnp.where(lane.astype(F32) == chosen, 1.0, 0.0)
    gate = jnp.sum(route * one_hot, axis=-1, keepdims=True)
    return scale, hat, normed, route, one_hot, gate


def hidden_kernel(experts, at, *refs):
    tok_ref, mix_refs, wout_ref = refs[0], refs[1:5], refs[5]
    gains_ref, small_ref, chosen_ref, hidden_ref, norm_ref, gate_ref = refs[6:]
    mixed = jnp.concatenate([r[...] for r in mix_refs], axis=0)
    both = mixed.astype(F32).T.astype(BF)
    hidden = tok_ref[...].astype(F32) + dot(both, wout_ref[...], NT)
    parts = router_parts(hidden, gains_ref[1:2, :], small_ref[...], to_column(chosen_ref[...]), experts)
    hidden_ref[...] = hidden
    norm_ref[...] = parts[2]
    gate_ref[...] = to_row(parts[5])


def expert_kernel(
    owner, at, pos_row, norm_ref, cot_ref, gate_ref, w_ref,
    b0, b1, b2, b3, eo_ref, x_ref, de_ref, act_ref, di_ref, eo_s, dr_s, pos_col,
):
    i = pl.program_id(0)
    z = at[0]
    rows = norm_ref.shape[0]
    width = norm_ref.shape[1]
    ff = w_ref.shape[1] // 2
    place = lax.broadcasted_iota(jnp.int32, (TILE, rows), 0) + i * TILE
    hit = pos_row[...] == place
    pick = jnp.where(hit, 1.0, 0.0).astype(BF)
    x = dot(pick, norm_ref[...]).astype(BF)
    cot = dot(pick, cot_ref[...])
    gate = jnp.sum(jnp.where(hit, gate_ref[...], 0.0), axis=1, keepdims=True)
    d_e = (gate * cot).astype(BF)
    w_in = w_ref[:, 0:ff]
    w_down = w_ref[:, ff : 2 * ff]
    inner = dot(x, w_in)
    half = 0.5 * (1.0 + lax.erf(inner * (0.5**0.5)))
    active = (inner * half).astype(BF)
    slope = half + inner * (jnp.exp(-0.5 * inner * inner) * 0.3989422804014327)
    d_inner = (dot(d_e, w_down) * slope).astype(BF)
    terms = dot(active, w_down, NT)
    d_rows = dot(d_inner, w_in, NT)
    d_gate = jnp.sum(cot * terms, axis=1, keepdims=True)
    lane = lax.broadcasted_iota(jnp.int32, (TILE, LANES), 1)
    hi, mid, low = (t.astype(F32) for t in split3(d_gate))
    extra = jnp.where(lane == 0, hi, jnp.where(lane == 1, mid, jnp.where(lane == 2, low, 0.0)))
    here = pl.ds(pl.multiple_of(i * TILE, TILE), TILE)
    eo_s[here, :] = terms.astype(BF)
    dr_s[here, :] = jnp.concatenate([d_rows.astype(BF), extra.astype(BF)], axis=1)
    x_ref[...] = x
    de_ref[...] = d_e
    act_ref[...] = active
    di_ref[...] = d_inner

    @pl.when(i == pl.num_programs(0) - 1)
    def _():
        total = dr_s.shape[0]
        part = rows // 4
        pos_col[...] = jnp.broadcast_to(pos_row[...].astype(F32), (LANES, rows)).T
        for r, back_ref in enumerate((b0, b1, b2, b3)):
            g = lax.rem(z + r, 4)
            mine = pl.ds(pl.multiple_of(g * part, part), part)
            place = lax.broadcasted_iota(jnp.int32, (part, total), 1).astype(F32)
            pick = jnp.where(pos_col[mine, 0:1] == place, 1.0, 0.0).astype(BF)
            back = dot(pick, dr_s[...])
            back_ref[0:part, :] = back[:, 0:width].astype(BF)
            tail = back[:, width : width + LANES].T
            d_gate = tail[0:1, :] + tail[1:2, :] + tail[2:3, :]
            row = lax.broadcasted_iota(jnp.int32, (16, part), 0)
            strip = jnp.where(row == 0, jnp.broadcast_to(d_gate, (16, part)), 0.0)
            fill = jnp.zeros((16, width - part), F32)
            back_ref[part : part + 16, :] = jnp.concatenate([strip, fill], axis=1).astype(BF)
            eo_ref[:, mine] = dot(pick, eo_s[...]).T.astype(BF)


def weight_grad_kernel(owner, slot, at, rows_ref, cols_ref, keep_ref, send_ref, acc):
    i = pl.program_id(0)
    last = pl.num_programs(0) - 1
    me = owner[i]
    before = owner[jnp.maximum(i - 1, 0)]
    after = owner[jnp.minimum(i + 1, last)]

    @pl.when((i == 0) | (before != me))
    def _():
        acc[...] = jnp.zeros_like(acc)

    acc[...] += dot(rows_ref[...], cols_ref[...], TN)

    @pl.when((i == last) | (after != me))
    def _():
        half = keep_ref.shape[0]
        keep_ref[...] = acc[pl.ds(pl.multiple_of(at[1] * half, half), half), :].astype(BF)
        send_ref[...] = acc[pl.ds(pl.multiple_of((1 - at[1]) * half, half), half), :].astype(BF)


def split_rows(at, first_slot, acc, outs):
    if len(outs) == 1:
        outs[0][...] = acc[...].astype(BF)
        return
    slot = first_slot
    for out in outs:
        step = out.shape[0] // 4
        for s in range(4):
            first = pl.multiple_of(at[slot], 8)
            out[s * step : (s + 1) * step, :] = acc[pl.ds(first, step), :].astype(BF)
            slot += 1


def hidden_back_kernel(experts, at, *refs):
    back_refs, (hidden_ref, cot_ref, gains_ref, router_ref, chosen_ref) = refs[:4], refs[4:9]
    wout_ref, mix_refs = refs[9], refs[10:14]
    dmix_refs, dh_ref, small_ref, gout_ref = refs[14:18], refs[18], refs[19], refs[20]
    part, model = hidden_ref.shape
    back = sum(r[...].astype(F32) for r in back_refs)
    gain = gains_ref[1:2, :]
    router = router_ref[...]
    scale, hat, normed, route, one_hot, gate = router_parts(
        hidden_ref[...], gain, router, to_column(chosen_ref[...]), experts
    )
    d_gate = to_column(back[part : part + 1, 0:part])
    d_logits = (d_gate * gate) * (one_hot - route)
    parts = split3(d_logits)
    d_normed = back[0:part, :]
    g_router = jnp.zeros((LANES, model), F32)
    for p in parts:
        d_normed = d_normed + dot(p, router, NT)
        g_router = g_router + dot(p, normed, TN)
    small_ref[...] = jnp.zeros_like(small_ref)
    small_ref[0:experts, :] = g_router[0:experts, :]
    small_ref[experts : experts + 1, :] = jnp.sum(d_normed * hat, axis=0, keepdims=True)
    d_hat = d_normed * gain
    d_hidden = cot_ref[...].astype(F32) + scale * (
        d_hat - hat * jnp.mean(d_hat * hat, axis=-1, keepdims=True)
    )
    d_attn = d_hidden.astype(BF)
    d_attn_t = d_hidden.T.astype(BF)
    d_mixed = dot(d_attn, wout_ref[...]).T.astype(BF)
    width = model // 4
    for s in range(4):
        r = (4 - s) % 4
        dmix_refs[r][...] = d_mixed[s * width : (s + 1) * width, :]
    dh_ref[...] = d_hidden
    mixed = jnp.concatenate([r[...] for r in mix_refs], axis=0)
    gout_ref[...] = dot(d_attn_t, mixed, NT)


def qkv_back_kernel(
    at, dq_ref, dkv_ref, got_ref, norm_ref, tok_ref, scale_ref, gains_ref, w_ref, dh_ref, gout_ref,
    terms_ref, gain_out_ref, *rest,
):
    *gw_refs, acc = rest
    i = pl.program_id(0)
    width = dq_ref.shape[0]
    dkv = dkv_ref[...].astype(F32) + got_ref[...].astype(F32)
    d_qkv = jnp.concatenate([dq_ref[...].astype(F32).T, dkv], axis=1).astype(BF)
    scale = to_column(scale_ref[...])
    hat = tok_ref[...].astype(F32) * scale
    terms = dot(d_qkv, w_ref[:, 0 : 3 * width], NT)
    d_hat = terms * gains_ref[0:1, :]
    mean = jnp.mean(d_hat * hat, axis=-1, keepdims=True)
    grad = scale * (d_hat - hat * mean) + jnp.where(i == at[0], dh_ref[...], 0.0)

    @pl.when(i == 0)
    def _():
        acc[:, 0 : 3 * width] = jnp.zeros((acc.shape[0], 3 * width), F32)
        acc[:, 3 * width :] = gout_ref[...]
        gain_out_ref[...] = jnp.zeros_like(gain_out_ref)

    gain_out_ref[0:1, :] += jnp.sum(terms * hat, axis=0, keepdims=True)
    acc[:, 0 : 3 * width] += dot(norm_ref[...], d_qkv, TN)
    terms_ref[...] = grad.T.astype(BF)

    @pl.when(i == pl.num_programs(0) - 1)
    def _():
        split_rows(at, 4, acc, gw_refs)


def out_kernel(eo_ref, hidden_ref, gate_ref, out_ref):
    out_ref[...] = (hidden_ref[...] + eo_ref[...].astype(F32) * gate_ref[...]).astype(BF)


def placement(chosen, experts, tiles):
    rows = chosen.shape[0]
    ids = jnp.arange(experts, dtype=jnp.int32)
    one_hot = chosen[:, None] == ids[None, :]
    below = jnp.arange(rows)[:, None] > jnp.arange(rows)[None, :]
    earlier = dot(below.astype(BF), one_hot.astype(BF)).astype(jnp.int32)
    count = jnp.sum(one_hot.astype(jnp.int32), axis=0)
    used = jnp.maximum((count + TILE - 1) // TILE, 1)
    ends = jnp.sum(jnp.where(ids[None, :] <= ids[:, None], used[None, :], 0), axis=1)
    first = (ends - used) * TILE
    pos = jnp.sum(jnp.where(one_hot, earlier + first[None, :], 0), axis=1).astype(jnp.int32)
    tile_ids = jnp.arange(tiles, dtype=jnp.int32)
    owner = jnp.sum((ends[None, :] <= tile_ids[:, None]).astype(jnp.int32), axis=1)
    return pos, jnp.minimum(owner, experts - 1).astype(jnp.int32)


def xor_step(x, axis, s):
    return lax.ppermute(x, axis, [(i, i ^ s) for i in range(lax.axis_size(axis))])


def turn(x, s):
    return lax.ppermute(x, "tp", [(i, (i + s) % 4) for i in range(4)])


def gather_turns(x):
    return [x] + [turn(x, s) for s in (1, 2, 3)]


def scatter_turns(pieces):
    return [pieces[0]] + [turn(pieces[r], r) for r in (1, 2, 3)]


def after(x, *others):
    return lax.optimization_barrier((x, others))[0]


def dense_scatter(parts):
    if len(parts) == 1:
        return lax.psum_scatter(parts[0], ("fsdp", "ctx"), scatter_dimension=0, tiled=True).astype(F32)
    keep, send = parts
    both = keep + xor_step(send, "ctx", 1)
    step = keep.shape[0] // 4
    total = both[0:step].astype(F32)
    for s in (1, 2, 3):
        total = total + xor_step(both[s * step : (s + 1) * step], "fsdp", s).astype(F32)
    return total


def sum_all(x):
    if lax.axis_size("fsdp") != 4 or lax.axis_size("ctx") != 2:
        return lax.psum(x, ("fsdp", "ctx", "tp"))
    x = x + xor_step(x, "ctx", 1)
    x = x + xor_step(x, "fsdp", 1) + xor_step(x, "fsdp", 2) + xor_step(x, "fsdp", 3)
    return x + turn(x, 1) + turn(x, 2) + turn(x, 3)


def shards(
    tokens,
    grad_out,
    w_qkv,
    w_attn_out,
    rel_bias,
    gain_attn,
    gain_ffn,
    w_router,
    w_in,
    w_down,
    expert_ids,
    doc_ids,
):
    rows, model = tokens.shape
    heads = rel_bias.shape[1]
    width = w_qkv.shape[2]
    own = w_qkv.shape[0]
    experts = w_router.shape[1]
    ff = w_in.shape[2]
    seq = doc_ids.shape[0]
    fsdp_n = lax.axis_size("fsdp")
    ctx_n = lax.axis_size("ctx")
    tp_n = lax.axis_size("tp")
    fsdp_at = lax.axis_index("fsdp")
    ctx_at = lax.axis_index("ctx")
    tp_at = lax.axis_index("tp")
    dense_at = fsdp_at * ctx_n + ctx_at
    part = rows // tp_n
    share = model // tp_n
    blocks = rows // BQ
    dense = ("fsdp", "ctx")
    square = fsdp_n == 4 and ctx_n == 2

    qkv_cols = 3 * width
    cols = qkv_cols + LANES
    small = call(
        pack_kernel,
        (1,),
        [whole(3, own, width), whole(experts, own), whole(1, own), whole(1, own)],
        whole(own, cols),
        shaped((own, cols), BF),
        name="pack_small",
    )(w_qkv.transpose(1, 0, 2), w_router.T, gain_attn[None, :], gain_ffn[None, :])
    half = model // ctx_n
    mine_rows = lambda at: jnp.concatenate(
        [lax.dynamic_slice_in_dim(w.reshape(-1, ff), at * half, half, 0) for w in (w_in, w_down)], axis=1
    )
    if square:
        near = jnp.stack([small] + [xor_step(small, "fsdp", s) for s in (1, 2, 3)])
        small_parts = [near, xor_step(near, "ctx", 1)]
        starts = [((fsdp_at ^ s) * 2 + c) * own for c in (ctx_at, 1 - ctx_at) for s in range(4)]
    else:
        small_parts = [lax.all_gather(small, dense, axis=0, tiled=True)[None]]
        starts = [jnp.int32(0)]
    tokens_other = xor_step(tokens, "ctx", 1)
    out_line = jnp.concatenate(gather_turns(w_attn_out), axis=1)
    out_all = lax.all_gather(out_line, dense, axis=0, tiled=True)
    w_half = mine_rows(ctx_at)

    tiles = (rows + experts * (TILE - 1)) // TILE
    pos, owner = placement(expert_ids[:, 0], experts, tiles)
    pos = pos[None, :]
    chosen = expert_ids[:, 0].astype(F32)[None, :]
    docs = doc_ids.astype(F32)[None, :]
    firsts = lax.dynamic_slice_in_dim(doc_ids.reshape(-1, BQ)[:, 0], ctx_at * blocks, blocks)
    lasts = lax.dynamic_slice_in_dim(doc_ids.reshape(-1, BQ)[:, BQ - 1], ctx_at * blocks, blocks)
    low = jnp.sum((doc_ids[None, :] < firsts[:, None]).astype(jnp.int32), axis=1) // BK
    high = (jnp.sum((doc_ids[None, :] <= lasts[:, None]).astype(jnp.int32), axis=1) + BK - 1) // BK
    info = jnp.concatenate(((ctx_at * blocks)[None], low, high, tp_at[None])).astype(jnp.int32)
    wrapped = jnp.arange(2 * BQ, dtype=jnp.int32)
    wrapped = jnp.where(wrapped < BQ, wrapped, wrapped - 2 * BQ)
    offsets = (jnp.arange(3, dtype=jnp.int32)[:, None] - 1) * BK - wrapped[None, :]
    selector = relative_bucket(offsets)[:, :, None] == jnp.arange(rel_bias.shape[0])[None, None, :]
    selector = selector.astype(F32)
    vectors = jnp.einsum("tcb,bh->htc", selector, rel_bias, precision=lax.Precision.HIGHEST)
    far = jnp.stack((rel_bias[15], rel_bias[31]))
    band = call(
        band_kernel,
        (1,),
        [whole(3 * heads, 2 * BQ)],
        whole(heads, 3, BK, BQ),
        shaped((heads, 3, BK, BQ), F32),
        name="bias_band",
    )(vectors.reshape(3 * heads, 2 * BQ))
    columns = tp_at * share
    starts = [s.astype(jnp.int32) for s in starts]
    at = jnp.stack([tp_at, ctx_at, ctx_at * blocks, fsdp_at] + starts).astype(jnp.int32)
    starts = jnp.stack(starts + [ctx_at * blocks]).astype(jnp.int32)
    early = (w_half, pos, owner, chosen, docs, info, band, far, at, starts, selector)
    (small_parts, tokens_other, early) = lax.optimization_barrier((small_parts, tokens_other, early))
    w_half, pos, owner, chosen, docs, info, band, far, at, starts, selector = early

    w_experts = lax.all_gather(w_half, dense, axis=0, tiled=True)
    slot = owner ^ fsdp_at if square else owner
    slot = slot.astype(jnp.int32)

    steps = seq // BQ
    n_own = steps // 2
    base = lambda i, at: at[len_starts] + i
    len_starts = starts.shape[0] - 1
    turned = lambda i, at: jnp.where(i < n_own, at[len_starts] + i, n_own - at[len_starts] + i - n_own)
    qkv_all, normed_one, scale_one, small_all, gains = call(
        partial(qkv_kernel, qkv_cols, experts, len(small_parts)),
        (steps,),
        [
            pl.BlockSpec((BQ, model), lambda i, at: (jnp.minimum(i, n_own - 1), 0)),
            pl.BlockSpec((BQ, model), lambda i, at: (jnp.maximum(i - n_own, 0), 0)),
            *[whole(*p.shape) for p in small_parts],
        ],
        [
            pl.BlockSpec((BQ, qkv_cols), lambda i, at: (turned(i, at), 0)),
            pl.BlockSpec((BQ, model), lambda i, at: (turned(i, at), 0)),
            pl.BlockSpec((1, BQ), lambda i, at: (0, turned(i, at))),
            whole(model, cols),
            whole(8, model),
        ],
        [
            shaped((seq, qkv_cols), BF),
            shaped((seq, model), BF),
            shaped((1, seq), F32),
            shaped((model, cols), BF),
            shaped((8, model), F32),
        ],
        prefetch=1,
        us=8,
        name="norm_qkv",
    )(starts, tokens, tokens_other, *small_parts)
    mixed, mixed_low, lse = attention_fwd(info, far, qkv_all, docs, docs, band, rows)
    mixed_turns = gather_turns(mixed_low)

    router_block = whole(model, LANES)
    router = small_all[:, qkv_cols:]
    hidden, normed_two, gate_row = call(
        partial(hidden_kernel, experts),
        (blocks,),
        [
            pl.BlockSpec((BQ, model), lambda i, at: (i, 0)),
            *[pl.BlockSpec((width, BQ), lambda i, at: (0, i))] * 4,
            whole(model, model),
            whole(8, model),
            router_block,
            pl.BlockSpec((1, BQ), lambda i, at: (0, i)),
        ],
        [
            pl.BlockSpec((BQ, model), lambda i, at: (i, 0)),
            pl.BlockSpec((BQ, model), lambda i, at: (i, 0)),
            pl.BlockSpec((1, BQ), lambda i, at: (0, i)),
        ],
        [shaped((rows, model), F32), shaped((rows, model), BF), shaped((1, rows), F32)],
        prefetch=1,
        us=7,
        name="hidden_router",
    )(at, tokens, *mixed_turns, out_all, gains, router, chosen)
    sorted_rows = tiles * TILE
    sorted_spec = lambda cols: pl.BlockSpec((TILE, cols), lambda i, *_: (i, 0))
    *back, eo_t, x_sorted, d_expert, active, d_inner = call(
        expert_kernel,
        (tiles,),
        [
            whole(1, rows),
            whole(rows, model),
            whole(rows, model),
            whole(1, rows),
            pl.BlockSpec((model, 2 * ff), lambda i, owner, at: (owner[i], 0)),
        ],
        [
            *[whole(part + 16, model)] * 4,
            whole(model, rows),
            sorted_spec(model),
            sorted_spec(model),
            sorted_spec(ff),
            sorted_spec(ff),
        ],
        [
            *[shaped((part + 16, model), BF)] * 4,
            shaped((model, rows), BF),
            shaped((sorted_rows, model), BF),
            shaped((sorted_rows, model), BF),
            shaped((sorted_rows, ff), BF),
            shaped((sorted_rows, ff), BF),
        ],
        scratch=[
            pltpu.VMEM((sorted_rows, model), BF),
            pltpu.VMEM((sorted_rows, model + LANES), BF),
            pltpu.VMEM((rows, LANES), F32),
        ],
        prefetch=2,
        us=30,
        name="experts",
    )(owner, at, pos, normed_two, grad_out, gate_row, w_experts)
    back_mine = scatter_turns(back)
    exchanged = []
    for left, right in ((x_sorted, d_inner), (d_expert, active)):
        keep, send = call(
            weight_grad_kernel,
            (tiles,),
            [sorted_spec(model), sorted_spec(ff)],
            [pl.BlockSpec((half, ff), lambda i, owner, slot, at: (slot[i], 0))] * 2,
            [shaped((experts * half, ff), BF)] * 2,
            scratch=[pltpu.VMEM((model, ff), F32)],
            prefetch=3,
            us=0.1,
            name="expert_weight_grads",
        )(owner, slot, at, left, right)
        exchanged.append((keep, xor_step(send, "ctx", 1)))
    (keep_in, got_in), (keep_down, got_down) = exchanged
    both_in = keep_in + got_in
    back_mine, both_in, keep_down = lax.optimization_barrier((back_mine, both_in, keep_down))

    small_rows = -(-(experts + 1) // 8) * 8
    row_block = pl.BlockSpec((part, model), lambda i, at: (at[0], 0))
    col_block = pl.BlockSpec((width, part), lambda i, at: (0, at[0]))
    piece = whole(width, part)
    grad_rows = [model // 2] * 2 if square else [model]
    outs = call(
        partial(hidden_back_kernel, experts),
        (1,),
        [
            *[whole(part + 16, model)] * 4,
            row_block,
            row_block,
            whole(8, model),
            router_block,
            pl.BlockSpec((1, part), lambda i, at: (0, at[0])),
            whole(model, model),
            *[col_block] * 4,
        ],
        [*[piece] * 4, whole(part, model), whole(small_rows, model), whole(model, model)],
        [
            *[shaped((width, part), BF)] * 4,
            shaped((part, model), F32),
            shaped((small_rows, model), F32),
            shaped((model, model), F32),
        ],
        prefetch=1,
        us=6,
        name="hidden_back",
    )(at, *back_mine, hidden, grad_out, gains, router, chosen, out_all, *mixed_turns)
    dmix_out, d_hidden, small_grads, grad_out_w = outs[0:4], outs[4], outs[5], outs[6]
    dmix = scatter_turns(dmix_out)
    both_down = keep_down + got_down
    expert_sums = []
    for both in (both_in, both_down):
        if square:
            pieces = [both[s * half : (s + 1) * half] for s in range(4)]
            expert_sums.append([pieces[0]] + [xor_step(pieces[s], "fsdp", s) for s in (1, 2, 3)])
        else:
            expert_sums.append([lax.psum_scatter(both, "fsdp", scatter_dimension=0, tiled=True)])
    in_sums, down_sums = expert_sums
    dmix, in_sums, eo_t = lax.optimization_barrier((dmix, in_sums, eo_t))
    eo_mine = lax.psum_scatter(eo_t, "tp", scatter_dimension=0, tiled=True)

    dq_t, dkv, skew, sides = attention_bwd(
        info, far, qkv_all, docs, docs, band, mixed, lse, dmix, rows
    )
    other = lax.dynamic_slice_in_dim(dkv, (1 - ctx_at) * rows, rows)
    got = lax.ppermute(other, "ctx", [(0, 1), (1, 0)])
    got, down_sums = lax.optimization_barrier((got, down_sums))
    outs = call(
        qkv_back_kernel,
        (blocks,),
        [
            pl.BlockSpec((width, BQ), lambda i, at: (0, i)),
            pl.BlockSpec((BQ, 2 * width), lambda i, at: (at[2] + i, 0)),
            pl.BlockSpec((BQ, 2 * width), lambda i, at: (i, 0)),
            pl.BlockSpec((BQ, model), lambda i, at: (at[2] + i, 0)),
            pl.BlockSpec((BQ, model), lambda i, at: (i, 0)),
            pl.BlockSpec((1, BQ), lambda i, at: (0, at[2] + i)),
            whole(8, model),
            whole(model, cols),
            whole(part, model),
            whole(model, model),
        ],
        [
            pl.BlockSpec((model, BQ), lambda i, at: (0, i)),
            whole(8, model),
            *[whole(n, qkv_cols + model) for n in grad_rows],
        ],
        [
            shaped((model, rows), BF),
            shaped((8, model), F32),
            *[shaped((n, qkv_cols + model), BF) for n in grad_rows],
        ],
        scratch=[pltpu.VMEM((model, qkv_cols + model), F32)],
        prefetch=1,
        us=9,
        name="qkv_back",
    )(at, dq_t, dkv, got, normed_one, tokens, scale_one, gains, small_all, d_hidden, grad_out_w)
    terms, gain_sum, grad_dense = outs[0], outs[1], outs[2:]
    grad_tokens = lax.psum_scatter(terms, "tp", scatter_dimension=0, tiled=True).astype(F32)
    grad_dense = dense_scatter(grad_dense)
    grad_out_mine = grad_dense[:, qkv_cols : qkv_cols + width]
    for s in (1, 2, 3):
        first = qkv_cols + s * width
        piece_s = grad_dense[:, first : first + width].astype(BF)
        grad_out_mine = grad_out_mine + turn(piece_s, 4 - s).astype(F32)
    grad_in_mine, grad_down_mine = (
        sum(p.astype(F32) for p in after(pieces, gain_sum)) for pieces in expert_sums
    )

    diagonals = skew[0 : 3 * heads].reshape(heads, 3, 2 * BQ)
    table = jnp.einsum("htc,tcb->bh", diagonals, selector, precision=lax.Precision.HIGHEST)
    side = jnp.sum(sides[0 : 2 * heads], axis=1).reshape(heads, 2)
    bucket_ids = jnp.arange(rel_bias.shape[0])[:, None]
    table = table + jnp.where(bucket_ids == 15, side[None, :, 0], 0.0)
    table = table + jnp.where(bucket_ids == 31, side[None, :, 1], 0.0)
    slots = jnp.where(jnp.arange(tp_n)[:, None] == tp_at, table.reshape(1, -1), 0.0).reshape(-1)
    slots = jnp.concatenate((slots, jnp.zeros((-slots.shape[0] % model,), F32))).reshape(-1, model)
    late_sums = sum_all(jnp.concatenate((small_grads, gain_sum, slots)))
    table_all = late_sums[small_rows + 8 :].reshape(-1)[: tp_n * table.size]
    table_all = table_all.reshape(tp_n, rel_bias.shape[0], heads)
    table_mine = lax.dynamic_index_in_dim(table_all, tp_at, 0, keepdims=False)
    table_rows = rel_bias.shape[0] // (fsdp_n * ctx_n)
    grad_table = lax.dynamic_slice_in_dim(table_mine, dense_at * table_rows, table_rows)
    small_mine = lax.dynamic_slice_in_dim(late_sums[: small_rows + 8], dense_at * own, own, 1)
    grad_router = small_mine[0:experts].T
    grad_gain_two = small_mine[experts]
    grad_gain_one = small_mine[small_rows]

    hidden_share = lax.dynamic_slice_in_dim(hidden, columns, share, 1).T
    share_block = pl.BlockSpec((share, BQ), lambda i, *_: (0, i))
    out_share = call(
        out_kernel,
        (blocks,),
        [share_block, share_block, pl.BlockSpec((1, BQ), lambda i: (0, i))],
        share_block,
        shaped((share, rows), BF),
        name="layer_output",
    )(eo_mine, hidden_share, gate_row)
    return (
        out_share.T,
        grad_tokens.T,
        grad_dense[:, 0:qkv_cols].reshape(own, 3, width),
        grad_out_mine,
        grad_table,
        grad_gain_one,
        grad_gain_two,
        grad_router,
        grad_in_mine[None],
        grad_down_mine[None],
    )


def solution(mesh):
    placed = (
        P(("fsdp", "ctx"), None),
        P(("fsdp", "ctx"), None),
        P(("fsdp", "ctx"), None, "tp"),
        P(("fsdp", "ctx"), "tp"),
        P(None, "tp"),
        P(("fsdp", "ctx")),
        P(("fsdp", "ctx")),
        P(("fsdp", "ctx"), None),
        P("fsdp", None, "tp"),
        P("fsdp", None, "tp"),
        P(("fsdp", "ctx"), None),
        P("fsdp"),
    )
    return jax.shard_map(
        shards,
        mesh=mesh,
        in_specs=placed,
        out_specs=(
            P(("fsdp", "ctx"), "tp"),
            P(("fsdp", "ctx"), "tp"),
            P(("fsdp", "ctx"), None, "tp"),
            P(("fsdp", "ctx"), "tp"),
            P(("fsdp", "ctx"), "tp"),
            P(("fsdp", "ctx")),
            P(("fsdp", "ctx")),
            P(("fsdp", "ctx"), None),
            P("fsdp", "ctx", "tp"),
            P("fsdp", "ctx", "tp"),
        ),
        check_vma=False,
    )
```

time: 506 us -> 361 us (0.71)
  waiting for transfers between devices: 259 us -> 69.2 us
  starting transfers between devices: 7.85 us -> 74.4 us
  blocking collectives: 44.9 us -> 0 us
  Pallas kernels: 119 us -> 151 us
  local copies, waits for them, and re-layouts: 50.8 us -> 24.9 us
  other arithmetic: 7.14 us -> 25.2 us
    reduce_scatter x4 -> x1, waiting for transfers between devices: 117 us -> 0.01 us  [shards(): lax.psum_scatter(terms, 'tp', scatter_dimension=0, tiled=True).astype(F32)]
    ppermute x0 -> x39, starting transfers between devices: none -> 74.2 us  [the longest x18 49.6 us: turn(): return lax.ppermute(x, 'tp', [(i, (i + s) % 4) for i in range(4)])]
    ppermute x0 -> x39, waiting for transfers between devices: none -> 67.5 us  [the longest x18 57.3 us: turn(): return lax.ppermute(x, 'tp', [(i, (i + s) % 4) for i in range(4)])]
    all_gather x4 -> x1, waiting for transfers between devices: 66.7 us -> 0.02 us  [shards(): out_all = lax.all_gather(out_line, dense, axis=0, tiled=True)]
    all_gather x1, waiting for transfers between devices: 50.2 us -> 0.01 us  [shards(): w_experts = lax.all_gather(w_half, dense, axis=0, tiled=True)]
    psum x1 -> x0, blocking collectives: 44.9 us -> none  [shards(): late_sums = lax.psum(late, ('fsdp', 'ctx', 'tp'))]
    pallas_call x7 -> x8, Pallas kernels: 67.3 us -> 90.7 us  [the longest x1 31.1 us: shards(): call(expert_kernel, (tiles,), [whole(1, rows), whole(rows, model), whole(...]
    unnamed x83 -> x59, local copies, waits for them, and re-layouts: 26.9 us -> 5.61 us
  transfers between devices with their start and end apart: 14 -> 44, of which waited for: 9 -> 13; matrix products, arithmetic and copies ran while one was open for 6% -> 13% of each run, Pallas kernels for 17% -> 29%
where the time goes in v2:
time: 361 us
  Pallas kernels  151 us (42%)
  starting transfers between devices  74.4 us (21%)
  waiting for transfers between devices  69.2 us (19%)
  other arithmetic  25.2 us (7%)
  local copies, waits for them, and re-layouts  24.9 us (7%)
  between operations  14.2 us (4%)
    ppermute x18, waiting for transfers between devices, turn(): return lax.ppermute(x, 'tp', [(i, (i + s) % 4) for i in range(4)])  57.3 us
    ppermute x18, starting transfers between devices, turn(): return lax.ppermute(x, 'tp', [(i, (i + s) % 4) for i in range(4)])  49.6 us
    pallas_call x1, Pallas kernels, shards(): call(expert_kernel, (tiles,), [whole(1, rows), whole(rows, model), whole(...  31.1 us
    pallas_call x1, Pallas kernels, attention_bwd(): pl.pallas_call(partial(bwd_kernel, heads), grid_spec=pltpu.PrefetchScalar...  26.2 us
    pallas_call x2, Pallas kernels, shards(): call(weight_grad_kernel, (tiles,), [sorted_spec(model), sorted_spec(ff)],...  25.2 us
    ppermute x21, starting transfers between devices, xor_step(): lax.ppermute(x, axis, [(i, i ^ s) for i in range(lax.axis_size(axis))])  24.5 us
    pallas_call x1, Pallas kernels, attention_fwd(): pl.pallas_call(partial(fwd_kernel, heads), grid_spec=pltpu.PrefetchScalar...  22.8 us
    pallas_call x1, Pallas kernels, shards(): call(qkv_back_kernel, (blocks,), [pl.BlockSpec((width, BQ), lambda i, at:...  12.4 us
  transfers between devices with their start and end apart: 44, of which 13 were waited for; matrix products, arithmetic and copies ran while one was open for 13% of the time, Pallas kernels for 29%

profile of v2, /device:TPU:0, one launch (start us, length us, event | category | flops | bytes accessed | tf_op | source)
XLA Modules:
  0.0 361.4 jit_solution(7595363852695337899)
XLA Ops:
  7.3 1.9 pack_small.1
  9.2 2.9 collective-permute-start
  12.1 1.5 collective-permute-start.1
  13.6 3.6 collective-permute-start.10
  17.3 1.0 collective-permute-start.9
  23.5 1.6 pad_maximum_fusion.2
  31.1 1.3 convert_bitcast_fusion.1.refs_8_
  32.4 1.8 fusion.4
  34.3 1.1 pad_maximum_fusion.1.refs_0_
  35.9 2.8 bias_band.1.band
  38.8 1.1 pad_maximum_fusion
  40.7 9.8 %norm_qkv.1 = (bf16[2048,576]{1,0:T(8,128)(2,1)}, bf16[2048,768]{1,0:T(8,128)(2,1)}, f32[1,2048]{1,0:T(1,128)}, bf16[768,704]{1,0:T(8,128)(2,1)}, f32[8,768]{1,0:T(8,128)}) custom-call(s32[9]{0:T(128)} %stack.82.at, bf16[1024,768]{1,0:T(8,128)(2,1)} %tok_ref.1, bf16[1024,768]{1,0:T(8,128)(2,1)} %collective-permute-done.4.other_ref, ...), custom_call_target="tpu_custom_call" | custom-call | flops 8000000000 | bytes 24000000 | tf_op jit(solution)/shard_map/norm_qkv/pallas_call | solution.py:767
  50.5 22.8 %attention_fwd.1 = (f32[192,1024]{1,0:T(8,128)}, bf16[192,1024]{1,0:T(8,128)(2,1)}, f32[3,1024]{1,0:T(4,128)}) custom-call(s32[10]{0:T(128)} %pad_add_fusion.info, f32[2,3]{1,0:T(2,128)} %pad_maximum_fusion.3.far, bf16[2048,576]{1,0:T(8,128)(2,1)} %get-tuple-element.92.qkv_all, f32[1,2048]{1,0:T(1,128)} %bitcast.66, f32[1,2048]{1,0:T(1,128)} %bitcast.67, ...), custom_call_target="tpu_custom_call" | custom-call | flops 19000000512 | bytes 57000000 | tf_op jit(solution)/shard_map/attention_fwd/pallas_call | solution.py:189
  73.3 3.3 collective-permute-start.5
  76.7 2.4 collective-permute-start.7
  79.1 1.8 slice.103.refs_7_
  81.4 6.1 %collective-permute-done.5.refs_2_.refs_11_ = bf16[192,1024]{1,0:T(8,128)(2,1)S(1)} collective-permute-done((bf16[192,1024]{1,0:T(8,128)(2,1)}, bf16[192,1024]{1,0:T(8,128)(2,1)S(1)}, u32[]{:S(2)}, u32[]{:S(2)}) %collective-permute-start.5) | collective-permute-done | bytes 393248 | tf_op jit(solution)/shard_map/ppermute | solution.py:630
  87.4 15.9 %collective-permute-done.6.refs_3_.refs_12_ = bf16[192,1024]{1,0:T(8,128)(2,1)S(1)} collective-permute-done((bf16[192,1024]{1,0:T(8,128)(2,1)}, bf16[192,1024]{1,0:T(8,128)(2,1)S(1)}, u32[]{:S(2)}, u32[]{:S(2)}) %collective-permute-start.6) | collective-permute-done | bytes 393248 | tf_op jit(solution)/shard_map/ppermute | solution.py:630
  104.3 8.0 %hidden_router.1 = (f32[1024,768]{1,0:T(8,128)}, bf16[1024,768]{1,0:T(8,128)(2,1)}, f32[1,1024]{1,0:T(1,128)}) custom-call(s32[12]{0:T(128)} %stack.81.at, bf16[1024,768]{1,0:T(8,128)(2,1)} %tok_ref.1, bf16[192,1024]{1,0:T(8,128)(2,1)} %get-tuple-element.95.refs_1_.refs_10_, bf16[192,1024]{1,0:T(8,128)(2,1)} %copy-done.20, bf16[192,1024]{1,0:T(8,128)(2,1)} %copy-done.21, ...), custom_call_target="tpu_custom_call" | custom-call | flops 7000000000 | bytes 21000000 | tf_op jit(solution)/shard_map/hidden_router/pallas_call | solution.py:798
  112.3 31.1 %experts.1 = (bf16[272,768]{1,0:T(8,128)(2,1)}, bf16[272,768]{1,0:T(8,128)(2,1)}, bf16[272,768]{1,0:T(8,128)(2,1)}, bf16[272,768]{1,0:T(8,128)(2,1)}, bf16[768,1...) custom-call(s32[11]{0:T(128)} %copy-done.14, ...), custom_call_target="tpu_custom_call" | custom-call | flops 30000001024 | bytes 90000000 | tf_op jit(solution)/shard_map/experts/pallas_call | solution.py:821
  143.4 12.6 %expert_weight_grads.2 = (bf16[1536,768]{1,0:T(8,128)(2,1)}, bf16[1536,768]{1,0:T(8,128)(2,1)}) custom-call(s32[11]{0:T(128)} %copy-done.14, s32[11]{0:T(128)} %broadcast_xor_fusion.slot, s32[12]{0:T(128)} %stack.81.at, bf16[1408,768]{1,0:T(8,128)(2,1)} %get-tuple-element.106.rows_ref, bf16[1408,768]{1,0:T(8,128)(2,1)} %get-tuple-element.107.cols_ref), custom_call_target="tpu_custom_call" | custom-call | flops 100000000 | bytes 300000 | tf_op jit(solution)/shard_map/expert_weight_grads/pallas_call | solution.py:859
  155.9 12.7 %expert_weight_grads.3 = (bf16[1536,768]{1,0:T(8,128)(2,1)}, bf16[1536,768]{1,0:T(8,128)(2,1)}) custom-call(s32[11]{0:T(128)} %copy-done.14, s32[11]{0:T(128)} %broadcast_xor_fusion.slot, s32[12]{0:T(128)} %stack.81.at, bf16[1408,768]{1,0:T(8,128)(2,1)} %get-tuple-element.110.rows_ref, bf16[1408,768]{1,0:T(8,128)(2,1)} %get-tuple-element.111.cols_ref), custom_call_target="tpu_custom_call" | custom-call | flops 100000000 | bytes 300000 | tf_op jit(solution)/shard_map/expert_weight_grads/pallas_call | solution.py:859
  169.1 8.7 %collective-permute-start.11 = (bf16[272,768]{1,0:T(8,128)(2,1)}, bf16[272,768]{1,0:T(8,128)(2,1)S(1)}, u32[]{:S(2)}, u32[]{:S(2)}) collective-permute-start(bf16[272,768]{1,0:T(8,128)(2,1)} %get-tuple-element.103), channel_id=1, source_target_pairs={{0,1},{1,2},{2,3},{3,0},{4,5},{5,6},{6,7},{7,4},{8,9},{9,10},{10,1... | collective-permute-start | bytes 1253384 | tf_op jit(solution)/shard_map/ppermute | solution.py:630
  177.8 2.2 collective-permute-start.12
  180.2 2.3 add.258
  182.5 7.8 %collective-permute-done.11.refs_1_ = bf16[272,768]{1,0:T(8,128)(2,1)S(1)} collective-permute-done((bf16[272,768]{1,0:T(8,128)(2,1)}, bf16[272,768]{1,0:T(8,128)(2,1)S(1)}, u32[]{:S(2)}, u32[]{:S(2)}) %collective-permute-start.11) | collective-permute-done | bytes 417824 | tf_op jit(solution)/shard_map/ppermute | solution.py:630
  190.3 17.4 %collective-permute-done.12.refs_2_ = bf16[272,768]{1,0:T(8,128)(2,1)} collective-permute-done((bf16[272,768]{1,0:T(8,128)(2,1)}, bf16[272,768]{1,0:T(8,128)(2,1)}, u32[]{:S(2)}, u32[]{:S(2)}) %collective-permute-start.12) | collective-permute-done | bytes 417824 | tf_op jit(solution)/shard_map/ppermute | solution.py:630
  207.7 1.5 fusion.25
  209.2 3.7 %collective-permute-start.18 = (bf16[384,768]{1,0:T(8,128)(2,1)}, bf16[384,768]{1,0:T(8,128)(2,1)}, u32[]{:S(2)}, u32[]{:S(2)}) collective-permute-start(bf16[384,768]{1,0:T(8,128)(2,1)} %get-tuple-element.218), channel_id=1, source_target_pairs={{0,8},{8,0},{16,24},{24,16},{1,9},{9,1},{17,25},{25,17},{2,10},{10... | collective-permute-start | bytes 1769480 | tf_op jit(solution)/shard_map/ppermute | solution.py:626
  212.9 1.5 collective-permute-start.20
  214.3 7.0 %hidden_back.1 = (bf16[192,256]{1,0:T(8,128)(2,1)}, bf16[192,256]{1,0:T(8,128)(2,1)}, bf16[192,256]{1,0:T(8,128)(2,1)}, bf16[192,256]{1,0:T(8,128)(2,1)}, f32[25...) custom-call(s32[12]{0:T(128)} %stack.81.at, bf16[272,768]{1,0:T(8,128)(2,1)} %get-tuple-element.113.refs_0_, ...), custom_call_target="tpu_custom_call" | custom-call | flops 6000000000 | bytes 18000000 | tf_op jit(solution)/shard_map/hidden_back/pallas_call | solution.py:880
  221.4 9.4 %collective-permute-start.15 = (bf16[192,256]{1,0:T(8,128)(2,1)}, bf16[192,256]{1,0:T(8,128)(2,1)S(1)}, u32[]{:S(2)}, u32[]{:S(2)}) collective-permute-start(bf16[192,256]{1,0:T(8,128)(2,1)} %get-tuple-element.119), channel_id=1, source_target_pairs={{0,1},{1,2},{2,3},{3,0},{4,5},{5,6},{6,7},{7,4},{8,9},{9,10},{10,1... | collective-permute-start | bytes 294920 | tf_op jit(solution)/shard_map/ppermute | solution.py:630
  230.8 2.4 copy.58
  233.2 1.0 collective-permute-start.16
  234.2 3.0 add.261
  237.2 1.5 collective-permute-start.17
  238.7 1.5 fusion.24
  241.3 2.1 collective-permute-start.23
  243.4 2.1 collective-permute-start.25
  245.5 26.2 %attention_bwd.1 = (bf16[192,1024]{1,0:T(8,128)(2,1)}, bf16[2048,384]{1,0:T(8,128)(2,1)}, f32[16,512]{1,0:T(8,128)}, f32[8,256]{1,0:T(8,128)}) custom-call(s32[10]{0:T(128)} %pad_add_fusion.info, f32[2,3]{1,0:T(2,128)} %pad_maximum_fusion.3.far, bf16[2048,576]{1,0:T(8,128)(2,1)} %get-tuple-element.92.qkv_all, f32[1,2048]{1,0:T(1,128)} %bitcast.68, ...), custom_call_target="tpu_custom_call" | custom-call | flops 24000000000 | bytes 72000000 | tf_op jit(solution)/shard_map/attention_bwd/pallas_call | solution.py:333
  271.7 2.1 constant_dynamic-slice_fusion
  275.0 1.5 collective-permute-done.21.got_ref
  276.5 12.4 %qkv_back.1 = (bf16[768,1024]{1,0:T(8,128)(2,1)}, f32[8,768]{1,0:T(8,128)}, bf16[384,1344]{1,0:T(8,128)(2,1)}, bf16[384,1344]{1,0:T(8,128)(2,1)}) custom-call(s32[12]{0:T(128)} %stack.81.at, bf16[192,1024]{1,0:T(8,128)(2,1)} %get-tuple-element.131.dq_ref, bf16[2048,384]{1,0:T(8,128)(2,1)} %get-tuple-element.132.dkv_ref, ...), custom_call_target="tpu_custom_call" | custom-call | flops 8999999488 | bytes 27000000 | tf_op jit(solution)/shard_map/qkv_back/pallas_call | solution.py:924
  289.9 0.9 dynamic-slice_bitcast_fusion.hidden_ref
  290.8 2.2 copy.59
  293.4 3.5 collective-permute-start.34
  296.9 1.5 collective-permute-start.36
  298.5 2.7 add_bitcast_fusion
  301.2 1.7 collective-permute-done.35
  302.9 5.3 %collective-permute-start.37 = (f32[17,768]{1,0:T(8,128)S(1)}, f32[17,768]{1,0:T(8,128)S(1)}, u32[]{:S(2)}, u32[]{:S(2)}) collective-permute-start(f32[17,768]{1,0:T(8,128)S(1)} %add_add_fusion.1), channel_id=1, source_target_pairs={{0,1},{1,2},{2,3},{3,0},{4,5},{5,6},{6,7},{7,4},{8,9},{9,10},{10,1... | collective-permute-start | bytes 156680 | tf_op jit(solution)/shard_map/ppermute | solution.py:630
  308.3 2.4 collective-permute-start.39
  310.6 2.7 add_bitcast_fusion.1
  313.4 5.1 %collective-permute-done.38 = f32[17,768]{1,0:T(8,128)S(1)} collective-permute-done((f32[17,768]{1,0:T(8,128)S(1)}, f32[17,768]{1,0:T(8,128)S(1)}, u32[]{:S(2)}, u32[]{:S(2)}) %collective-permute-start.38) | collective-permute-done | bytes 52256 | tf_op jit(solution)/shard_map/ppermute | solution.py:630
  318.6 1.7 copy.60
  320.7 1.5 collective-permute-start.28
  322.2 1.9 collective-permute-start.29
  325.6 4.2 %collective-permute-done.27 = bf16[96,1344]{1,0:T(8,128)(2,1)S(1)} collective-permute-done((bf16[96,1344]{1,0:T(8,128)(2,1)S(1)}, bf16[96,1344]{1,0:T(8,128)(2,1)S(1)}, u32[]{:S(2)}, u32[]{:S(2)}) %collective-permute-start.27) | collective-permute-done | bytes 258080 | tf_op jit(solution)/shard_map/ppermute | solution.py:626
  329.9 4.3 %collective-permute-done.28 = bf16[96,1344]{1,0:T(8,128)(2,1)S(1)} collective-permute-done((bf16[96,1344]{1,0:T(8,128)(2,1)S(1)}, bf16[96,1344]{1,0:T(8,128)(2,1)S(1)}, u32[]{:S(2)}, u32[]{:S(2)}) %collective-permute-start.28) | collective-permute-done | bytes 258080 | tf_op jit(solution)/shard_map/ppermute | solution.py:626
  334.4 7.8 %collective-permute-start.30 = (bf16[96,192]{1,0:T(8,128)(2,1)S(1)}, bf16[96,192]{1,0:T(8,128)(2,1)S(1)}, u32[]{:S(2)}, u32[]{:S(2)}) collective-permute-start(bf16[96,192]{1,0:T(8,128)(2,1)S(1)} %get-tuple-element.223), channel_id=1, source_target_pairs={{0,3},{1,0},{2,1},{3,2},{4,7},{5,4},{6,5},{7,6},{8,11},{9,8},{10,9... | collective-permute-start | bytes 110600 | tf_op jit(solution)/shard_map/ppermute | solution.py:630
  343.7 0.9 copy.64
  344.6 2.6 collective-permute-done.31
  347.2 1.6 collective-permute-done.32
  349.5 3.3 layer_output.1
  352.9 2.0 convert_bitcast_fusion
  (174 shorter events, 22.8 us)
Async XLA Ops:
  7.2 96.2 %all-gather.3.cloned.1.call-start = ((), (), s32[]{:S(2)}) async-start(), calls=%async_computation.2 | async-start | bytes 1327104 | tf_op jit(solution)/shard_map/all_gather | solution.py:722
  7.2 11.0 %copy-start.8 = (s32[2048]{0:T(1024)S(1)}, s32[2048]{0:T(1024)}, u32[]{:S(2)}) copy-start(s32[2048]{0:T(1024)} %param.23) | copy-start | bytes 24580
  7.2 11.4 %copy-start.11 = (s32[1024,1]{0,1:T(1,128)S(1)}, s32[1024,1]{0,1:T(1,128)}, u32[]{:S(2)}) copy-start(s32[1024,1]{0,1:T(1,128)} %param.22) | copy-start | bytes 12292
  7.2 12.2 %copy-start.13 = (f32[32,3]{0,1:T(4,128)S(1)}, f32[32,3]{0,1:T(4,128)}, u32[]{:S(2)}) copy-start(f32[32,3]{0,1:T(4,128)} %param.16) | copy-start | bytes 1156
  7.3 14.3 %copy-start.5 = (bf16[1,768,768]{2,1,0:T(8,128)(2,1)S(1)}, bf16[1,768,768]{2,1,0:T(8,128)(2,1)}, u32[]{:S(2)}) copy-start(bf16[1,768,768]{2,1,0:T(8,128)(2,1)} %param.21) | copy-start | bytes 3538948
  7.3 14.3 %copy-start.6 = (bf16[1,768,768]{2,1,0:T(8,128)(2,1)S(1)}, bf16[1,768,768]{2,1,0:T(8,128)(2,1)}, u32[]{:S(2)}) copy-start(bf16[1,768,768]{2,1,0:T(8,128)(2,1)} %param.20) | copy-start | bytes 3538948
  9.2 25.1 %collective-permute-start = (bf16[96,704]{1,0:T(8,128)(2,1)}, bf16[96,704]{1,0:T(8,128)(2,1)}, u32[]{:S(2)}, u32[]{:S(2)}) collective-permute-start(bf16[96,704]{1,0:T(8,128)(2,1)} %pack_small.1), channel_id=1, source_target_pairs={{0,8},{8,0},{16,24},{24,16},{1,9},{9,1},{17,25},{25,17},{2,10},{10... | collective-permute-start | bytes 405512 | tf_op jit(solution)/shard_map/ppermute | solution.py:626
  12.1 22.1 %collective-permute-start.1 = (bf16[96,704]{1,0:T(8,128)(2,1)}, bf16[96,704]{1,0:T(8,128)(2,1)}, u32[]{:S(2)}, u32[]{:S(2)}) collective-permute-start(bf16[96,704]{1,0:T(8,128)(2,1)} %pack_small.1), channel_id=1, source_target_pairs={{0,16},{8,24},{16,0},{24,8},{1,17},{9,25},{17,1},{25,9},{2,18},{10... | collective-permute-start | bytes 405512 | tf_op jit(solution)/shard_map/ppermute | solution.py:626
  13.6 9.1 %collective-permute-start.10 = (bf16[96,192]{1,0:T(8,128)(2,1)}, bf16[96,192]{1,0:T(8,128)(2,1)}, u32[]{:S(2)}, u32[]{:S(2)}) collective-permute-start(bf16[96,192]{1,0:T(8,128)(2,1)} %param.15), channel_id=1, source_target_pairs={{0,3},{1,0},{2,1},{3,2},{4,7},{5,4},{6,5},{7,6},{8,11},{9,8},{10,9... | collective-permute-start | bytes 110600 | tf_op jit(solution)/shard_map/ppermute | solution.py:630
  17.2 6.2 %collective-permute-start.8 = (bf16[96,192]{1,0:T(8,128)(2,1)}, bf16[96,192]{1,0:T(8,128)(2,1)}, u32[]{:S(2)}, u32[]{:S(2)}) collective-permute-start(bf16[96,192]{1,0:T(8,128)(2,1)} %param.15), channel_id=1, source_target_pairs={{0,1},{1,2},{2,3},{3,0},{4,5},{5,6},{6,7},{7,4},{8,9},{9,10},{10,1... | collective-permute-start | bytes 110600 | tf_op jit(solution)/shard_map/ppermute | solution.py:630
  17.3 6.2 %collective-permute-start.9 = (bf16[96,192]{1,0:T(8,128)(2,1)}, bf16[96,192]{1,0:T(8,128)(2,1)}, u32[]{:S(2)}, u32[]{:S(2)}) collective-permute-start(bf16[96,192]{1,0:T(8,128)(2,1)} %param.15), channel_id=1, source_target_pairs={{0,2},{1,3},{2,0},{3,1},{4,6},{5,7},{6,4},{7,5},{8,10},{9,11},{10,... | collective-permute-start | bytes 110600 | tf_op jit(solution)/shard_map/ppermute | solution.py:630
  18.7 2.8 copy-start.17
  18.9 2.6 copy-start.26
  22.2 12.1 %copy-start.7 = (bf16[96,704]{1,0:T(8,128)(2,1)S(1)}, bf16[96,704]{1,0:T(8,128)(2,1)}, u32[]{:S(2)}) copy-start(bf16[96,704]{1,0:T(8,128)(2,1)} %pack_small.1) | copy-start | bytes 405508
  22.7 11.5 %collective-permute-start.2 = (bf16[96,704]{1,0:T(8,128)(2,1)}, bf16[96,704]{1,0:T(8,128)(2,1)S(1)}, u32[]{:S(2)}, u32[]{:S(2)}) collective-permute-start(bf16[96,704]{1,0:T(8,128)(2,1)} %pack_small.1), channel_id=1, source_target_pairs={{0,24},{8,16},{16,8},{24,0},{1,25},{9,17},{17,9},{25,1},{2,26},{10... | collective-permute-start | bytes 405512 | tf_op jit(solution)/shard_map/ppermute | solution.py:626
  23.5 16.4 %collective-permute-start.4 = (bf16[1024,768]{1,0:T(8,128)(2,1)}, bf16[1024,768]{1,0:T(8,128)(2,1)}, u32[]{:S(2)}, u32[]{:S(2)}) collective-permute-start(bf16[1024,768]{1,0:T(8,128)(2,1)} %tok_ref.1), channel_id=1, source_target_pairs={{0,4},{4,0},{1,5},{5,1},{2,6},{6,2},{3,7},{7,3},{8,12},{12,8},{9,1... | collective-permute-start | bytes 4718600 | tf_op jit(solution)/shard_map/ppermute | solution.py:626
  25.1 87.2 %all-gather.5.cloned.1.call-start = ((), (), s32[]{:S(2)}) async-start(), calls=%async_computation.3 | async-start | bytes 10616832 | tf_op jit(solution)/shard_map/all_gather | solution.py:758
  30.4 50.4 %copy-start.14 = (s32[11]{0:T(128)}, s32[11]{0:T(128)S(1)}, u32[]{:S(2)}) copy-start(s32[11]{0:T(128)S(1)} %broadcast_minimum_fusion.owner) | copy-start | bytes 136
  35.3 3.4 copy-start.4
  35.3 4.5 %collective-permute-start.3 = (bf16[4,96,704]{2,1,0:T(8,128)(2,1)S(1)}, bf16[4,96,704]{2,1,0:T(8,128)(2,1)S(1)}, u32[]{:S(2)}, u32[]{:S(2)}) collective-permute-start(bf16[4,96,704]{2,1,0:T(8,128)(2,1)S(1)} %pad_maximum_fusion.1.refs_0_), channel_id=1, source_target_pairs={{0,4},{4,0},{1,5},{5,1},{2,6},{6,2},{3,7},{7,3},{8,12},{12,8},{9,1... | collective-permute-start | bytes 1622024 | tf_op jit(solution)/shard_map/ppermute | solution.py:626
  39.9 309.6 %reduce-scatter.3.cloned.1.call-start = ((), (), s32[]{:S(2)}) async-start(), calls=%async_computation.4 | async-start | bytes 1966080 | tf_op jit(solution)/shard_map/reduce_scatter | solution.py:916
  73.3 14.1 %collective-permute-start.5 = (bf16[192,1024]{1,0:T(8,128)(2,1)}, bf16[192,1024]{1,0:T(8,128)(2,1)S(1)}, u32[]{:S(2)}, u32[]{:S(2)}) collective-permute-start(bf16[192,1024]{1,0:T(8,128)(2,1)} %get-tuple-element.95.refs_1_.refs_10_), channel_id=1, source_target_pairs={{0,1},{1,2},{2,3},{3,0},{4,5},{5,6},{6,7},{7,4},{8,9},{9,10},{10,1... | collective-permute-start | bytes 1179656 | tf_op jit(solution)/shard_map/ppermute | solution.py:630
  76.6 26.8 %collective-permute-start.6 = (bf16[192,1024]{1,0:T(8,128)(2,1)}, bf16[192,1024]{1,0:T(8,128)(2,1)S(1)}, u32[]{:S(2)}, u32[]{:S(2)}) collective-permute-start(bf16[192,1024]{1,0:T(8,128)(2,1)} %get-tuple-element.95.refs_1_.refs_10_), channel_id=1, source_target_pairs={{0,2},{1,3},{2,0},{3,1},{4,6},{5,7},{6,4},{7,5},{8,10},{9,11},{10,... | collective-permute-start | bytes 1179656 | tf_op jit(solution)/shard_map/ppermute | solution.py:630
  76.7 26.7 %collective-permute-start.7 = (bf16[192,1024]{1,0:T(8,128)(2,1)}, bf16[192,1024]{1,0:T(8,128)(2,1)S(1)}, u32[]{:S(2)}, u32[]{:S(2)}) collective-permute-start(bf16[192,1024]{1,0:T(8,128)(2,1)} %get-tuple-element.95.refs_1_.refs_10_), channel_id=1, source_target_pairs={{0,3},{1,0},{2,1},{3,2},{4,7},{5,4},{6,5},{7,6},{8,11},{9,8},{10,9... | collective-permute-start | bytes 1179656 | tf_op jit(solution)/shard_map/ppermute | solution.py:630
  87.4 16.0 %copy-start.20 = (bf16[192,1024]{1,0:T(8,128)(2,1)}, bf16[192,1024]{1,0:T(8,128)(2,1)S(1)}, u32[]{:S(2)}) copy-start(bf16[192,1024]{1,0:T(8,128)(2,1)S(1)} %collective-permute-done.5.refs_2_.refs_11_) | copy-start | bytes 1179652
  155.9 24.3 %collective-permute-start.14 = (bf16[1536,768]{1,0:T(8,128)(2,1)}, bf16[1536,768]{1,0:T(8,128)(2,1)}, u32[]{:S(2)}, u32[]{:S(2)}) collective-permute-start(bf16[1536,768]{1,0:T(8,128)(2,1)} %get-tuple-element.109), channel_id=1, source_target_pairs={{0,4},{4,0},{1,5},{5,1},{2,6},{6,2},{3,7},{7,3},{8,12},{12,8},{9,1... | collective-permute-start | bytes 7077896 | tf_op jit(solution)/shard_map/ppermute | solution.py:626
  155.9 24.3 %copy-start.2 = (bf16[1536,768]{1,0:T(8,128)(2,1)S(1)}, bf16[1536,768]{1,0:T(8,128)(2,1)}, u32[]{:S(2)}) copy-start(bf16[1536,768]{1,0:T(8,128)(2,1)} %get-tuple-element.108) | copy-start | bytes 7077892
  168.6 64.6 %collective-permute-start.22 = (bf16[1536,768]{1,0:T(8,128)(2,1)}, bf16[1536,768]{1,0:T(8,128)(2,1)}, u32[]{:S(2)}, u32[]{:S(2)}) collective-permute-start(bf16[1536,768]{1,0:T(8,128)(2,1)} %get-tuple-element.134), channel_id=1, source_target_pairs={{0,4},{4,0},{1,5},{5,1},{2,6},{6,2},{3,7},{7,3},{8,12},{12,8},{9,1... | collective-permute-start | bytes 7077896 | tf_op jit(solution)/shard_map/ppermute | solution.py:626
  169.1 21.2 %collective-permute-start.11 = (bf16[272,768]{1,0:T(8,128)(2,1)}, bf16[272,768]{1,0:T(8,128)(2,1)S(1)}, u32[]{:S(2)}, u32[]{:S(2)}) collective-permute-start(bf16[272,768]{1,0:T(8,128)(2,1)} %get-tuple-element.103), channel_id=1, source_target_pairs={{0,1},{1,2},{2,3},{3,0},{4,5},{5,6},{6,7},{7,4},{8,9},{9,10},{10,1... | collective-permute-start | bytes 1253384 | tf_op jit(solution)/shard_map/ppermute | solution.py:630
  177.8 29.9 %collective-permute-start.12 = (bf16[272,768]{1,0:T(8,128)(2,1)}, bf16[272,768]{1,0:T(8,128)(2,1)}, u32[]{:S(2)}, u32[]{:S(2)}) collective-permute-start(bf16[272,768]{1,0:T(8,128)(2,1)} %get-tuple-element.104), channel_id=1, source_target_pairs={{0,2},{1,3},{2,0},{3,1},{4,6},{5,7},{6,4},{7,5},{8,10},{9,11},{10,... | collective-permute-start | bytes 1253384 | tf_op jit(solution)/shard_map/ppermute | solution.py:630
  180.1 27.6 %collective-permute-start.13 = (bf16[272,768]{1,0:T(8,128)(2,1)}, bf16[272,768]{1,0:T(8,128)(2,1)}, u32[]{:S(2)}, u32[]{:S(2)}) collective-permute-start(bf16[272,768]{1,0:T(8,128)(2,1)} %get-tuple-element.105), channel_id=1, source_target_pairs={{0,3},{1,0},{2,1},{3,2},{4,7},{5,4},{6,5},{7,6},{8,11},{9,8},{10,9... | collective-permute-start | bytes 1253384 | tf_op jit(solution)/shard_map/ppermute | solution.py:630
  190.3 18.8 %copy-start.19 = (bf16[272,768]{1,0:T(8,128)(2,1)}, bf16[272,768]{1,0:T(8,128)(2,1)S(1)}, u32[]{:S(2)}) copy-start(bf16[272,768]{1,0:T(8,128)(2,1)S(1)} %collective-permute-done.11.refs_1_) | copy-start | bytes 1253380
  209.2 34.2 %collective-permute-start.18 = (bf16[384,768]{1,0:T(8,128)(2,1)}, bf16[384,768]{1,0:T(8,128)(2,1)}, u32[]{:S(2)}, u32[]{:S(2)}) collective-permute-start(bf16[384,768]{1,0:T(8,128)(2,1)} %get-tuple-element.218), channel_id=1, source_target_pairs={{0,8},{8,0},{16,24},{24,16},{1,9},{9,1},{17,25},{25,17},{2,10},{10... | collective-permute-start | bytes 1769480 | tf_op jit(solution)/shard_map/ppermute | solution.py:626
  212.9 32.6 %collective-permute-start.19 = (bf16[384,768]{1,0:T(8,128)(2,1)}, bf16[384,768]{1,0:T(8,128)(2,1)}, u32[]{:S(2)}, u32[]{:S(2)}) collective-permute-start(bf16[384,768]{1,0:T(8,128)(2,1)} %get-tuple-element.217), channel_id=1, source_target_pairs={{0,16},{8,24},{16,0},{24,8},{1,17},{9,25},{17,1},{25,9},{2,18},{10... | collective-permute-start | bytes 1769480 | tf_op jit(solution)/shard_map/ppermute | solution.py:626
  212.9 32.6 %collective-permute-start.20 = (bf16[384,768]{1,0:T(8,128)(2,1)}, bf16[384,768]{1,0:T(8,128)(2,1)}, u32[]{:S(2)}, u32[]{:S(2)}) collective-permute-start(bf16[384,768]{1,0:T(8,128)(2,1)} %get-tuple-element.216), channel_id=1, source_target_pairs={{0,24},{8,16},{16,8},{24,0},{1,25},{9,17},{17,9},{25,1},{2,26},{10... | collective-permute-start | bytes 1769480 | tf_op jit(solution)/shard_map/ppermute | solution.py:626
  221.4 15.8 %collective-permute-start.15 = (bf16[192,256]{1,0:T(8,128)(2,1)}, bf16[192,256]{1,0:T(8,128)(2,1)S(1)}, u32[]{:S(2)}, u32[]{:S(2)}) collective-permute-start(bf16[192,256]{1,0:T(8,128)(2,1)} %get-tuple-element.119), channel_id=1, source_target_pairs={{0,1},{1,2},{2,3},{3,0},{4,5},{5,6},{6,7},{7,4},{8,9},{9,10},{10,1... | collective-permute-start | bytes 294920 | tf_op jit(solution)/shard_map/ppermute | solution.py:630
  233.2 4.0 %copy-start.25 = (bf16[192,256]{1,0:T(8,128)(2,1)S(1)}, bf16[192,256]{1,0:T(8,128)(2,1)}, u32[]{:S(2)}) copy-start(bf16[192,256]{1,0:T(8,128)(2,1)} %get-tuple-element.121) | copy-start | bytes 294916
  233.2 7.5 %collective-permute-start.16 = (bf16[192,256]{1,0:T(8,128)(2,1)}, bf16[192,256]{1,0:T(8,128)(2,1)S(1)}, u32[]{:S(2)}, u32[]{:S(2)}) collective-permute-start(bf16[192,256]{1,0:T(8,128)(2,1)} %get-tuple-element.120), channel_id=1, source_target_pairs={{0,2},{1,3},{2,0},{3,1},{4,6},{5,7},{6,4},{7,5},{8,10},{9,11},{10,... | collective-permute-start | bytes 294920 | tf_op jit(solution)/shard_map/ppermute | solution.py:630
  237.2 3.1 copy-start.23
  237.2 6.2 %collective-permute-start.17 = (bf16[192,256]{1,0:T(8,128)(2,1)S(1)}, bf16[192,256]{1,0:T(8,128)(2,1)}, u32[]{:S(2)}, u32[]{:S(2)}) collective-permute-start(bf16[192,256]{1,0:T(8,128)(2,1)S(1)} %copy-done.25), channel_id=1, source_target_pairs={{0,3},{1,0},{2,1},{3,2},{4,7},{5,4},{6,5},{7,6},{8,11},{9,8},{10,9... | collective-permute-start | bytes 294920 | tf_op jit(solution)/shard_map/ppermute | solution.py:630
  241.3 33.6 %collective-permute-start.23 = (bf16[384,768]{1,0:T(8,128)(2,1)}, bf16[384,768]{1,0:T(8,128)(2,1)}, u32[]{:S(2)}, u32[]{:S(2)}) collective-permute-start(bf16[384,768]{1,0:T(8,128)(2,1)} %get-tuple-element.214), channel_id=1, source_target_pairs={{0,8},{8,0},{16,24},{24,16},{1,9},{9,1},{17,25},{25,17},{2,10},{10... | collective-permute-start | bytes 1769480 | tf_op jit(solution)/shard_map/ppermute | solution.py:626
  243.4 31.6 %collective-permute-start.24 = (bf16[384,768]{1,0:T(8,128)(2,1)}, bf16[384,768]{1,0:T(8,128)(2,1)}, u32[]{:S(2)}, u32[]{:S(2)}) collective-permute-start(bf16[384,768]{1,0:T(8,128)(2,1)} %get-tuple-element.213), channel_id=1, source_target_pairs={{0,16},{8,24},{16,0},{24,8},{1,17},{9,25},{17,1},{25,9},{2,18},{10... | collective-permute-start | bytes 1769480 | tf_op jit(solution)/shard_map/ppermute | solution.py:626
  243.4 31.6 %collective-permute-start.25 = (bf16[384,768]{1,0:T(8,128)(2,1)}, bf16[384,768]{1,0:T(8,128)(2,1)}, u32[]{:S(2)}, u32[]{:S(2)}) collective-permute-start(bf16[384,768]{1,0:T(8,128)(2,1)} %get-tuple-element.212), channel_id=1, source_target_pairs={{0,24},{8,16},{16,8},{24,0},{1,25},{9,17},{17,9},{25,1},{2,26},{10... | collective-permute-start | bytes 1769480 | tf_op jit(solution)/shard_map/ppermute | solution.py:626
  245.5 107.4 %reduce-scatter.5.cloned.1.call-start = ((), (), s32[]{:S(2)}) async-start(), calls=%async_computation.5 | async-start | bytes 1966080 | tf_op jit(solution)/shard_map/reduce_scatter | solution.py:955
  271.7 2.1 copy-start.12
  271.7 2.3 copy-start.9
  273.8 2.6 collective-permute-start.21
  289.6 3.8 %collective-permute-start.33 = (f32[17,768]{1,0:T(8,128)S(1)}, f32[17,768]{1,0:T(8,128)S(1)}, u32[]{:S(2)}, u32[]{:S(2)}) collective-permute-start(f32[17,768]{1,0:T(8,128)S(1)} %dynamic-update-slice.2), channel_id=1, source_target_pairs={{0,4},{4,0},{1,5},{5,1},{2,6},{6,2},{3,7},{7,3},{8,12},{12,8},{9,1... | collective-permute-start | bytes 156680 | tf_op jit(solution)/shard_map/ppermute | solution.py:626
  290.8 7.7 %copy-start.1 = (bf16[384,768]{1,0:T(8,128)(2,1)S(1)}, bf16[384,768]{1,0:T(8,128)(2,1)}, u32[]{:S(2)}) copy-start(bf16[384,768]{1,0:T(8,128)(2,1)} %get-tuple-element.152) | copy-start | bytes 1769476
  293.0 25.6 %collective-permute-start.26 = (bf16[384,1344]{0,1:T(8,128)(2,1)S(1)}, bf16[384,1344]{0,1:T(8,128)(2,1)}, u32[]{:S(2)}, u32[]{:S(2)}) collective-permute-start(bf16[384,1344]{0,1:T(8,128)(2,1)S(1)} %copy.59), channel_id=1, source_target_pairs={{0,4},{4,0},{1,5},{5,1},{2,6},{6,2},{3,7},{7,3},{8,12},{12,8},{9,1... | collective-permute-start | bytes 3096584 | tf_op jit(solution)/shard_map/ppermute | solution.py:626
  293.4 17.2 %copy-start = (bf16[384,768]{1,0:T(8,128)(2,1)S(1)}, bf16[384,768]{1,0:T(8,128)(2,1)}, u32[]{:S(2)}) copy-start(bf16[384,768]{1,0:T(8,128)(2,1)} %get-tuple-element.148) | copy-start | bytes 1769476
  293.4 7.7 %collective-permute-start.34 = (f32[17,768]{1,0:T(8,128)S(1)}, f32[17,768]{1,0:T(8,128)S(1)}, u32[]{:S(2)}, u32[]{:S(2)}) collective-permute-start(f32[17,768]{1,0:T(8,128)S(1)} %add.271), channel_id=1, source_target_pairs={{0,8},{8,0},{16,24},{24,16},{1,9},{9,1},{17,25},{25,17},{2,10},{10... | collective-permute-start | bytes 156680 | tf_op jit(solution)/shard_map/ppermute | solution.py:626
  296.9 5.9 %collective-permute-start.35 = (f32[17,768]{1,0:T(8,128)S(1)}, f32[17,768]{1,0:T(8,128)S(1)}, u32[]{:S(2)}, u32[]{:S(2)}) collective-permute-start(f32[17,768]{1,0:T(8,128)S(1)} %add.271), channel_id=1, source_target_pairs={{0,16},{8,24},{16,0},{24,8},{1,17},{9,25},{17,1},{25,9},{2,18},{10... | collective-permute-start | bytes 156680 | tf_op jit(solution)/shard_map/ppermute | solution.py:626
  296.9 5.9 %collective-permute-start.36 = (f32[17,768]{1,0:T(8,128)S(1)}, f32[17,768]{1,0:T(8,128)S(1)}, u32[]{:S(2)}, u32[]{:S(2)}) collective-permute-start(f32[17,768]{1,0:T(8,128)S(1)} %add.271), channel_id=1, source_target_pairs={{0,24},{8,16},{16,8},{24,0},{1,25},{9,17},{17,9},{25,1},{2,26},{10... | collective-permute-start | bytes 156680 | tf_op jit(solution)/shard_map/ppermute | solution.py:626
  302.9 10.5 %collective-permute-start.37 = (f32[17,768]{1,0:T(8,128)S(1)}, f32[17,768]{1,0:T(8,128)S(1)}, u32[]{:S(2)}, u32[]{:S(2)}) collective-permute-start(f32[17,768]{1,0:T(8,128)S(1)} %add_add_fusion.1), channel_id=1, source_target_pairs={{0,1},{1,2},{2,3},{3,0},{4,5},{5,6},{6,7},{7,4},{8,9},{9,10},{10,1... | collective-permute-start | bytes 156680 | tf_op jit(solution)/shard_map/ppermute | solution.py:630
  308.2 10.3 %collective-permute-start.38 = (f32[17,768]{1,0:T(8,128)S(1)}, f32[17,768]{1,0:T(8,128)S(1)}, u32[]{:S(2)}, u32[]{:S(2)}) collective-permute-start(f32[17,768]{1,0:T(8,128)S(1)} %add_add_fusion.1), channel_id=1, source_target_pairs={{0,2},{1,3},{2,0},{3,1},{4,6},{5,7},{6,4},{7,5},{8,10},{9,11},{10,... | collective-permute-start | bytes 156680 | tf_op jit(solution)/shard_map/ppermute | solution.py:630
  308.3 10.3 %collective-permute-start.39 = (f32[17,768]{1,0:T(8,128)S(1)}, f32[17,768]{1,0:T(8,128)S(1)}, u32[]{:S(2)}, u32[]{:S(2)}) collective-permute-start(f32[17,768]{1,0:T(8,128)S(1)} %add_add_fusion.1), channel_id=1, source_target_pairs={{0,3},{1,0},{2,1},{3,2},{4,7},{5,4},{6,5},{7,6},{8,11},{9,8},{10,9... | collective-permute-start | bytes 156680 | tf_op jit(solution)/shard_map/ppermute | solution.py:630
  313.4 6.9 %copy-start.3 = (bf16[384,1344]{1,0:T(8,128)(2,1)S(1)}, bf16[384,1344]{1,0:T(8,128)(2,1)}, u32[]{:S(2)}) copy-start(bf16[384,1344]{1,0:T(8,128)(2,1)} %get-tuple-element.141) | copy-start | bytes 3096580
  320.6 9.2 %collective-permute-start.27 = (bf16[96,1344]{1,0:T(8,128)(2,1)S(1)}, bf16[96,1344]{1,0:T(8,128)(2,1)S(1)}, u32[]{:S(2)}, u32[]{:S(2)}) collective-permute-start(bf16[96,1344]{1,0:T(8,128)(2,1)S(1)} %get-tuple-element.220), channel_id=1, source_target_pairs={{0,8},{8,0},{16,24},{24,16},{1,9},{9,1},{17,25},{25,17},{2,10},{10... | collective-permute-start | bytes 774152 | tf_op jit(solution)/shard_map/ppermute | solution.py:626
  320.7 13.4 %collective-permute-start.28 = (bf16[96,1344]{1,0:T(8,128)(2,1)S(1)}, bf16[96,1344]{1,0:T(8,128)(2,1)S(1)}, u32[]{:S(2)}, u32[]{:S(2)}) collective-permute-start(bf16[96,1344]{1,0:T(8,128)(2,1)S(1)} %get-tuple-element.222), channel_id=1, source_target_pairs={{0,16},{8,24},{16,0},{24,8},{1,17},{9,25},{17,1},{25,9},{2,18},{10... | collective-permute-start | bytes 774152 | tf_op jit(solution)/shard_map/ppermute | solution.py:626
  322.2 11.9 %collective-permute-start.29 = (bf16[96,1344]{1,0:T(8,128)(2,1)S(1)}, bf16[96,1344]{1,0:T(8,128)(2,1)S(1)}, u32[]{:S(2)}, u32[]{:S(2)}) collective-permute-start(bf16[96,1344]{1,0:T(8,128)(2,1)S(1)} %get-tuple-element.221), channel_id=1, source_target_pairs={{0,24},{8,16},{16,8},{24,0},{1,25},{9,17},{17,9},{25,1},{2,26},{10... | collective-permute-start | bytes 774152 | tf_op jit(solution)/shard_map/ppermute | solution.py:626
  334.4 10.2 %collective-permute-start.30 = (bf16[96,192]{1,0:T(8,128)(2,1)S(1)}, bf16[96,192]{1,0:T(8,128)(2,1)S(1)}, u32[]{:S(2)}, u32[]{:S(2)}) collective-permute-start(bf16[96,192]{1,0:T(8,128)(2,1)S(1)} %get-tuple-element.223), channel_id=1, source_target_pairs={{0,3},{1,0},{2,1},{3,2},{4,7},{5,4},{6,5},{7,6},{8,11},{9,8},{10,9... | collective-permute-start | bytes 110600 | tf_op jit(solution)/shard_map/ppermute | solution.py:630
  342.2 5.0 %collective-permute-start.31 = (bf16[96,192]{1,0:T(8,128)(2,1)S(1)}, bf16[96,192]{1,0:T(8,128)(2,1)S(1)}, u32[]{:S(2)}, u32[]{:S(2)}) collective-permute-start(bf16[96,192]{1,0:T(8,128)(2,1)S(1)} %get-tuple-element.225), channel_id=1, source_target_pairs={{0,2},{1,3},{2,0},{3,1},{4,6},{5,7},{6,4},{7,5},{8,10},{9,11},{10,... | collective-permute-start | bytes 110600 | tf_op jit(solution)/shard_map/ppermute | solution.py:630
  342.9 5.9 %collective-permute-start.32 = (bf16[96,192]{1,0:T(8,128)(2,1)S(1)}, bf16[96,192]{1,0:T(8,128)(2,1)S(1)}, u32[]{:S(2)}, u32[]{:S(2)}) collective-permute-start(bf16[96,192]{1,0:T(8,128)(2,1)S(1)} %get-tuple-element.224), channel_id=1, source_target_pairs={{0,1},{1,2},{2,3},{3,0},{4,5},{5,6},{6,7},{7,4},{8,9},{9,10},{10,1... | collective-permute-start | bytes 110600 | tf_op jit(solution)/shard_map/ppermute | solution.py:630
  (7 other events, 6.6 us)
Sparse Core Ops, SparseCore 0:
  25.2 25.0 all-gather.2
  52.8 58.8 all-gather.4
  245.6 37.7 reduce-scatter.2
  290.0 44.1 reduce-scatter.4

commit v3 on v2

--- a/solution.py
+++ b/solution.py
@@ -10,7 +10,7 @@
 norm_eps = 1e-06
 bucket_edges = (12, 16, 23, 32, 46, 64, 91)
 LANES = 128
-TILE = 128
+TILE = 256
 MIB = 1024 * 1024
 NT = (((1,), (1,)), ((), ()))
 TN = (((0,), (0,)), ((), ()))
@@ -25,7 +25,7 @@
 BF = jnp.bfloat16
 
 
-def call(kernel, grid, in_specs, out_specs, out_shape, scratch=(), prefetch=0, vmem=58, name=None, us=1):
+def call(kernel, grid, in_specs, out_specs, out_shape, scratch=(), prefetch=0, vmem=58, name=None):
     return pl.pallas_call(
         kernel,
         grid_spec=pltpu.PrefetchScalarGridSpec(
@@ -40,7 +40,7 @@
             dimension_semantics=("arbitrary",) * len(grid), vmem_limit_bytes=vmem * MIB
         ),
         cost_estimate=pl.CostEstimate(
-            flops=int(us * 1e9), bytes_accessed=int(us * 3e6), transcendentals=0
+            flops=10**7, bytes_accessed=10**5, transcendentals=0
         ),
         name=name,
     )
@@ -140,9 +140,9 @@
                 v_t[h, 0:HD, rows] = vt[h * HD : (h + 1) * HD, :]
                 v_t[h, HD : HD + 16, rows] = ones_rows(BK)
 
-    qb = info[0] + i
-    lo = info[1 + i]
-    hi = info[1 + pl.num_programs(0) + i]
+    qb = info[0, 0] + i
+    lo = info[0, 1 + i]
+    hi = info[0, 1 + pl.num_programs(0) + i]
     qt = (qkv_all[pl.ds(pl.multiple_of(qb * BQ, BQ), BQ), 0:width].astype(F32) * (HD**-0.5)).T.astype(BF)
     side = query_side(drow[...], BQ, None)
     q_aug = [jnp.concatenate([qt[h * HD : (h + 1) * HD, :], side], axis=0) for h in range(heads)]
@@ -163,14 +163,14 @@
     carry = tuple(
         (jnp.full((1, BQ), FLOOR, F32), jnp.zeros((HD + 16, BQ), F32)) for _ in range(heads)
     )
-    carry = lax.fori_loop(lo, jnp.minimum(hi, qb - 1), lambda kb, c: step(kb, c, lambda h, _: far[0, h]), carry)
+    carry = lax.fori_loop(lo, jnp.minimum(hi, qb - 1), lambda kb, c: step(kb, c, lambda h, _: far[h, 15]), carry)
     carry = lax.fori_loop(
         jnp.maximum(lo, qb - 1),
         jnp.minimum(hi, qb + 2),
         lambda kb, c: step(kb, c, lambda h, t: band[h, t - qb + 1]),
         carry,
     )
-    carry = lax.fori_loop(jnp.maximum(lo, qb + 2), hi, lambda kb, c: step(kb, c, lambda h, _: far[1, h]), carry)
+    carry = lax.fori_loop(jnp.maximum(lo, qb + 2), hi, lambda kb, c: step(kb, c, lambda h, _: far[h, 31]), carry)
     for h in range(heads):
         peak, acc = carry[h]
         total = acc[HD : HD + 1, :]
@@ -195,7 +195,7 @@
                 pl.BlockSpec(memory_space=pltpu.SMEM),
                 full((seq, cols)),
                 full((1, seq)),
-                pl.BlockSpec((1, BQ), lambda i, info: (0, info[0] + i)),
+                pl.BlockSpec((1, BQ), lambda i, info: (0, info[0, 0] + i)),
                 full((heads, 3, BK, BQ)),
             ],
             out_specs=[
@@ -217,7 +217,7 @@
             dimension_semantics=("arbitrary",), vmem_limit_bytes=58 * 1024 * 1024
         ),
         cost_estimate=pl.CostEstimate(
-            flops=int(19 * 1e9), bytes_accessed=int(19 * 3e6), transcendentals=0
+            flops=10**7, bytes_accessed=10**5, transcendentals=0
         ),
         name="attention_fwd",
     )(info, far, qkv_all, dcol, drow, band)
@@ -251,10 +251,10 @@
                 k_t[h, HD : HD + 16, rows] = ones_rows(BK)
 
     steps = pl.num_programs(0)
-    block = lax.rem(info[1 + 2 * steps] + steps - i, steps)
-    qb = info[0] + block
-    lo = info[1 + block]
-    hi = info[1 + steps + block]
+    block = lax.rem(info[0, 1 + 2 * steps] + steps - i, steps)
+    qb = info[0, 0] + block
+    lo = info[0, 1 + block]
+    hi = info[0, 1 + steps + block]
     dmix = m0[...]
     for s, ref in ((1, m1), (2, m2), (3, m3)):
         dmix = jnp.where(i == s, ref[...], dmix)
@@ -270,7 +270,7 @@
         cols = slice(h * HD, (h + 1) * HD)
         lse = lse_ref[h : h + 1, :]
         kinds = []
-        for tail in (far[0, h] - lse, -lse, far[1, h] - lse):
+        for tail in (far[h, 15] - lse, -lse, far[h, 31] - lse):
             kinds.append(jnp.concatenate([qt[cols, :], query_side(drow[...], BQ, tail)], axis=0))
         q_aug.append(kinds)
         delta = -jnp.sum(dmix_t[cols, :] * mixed_ref[cols, :], axis=0, keepdims=True)
@@ -329,7 +329,7 @@
     heads = width // HD
     steps = rows // BQ
     full = lambda shape: pl.BlockSpec(shape, lambda i, info: (0,) * len(shape))
-    block = lambda i, info: lax.rem(info[1 + 2 * steps] + steps - i, steps)
+    block = lambda i, info: lax.rem(info[0, 1 + 2 * steps] + steps - i, steps)
     return pl.pallas_call(
         partial(bwd_kernel, heads),
         grid_spec=pltpu.PrefetchScalarGridSpec(
@@ -339,7 +339,7 @@
                 pl.BlockSpec(memory_space=pltpu.SMEM),
                 full((seq, cols)),
                 full((1, seq)),
-                pl.BlockSpec((1, BQ), lambda i, info: (0, info[0] + block(i, info))),
+                pl.BlockSpec((1, BQ), lambda i, info: (0, info[0, 0] + block(i, info))),
                 full((heads, 3, BK, BQ)),
                 pl.BlockSpec((width, BQ), lambda i, info: (0, block(i, info))),
                 pl.BlockSpec((heads, BQ), lambda i, info: (0, block(i, info))),
@@ -369,30 +369,100 @@
             dimension_semantics=("arbitrary",), vmem_limit_bytes=58 * 1024 * 1024
         ),
         cost_estimate=pl.CostEstimate(
-            flops=int(24 * 1e9), bytes_accessed=int(24 * 3e6), transcendentals=0
+            flops=10**7, bytes_accessed=10**5, transcendentals=0
         ),
         name="attention_bwd",
     )(info, far, qkv_all, dcol, drow, band, mixed, lse, *dmix)
 
 
-def band_kernel(vec_ref, band_ref):
+def plan_kernel(
+    experts, own, table_rows, at, ids_ref, docs_ref, table_ref,
+    pos_ref, owner_ref, chosen_ref, docs_out, info_ref, band_ref, diag_ref, spread_ref,
+):
+    rows = ids_ref.shape[1]
+    seq = docs_ref.shape[1]
     heads = band_ref.shape[0]
+    buckets = table_ref.shape[1]
+    blocks = rows // BQ
+    chosen = ids_ref[...].astype(F32)
+    chosen_ref[...] = chosen
+    docs = docs_ref[...].astype(F32)
+    docs_out[...] = docs
+    expert_rows = -(-experts // 8) * 8
+    one_hot = lax.broadcasted_iota(jnp.int32, (expert_rows, rows), 0).astype(F32) == chosen
+    one_hot = jnp.where(one_hot, 1.0, 0.0)
+    low_rows = lax.broadcasted_iota(jnp.int32, (rows, rows), 0)
+    before = jnp.where(low_rows < lax.broadcasted_iota(jnp.int32, (rows, rows), 1), 1.0, 0.0)
+    earlier = dot(one_hot.astype(BF), before.astype(BF))
+    lane = lax.broadcasted_iota(jnp.int32, (1, LANES), 1)
+    lane_f = lane.astype(F32)
+    pos = jnp.zeros((1, rows), F32)
+    owner = jnp.zeros((1, LANES), F32)
+    end = jnp.zeros((1, 1), F32)
+    for e in range(experts):
+        hit = one_hot[e : e + 1, :]
+        count = jnp.sum(hit, axis=1, keepdims=True)
+        pos = pos + hit * (earlier[e : e + 1, :] + end * TILE)
+        end = end + jnp.maximum(jnp.floor((count + (TILE - 1)) * (1.0 / TILE)), 1.0)
+        owner = owner + jnp.where(end <= lane_f, 1.0, 0.0)
+    pos_ref[...] = pos.astype(jnp.int32)
+    owner = jnp.minimum(owner, experts - 1.0)
+    owner_ref[...] = jnp.where(lane == LANES - 1, end, owner).astype(jnp.int32)
+    base = at[2]
+    info = jnp.where(lane == 0, base, jnp.where(lane == 1 + 2 * blocks, at[0], 0)).astype(F32)
+    for b in range(seq // BQ):
+        first = docs[:, b * BQ : b * BQ + 1]
+        last = docs[:, (b + 1) * BQ - 1 : (b + 1) * BQ]
+        low = jnp.sum(jnp.where(docs < first, 1.0, 0.0), axis=1, keepdims=True)
+        high = jnp.sum(jnp.where(docs <= last, 1.0, 0.0), axis=1, keepdims=True)
+        here = (b >= base) & (b < base + blocks)
+        low_at = (lane == 1 + b - base) & here
+        high_at = (lane == 1 + blocks + b - base) & here
+        info = info + jnp.where(low_at, jnp.floor(low * (1.0 / BK)), 0.0)
+        info = info + jnp.where(high_at, jnp.floor((high + (BK - 1)) * (1.0 / BK)), 0.0)
+    info_ref[...] = info.astype(jnp.int32)
+    span = 3 * 2 * BQ
+    column = lax.broadcasted_iota(jnp.int32, (8, span), 1)
+    tile = (column >= 2 * BQ).astype(jnp.int32) + (column >= 4 * BQ).astype(jnp.int32)
+    inside = column - tile * (2 * BQ)
+    wrapped = jnp.where(inside < BQ, inside, inside - 2 * BQ)
+    bucket = relative_bucket((tile - 1) * BK - wrapped)[0:1, :].astype(F32)
+    which = lax.broadcasted_iota(jnp.int32, (buckets, span), 0).astype(F32)
+    pick = jnp.where(which == bucket, 1.0, 0.0).astype(BF)
+    wide = jnp.concatenate([table_ref[...], jnp.zeros((8 - heads, buckets), F32)], axis=0)
+    vectors = sum(dot(p, pick) for p in split3(wide))
     for h in range(heads):
         for t in range(3):
-            wide = jnp.broadcast_to(vec_ref[3 * h + t : 3 * h + t + 1, :], (BK, 2 * BQ))
+            line = vectors[h : h + 1, t * 2 * BQ : (t + 1) * 2 * BQ]
+            wide = jnp.broadcast_to(line, (BK, 2 * BQ))
             band_ref[h, t] = pltpu.roll(wide, 0, 1, stride=1, stride_axis=0)[:, 0:BQ]
-
-
-def pack_kernel(qkv_ref, router_ref, one_ref, two_ref, out_ref):
+    by_column = to_column(bucket)
+    lanes = lax.broadcasted_iota(jnp.int32, (span, LANES), 1).astype(F32)
+    diag_ref[...] = jnp.where(by_column == lanes, 1.0, 0.0).astype(BF)
+    model = spread_ref.shape[1]
+    row_ids = lax.broadcasted_iota(jnp.int32, (8, model), 1)
+    target = jnp.full((8, model), -1, jnp.int32)
+    for b in range(buckets):
+        target = jnp.where(row_ids == b // table_rows * own + b % table_rows, b, target)
+    down = lax.broadcasted_iota(jnp.int32, (LANES, model), 0).astype(F32)
+    spread_ref[...] = jnp.where(down == target[0:1, :].astype(F32), 1.0, 0.0).astype(BF)
+
+
+def pack_kernel(o0, o1, o2, o3, qkv_ref, router_ref, one_ref, two_ref, out_ref):
     experts, rows = router_ref.shape
     fill = jnp.zeros((LANES - experts - 2, rows), F32)
     tail = [r[...].astype(F32) for r in (router_ref, one_ref, two_ref)]
     tail = jnp.concatenate([*tail, fill], axis=0).T.astype(BF)
-    out_ref[...] = jnp.concatenate([*(qkv_ref[c] for c in range(3)), tail], axis=1)
+    parts = [r[...] for r in (o0, o1, o2, o3)] + [qkv_ref[c] for c in range(3)]
+    used = sum(p.shape[1] for p in parts)
+    gap = out_ref.shape[1] - used - LANES
+    if gap:
+        parts.append(jnp.zeros((rows, gap), BF))
+    out_ref[...] = jnp.concatenate([*parts, tail], axis=1)
 
 
 def qkv_kernel(
-    cols, experts, count, at, own_ref, other_ref, *refs
+    first_col, cols, experts, count, at, own_ref, other_ref, *refs
 ):
     pieces = refs[:count]
     qkv_ref, norm_ref, scale_ref, small_ref, gains_ref = refs[count:]
@@ -403,10 +473,10 @@
         slot = 0
         for piece in pieces:
             for s in range(piece.shape[0]):
-                first = pl.multiple_of(at[slot], 16)
+                first = pl.multiple_of(at[4 + slot], 16)
                 small_ref[pl.ds(first, piece.shape[1]), :] = piece[s]
                 slot += 1
-        tail = small_ref[:, cols:].astype(F32).T
+        tail = small_ref[:, small_ref.shape[1] - LANES :].astype(F32).T
         gains_ref[...] = tail[experts : experts + 8, :]
 
     x = jnp.where(i < pl.num_programs(0) // 2, own_ref[...], other_ref[...]).astype(F32)
@@ -414,7 +484,7 @@
     normed = (x * scale * gains_ref[0:1, :]).astype(BF)
     norm_ref[...] = normed
     scale_ref[...] = to_row(scale)
-    qkv_ref[...] = dot(normed, small_ref[:, 0:cols]).astype(BF)
+    qkv_ref[...] = dot(normed, small_ref[:, first_col : first_col + cols]).astype(BF)
 
 
 def router_parts(hidden, gain, router, chosen, experts):
@@ -432,7 +502,7 @@
 
 def hidden_kernel(experts, at, *refs):
     tok_ref, mix_refs, wout_ref = refs[0], refs[1:5], refs[5]
-    gains_ref, small_ref, chosen_ref, hidden_ref, norm_ref, gate_ref = refs[6:]
+    gains_ref, small_ref, chosen_ref, hidden_ref, norm_ref, gate_ref, share_ref, turn_s = refs[6:]
     mixed = jnp.concatenate([r[...] for r in mix_refs], axis=0)
     both = mixed.astype(F32).T.astype(BF)
     hidden = tok_ref[...].astype(F32) + dot(both, wout_ref[...], NT)
@@ -440,56 +510,93 @@
     hidden_ref[...] = hidden
     norm_ref[...] = parts[2]
     gate_ref[...] = to_row(parts[5])
+    turn_s[...] = hidden.T
+    share = share_ref.shape[0]
+    share_ref[...] = turn_s[pl.ds(pl.multiple_of(at[0] * share, share), share), :]
+
+
+def sort_kernel(owner, pos_row, rows_ref, out_ref):
+    i = pl.program_id(0)
+    place = lax.broadcasted_iota(jnp.int32, (TILE, pos_row.shape[1]), 0) + i * TILE
+    pick = jnp.where(pos_row[...] == place, 1.0, 0.0).astype(BF)
+    out_ref[...] = dot(pick, rows_ref[...]).astype(BF)
+
+
+def pick_back(pos_col, total):
+    place = lax.broadcasted_iota(jnp.int32, (pos_col.shape[0], total), 1).astype(F32)
+    return jnp.where(pos_col == place, 1.0, 0.0).astype(BF)
+
+
+def unsort_kernel(owner, at, pos_row, sorted_ref, e0, e1, e2, e3, pos_col, turn_s):
+    rows = pos_row.shape[1]
+    part = turn_s.shape[1]
+    pos_col[...] = jnp.broadcast_to(pos_row[...].astype(F32), (LANES, rows)).T
+    for g in range(rows // part):
+        mine = slice(g * part, (g + 1) * part)
+        pick = pick_back(pos_col[mine, 0:1], sorted_ref.shape[0])
+        turn_s[...] = dot(pick, sorted_ref[...]).T.astype(BF)
+        for step, out in enumerate((e0, e1, e2, e3)):
+            share = out.shape[0]
+            first = pl.multiple_of(lax.rem(at[0] + step, 4) * share, share)
+            out[:, mine] = turn_s[pl.ds(first, share), :]
 
 
 def expert_kernel(
     owner, at, pos_row, norm_ref, cot_ref, gate_ref, w_ref,
-    b0, b1, b2, b3, eo_ref, x_ref, de_ref, act_ref, di_ref, eo_s, dr_s, pos_col,
+    b0, b1, b2, b3, eo_ref, x_ref, de_ref, act_ref, di_ref, dr_s, pos_col,
 ):
     i = pl.program_id(0)
     z = at[0]
     rows = norm_ref.shape[0]
     width = norm_ref.shape[1]
     ff = w_ref.shape[1] // 2
-    place = lax.broadcasted_iota(jnp.int32, (TILE, rows), 0) + i * TILE
-    hit = pos_row[...] == place
-    pick = jnp.where(hit, 1.0, 0.0).astype(BF)
-    x = dot(pick, norm_ref[...]).astype(BF)
-    cot = dot(pick, cot_ref[...])
-    gate = jnp.sum(jnp.where(hit, gate_ref[...], 0.0), axis=1, keepdims=True)
-    d_e = (gate * cot).astype(BF)
-    w_in = w_ref[:, 0:ff]
-    w_down = w_ref[:, ff : 2 * ff]
-    inner = dot(x, w_in)
-    half = 0.5 * (1.0 + lax.erf(inner * (0.5**0.5)))
-    active = (inner * half).astype(BF)
-    slope = half + inner * (jnp.exp(-0.5 * inner * inner) * 0.3989422804014327)
-    d_inner = (dot(d_e, w_down) * slope).astype(BF)
-    terms = dot(active, w_down, NT)
-    d_rows = dot(d_inner, w_in, NT)
-    d_gate = jnp.sum(cot * terms, axis=1, keepdims=True)
-    lane = lax.broadcasted_iota(jnp.int32, (TILE, LANES), 1)
-    hi, mid, low = (t.astype(F32) for t in split3(d_gate))
-    extra = jnp.where(lane == 0, hi, jnp.where(lane == 1, mid, jnp.where(lane == 2, low, 0.0)))
     here = pl.ds(pl.multiple_of(i * TILE, TILE), TILE)
-    eo_s[here, :] = terms.astype(BF)
-    dr_s[here, :] = jnp.concatenate([d_rows.astype(BF), extra.astype(BF)], axis=1)
-    x_ref[...] = x
-    de_ref[...] = d_e
-    act_ref[...] = active
-    di_ref[...] = d_inner
+    used = i < owner[0, LANES - 1]
+
+    @pl.when(used)
+    def _():
+        place = lax.broadcasted_iota(jnp.int32, (TILE, rows), 0) + i * TILE
+        hit = pos_row[...] == place
+        pick = jnp.where(hit, 1.0, 0.0).astype(BF)
+        x = dot(pick, norm_ref[...]).astype(BF)
+        cot = cot_ref[...].astype(F32)
+        gate = jnp.sum(jnp.where(hit, gate_ref[...], 0.0), axis=1, keepdims=True)
+        d_e = (gate * cot).astype(BF)
+        w_in = w_ref[:, 0:ff]
+        w_down = w_ref[:, ff : 2 * ff]
+        d_act = dot(d_e, w_down)
+        inner = dot(x, w_in)
+        half = 0.5 * (1.0 + lax.erf(inner * (0.5**0.5)))
+        active = (inner * half).astype(BF)
+        slope = half + inner * (jnp.exp(-0.5 * inner * inner) * 0.3989422804014327)
+        d_inner = (d_act * slope).astype(BF)
+        d_rows = dot(d_inner, w_in, NT)
+        terms = dot(active, w_down, NT)
+        d_gate = jnp.sum(cot * terms, axis=1, keepdims=True)
+        lane = lax.broadcasted_iota(jnp.int32, (TILE, LANES), 1)
+        hi, mid, low = (t.astype(F32) for t in split3(d_gate))
+        extra = jnp.where(lane == 0, hi, jnp.where(lane == 1, mid, jnp.where(lane == 2, low, 0.0)))
+        dr_s[here, :] = jnp.concatenate([d_rows.astype(BF), extra.astype(BF)], axis=1)
+        eo_ref[...] = terms.astype(BF)
+        x_ref[...] = x
+        de_ref[...] = d_e
+        act_ref[...] = active
+        di_ref[...] = d_inner
+
+    @pl.when(jnp.logical_not(used))
+    def _():
+        dr_s[here, :] = jnp.zeros((TILE, dr_s.shape[1]), BF)
+        for ref in (eo_ref, x_ref, de_ref, act_ref, di_ref):
+            ref[...] = jnp.zeros_like(ref)
 
     @pl.when(i == pl.num_programs(0) - 1)
     def _():
-        total = dr_s.shape[0]
         part = rows // 4
         pos_col[...] = jnp.broadcast_to(pos_row[...].astype(F32), (LANES, rows)).T
         for r, back_ref in enumerate((b0, b1, b2, b3)):
             g = lax.rem(z + r, 4)
             mine = pl.ds(pl.multiple_of(g * part, part), part)
-            place = lax.broadcasted_iota(jnp.int32, (part, total), 1).astype(F32)
-            pick = jnp.where(pos_col[mine, 0:1] == place, 1.0, 0.0).astype(BF)
-            back = dot(pick, dr_s[...])
+            back = dot(pick_back(pos_col[mine, 0:1], dr_s.shape[0]), dr_s[...])
             back_ref[0:part, :] = back[:, 0:width].astype(BF)
             tail = back[:, width : width + LANES].T
             d_gate = tail[0:1, :] + tail[1:2, :] + tail[2:3, :]
@@ -497,27 +604,32 @@
             strip = jnp.where(row == 0, jnp.broadcast_to(d_gate, (16, part)), 0.0)
             fill = jnp.zeros((16, width - part), F32)
             back_ref[part : part + 16, :] = jnp.concatenate([strip, fill], axis=1).astype(BF)
-            eo_ref[:, mine] = dot(pick, eo_s[...]).T.astype(BF)
-
-
-def weight_grad_kernel(owner, slot, at, rows_ref, cols_ref, keep_ref, send_ref, acc):
+
+
+def weight_grad_kernel(owner, x_ref, di_ref, de_ref, act_ref, out_ref, acc):
     i = pl.program_id(0)
     last = pl.num_programs(0) - 1
-    me = owner[i]
-    before = owner[jnp.maximum(i - 1, 0)]
-    after = owner[jnp.minimum(i + 1, last)]
-
-    @pl.when((i == 0) | (before != me))
+    me = owner[0, i]
+    before = owner[0, jnp.maximum(i - 1, 0)]
+    after = owner[0, jnp.minimum(i + 1, last)]
+    ff = di_ref.shape[1]
+
+    first = (i == 0) | (before != me)
+    used = i < owner[0, LANES - 1]
+
+    @pl.when(first)
     def _():
-        acc[...] = jnp.zeros_like(acc)
-
-    acc[...] += dot(rows_ref[...], cols_ref[...], TN)
+        acc[:, 0:ff] = dot(x_ref[...], di_ref[...], TN)
+        acc[:, ff : 2 * ff] = dot(de_ref[...], act_ref[...], TN)
+
+    @pl.when(jnp.logical_not(first) & used)
+    def _():
+        acc[:, 0:ff] += dot(x_ref[...], di_ref[...], TN)
+        acc[:, ff : 2 * ff] += dot(de_ref[...], act_ref[...], TN)
 
     @pl.when((i == last) | (after != me))
     def _():
-        half = keep_ref.shape[0]
-        keep_ref[...] = acc[pl.ds(pl.multiple_of(at[1] * half, half), half), :].astype(BF)
-        send_ref[...] = acc[pl.ds(pl.multiple_of((1 - at[1]) * half, half), half), :].astype(BF)
+        out_ref[...] = acc[...].astype(BF)
 
 
 def split_rows(at, first_slot, acc, outs):
@@ -568,59 +680,89 @@
         dmix_refs[r][...] = d_mixed[s * width : (s + 1) * width, :]
     dh_ref[...] = d_hidden
     mixed = jnp.concatenate([r[...] for r in mix_refs], axis=0)
-    gout_ref[...] = dot(d_attn_t, mixed, NT)
+    gout_ref[...] = dot(d_attn_t, mixed, NT).astype(BF)
 
 
 def qkv_back_kernel(
-    at, dq_ref, dkv_ref, got_ref, norm_ref, tok_ref, scale_ref, gains_ref, w_ref, dh_ref, gout_ref,
-    terms_ref, gain_out_ref, *rest,
+    first_col, experts, heads, at, dq_ref, dkv_ref, got_ref, norm_ref, tok_ref, scale_ref, gains_ref, w_ref,
+    dh_ref, gout_ref, small_ref, skew_ref, sides_ref, diag_ref, spread_ref,
+    terms_ref, *rest,
 ):
-    *gw_refs, acc = rest
+    *gw_refs, acc, gain_s = rest
     i = pl.program_id(0)
     width = dq_ref.shape[0]
+    cols = 3 * width
+    model = tok_ref.shape[1]
     dkv = dkv_ref[...].astype(F32) + got_ref[...].astype(F32)
     d_qkv = jnp.concatenate([dq_ref[...].astype(F32).T, dkv], axis=1).astype(BF)
     scale = to_column(scale_ref[...])
     hat = tok_ref[...].astype(F32) * scale
-    terms = dot(d_qkv, w_ref[:, 0 : 3 * width], NT)
+    terms = dot(d_qkv, w_ref[:, first_col : first_col + cols], NT)
     d_hat = terms * gains_ref[0:1, :]
     mean = jnp.mean(d_hat * hat, axis=-1, keepdims=True)
     grad = scale * (d_hat - hat * mean) + jnp.where(i == at[0], dh_ref[...], 0.0)
 
     @pl.when(i == 0)
     def _():
-        acc[:, 0 : 3 * width] = jnp.zeros((acc.shape[0], 3 * width), F32)
-        acc[:, 3 * width :] = gout_ref[...]
-        gain_out_ref[...] = jnp.zeros_like(gain_out_ref)
-
-    gain_out_ref[0:1, :] += jnp.sum(terms * hat, axis=0, keepdims=True)
-    acc[:, 0 : 3 * width] += dot(norm_ref[...], d_qkv, TN)
+        wide = acc.shape[1] - model - LANES
+        acc[:, 0:wide] = jnp.zeros((model, wide), F32)
+        acc[:, wide : wide + model] = gout_ref[...].astype(F32)
+        gain_s[...] = jnp.zeros_like(gain_s)
+
+    gain_s[0:1, :] += jnp.sum(terms * hat, axis=0, keepdims=True)
+    acc[:, 0:cols] += dot(norm_ref[...], d_qkv, TN)
     terms_ref[...] = grad.T.astype(BF)
 
     @pl.when(i == pl.num_programs(0) - 1)
     def _():
+        rows = [small_ref[0 : experts + 1, :], gain_s[0:1, :]]
+        lines = []
+        sides = []
+        for h in range(8):
+            k = min(h, heads - 1)
+            lines.append(jnp.concatenate([skew_ref[3 * k + t : 3 * k + t + 1, :] for t in range(3)], axis=1))
+            sides.append(jnp.sum(sides_ref[2 * k : 2 * k + 2, :], axis=1, keepdims=True))
+        lane = lax.broadcasted_iota(jnp.int32, (8, LANES), 1)
+        table = sum(dot(p, diag_ref[...]) for p in split3(jnp.concatenate(lines, axis=0)))
+        table = table + jnp.where(lane == 15, jnp.concatenate([s[0:1, :] for s in sides], axis=0), 0.0)
+        table = table + jnp.where(lane == 31, jnp.concatenate([s[1:2, :] for s in sides], axis=0), 0.0)
+        spread = sum(dot(p, spread_ref[...]) for p in split3(table))
+        rows.append(spread[0:heads, :])
+        rows.append(jnp.zeros((LANES - experts - 2 - heads, model), F32))
+        acc[:, acc.shape[1] - LANES :] = jnp.concatenate(rows, axis=0).T
         split_rows(at, 4, acc, gw_refs)
 
 
-def out_kernel(eo_ref, hidden_ref, gate_ref, out_ref):
-    out_ref[...] = (hidden_ref[...] + eo_ref[...].astype(F32) * gate_ref[...]).astype(BF)
-
-
-def placement(chosen, experts, tiles):
-    rows = chosen.shape[0]
-    ids = jnp.arange(experts, dtype=jnp.int32)
-    one_hot = chosen[:, None] == ids[None, :]
-    below = jnp.arange(rows)[:, None] > jnp.arange(rows)[None, :]
-    earlier = dot(below.astype(BF), one_hot.astype(BF)).astype(jnp.int32)
-    count = jnp.sum(one_hot.astype(jnp.int32), axis=0)
-    used = jnp.maximum((count + TILE - 1) // TILE, 1)
-    ends = jnp.sum(jnp.where(ids[None, :] <= ids[:, None], used[None, :], 0), axis=1)
-    first = (ends - used) * TILE
-    pos = jnp.sum(jnp.where(one_hot, earlier + first[None, :], 0), axis=1).astype(jnp.int32)
-    tile_ids = jnp.arange(tiles, dtype=jnp.int32)
-    owner = jnp.sum((ends[None, :] <= tile_ids[:, None]).astype(jnp.int32), axis=1)
-    return pos, jnp.minimum(owner, experts - 1).astype(jnp.int32)
-
+def out_kernel(e0, e1, e2, e3, hidden_ref, gate_ref, out_ref):
+    total = sum(r[...].astype(F32) for r in (e0, e1, e2, e3))
+    out_ref[...] = (hidden_ref[...] + total * gate_ref[...]).astype(BF)
+
+
+def pair_sum_kernel(keep_ref, got_ref, *outs):
+    step = outs[0].shape[0]
+    for s, out in enumerate(outs):
+        rows = slice(s * step, (s + 1) * step)
+        out[...] = (keep_ref[rows, :].astype(F32) + got_ref[rows, :].astype(F32)).astype(BF)
+
+
+def dense_sum_kernel(cols, count, *refs):
+    parts, (qkv_ref, late_ref, *outs) = refs[:count], refs[count:]
+    total = sum(r[...].astype(F32) for r in parts)
+    width = qkv_ref.shape[2]
+    for c in range(3):
+        qkv_ref[c] = total[:, c * width : (c + 1) * width]
+    late = total[:, total.shape[1] - LANES :]
+    late_ref[...] = late.T
+    for s, out in enumerate(outs):
+        piece = total[:, cols + s * width : cols + (s + 1) * width]
+        gap = jnp.zeros((late.shape[0], out.shape[1] - LANES - width), F32)
+        out[...] = jnp.concatenate([late, piece, gap], axis=1).astype(BF)
+
+
+def last_sum_kernel(p0, p1, p2, p3, out_ref, late_ref):
+    total = sum(r[...].astype(F32) for r in (p0, p1, p2, p3))
+    out_ref[...] = total[:, LANES : LANES + out_ref.shape[1]]
+    late_ref[...] = total[:, 0:LANES].T
 
 def xor_step(x, axis, s):
     return lax.ppermute(x, axis, [(i, i ^ s) for i in range(lax.axis_size(axis))])
@@ -640,26 +782,6 @@
 
 def after(x, *others):
     return lax.optimization_barrier((x, others))[0]
-
-
-def dense_scatter(parts):
-    if len(parts) == 1:
-        return lax.psum_scatter(parts[0], ("fsdp", "ctx"), scatter_dimension=0, tiled=True).astype(F32)
-    keep, send = parts
-    both = keep + xor_step(send, "ctx", 1)
-    step = keep.shape[0] // 4
-    total = both[0:step].astype(F32)
-    for s in (1, 2, 3):
-        total = total + xor_step(both[s * step : (s + 1) * step], "fsdp", s).astype(F32)
-    return total
-
-
-def sum_all(x):
-    if lax.axis_size("fsdp") != 4 or lax.axis_size("ctx") != 2:
-        return lax.psum(x, ("fsdp", "ctx", "tp"))
-    x = x + xor_step(x, "ctx", 1)
-    x = x + xor_step(x, "fsdp", 1) + xor_step(x, "fsdp", 2) + xor_step(x, "fsdp", 3)
-    return x + turn(x, 1) + turn(x, 2) + turn(x, 3)
 
 
 def shards(
@@ -696,76 +818,91 @@
     dense = ("fsdp", "ctx")
     square = fsdp_n == 4 and ctx_n == 2
 
+    wide_cols = -(-3 * width // LANES) * LANES
+    late_at = wide_cols + model
+    table_rows = rel_bias.shape[0] // (fsdp_n * ctx_n)
+    if square:
+        starts = [((fsdp_at ^ s) * 2 + c) * own for c in (ctx_at, 1 - ctx_at) for s in range(4)]
+    else:
+        starts = [0]
+    at = jnp.stack([jnp.int32(v) for v in (tp_at, ctx_at, ctx_at * blocks, fsdp_at, *starts)])
+
     qkv_cols = 3 * width
-    cols = qkv_cols + LANES
+    first_col = model
+    cols = -(-(model + qkv_cols) // LANES) * LANES + LANES
     small = call(
         pack_kernel,
         (1,),
-        [whole(3, own, width), whole(experts, own), whole(1, own), whole(1, own)],
+        [
+            *[whole(own, width)] * 4,
+            whole(3, own, width),
+            whole(experts, own),
+            whole(1, own),
+            whole(1, own),
+        ],
         whole(own, cols),
         shaped((own, cols), BF),
         name="pack_small",
-    )(w_qkv.transpose(1, 0, 2), w_router.T, gain_attn[None, :], gain_ffn[None, :])
+    )(
+        *gather_turns(w_attn_out),
+        w_qkv.transpose(1, 0, 2),
+        w_router.T,
+        gain_attn[None, :],
+        gain_ffn[None, :],
+    )
+    tokens_other = xor_step(tokens, "ctx", 1)
     half = model // ctx_n
-    mine_rows = lambda at: jnp.concatenate(
-        [lax.dynamic_slice_in_dim(w.reshape(-1, ff), at * half, half, 0) for w in (w_in, w_down)], axis=1
+    w_half = jnp.concatenate(
+        [lax.dynamic_slice_in_dim(w.reshape(-1, ff), ctx_at * half, half, 0) for w in (w_in, w_down)],
+        axis=1,
     )
+
+    tiles = (rows + experts * (TILE - 1)) // TILE
+    span = 6 * BQ
+    table = rel_bias.T
+    pos, owner, chosen, docs, info, band, diag, spread = call(
+        partial(plan_kernel, experts, own, table_rows),
+        (1,),
+        [whole(1, rows), whole(1, seq), whole(*table.shape)],
+        [
+            whole(1, rows),
+            whole(1, LANES),
+            whole(1, rows),
+            whole(1, seq),
+            whole(1, LANES),
+            whole(heads, 3, BK, BQ),
+            whole(span, LANES),
+            whole(LANES, model),
+        ],
+        [
+            shaped((1, rows), jnp.int32),
+            shaped((1, LANES), jnp.int32),
+            shaped((1, rows), F32),
+            shaped((1, seq), F32),
+            shaped((1, LANES), jnp.int32),
+            shaped((heads, 3, BK, BQ), F32),
+            shaped((span, LANES), BF),
+            shaped((LANES, model), BF),
+        ],
+        prefetch=1,
+        name="plan",
+    )(at, expert_ids.T, doc_ids[None, :], table)
     if square:
-        near = jnp.stack([small] + [xor_step(small, "fsdp", s) for s in (1, 2, 3)])
+        near = [small] + [xor_step(small, "fsdp", s) for s in (1, 2, 3)]
+        near, w_half, band = lax.optimization_barrier((near, w_half, band))
+        near = jnp.stack(near)
         small_parts = [near, xor_step(near, "ctx", 1)]
-        starts = [((fsdp_at ^ s) * 2 + c) * own for c in (ctx_at, 1 - ctx_at) for s in range(4)]
     else:
         small_parts = [lax.all_gather(small, dense, axis=0, tiled=True)[None]]
-        starts = [jnp.int32(0)]
-    tokens_other = xor_step(tokens, "ctx", 1)
-    out_line = jnp.concatenate(gather_turns(w_attn_out), axis=1)
-    out_all = lax.all_gather(out_line, dense, axis=0, tiled=True)
-    w_half = mine_rows(ctx_at)
-
-    tiles = (rows + experts * (TILE - 1)) // TILE
-    pos, owner = placement(expert_ids[:, 0], experts, tiles)
-    pos = pos[None, :]
-    chosen = expert_ids[:, 0].astype(F32)[None, :]
-    docs = doc_ids.astype(F32)[None, :]
-    firsts = lax.dynamic_slice_in_dim(doc_ids.reshape(-1, BQ)[:, 0], ctx_at * blocks, blocks)
-    lasts = lax.dynamic_slice_in_dim(doc_ids.reshape(-1, BQ)[:, BQ - 1], ctx_at * blocks, blocks)
-    low = jnp.sum((doc_ids[None, :] < firsts[:, None]).astype(jnp.int32), axis=1) // BK
-    high = (jnp.sum((doc_ids[None, :] <= lasts[:, None]).astype(jnp.int32), axis=1) + BK - 1) // BK
-    info = jnp.concatenate(((ctx_at * blocks)[None], low, high, tp_at[None])).astype(jnp.int32)
-    wrapped = jnp.arange(2 * BQ, dtype=jnp.int32)
-    wrapped = jnp.where(wrapped < BQ, wrapped, wrapped - 2 * BQ)
-    offsets = (jnp.arange(3, dtype=jnp.int32)[:, None] - 1) * BK - wrapped[None, :]
-    selector = relative_bucket(offsets)[:, :, None] == jnp.arange(rel_bias.shape[0])[None, None, :]
-    selector = selector.astype(F32)
-    vectors = jnp.einsum("tcb,bh->htc", selector, rel_bias, precision=lax.Precision.HIGHEST)
-    far = jnp.stack((rel_bias[15], rel_bias[31]))
-    band = call(
-        band_kernel,
-        (1,),
-        [whole(3 * heads, 2 * BQ)],
-        whole(heads, 3, BK, BQ),
-        shaped((heads, 3, BK, BQ), F32),
-        name="bias_band",
-    )(vectors.reshape(3 * heads, 2 * BQ))
-    columns = tp_at * share
-    starts = [s.astype(jnp.int32) for s in starts]
-    at = jnp.stack([tp_at, ctx_at, ctx_at * blocks, fsdp_at] + starts).astype(jnp.int32)
-    starts = jnp.stack(starts + [ctx_at * blocks]).astype(jnp.int32)
-    early = (w_half, pos, owner, chosen, docs, info, band, far, at, starts, selector)
-    (small_parts, tokens_other, early) = lax.optimization_barrier((small_parts, tokens_other, early))
-    w_half, pos, owner, chosen, docs, info, band, far, at, starts, selector = early
+    small_parts, tokens_other, w_half = lax.optimization_barrier((small_parts, tokens_other, w_half))
 
     w_experts = lax.all_gather(w_half, dense, axis=0, tiled=True)
-    slot = owner ^ fsdp_at if square else owner
-    slot = slot.astype(jnp.int32)
 
     steps = seq // BQ
     n_own = steps // 2
-    base = lambda i, at: at[len_starts] + i
-    len_starts = starts.shape[0] - 1
-    turned = lambda i, at: jnp.where(i < n_own, at[len_starts] + i, n_own - at[len_starts] + i - n_own)
+    turned = lambda i, at: jnp.where(i < n_own, at[2] + i, i - at[2])
     qkv_all, normed_one, scale_one, small_all, gains = call(
-        partial(qkv_kernel, qkv_cols, experts, len(small_parts)),
+        partial(qkv_kernel, first_col, qkv_cols, experts, len(small_parts)),
         (steps,),
         [
             pl.BlockSpec((BQ, model), lambda i, at: (jnp.minimum(i, n_own - 1), 0)),
@@ -787,21 +924,32 @@
             shaped((8, model), F32),
         ],
         prefetch=1,
-        us=8,
         name="norm_qkv",
-    )(starts, tokens, tokens_other, *small_parts)
-    mixed, mixed_low, lse = attention_fwd(info, far, qkv_all, docs, docs, band, rows)
+    )(at, tokens, tokens_other, *small_parts)
+    mixed, mixed_low, lse = attention_fwd(info, table, qkv_all, docs, docs, band, rows)
     mixed_turns = gather_turns(mixed_low)
-
-    router_block = whole(model, LANES)
-    router = small_all[:, qkv_cols:]
-    hidden, normed_two, gate_row = call(
+    sorted_rows = tiles * TILE
+    sorted_spec = lambda cols: pl.BlockSpec((TILE, cols), lambda i, *_: (i, 0))
+    cot_sorted = call(
+        sort_kernel,
+        (tiles,),
+        [whole(1, rows), whole(rows, model)],
+        sorted_spec(model),
+        shaped((sorted_rows, model), BF),
+        prefetch=1,
+        name="sort_cotangents",
+    )(owner, pos, after(grad_out, mixed_low))
+    mixed_turns, cot_sorted = lax.optimization_barrier((mixed_turns, cot_sorted))
+
+    router_block = pl.BlockSpec((model, LANES), lambda i, at: (0, cols // LANES - 1))
+    out_block = pl.BlockSpec((model, model), lambda i, at: (0, 0))
+    hidden, normed_two, gate_row, hidden_share = call(
         partial(hidden_kernel, experts),
         (blocks,),
         [
             pl.BlockSpec((BQ, model), lambda i, at: (i, 0)),
             *[pl.BlockSpec((width, BQ), lambda i, at: (0, i))] * 4,
-            whole(model, model),
+            out_block,
             whole(8, model),
             router_block,
             pl.BlockSpec((1, BQ), lambda i, at: (0, i)),
@@ -810,27 +958,31 @@
             pl.BlockSpec((BQ, model), lambda i, at: (i, 0)),
             pl.BlockSpec((BQ, model), lambda i, at: (i, 0)),
             pl.BlockSpec((1, BQ), lambda i, at: (0, i)),
-        ],
-        [shaped((rows, model), F32), shaped((rows, model), BF), shaped((1, rows), F32)],
+            pl.BlockSpec((share, BQ), lambda i, at: (0, i)),
+        ],
+        [
+            shaped((rows, model), F32),
+            shaped((rows, model), BF),
+            shaped((1, rows), F32),
+            shaped((share, rows), F32),
+        ],
+        scratch=[pltpu.VMEM((model, BQ), F32)],
         prefetch=1,
-        us=7,
         name="hidden_router",
-    )(at, tokens, *mixed_turns, out_all, gains, router, chosen)
-    sorted_rows = tiles * TILE
-    sorted_spec = lambda cols: pl.BlockSpec((TILE, cols), lambda i, *_: (i, 0))
-    *back, eo_t, x_sorted, d_expert, active, d_inner = call(
+    )(at, tokens, *mixed_turns, small_all, gains, small_all, chosen)
+    *back, eo_sorted, x_sorted, d_expert, active, d_inner = call(
         expert_kernel,
         (tiles,),
         [
             whole(1, rows),
             whole(rows, model),
-            whole(rows, model),
+            sorted_spec(model),
             whole(1, rows),
-            pl.BlockSpec((model, 2 * ff), lambda i, owner, at: (owner[i], 0)),
+            pl.BlockSpec((model, 2 * ff), lambda i, owner, at: (owner[0, i], 0)),
         ],
         [
             *[whole(part + 16, model)] * 4,
-            whole(model, rows),
+            sorted_spec(model),
             sorted_spec(model),
             sorted_spec(model),
             sorted_spec(ff),
@@ -838,39 +990,43 @@
         ],
         [
             *[shaped((part + 16, model), BF)] * 4,
-            shaped((model, rows), BF),
+            shaped((sorted_rows, model), BF),
             shaped((sorted_rows, model), BF),
             shaped((sorted_rows, model), BF),
             shaped((sorted_rows, ff), BF),
             shaped((sorted_rows, ff), BF),
         ],
         scratch=[
-            pltpu.VMEM((sorted_rows, model), BF),
             pltpu.VMEM((sorted_rows, model + LANES), BF),
             pltpu.VMEM((rows, LANES), F32),
         ],
         prefetch=2,
-        us=30,
         name="experts",
-    )(owner, at, pos, normed_two, grad_out, gate_row, w_experts)
+    )(owner, at, pos, normed_two, cot_sorted, gate_row, w_experts)
     back_mine = scatter_turns(back)
-    exchanged = []
-    for left, right in ((x_sorted, d_inner), (d_expert, active)):
-        keep, send = call(
-            weight_grad_kernel,
-            (tiles,),
-            [sorted_spec(model), sorted_spec(ff)],
-            [pl.BlockSpec((half, ff), lambda i, owner, slot, at: (slot[i], 0))] * 2,
-            [shaped((experts * half, ff), BF)] * 2,
-            scratch=[pltpu.VMEM((model, ff), F32)],
-            prefetch=3,
-            us=0.1,
-            name="expert_weight_grads",
-        )(owner, slot, at, left, right)
-        exchanged.append((keep, xor_step(send, "ctx", 1)))
-    (keep_in, got_in), (keep_down, got_down) = exchanged
-    both_in = keep_in + got_in
-    back_mine, both_in, keep_down = lax.optimization_barrier((back_mine, both_in, keep_down))
+    back_got = back_mine[1:]
+    grad_experts = call(
+        weight_grad_kernel,
+        (tiles,),
+        [sorted_spec(model), sorted_spec(ff), sorted_spec(model), sorted_spec(ff)],
+        pl.BlockSpec((model, 2 * ff), lambda i, owner: (owner[0, i], 0)),
+        shaped((experts * model, 2 * ff), BF),
+        scratch=[pltpu.VMEM((model, 2 * ff), F32)],
+        prefetch=1,
+        name="expert_weight_grads",
+    )(owner, x_sorted, d_inner, d_expert, active)
+    eo_out = call(
+        unsort_kernel,
+        (1,),
+        [whole(1, rows), whole(sorted_rows, model)],
+        [whole(share, rows)] * 4,
+        [shaped((share, rows), BF)] * 4,
+        scratch=[pltpu.VMEM((rows, LANES), F32), pltpu.VMEM((model, part), BF)],
+        prefetch=2,
+        name="unsort_outputs",
+    )(owner, at, pos, after(eo_sorted, grad_experts))
+    back_mine, eo_out = lax.optimization_barrier((back_mine, eo_out))
+    grad_experts = lax.psum_scatter(after(grad_experts, back_got), dense, scatter_dimension=0, tiled=True)
 
     small_rows = -(-(experts + 1) // 8) * 8
     row_block = pl.BlockSpec((part, model), lambda i, at: (at[0], 0))
@@ -887,7 +1043,7 @@
             whole(8, model),
             router_block,
             pl.BlockSpec((1, part), lambda i, at: (0, at[0])),
-            whole(model, model),
+            out_block,
             *[col_block] * 4,
         ],
         [*[piece] * 4, whole(part, model), whole(small_rows, model), whole(model, model)],
@@ -895,34 +1051,24 @@
             *[shaped((width, part), BF)] * 4,
             shaped((part, model), F32),
             shaped((small_rows, model), F32),
-            shaped((model, model), F32),
+            shaped((model, model), BF),
         ],
         prefetch=1,
-        us=6,
         name="hidden_back",
-    )(at, *back_mine, hidden, grad_out, gains, router, chosen, out_all, *mixed_turns)
+    )(at, *back_mine, hidden, grad_out, gains, small_all, chosen, small_all, *mixed_turns)
     dmix_out, d_hidden, small_grads, grad_out_w = outs[0:4], outs[4], outs[5], outs[6]
     dmix = scatter_turns(dmix_out)
-    both_down = keep_down + got_down
-    expert_sums = []
-    for both in (both_in, both_down):
-        if square:
-            pieces = [both[s * half : (s + 1) * half] for s in range(4)]
-            expert_sums.append([pieces[0]] + [xor_step(pieces[s], "fsdp", s) for s in (1, 2, 3)])
-        else:
-            expert_sums.append([lax.psum_scatter(both, "fsdp", scatter_dimension=0, tiled=True)])
-    in_sums, down_sums = expert_sums
-    dmix, in_sums, eo_t = lax.optimization_barrier((dmix, in_sums, eo_t))
-    eo_mine = lax.psum_scatter(eo_t, "tp", scatter_dimension=0, tiled=True)
+    dmix, eo_out = lax.optimization_barrier((dmix, eo_out))
+    eo_mine = scatter_turns(eo_out)
 
     dq_t, dkv, skew, sides = attention_bwd(
-        info, far, qkv_all, docs, docs, band, mixed, lse, dmix, rows
+        info, table, qkv_all, docs, docs, band, mixed, lse, dmix, rows
     )
+    dkv, eo_mine = lax.optimization_barrier((dkv, eo_mine))
     other = lax.dynamic_slice_in_dim(dkv, (1 - ctx_at) * rows, rows)
     got = lax.ppermute(other, "ctx", [(0, 1), (1, 0)])
-    got, down_sums = lax.optimization_barrier((got, down_sums))
     outs = call(
-        qkv_back_kernel,
+        partial(qkv_back_kernel, first_col, experts, heads),
         (blocks,),
         [
             pl.BlockSpec((width, BQ), lambda i, at: (0, i)),
@@ -935,74 +1081,92 @@
             whole(model, cols),
             whole(part, model),
             whole(model, model),
+            whole(small_rows, model),
+            whole(16, 2 * BK),
+            whole(8, BQ),
+            whole(span, LANES),
+            whole(LANES, model),
         ],
         [
             pl.BlockSpec((model, BQ), lambda i, at: (0, i)),
-            whole(8, model),
-            *[whole(n, qkv_cols + model) for n in grad_rows],
+            *[whole(n, late_at + LANES) for n in grad_rows],
         ],
         [
             shaped((model, rows), BF),
-            shaped((8, model), F32),
-            *[shaped((n, qkv_cols + model), BF) for n in grad_rows],
-        ],
-        scratch=[pltpu.VMEM((model, qkv_cols + model), F32)],
+            *[shaped((n, late_at + LANES), BF) for n in grad_rows],
+        ],
+        scratch=[pltpu.VMEM((model, late_at + LANES), F32), pltpu.VMEM((8, model), F32)],
         prefetch=1,
-        us=9,
         name="qkv_back",
-    )(at, dq_t, dkv, got, normed_one, tokens, scale_one, gains, small_all, d_hidden, grad_out_w)
-    terms, gain_sum, grad_dense = outs[0], outs[1], outs[2:]
+    )(
+        at, dq_t, dkv, got, normed_one, tokens, scale_one, gains, small_all, d_hidden, grad_out_w,
+        small_grads, skew, sides, diag, spread,
+    )
+    terms, grad_dense = outs[0], outs[1:]
+    terms, grad_experts = lax.optimization_barrier((terms, grad_experts))
     grad_tokens = lax.psum_scatter(terms, "tp", scatter_dimension=0, tiled=True).astype(F32)
-    grad_dense = dense_scatter(grad_dense)
-    grad_out_mine = grad_dense[:, qkv_cols : qkv_cols + width]
-    for s in (1, 2, 3):
-        first = qkv_cols + s * width
-        piece_s = grad_dense[:, first : first + width].astype(BF)
-        grad_out_mine = grad_out_mine + turn(piece_s, 4 - s).astype(F32)
-    grad_in_mine, grad_down_mine = (
-        sum(p.astype(F32) for p in after(pieces, gain_sum)) for pieces in expert_sums
-    )
-
-    diagonals = skew[0 : 3 * heads].reshape(heads, 3, 2 * BQ)
-    table = jnp.einsum("htc,tcb->bh", diagonals, selector, precision=lax.Precision.HIGHEST)
-    side = jnp.sum(sides[0 : 2 * heads], axis=1).reshape(heads, 2)
-    bucket_ids = jnp.arange(rel_bias.shape[0])[:, None]
-    table = table + jnp.where(bucket_ids == 15, side[None, :, 0], 0.0)
-    table = table + jnp.where(bucket_ids == 31, side[None, :, 1], 0.0)
-    slots = jnp.where(jnp.arange(tp_n)[:, None] == tp_at, table.reshape(1, -1), 0.0).reshape(-1)
-    slots = jnp.concatenate((slots, jnp.zeros((-slots.shape[0] % model,), F32))).reshape(-1, model)
-    late_sums = sum_all(jnp.concatenate((small_grads, gain_sum, slots)))
-    table_all = late_sums[small_rows + 8 :].reshape(-1)[: tp_n * table.size]
-    table_all = table_all.reshape(tp_n, rel_bias.shape[0], heads)
-    table_mine = lax.dynamic_index_in_dim(table_all, tp_at, 0, keepdims=False)
-    table_rows = rel_bias.shape[0] // (fsdp_n * ctx_n)
-    grad_table = lax.dynamic_slice_in_dim(table_mine, dense_at * table_rows, table_rows)
-    small_mine = lax.dynamic_slice_in_dim(late_sums[: small_rows + 8], dense_at * own, own, 1)
-    grad_router = small_mine[0:experts].T
-    grad_gain_two = small_mine[experts]
-    grad_gain_one = small_mine[small_rows]
-
-    hidden_share = lax.dynamic_slice_in_dim(hidden, columns, share, 1).T
+    dense_cols = late_at + LANES
+    piece_cols = -(-(LANES + width) // LANES) * LANES
+    if square:
+        keep, send = grad_dense
+        pieces = call(
+            pair_sum_kernel,
+            (1,),
+            [whole(4 * own, dense_cols)] * 2,
+            [whole(own, dense_cols)] * 4,
+            [shaped((own, dense_cols), BF)] * 4,
+            name="dense_pair_sum",
+        )(keep, xor_step(send, "ctx", 1))
+        pieces = [pieces[0]] + [xor_step(pieces[s], "fsdp", s) for s in (1, 2, 3)]
+    else:
+        pieces = [lax.psum_scatter(grad_dense[0], dense, scatter_dimension=0, tiled=True)]
+    grad_qkv, grad_late, *pieces = call(
+        partial(dense_sum_kernel, wide_cols, len(pieces)),
+        (1,),
+        [whole(own, dense_cols)] * len(pieces),
+        [whole(3, own, width), whole(LANES, own), *[whole(own, piece_cols)] * 4],
+        [
+            shaped((3, own, width), F32),
+            shaped((LANES, own), F32),
+            *[shaped((own, piece_cols), BF)] * 4,
+        ],
+        name="dense_sum",
+    )(*pieces)
+    pieces = [pieces[0]] + [turn(pieces[s], 4 - s) for s in (1, 2, 3)]
+    grad_out_mine, grad_small = call(
+        last_sum_kernel,
+        (1,),
+        [whole(own, piece_cols)] * 4,
+        [whole(own, width), whole(LANES, own)],
+        [shaped((own, width), F32), shaped((LANES, own), F32)],
+        name="last_sum",
+    )(*pieces)
+    grad_table = grad_late[experts + 2 : experts + 2 + heads, 0:table_rows].T
+    grad_router = grad_small[0:experts].T
+    grad_gain_two = grad_small[experts]
+    grad_gain_one = grad_small[experts + 1]
+
+    hidden_share = after(hidden_share, grad_qkv)
     share_block = pl.BlockSpec((share, BQ), lambda i, *_: (0, i))
     out_share = call(
         out_kernel,
         (blocks,),
-        [share_block, share_block, pl.BlockSpec((1, BQ), lambda i: (0, i))],
+        [*[share_block] * 5, pl.BlockSpec((1, BQ), lambda i: (0, i))],
         share_block,
         shaped((share, rows), BF),
         name="layer_output",
-    )(eo_mine, hidden_share, gate_row)
+    )(*eo_mine, hidden_share, gate_row)
     return (
         out_share.T,
         grad_tokens.T,
-        grad_dense[:, 0:qkv_cols].reshape(own, 3, width),
+        grad_qkv.transpose(1, 0, 2),
         grad_out_mine,
         grad_table,
         grad_gain_one,
         grad_gain_two,
         grad_router,
-        grad_in_mine[None],
-        grad_down_mine[None],
+        grad_experts[None, :, 0:ff].astype(F32),
+        grad_experts[None, :, ff:].astype(F32),
     )
 
 

time: 361 us -> 321 us (0.89)
  starting transfers between devices: 74.4 us -> 52.2 us
  other arithmetic: 25.2 us -> 5.83 us
  waiting for transfers between devices: 69.2 us -> 79.5 us
  local copies, waits for them, and re-layouts: 24.9 us -> 15.8 us
    ppermute x21 -> x9, starting transfers between devices: 24.5 us -> 10.9 us  [xor_step(): lax.ppermute(x, axis, [(i, i ^ s) for i in range(lax.axis_size(axis))])]
    ppermute x21 -> x9, waiting for transfers between devices: 10.2 us -> 23.3 us  [xor_step(): lax.ppermute(x, axis, [(i, i ^ s) for i in range(lax.axis_size(axis))])]
    ppermute x18, waiting for transfers between devices: 57.3 us -> 48.5 us  [turn(): return lax.ppermute(x, 'tp', [(i, (i + s) % 4) for i in range(4)])]
    ppermute x18, starting transfers between devices: 49.6 us -> 41.1 us  [turn(): return lax.ppermute(x, 'tp', [(i, (i + s) % 4) for i in range(4)])]
    add x8 -> x0, other arithmetic: 6.38 us -> none  [the longest x1 2.99 us: shards(): both_down = keep_down + got_down]
    broadcast_in_dim x2 -> x0, other arithmetic: 5.44 us -> none  [the longest x1 2.73 us: shards(): grad_in_mine[None]]
    slice x12 -> x0, local copies, waits for them, and re-layouts: 5.41 us -> none  [the longest x2 2.96 us: shards(): pieces = [both[s * half:(s + 1) * half] for s in range(4)]]
    reduce_scatter x1, waiting for transfers between devices: 0.01 us -> 5.38 us  [shards(): lax.psum_scatter(after(grad_experts, back_got), dense, scatter_dimension=...]
  transfers between devices with their start and end apart: 44 -> 31, of which waited for: 13 -> 19; matrix products, arithmetic and copies ran while one was open for 13% -> 4% of each run, Pallas kernels for 29% -> 41%
where the time goes in v3:
time: 321 us; the launch traced here: 322 us
  Pallas kernels  154 us (48%)
  waiting for transfers between devices  79.5 us (25%)
  starting transfers between devices  52.2 us (16%)
  local copies, waits for them, and re-layouts  15.8 us (5%)
  between operations  14 us (4%)
  other arithmetic  5.83 us (2%)
    ppermute x18, waiting for transfers between devices, turn(): return lax.ppermute(x, 'tp', [(i, (i + s) % 4) for i in range(4)])  48.5 us
    ppermute x18, starting transfers between devices, turn(): return lax.ppermute(x, 'tp', [(i, (i + s) % 4) for i in range(4)])  41.1 us
    pallas_call x1, Pallas kernels, attention_bwd(): pl.pallas_call(partial(bwd_kernel, heads), grid_spec=pltpu.PrefetchScalar...  26.2 us
    ppermute x9, waiting for transfers between devices, xor_step(): lax.ppermute(x, axis, [(i, i ^ s) for i in range(lax.axis_size(axis))])  23.3 us
    pallas_call x1, Pallas kernels, attention_fwd(): pl.pallas_call(partial(fwd_kernel, heads), grid_spec=pltpu.PrefetchScalar...  22.8 us
    pallas_call x1, Pallas kernels, shards(): call(expert_kernel, (tiles,), [whole(1, rows), whole(rows, model), sorted...  21.9 us
    pallas_call x1, Pallas kernels, shards(): call(partial(qkv_back_kernel, first_col, experts, heads), (blocks,), [pl....  13.4 us
    pallas_call x1, Pallas kernels, shards(): call(weight_grad_kernel, (tiles,), [sorted_spec(model), sorted_spec(ff),...  12.8 us
  transfers between devices with their start and end apart: 31, of which 19 were waited for; matrix products, arithmetic and copies ran while one was open for 4% of the time, Pallas kernels for 41%

profile of v3, /device:TPU:0, one launch (start us, length us, event | category | flops | bytes accessed | tf_op | source)
XLA Modules:
  0.0 321.7 jit_solution(2199337474030199541)
XLA Ops:
  7.2 4.1 %collective-permute-start.1 = (bf16[96,192]{1,0:T(8,128)(2,1)}, bf16[96,192]{1,0:T(8,128)(2,1)S(1)}, u32[]{:S(2)}, u32[]{:S(2)}) collective-permute-start(bf16[96,192]{1,0:T(8,128)(2,1)} %o0.1), channel_id=1, source_target_pairs={{0,2},{1,3},{2,0},{3,1},{4,6},{5,7},{6,4},{7,5},{8,10},{9,11},{10,... | collective-permute-start | bytes 110600 | tf_op jit(solution)/shard_map/ppermute | solution.py:772
  11.3 1.6 collective-permute-start
  12.9 2.2 collective-permute-start.2
  15.2 2.4 collective-permute-done.o1
  18.4 1.9 pack_small.1
  20.2 2.4 collective-permute-start.5
  23.7 1.3 dynamic-slice_bitcast_fusion
  25.1 1.1 pad_maximum_fusion
  26.8 4.2 %plan.1 = (s32[1,1024]{1,0:T(1,128)}, s32[1,128]{1,0:T(1,128)}, f32[1,1024]{1,0:T(1,128)}, f32[1,2048]{1,0:T(1,128)}, s32[1,128]{1,0:T(1,128)}, /*index=5*/f32[3...) custom-call(s32[12]{0:T(128)} %stack.66.at, s32[1,1024]{1,0:T(1,128)} %bitcast.58, ...), custom_call_target="tpu_custom_call" | custom-call | flops 10000000 | bytes 100000 | tf_op jit(solution)/shard_map/plan/pallas_call | solution.py:863
  31.3 3.4 %collective-permute-done.4 = bf16[96,1536]{1,0:T(8,128)(2,1)S(1)} collective-permute-done((bf16[96,1536]{1,0:T(8,128)(2,1)}, bf16[96,1536]{1,0:T(8,128)(2,1)S(1)}, u32[]{:S(2)}, u32[]{:S(2)}) %collective-permute-start.4) | collective-permute-done | bytes 294944 | tf_op jit(solution)/shard_map/ppermute | solution.py:768
  35.4 1.2 pad_maximum_fusion.1.refs_0_
  36.7 2.8 collective-permute-done.6.refs_1_
  39.6 1.0 copy-done.8
  40.7 1.1 copy-done.4
  41.7 10.7 %norm_qkv.1 = (bf16[2048,576]{1,0:T(8,128)(2,1)}, bf16[2048,768]{1,0:T(8,128)(2,1)}, f32[1,2048]{1,0:T(1,128)}, bf16[768,1536]{1,0:T(8,128)(2,1)}, f32[8,768]{1,0:T(8,128)}) custom-call(s32[12]{0:T(128)} %stack.66.at, bf16[1024,768]{1,0:T(8,128)(2,1)} %tok_ref.1, bf16[1024,768]{1,0:T(8,128)(2,1)} %copy-done.4, bf16[4,96,1536]{2,1,0:T(8,128)(2,1)} %copy-done, ...), custom_call_target="tpu_custom_call" | custom-call | flops 10000000 | bytes 100000 | tf_op jit(solution)/shard_map/norm_qkv/pallas_call | solution.py:904
  52.4 22.8 %attention_fwd.1 = (f32[192,1024]{1,0:T(8,128)}, bf16[192,1024]{1,0:T(8,128)(2,1)}, f32[3,1024]{1,0:T(4,128)}) custom-call(s32[1,128]{1,0:T(1,128)} %get-tuple-element.111.info, f32[3,32]{1,0:T(4,128)} %bitcast.51, bf16[2048,576]{1,0:T(8,128)(2,1)} %get-tuple-element.121.qkv_all, f32[1,2048]{1,0:T(1,128)} %get-tuple-element.122.dcol.drow, ...), custom_call_target="tpu_custom_call" | custom-call | flops 10000000 | bytes 100000 | tf_op jit(solution)/shard_map/attention_fwd/pallas_call | solution.py:189
  75.3 3.5 %collective-permute-start.10 = (bf16[192,1024]{1,0:T(8,128)(2,1)}, bf16[192,1024]{1,0:T(8,128)(2,1)S(1)}, u32[]{:S(2)}, u32[]{:S(2)}) collective-permute-start(bf16[192,1024]{1,0:T(8,128)(2,1)} %get-tuple-element.130.refs_1_.refs_10_), channel_id=1, source_target_pairs={{0,3},{1,0},{2,1},{3,2},{4,7},{5,4},{6,5},{7,6},{8,11},{9,8},{10,9... | collective-permute-start | bytes 1179656 | tf_op jit(solution)/shard_map/ppermute | solution.py:772
  79.4 7.5 %sort_cotangents.1.cot_ref = bf16[1792,768]{1,0:T(8,128)(2,1)} custom-call(s32[1,128]{1,0:T(1,128)} %get-tuple-element.126.owner, s32[1,1024]{1,0:T(1,128)} %get-tuple-element.127.pos_row, bf16[1024,768]{1,0:T(8,128)(2,1)} %refs_5_.1), custom_call_target="tpu_custom_call" | custom-call | flops 10000000 | bytes 100000 | tf_op jit(solution)/shard_map/sort_cotangents/pallas_call | solution.py:933
  86.9 2.0 collective-permute-done.10.refs_4_.refs_13_
  88.8 22.6 %collective-permute-done.9.refs_3_.refs_12_ = bf16[192,1024]{1,0:T(8,128)(2,1)S(1)} collective-permute-done((bf16[192,1024]{1,0:T(8,128)(2,1)}, bf16[192,1024]{1,0:T(8,128)(2,1)S(1)}, u32[]{:S(2)}, u32[]{:S(2)}) %collective-permute-start.9) | collective-permute-done | bytes 393248 | tf_op jit(solution)/shard_map/ppermute | solution.py:772
  111.4 0.7 copy-done.2
  112.3 8.7 %hidden_router.1 = (f32[1024,768]{1,0:T(8,128)}, bf16[1024,768]{1,0:T(8,128)(2,1)}, f32[1,1024]{1,0:T(1,128)}, f32[192,1024]{1,0:T(8,128)}) custom-call(s32[12]{0:T(128)} %stack.66.at, bf16[1024,768]{1,0:T(8,128)(2,1)} %tok_ref.1, bf16[192,1024]{1,0:T(8,128)(2,1)} %get-tuple-element.130.refs_1_.refs_10_, bf16[192,1024]{1,0:T(8,128)(2,1)} %copy-done.3, ...), custom_call_target="tpu_custom_call" | custom-call | flops 10000000 | bytes 100000 | tf_op jit(solution)/shard_map/hidden_router/pallas_call | solution.py:946
  120.9 21.9 %experts.1 = (bf16[272,768]{1,0:T(8,128)(2,1)}, bf16[272,768]{1,0:T(8,128)(2,1)}, bf16[272,768]{1,0:T(8,128)(2,1)}, bf16[272,768]{1,0:T(8,128)(2,1)}, bf16[1792,...) custom-call(s32[1,128]{1,0:T(1,128)} %get-tuple-element.126.owner, ...), custom_call_target="tpu_custom_call" | custom-call | flops 10000000 | bytes 100000 | tf_op jit(solution)/shard_map/experts/pallas_call | solution.py:973
  142.8 2.2 collective-permute-start.11
  145.0 1.9 collective-permute-start.12
  146.9 2.8 collective-permute-start.13
  149.8 12.8 %expert_weight_grads.1 = bf16[3072,1536]{1,0:T(8,128)(2,1)} custom-call(s32[1,128]{1,0:T(1,128)} %get-tuple-element.126.owner, bf16[1792,768]{1,0:T(8,128)(2,1)} %get-tuple-element.146.x_ref, bf16[1792,768]{1,0:T(8,128)(2,1)} %get-tuple-element.147.di_ref, bf16[1792,768]{1,0:T(8,128)(2,1)} %get-tuple-element.148.de_ref, ...), custom_call_target="tpu_custom_call" | custom-call | flops 10000000 | bytes 100000 | tf_op jit(solution)/shard_map/expert_weight_grads/pallas_call | solution.py:1008
  162.6 11.1 %collective-permute-done.12.refs_2_ = bf16[272,768]{1,0:T(8,128)(2,1)S(1)} collective-permute-done((bf16[272,768]{1,0:T(8,128)(2,1)}, bf16[272,768]{1,0:T(8,128)(2,1)S(1)}, u32[]{:S(2)}, u32[]{:S(2)}) %collective-permute-start.12) | collective-permute-done | bytes 417824 | tf_op jit(solution)/shard_map/ppermute | solution.py:772
  173.8 0.7 copy-done.11
  174.7 7.2 %unsort_outputs.1 = (bf16[192,1024]{1,0:T(8,128)(2,1)}, bf16[192,1024]{1,0:T(8,128)(2,1)}, bf16[192,1024]{1,0:T(8,128)(2,1)}, bf16[192,1024]{1,0:T(8,128)(2,1)}) custom-call(s32[1,128]{1,0:T(1,128)} %get-tuple-element.126.owner, s32[12]{0:T(128)} %stack.66.at, s32[1,1024]{1,0:T(1,128)} %get-tuple-element.127.pos_row, ...), custom_call_target="tpu_custom_call" | custom-call | flops 10000000 | bytes 100000 | tf_op jit(solution)/shard_map/unsort_outputs/pallas_call | solution.py:1018
  181.8 6.8 %hidden_back.1 = (bf16[192,256]{1,0:T(8,128)(2,1)}, bf16[192,256]{1,0:T(8,128)(2,1)}, bf16[192,256]{1,0:T(8,128)(2,1)}, bf16[192,256]{1,0:T(8,128)(2,1)}, f32[25...) custom-call(s32[12]{0:T(128)} %stack.66.at, bf16[272,768]{1,0:T(8,128)(2,1)} %get-tuple-element.155.refs_0_, ...), custom_call_target="tpu_custom_call" | custom-call | flops 10000000 | bytes 100000 | tf_op jit(solution)/shard_map/hidden_back/pallas_call | solution.py:1036
  188.6 10.0 %collective-permute-start.14 = (bf16[192,256]{1,0:T(8,128)(2,1)}, bf16[192,256]{1,0:T(8,128)(2,1)S(1)}, u32[]{:S(2)}, u32[]{:S(2)}) collective-permute-start(bf16[192,256]{1,0:T(8,128)(2,1)} %get-tuple-element.161), channel_id=1, source_target_pairs={{0,1},{1,2},{2,3},{3,0},{4,5},{5,6},{6,7},{7,4},{8,9},{9,10},{10,1... | collective-permute-start | bytes 294920 | tf_op jit(solution)/shard_map/ppermute | solution.py:772
  198.6 2.8 collective-permute-start.15
  201.5 3.3 %collective-permute-done.14.m1 = bf16[192,256]{1,0:T(8,128)(2,1)S(1)} collective-permute-done((bf16[192,256]{1,0:T(8,128)(2,1)}, bf16[192,256]{1,0:T(8,128)(2,1)S(1)}, u32[]{:S(2)}, u32[]{:S(2)}) %collective-permute-start.14) | collective-permute-done | bytes 98336 | tf_op jit(solution)/shard_map/ppermute | solution.py:772
  204.7 2.5 collective-permute-done.15.m2
  207.4 2.4 collective-permute-start.17
  209.9 1.3 collective-permute-start.18
  211.1 1.1 collective-permute-start.19
  212.3 26.2 %attention_bwd.1 = (bf16[192,1024]{1,0:T(8,128)(2,1)}, bf16[2048,384]{1,0:T(8,128)(2,1)}, f32[16,512]{1,0:T(8,128)}, f32[8,256]{1,0:T(8,128)}) custom-call(s32[1,128]{1,0:T(1,128)} %get-tuple-element.111.info, f32[3,32]{1,0:T(4,128)} %bitcast.52, bf16[2048,576]{1,0:T(8,128)(2,1)} %get-tuple-element.121.qkv_all, f32[1,2048]{1,0:T(1,128)} %get-tuple-element.122.dcol.drow, ...), custom_call_target="tpu_custom_call" | custom-call | flops 10000000 | bytes 100000 | tf_op jit(solution)/shard_map/attention_bwd/pallas_call | solution.py:333
  238.5 1.6 constant_dynamic-slice_fusion
  240.2 2.3 collective-permute-done.20.got_ref
  242.5 0.9 copy-done.9
  243.4 13.4 %qkv_back.1 = (bf16[768,1024]{1,0:T(8,128)(2,1)}, bf16[384,1536]{1,0:T(8,128)(2,1)}, bf16[384,1536]{1,0:T(8,128)(2,1)}) custom-call(s32[12]{0:T(128)} %stack.66.at, bf16[192,1024]{1,0:T(8,128)(2,1)} %get-tuple-element.182.dq_ref, bf16[2048,384]{1,0:T(8,128)(2,1)} %get-tuple-element.183.dkv_ref, bf16[1024,384]{1,0:T(8,128)(2,1)} %copy-done.9, ...), custom_call_target="tpu_custom_call" | custom-call | flops 10000000 | bytes 100000 | tf_op jit(solution)/shard_map/qkv_back/pallas_call | solution.py:1070
  256.9 5.4 %reduce-scatter.3.cloned.1.call-done = bf16[384,1536]{1,0:T(8,128)(2,1)} async-done(((bf16[3072,1536]{1,0:T(8,128)(2,1)}), bf16[384,1536]{1,0:T(8,128)(2,1)}) %reduce-scatter.3.cloned.1.call-update) | async-done | bytes 1179664 | tf_op jit(solution)/shard_map/reduce_scatter | solution.py:1029
  262.3 2.8 collective-permute-done.21.got_ref
  265.2 1.0 copy-done.7
  266.2 2.7 dense_pair_sum.1
  268.9 1.3 collective-permute-start.22
  270.2 4.4 %collective-permute-start.23 = (bf16[96,1536]{1,0:T(8,128)(2,1)}, bf16[96,1536]{1,0:T(8,128)(2,1)S(1)}, u32[]{:S(2)}, u32[]{:S(2)}) collective-permute-start(bf16[96,1536]{1,0:T(8,128)(2,1)} %get-tuple-element.197), channel_id=1, source_target_pairs={{0,16},{8,24},{16,0},{24,8},{1,17},{9,25},{17,1},{25,9},{2,18},{10... | collective-permute-start | bytes 884744 | tf_op jit(solution)/shard_map/ppermute | solution.py:768
  274.7 1.5 collective-permute-start.24
  276.1 2.5 collective-permute-done.22.refs_1_
  278.7 9.4 %collective-permute-done.23.refs_2_ = bf16[96,1536]{1,0:T(8,128)(2,1)S(1)} collective-permute-done((bf16[96,1536]{1,0:T(8,128)(2,1)}, bf16[96,1536]{1,0:T(8,128)(2,1)S(1)}, u32[]{:S(2)}, u32[]{:S(2)}) %collective-permute-start.23) | collective-permute-done | bytes 294944 | tf_op jit(solution)/shard_map/ppermute | solution.py:768
  288.1 1.8 collective-permute-done.24.refs_3_
  289.9 0.7 copy-done.19
  290.6 2.2 dense_sum.1
  292.8 3.8 %collective-permute-start.25 = (bf16[96,384]{1,0:T(8,128)(2,1)}, bf16[96,384]{1,0:T(8,128)(2,1)S(1)}, u32[]{:S(2)}, u32[]{:S(2)}) collective-permute-start(bf16[96,384]{1,0:T(8,128)(2,1)} %get-tuple-element.205), channel_id=1, source_target_pairs={{0,3},{1,0},{2,1},{3,2},{4,7},{5,4},{6,5},{7,6},{8,11},{9,8},{10,9... | collective-permute-start | bytes 221192 | tf_op jit(solution)/shard_map/ppermute | solution.py:772
  297.3 0.7 slice_bitcast_fusion.1
  298.6 3.7 %layer_output.1 = bf16[192,1024]{1,0:T(8,128)(2,1)} custom-call(bf16[192,1024]{1,0:T(8,128)(2,1)} %get-tuple-element.177.e0, bf16[192,1024]{1,0:T(8,128)(2,1)} %copy-done.13, bf16[192,1024]{1,0:T(8,128)(2,1)} %copy-done.14, bf16[192,1024]{1,0:T(8,128)(2,1)} %copy-done.15, f32[192,1024]{1,0:T(8,128)} %get-tuple-element.200.hidden_ref, ...), custom_call_target="tpu_custom_call" | custom-call | flops 10000000 | bytes 100000 | tf_op jit(solution)/shard_map/layer_output/pallas_call | solution.py:1151
  302.4 4.3 %collective-permute-done.26.p2 = bf16[96,384]{1,0:T(8,128)(2,1)S(1)} collective-permute-done((bf16[96,384]{1,0:T(8,128)(2,1)}, bf16[96,384]{1,0:T(8,128)(2,1)S(1)}, u32[]{:S(2)}, u32[]{:S(2)}) %collective-permute-start.26) | collective-permute-done | bytes 73760 | tf_op jit(solution)/shard_map/ppermute | solution.py:772
  307.4 1.7 last_sum.1
  309.1 1.3 slice_bitcast_fusion.2
  310.4 1.3 slice_bitcast_fusion
  311.6 1.6 bitcast_convert_fusion
  313.2 2.0 convert_bitcast_fusion
  (94 shorter events, 7.0 us)
Async XLA Ops:
  7.2 113.8 %all-gather.2.cloned.1.call-start = ((), (), s32[]{:S(2)}) async-start(), calls=%async_computation.2 | async-start | bytes 10616832 | tf_op jit(solution)/shard_map/all_gather | solution.py:899
  7.2 7.9 %collective-permute-start.1 = (bf16[96,192]{1,0:T(8,128)(2,1)}, bf16[96,192]{1,0:T(8,128)(2,1)S(1)}, u32[]{:S(2)}, u32[]{:S(2)}) collective-permute-start(bf16[96,192]{1,0:T(8,128)(2,1)} %o0.1), channel_id=1, source_target_pairs={{0,2},{1,3},{2,0},{3,1},{4,6},{5,7},{6,4},{7,5},{8,10},{9,11},{10,... | collective-permute-start | bytes 110600 | tf_op jit(solution)/shard_map/ppermute | solution.py:772
  11.3 6.2 %collective-permute-start = (bf16[96,192]{1,0:T(8,128)(2,1)}, bf16[96,192]{1,0:T(8,128)(2,1)S(1)}, u32[]{:S(2)}, u32[]{:S(2)}) collective-permute-start(bf16[96,192]{1,0:T(8,128)(2,1)} %o0.1), channel_id=1, source_target_pairs={{0,1},{1,2},{2,3},{3,0},{4,5},{5,6},{6,7},{7,4},{8,9},{9,10},{10,1... | collective-permute-start | bytes 110600 | tf_op jit(solution)/shard_map/ppermute | solution.py:772
  12.9 4.8 %collective-permute-start.2 = (bf16[96,192]{1,0:T(8,128)(2,1)}, bf16[96,192]{1,0:T(8,128)(2,1)S(1)}, u32[]{:S(2)}, u32[]{:S(2)}) collective-permute-start(bf16[96,192]{1,0:T(8,128)(2,1)} %o0.1), channel_id=1, source_target_pairs={{0,3},{1,0},{2,1},{3,2},{4,7},{5,4},{6,5},{7,6},{8,11},{9,8},{10,9... | collective-permute-start | bytes 110600 | tf_op jit(solution)/shard_map/ppermute | solution.py:772
  15.2 25.4 %collective-permute-start.7 = (bf16[1024,768]{1,0:T(8,128)(2,1)}, bf16[1024,768]{1,0:T(8,128)(2,1)S(1)}, u32[]{:S(2)}, u32[]{:S(2)}) collective-permute-start(bf16[1024,768]{1,0:T(8,128)(2,1)} %tok_ref.1), channel_id=1, source_target_pairs={{0,4},{4,0},{1,5},{5,1},{2,6},{6,2},{3,7},{7,3},{8,12},{12,8},{9,1... | collective-permute-start | bytes 4718600 | tf_op jit(solution)/shard_map/ppermute | solution.py:768
  15.2 2.6 copy-start.26
  17.5 0.6 copy-start.27
  17.7 0.6 copy-start.28
  20.2 11.1 %collective-permute-start.5 = (bf16[96,1536]{1,0:T(8,128)(2,1)}, bf16[96,1536]{1,0:T(8,128)(2,1)S(1)}, u32[]{:S(2)}, u32[]{:S(2)}) collective-permute-start(bf16[96,1536]{1,0:T(8,128)(2,1)} %pack_small.1), channel_id=1, source_target_pairs={{0,24},{8,16},{16,8},{24,0},{1,25},{9,17},{17,9},{25,1},{2,26},{10... | collective-permute-start | bytes 884744 | tf_op jit(solution)/shard_map/ppermute | solution.py:768
  22.7 12.0 %collective-permute-start.4 = (bf16[96,1536]{1,0:T(8,128)(2,1)}, bf16[96,1536]{1,0:T(8,128)(2,1)S(1)}, u32[]{:S(2)}, u32[]{:S(2)}) collective-permute-start(bf16[96,1536]{1,0:T(8,128)(2,1)} %pack_small.1), channel_id=1, source_target_pairs={{0,16},{8,24},{16,0},{24,8},{1,17},{9,25},{17,1},{25,9},{2,18},{10... | collective-permute-start | bytes 884744 | tf_op jit(solution)/shard_map/ppermute | solution.py:768
  23.2 11.7 %collective-permute-start.3 = (bf16[96,1536]{1,0:T(8,128)(2,1)}, bf16[96,1536]{1,0:T(8,128)(2,1)}, u32[]{:S(2)}, u32[]{:S(2)}) collective-permute-start(bf16[96,1536]{1,0:T(8,128)(2,1)} %pack_small.1), channel_id=1, source_target_pairs={{0,8},{8,0},{16,24},{24,16},{1,9},{9,1},{17,25},{25,17},{2,10},{10... | collective-permute-start | bytes 884744 | tf_op jit(solution)/shard_map/ppermute | solution.py:768
  25.0 10.4 %copy-start.5 = (bf16[96,1536]{1,0:T(8,128)(2,1)S(1)}, bf16[96,1536]{1,0:T(8,128)(2,1)}, u32[]{:S(2)}) copy-start(bf16[96,1536]{1,0:T(8,128)(2,1)} %pack_small.1) | copy-start | bytes 884740
  34.7 0.7 copy-start.16
  36.6 4.0 %copy-start = (bf16[4,96,1536]{2,1,0:T(8,128)(2,1)}, bf16[4,96,1536]{2,1,0:T(8,128)(2,1)S(1)}, u32[]{:S(2)}) copy-start(bf16[4,96,1536]{2,1,0:T(8,128)(2,1)S(1)} %pad_maximum_fusion.1.refs_0_) | copy-start | bytes 3538948
  36.6 2.9 collective-permute-start.6
  39.6 1.0 copy-start.8
  40.6 1.1 copy-start.4
  40.6 221.6 %reduce-scatter.3.cloned.1.call-start = ((), (), s32[]{:S(2)}) async-start(), calls=%async_computation.3 | async-start | bytes 10616832 | tf_op jit(solution)/shard_map/reduce_scatter | solution.py:1029
  75.3 13.6 %collective-permute-start.10 = (bf16[192,1024]{1,0:T(8,128)(2,1)}, bf16[192,1024]{1,0:T(8,128)(2,1)S(1)}, u32[]{:S(2)}, u32[]{:S(2)}) collective-permute-start(bf16[192,1024]{1,0:T(8,128)(2,1)} %get-tuple-element.130.refs_1_.refs_10_), channel_id=1, source_target_pairs={{0,3},{1,0},{2,1},{3,2},{4,7},{5,4},{6,5},{7,6},{8,11},{9,8},{10,9... | collective-permute-start | bytes 1179656 | tf_op jit(solution)/shard_map/ppermute | solution.py:772
  78.8 32.6 %collective-permute-start.9 = (bf16[192,1024]{1,0:T(8,128)(2,1)}, bf16[192,1024]{1,0:T(8,128)(2,1)S(1)}, u32[]{:S(2)}, u32[]{:S(2)}) collective-permute-start(bf16[192,1024]{1,0:T(8,128)(2,1)} %get-tuple-element.130.refs_1_.refs_10_), channel_id=1, source_target_pairs={{0,2},{1,3},{2,0},{3,1},{4,6},{5,7},{6,4},{7,5},{8,10},{9,11},{10,... | collective-permute-start | bytes 1179656 | tf_op jit(solution)/shard_map/ppermute | solution.py:772
  78.8 32.6 %collective-permute-start.8 = (bf16[192,1024]{1,0:T(8,128)(2,1)}, bf16[192,1024]{1,0:T(8,128)(2,1)S(1)}, u32[]{:S(2)}, u32[]{:S(2)}) collective-permute-start(bf16[192,1024]{1,0:T(8,128)(2,1)} %get-tuple-element.130.refs_1_.refs_10_), channel_id=1, source_target_pairs={{0,1},{1,2},{2,3},{3,0},{4,5},{5,6},{6,7},{7,4},{8,9},{9,10},{10,1... | collective-permute-start | bytes 1179656 | tf_op jit(solution)/shard_map/ppermute | solution.py:772
  88.8 22.6 %copy-start.1 = (bf16[192,1024]{1,0:T(8,128)(2,1)}, bf16[192,1024]{1,0:T(8,128)(2,1)S(1)}, u32[]{:S(2)}) copy-start(bf16[192,1024]{1,0:T(8,128)(2,1)S(1)} %collective-permute-done.10.refs_4_.refs_13_) | copy-start | bytes 1179652
  111.4 0.7 copy-start.2
  111.4 0.9 copy-start.3
  142.8 19.8 %collective-permute-start.11 = (bf16[272,768]{1,0:T(8,128)(2,1)}, bf16[272,768]{1,0:T(8,128)(2,1)S(1)}, u32[]{:S(2)}, u32[]{:S(2)}) collective-permute-start(bf16[272,768]{1,0:T(8,128)(2,1)} %get-tuple-element.142), channel_id=1, source_target_pairs={{0,1},{1,2},{2,3},{3,0},{4,5},{5,6},{6,7},{7,4},{8,9},{9,10},{10,1... | collective-permute-start | bytes 1253384 | tf_op jit(solution)/shard_map/ppermute | solution.py:772
  145.0 28.7 %collective-permute-start.12 = (bf16[272,768]{1,0:T(8,128)(2,1)}, bf16[272,768]{1,0:T(8,128)(2,1)S(1)}, u32[]{:S(2)}, u32[]{:S(2)}) collective-permute-start(bf16[272,768]{1,0:T(8,128)(2,1)} %get-tuple-element.143), channel_id=1, source_target_pairs={{0,2},{1,3},{2,0},{3,1},{4,6},{5,7},{6,4},{7,5},{8,10},{9,11},{10,... | collective-permute-start | bytes 1253384 | tf_op jit(solution)/shard_map/ppermute | solution.py:772
  146.9 26.8 %collective-permute-start.13 = (bf16[272,768]{1,0:T(8,128)(2,1)}, bf16[272,768]{1,0:T(8,128)(2,1)S(1)}, u32[]{:S(2)}, u32[]{:S(2)}) collective-permute-start(bf16[272,768]{1,0:T(8,128)(2,1)} %get-tuple-element.144), channel_id=1, source_target_pairs={{0,3},{1,0},{2,1},{3,2},{4,7},{5,4},{6,5},{7,6},{8,11},{9,8},{10,9... | collective-permute-start | bytes 1253384 | tf_op jit(solution)/shard_map/ppermute | solution.py:772
  162.6 11.2 %copy-start.10 = (bf16[272,768]{1,0:T(8,128)(2,1)}, bf16[272,768]{1,0:T(8,128)(2,1)S(1)}, u32[]{:S(2)}) copy-start(bf16[272,768]{1,0:T(8,128)(2,1)S(1)} %collective-permute-done.11.refs_1_) | copy-start | bytes 1253380
  173.7 0.8 copy-start.11
  173.7 0.9 copy-start.12
  174.7 138.5 %reduce-scatter.5.cloned.1.call-start = ((), (), s32[]{:S(2)}) async-start(), calls=%async_computation.4 | async-start | bytes 1966080 | tf_op jit(solution)/shard_map/reduce_scatter | solution.py:1107
  181.8 25.6 %copy-start.32 = (bf16[192,1024]{1,0:T(8,128)(2,1)S(1)}, bf16[192,1024]{1,0:T(8,128)(2,1)}, u32[]{:S(2)}) copy-start(bf16[192,1024]{1,0:T(8,128)(2,1)} %get-tuple-element.174) | copy-start | bytes 1179652
  181.8 28.0 %copy-start.31 = (bf16[192,1024]{1,0:T(8,128)(2,1)S(1)}, bf16[192,1024]{1,0:T(8,128)(2,1)}, u32[]{:S(2)}) copy-start(bf16[192,1024]{1,0:T(8,128)(2,1)} %get-tuple-element.175) | copy-start | bytes 1179652
  181.8 29.3 %copy-start.30 = (bf16[192,1024]{1,0:T(8,128)(2,1)S(1)}, bf16[192,1024]{1,0:T(8,128)(2,1)}, u32[]{:S(2)}) copy-start(bf16[192,1024]{1,0:T(8,128)(2,1)} %get-tuple-element.176) | copy-start | bytes 1179652
  188.6 16.1 %collective-permute-start.14 = (bf16[192,256]{1,0:T(8,128)(2,1)}, bf16[192,256]{1,0:T(8,128)(2,1)S(1)}, u32[]{:S(2)}, u32[]{:S(2)}) collective-permute-start(bf16[192,256]{1,0:T(8,128)(2,1)} %get-tuple-element.161), channel_id=1, source_target_pairs={{0,1},{1,2},{2,3},{3,0},{4,5},{5,6},{6,7},{7,4},{8,9},{9,10},{10,1... | collective-permute-start | bytes 294920 | tf_op jit(solution)/shard_map/ppermute | solution.py:772
  198.6 8.6 %collective-permute-start.15 = (bf16[192,256]{1,0:T(8,128)(2,1)}, bf16[192,256]{1,0:T(8,128)(2,1)S(1)}, u32[]{:S(2)}, u32[]{:S(2)}) collective-permute-start(bf16[192,256]{1,0:T(8,128)(2,1)} %get-tuple-element.162), channel_id=1, source_target_pairs={{0,2},{1,3},{2,0},{3,1},{4,6},{5,7},{6,4},{7,5},{8,10},{9,11},{10,... | collective-permute-start | bytes 294920 | tf_op jit(solution)/shard_map/ppermute | solution.py:772
  201.5 6.0 %collective-permute-start.16 = (bf16[192,256]{1,0:T(8,128)(2,1)}, bf16[192,256]{1,0:T(8,128)(2,1)S(1)}, u32[]{:S(2)}, u32[]{:S(2)}) collective-permute-start(bf16[192,256]{1,0:T(8,128)(2,1)} %get-tuple-element.163), channel_id=1, source_target_pairs={{0,3},{1,0},{2,1},{3,2},{4,7},{5,4},{6,5},{7,6},{8,11},{9,8},{10,9... | collective-permute-start | bytes 294920 | tf_op jit(solution)/shard_map/ppermute | solution.py:772
  204.7 7.6 %copy-start.20 = (bf16[192,256]{1,0:T(8,128)(2,1)}, bf16[192,256]{1,0:T(8,128)(2,1)S(1)}, u32[]{:S(2)}) copy-start(bf16[192,256]{1,0:T(8,128)(2,1)S(1)} %collective-permute-done.14.m1) | copy-start | bytes 294916
  207.3 5.0 %copy-start.21 = (bf16[192,256]{1,0:T(8,128)(2,1)}, bf16[192,256]{1,0:T(8,128)(2,1)S(1)}, u32[]{:S(2)}) copy-start(bf16[192,256]{1,0:T(8,128)(2,1)S(1)} %collective-permute-done.15.m2) | copy-start | bytes 294916
  207.4 4.9 %copy-start.22 = (bf16[192,256]{1,0:T(8,128)(2,1)}, bf16[192,256]{1,0:T(8,128)(2,1)S(1)}, u32[]{:S(2)}) copy-start(bf16[192,256]{1,0:T(8,128)(2,1)S(1)} %collective-permute-done.16.m3) | copy-start | bytes 294916
  207.4 31.1 %collective-permute-start.17 = (bf16[192,1024]{1,0:T(8,128)(2,1)S(1)}, bf16[192,1024]{1,0:T(8,128)(2,1)S(1)}, u32[]{:S(2)}, u32[]{:S(2)}) collective-permute-start(bf16[192,1024]{1,0:T(8,128)(2,1)S(1)} %copy-done.32), channel_id=1, source_target_pairs={{0,1},{1,2},{2,3},{3,0},{4,5},{5,6},{6,7},{7,4},{8,9},{9,10},{10,1... | collective-permute-start | bytes 1179656 | tf_op jit(solution)/shard_map/ppermute | solution.py:772
  209.9 28.6 %collective-permute-start.18 = (bf16[192,1024]{1,0:T(8,128)(2,1)S(1)}, bf16[192,1024]{1,0:T(8,128)(2,1)S(1)}, u32[]{:S(2)}, u32[]{:S(2)}) collective-permute-start(bf16[192,1024]{1,0:T(8,128)(2,1)S(1)} %copy-done.31), channel_id=1, source_target_pairs={{0,2},{1,3},{2,0},{3,1},{4,6},{5,7},{6,4},{7,5},{8,10},{9,11},{10,... | collective-permute-start | bytes 1179656 | tf_op jit(solution)/shard_map/ppermute | solution.py:772
  211.1 27.4 %collective-permute-start.19 = (bf16[192,1024]{1,0:T(8,128)(2,1)S(1)}, bf16[192,1024]{1,0:T(8,128)(2,1)S(1)}, u32[]{:S(2)}, u32[]{:S(2)}) collective-permute-start(bf16[192,1024]{1,0:T(8,128)(2,1)S(1)} %copy-done.30), channel_id=1, source_target_pairs={{0,3},{1,0},{2,1},{3,2},{4,7},{5,4},{6,5},{7,6},{8,11},{9,8},{10,9... | collective-permute-start | bytes 1179656 | tf_op jit(solution)/shard_map/ppermute | solution.py:772
  238.5 18.3 %copy-start.13 = (bf16[192,1024]{1,0:T(8,128)(2,1)}, bf16[192,1024]{1,0:T(8,128)(2,1)S(1)}, u32[]{:S(2)}) copy-start(bf16[192,1024]{1,0:T(8,128)(2,1)S(1)} %collective-permute-done.17.e1) | copy-start | bytes 1179652
  238.5 18.3 %copy-start.14 = (bf16[192,1024]{1,0:T(8,128)(2,1)}, bf16[192,1024]{1,0:T(8,128)(2,1)S(1)}, u32[]{:S(2)}) copy-start(bf16[192,1024]{1,0:T(8,128)(2,1)S(1)} %collective-permute-done.18.e2) | copy-start | bytes 1179652
  238.5 18.3 %copy-start.15 = (bf16[192,1024]{1,0:T(8,128)(2,1)}, bf16[192,1024]{1,0:T(8,128)(2,1)S(1)}, u32[]{:S(2)}) copy-start(bf16[192,1024]{1,0:T(8,128)(2,1)S(1)} %collective-permute-done.19.e3) | copy-start | bytes 1179652
  240.2 2.4 collective-permute-start.20
  242.5 0.9 copy-start.9
  256.8 5.4 %copy-start.29 = (bf16[384,1536]{1,0:T(8,128)(2,1)S(1)}, bf16[384,1536]{1,0:T(8,128)(2,1)}, u32[]{:S(2)}) copy-start(bf16[384,1536]{1,0:T(8,128)(2,1)} %get-tuple-element.194) | copy-start | bytes 3538948
  262.3 2.9 collective-permute-start.21
  265.2 1.0 copy-start.7
  268.9 9.8 %collective-permute-start.22 = (bf16[96,1536]{1,0:T(8,128)(2,1)}, bf16[96,1536]{1,0:T(8,128)(2,1)S(1)}, u32[]{:S(2)}, u32[]{:S(2)}) collective-permute-start(bf16[96,1536]{1,0:T(8,128)(2,1)} %get-tuple-element.196), channel_id=1, source_target_pairs={{0,8},{8,0},{16,24},{24,16},{1,9},{9,1},{17,25},{25,17},{2,10},{10... | collective-permute-start | bytes 884744 | tf_op jit(solution)/shard_map/ppermute | solution.py:768
  270.2 17.9 %collective-permute-start.23 = (bf16[96,1536]{1,0:T(8,128)(2,1)}, bf16[96,1536]{1,0:T(8,128)(2,1)S(1)}, u32[]{:S(2)}, u32[]{:S(2)}) collective-permute-start(bf16[96,1536]{1,0:T(8,128)(2,1)} %get-tuple-element.197), channel_id=1, source_target_pairs={{0,16},{8,24},{16,0},{24,8},{1,17},{9,25},{17,1},{25,9},{2,18},{10... | collective-permute-start | bytes 884744 | tf_op jit(solution)/shard_map/ppermute | solution.py:768
  274.7 15.2 %collective-permute-start.24 = (bf16[96,1536]{1,0:T(8,128)(2,1)}, bf16[96,1536]{1,0:T(8,128)(2,1)S(1)}, u32[]{:S(2)}, u32[]{:S(2)}) collective-permute-start(bf16[96,1536]{1,0:T(8,128)(2,1)} %get-tuple-element.198), channel_id=1, source_target_pairs={{0,24},{8,16},{16,8},{24,0},{1,25},{9,17},{17,9},{25,1},{2,26},{10... | collective-permute-start | bytes 884744 | tf_op jit(solution)/shard_map/ppermute | solution.py:768
  278.7 11.2 %copy-start.17 = (bf16[96,1536]{1,0:T(8,128)(2,1)}, bf16[96,1536]{1,0:T(8,128)(2,1)S(1)}, u32[]{:S(2)}) copy-start(bf16[96,1536]{1,0:T(8,128)(2,1)S(1)} %collective-permute-done.22.refs_1_) | copy-start | bytes 884740
  288.1 1.8 copy-start.18
  289.9 0.7 copy-start.19
  292.8 9.5 %collective-permute-start.25 = (bf16[96,384]{1,0:T(8,128)(2,1)}, bf16[96,384]{1,0:T(8,128)(2,1)S(1)}, u32[]{:S(2)}, u32[]{:S(2)}) collective-permute-start(bf16[96,384]{1,0:T(8,128)(2,1)} %get-tuple-element.205), channel_id=1, source_target_pairs={{0,3},{1,0},{2,1},{3,2},{4,7},{5,4},{6,5},{7,6},{8,11},{9,8},{10,9... | collective-permute-start | bytes 221192 | tf_op jit(solution)/shard_map/ppermute | solution.py:772
  296.7 10.0 %collective-permute-start.26 = (bf16[96,384]{1,0:T(8,128)(2,1)}, bf16[96,384]{1,0:T(8,128)(2,1)S(1)}, u32[]{:S(2)}, u32[]{:S(2)}) collective-permute-start(bf16[96,384]{1,0:T(8,128)(2,1)} %get-tuple-element.206), channel_id=1, source_target_pairs={{0,2},{1,3},{2,0},{3,1},{4,6},{5,7},{6,4},{7,5},{8,10},{9,11},{10,... | collective-permute-start | bytes 221192 | tf_op jit(solution)/shard_map/ppermute | solution.py:772
  297.2 9.5 %collective-permute-start.27 = (bf16[96,384]{1,0:T(8,128)(2,1)}, bf16[96,384]{1,0:T(8,128)(2,1)S(1)}, u32[]{:S(2)}, u32[]{:S(2)}) collective-permute-start(bf16[96,384]{1,0:T(8,128)(2,1)} %get-tuple-element.207), channel_id=1, source_target_pairs={{0,1},{1,2},{2,3},{3,0},{4,5},{5,6},{6,7},{7,4},{8,9},{9,10},{10,1... | collective-permute-start | bytes 221192 | tf_op jit(solution)/shard_map/ppermute | solution.py:772
  298.6 13.0 %copy-start.6 = (bf16[384,1536]{1,0:T(8,128)(2,1)S(1)}, bf16[384,1536]{1,0:T(8,128)(2,1)}, u32[]{:S(2)}) copy-start(bf16[384,1536]{1,0:T(8,128)(2,1)} %reduce-scatter.3.cloned.1.call-done) | copy-start | bytes 3538948
  302.4 4.3 %copy-start.23 = (bf16[96,384]{1,0:T(8,128)(2,1)}, bf16[96,384]{1,0:T(8,128)(2,1)S(1)}, u32[]{:S(2)}) copy-start(bf16[96,384]{1,0:T(8,128)(2,1)S(1)} %collective-permute-done.25.p1) | copy-start | bytes 221188
  306.7 0.6 copy-start.24
  306.7 0.7 copy-start.25
Sparse Core Ops, SparseCore 0:
  40.7 59.2 all-gather.1
  173.9 88.3 reduce-scatter.2
  264.5 39.6 reduce-scatter.4

commit v4 on v3

--- a/solution.py
+++ b/solution.py
@@ -25,7 +25,7 @@
 BF = jnp.bfloat16
 
 
-def call(kernel, grid, in_specs, out_specs, out_shape, scratch=(), prefetch=0, vmem=58, name=None):
+def call(kernel, grid, in_specs, out_specs, out_shape, scratch=(), prefetch=0, vmem=58, name=None, aliases={}):
     return pl.pallas_call(
         kernel,
         grid_spec=pltpu.PrefetchScalarGridSpec(
@@ -36,6 +36,7 @@
             scratch_shapes=list(scratch),
         ),
         out_shape=out_shape,
+        input_output_aliases=aliases,
         compiler_params=pltpu.CompilerParams(
             dimension_semantics=("arbitrary",) * len(grid), vmem_limit_bytes=vmem * MIB
         ),
@@ -123,27 +124,33 @@
     return jnp.where(lax.broadcasted_iota(jnp.int32, (16, cols), 0) == 0, 1.0, 0.0).astype(BF)
 
 
-def fwd_kernel(heads, info, far, qkv_all, dcol, drow, band, mixed_ref, low_ref, lse_ref, k_aug, v_t):
+def fwd_kernel(heads, first_block, blocks, info, far, qkv_ref, dcol, drow, band, *refs):
     i = pl.program_id(0)
-    seq = qkv_all.shape[0]
     width = heads * HD
-
-    @pl.when(i == 0)
-    def _():
-        for r in range(seq // BK):
-            rows = pl.ds(r * BK, BK)
-            side = key_side(to_column(dcol[:, r * BK : (r + 1) * BK]), BK).astype(BF)
-            vt = qkv_all[rows, 2 * width : 3 * width].astype(F32).T.astype(BF)
-            for h in range(heads):
-                k = qkv_all[rows, width + h * HD : width + (h + 1) * HD]
-                k_aug[h, rows, :] = jnp.concatenate([k, side], axis=1)
-                v_t[h, 0:HD, rows] = vt[h * HD : (h + 1) * HD, :]
-                v_t[h, HD : HD + 16, rows] = ones_rows(BK)
-
-    qb = info[0, 0] + i
-    lo = info[0, 1 + i]
-    hi = info[0, 1 + pl.num_programs(0) + i]
-    qt = (qkv_all[pl.ds(pl.multiple_of(qb * BQ, BQ), BQ), 0:width].astype(F32) * (HD**-0.5)).T.astype(BF)
+    block = first_block + i
+    qb = info[0, 0] + block
+    lo = info[0, 1 + block]
+    hi = info[0, 1 + blocks + block]
+    if first_block:
+        k_aug, v_t, _, _, mixed_ref, low_ref, lse_ref = refs
+        q = qkv_ref[:, 0:width]
+    else:
+        mixed_ref, low_ref, lse_ref, k_aug, v_t = refs
+        q = qkv_ref[pl.ds(pl.multiple_of(qb * BQ, BQ), BQ), 0:width]
+
+        @pl.when(i == 0)
+        def _():
+            for r in range(qkv_ref.shape[0] // BK):
+                rows = pl.ds(r * BK, BK)
+                side = key_side(to_column(dcol[:, r * BK : (r + 1) * BK]), BK).astype(BF)
+                vt = qkv_ref[rows, 2 * width : 3 * width].astype(F32).T.astype(BF)
+                for h in range(heads):
+                    k = qkv_ref[rows, width + h * HD : width + (h + 1) * HD]
+                    k_aug[h, rows, :] = jnp.concatenate([k, side], axis=1)
+                    v_t[h, 0:HD, rows] = vt[h * HD : (h + 1) * HD, :]
+                    v_t[h, HD : HD + 16, rows] = ones_rows(BK)
+
+    qt = (q.astype(F32) * (HD**-0.5)).T.astype(BF)
     side = query_side(drow[...], BQ, None)
     q_aug = [jnp.concatenate([qt[h * HD : (h + 1) * HD, :], side], axis=0) for h in range(heads)]
 
@@ -180,52 +187,60 @@
         lse_ref[h : h + 1, :] = peak + jnp.log(total)
 
 
-def attention_fwd(info, far, qkv_all, dcol, drow, band, rows):
+def attention_fwd(info, far, qkv_all, docs, band, rows, before=None):
     seq, cols = qkv_all.shape
     width = cols // 3
     heads = width // HD
-    steps = rows // BQ
+    blocks = rows // BQ
+    steps = blocks // 2
+    first = 0 if before is None else steps
     full = lambda shape: pl.BlockSpec(shape, lambda i, info: (0,) * len(shape))
+    kept = [(heads, seq, 2 * HD), (heads, HD + 16, seq)]
+    out_specs = [
+        pl.BlockSpec((width, BQ), lambda i, info: (0, first + i)),
+        pl.BlockSpec((width, BQ), lambda i, info: (0, i)),
+        pl.BlockSpec((heads, BQ), lambda i, info: (0, first + i)),
+    ]
+    out_shape = [
+        jax.ShapeDtypeStruct((width, rows), F32),
+        jax.ShapeDtypeStruct((width, rows // 2), BF),
+        jax.ShapeDtypeStruct((heads, rows), F32),
+    ]
+    in_specs = [
+        pl.BlockSpec(memory_space=pltpu.SMEM),
+        full((seq, cols)) if before is None else pl.BlockSpec((BQ, cols), lambda i, info: (info[0, 0] + first + i, 0)),
+        full((1, seq)),
+        pl.BlockSpec((1, BQ), lambda i, info: (0, info[0, 0] + first + i)),
+        full((heads, 3, BK, BQ)),
+    ]
+    operands = [info, far, qkv_all, docs, docs, band]
+    aliases = {}
+    if before is None:
+        out_specs += [full(s) for s in kept]
+        out_shape += [jax.ShapeDtypeStruct(s, BF) for s in kept]
+    else:
+        mixed, lse, k_aug, v_t = before
+        in_specs += [full(s) for s in kept] + [pl.BlockSpec(memory_space=pl.ANY)] * 2
+        operands += [k_aug, v_t, mixed, lse]
+        aliases = {8: 0, 9: 2}
     return pl.pallas_call(
-        partial(fwd_kernel, heads),
+        partial(fwd_kernel, heads, first, blocks),
         grid_spec=pltpu.PrefetchScalarGridSpec(
-            num_scalar_prefetch=1,
-            grid=(steps,),
-            in_specs=[
-                pl.BlockSpec(memory_space=pltpu.SMEM),
-                full((seq, cols)),
-                full((1, seq)),
-                pl.BlockSpec((1, BQ), lambda i, info: (0, info[0, 0] + i)),
-                full((heads, 3, BK, BQ)),
-            ],
-            out_specs=[
-                pl.BlockSpec((width, BQ), lambda i, info: (0, i)),
-                pl.BlockSpec((width, BQ), lambda i, info: (0, i)),
-                pl.BlockSpec((heads, BQ), lambda i, info: (0, i)),
-            ],
-            scratch_shapes=[
-                pltpu.VMEM((heads, seq, 2 * HD), BF),
-                pltpu.VMEM((heads, HD + 16, seq), BF),
-            ],
+            num_scalar_prefetch=1, grid=(steps,), in_specs=in_specs, out_specs=out_specs
         ),
-        out_shape=[
-            jax.ShapeDtypeStruct((width, rows), F32),
-            jax.ShapeDtypeStruct((width, rows), BF),
-            jax.ShapeDtypeStruct((heads, rows), F32),
-        ],
+        out_shape=out_shape,
+        input_output_aliases=aliases,
         compiler_params=pltpu.CompilerParams(
             dimension_semantics=("arbitrary",), vmem_limit_bytes=58 * 1024 * 1024
         ),
-        cost_estimate=pl.CostEstimate(
-            flops=10**7, bytes_accessed=10**5, transcendentals=0
-        ),
+        cost_estimate=pl.CostEstimate(flops=10**7, bytes_accessed=10**5, transcendentals=0),
         name="attention_fwd",
-    )(info, far, qkv_all, dcol, drow, band)
+    )(*operands)
 
 
 def bwd_kernel(
-    heads, info, far, qkv_all, dcol, drow, band, mixed_ref, lse_ref, m0, m1, m2, m3,
-    dq_ref, dkv_ref, skew_ref, side_ref, k_aug, v_aug, k_t, near_acc, dkv_acc,
+    heads, info, far, qkv_all, dcol, drow, band, mixed_ref, lse_ref, m0, m1, m2, m3, k_aug,
+    dq_ref, dkv_ref, skew_ref, side_ref, v_aug, k_t, near_acc, dkv_acc,
 ):
     i = pl.program_id(0)
     seq = qkv_all.shape[0]
@@ -238,14 +253,11 @@
         side_ref[...] = jnp.zeros_like(side_ref)
         for r in range(seq // BK):
             rows = pl.ds(r * BK, BK)
-            side = key_side(to_column(dcol[:, r * BK : (r + 1) * BK]), BK).astype(BF)
             lane = lax.broadcasted_iota(jnp.int32, (BK, HD), 1)
             ones = jnp.where(lane < 3, 1.0, 0.0).astype(BF)
             kt = qkv_all[rows, width : 2 * width].astype(F32).T.astype(BF)
             for h in range(heads):
-                k = qkv_all[rows, width + h * HD : width + (h + 1) * HD]
                 v = qkv_all[rows, 2 * width + h * HD : 2 * width + (h + 1) * HD]
-                k_aug[h, rows, :] = jnp.concatenate([k, side], axis=1)
                 v_aug[h, rows, :] = jnp.concatenate([v, ones], axis=1)
                 k_t[h, 0:HD, rows] = kt[h * HD : (h + 1) * HD, :]
                 k_t[h, HD : HD + 16, rows] = ones_rows(BK)
@@ -323,7 +335,7 @@
             dkv_ref[rows, :] = jnp.concatenate(dk + dv, axis=1).astype(BF)
 
 
-def attention_bwd(info, far, qkv_all, dcol, drow, band, mixed, lse, dmix, rows):
+def attention_bwd(info, far, qkv_all, dcol, drow, band, mixed, lse, dmix, k_aug, rows):
     seq, cols = qkv_all.shape
     width = cols // 3
     heads = width // HD
@@ -344,6 +356,7 @@
                 pl.BlockSpec((width, BQ), lambda i, info: (0, block(i, info))),
                 pl.BlockSpec((heads, BQ), lambda i, info: (0, block(i, info))),
                 *[full((width, BQ))] * 4,
+                full((heads, seq, 2 * HD)),
             ],
             out_specs=[
                 pl.BlockSpec((width, BQ), lambda i, info: (0, block(i, info))),
@@ -352,7 +365,6 @@
                 full((8, BQ)),
             ],
             scratch_shapes=[
-                pltpu.VMEM((heads, seq, 2 * HD), BF),
                 pltpu.VMEM((heads, seq, 2 * HD), BF),
                 pltpu.VMEM((heads, HD + 16, seq), BF),
                 pltpu.VMEM((heads, 3, BK, BQ), F32),
@@ -372,7 +384,7 @@
             flops=10**7, bytes_accessed=10**5, transcendentals=0
         ),
         name="attention_bwd",
-    )(info, far, qkv_all, dcol, drow, band, mixed, lse, *dmix)
+    )(info, far, qkv_all, dcol, drow, band, mixed, lse, *dmix, k_aug)
 
 
 def plan_kernel(
@@ -448,12 +460,12 @@
     spread_ref[...] = jnp.where(down == target[0:1, :].astype(F32), 1.0, 0.0).astype(BF)
 
 
-def pack_kernel(o0, o1, o2, o3, qkv_ref, router_ref, one_ref, two_ref, out_ref):
+def pack_kernel(qkv_ref, router_ref, one_ref, two_ref, out_ref):
     experts, rows = router_ref.shape
     fill = jnp.zeros((LANES - experts - 2, rows), F32)
     tail = [r[...].astype(F32) for r in (router_ref, one_ref, two_ref)]
     tail = jnp.concatenate([*tail, fill], axis=0).T.astype(BF)
-    parts = [r[...] for r in (o0, o1, o2, o3)] + [qkv_ref[c] for c in range(3)]
+    parts = [qkv_ref[c] for c in range(3)]
     used = sum(p.shape[1] for p in parts)
     gap = out_ref.shape[1] - used - LANES
     if gap:
@@ -500,12 +512,12 @@
     return scale, hat, normed, route, one_hot, gate
 
 
-def hidden_kernel(experts, at, *refs):
+def hidden_kernel(experts, skipped, at, *refs):
     tok_ref, mix_refs, wout_ref = refs[0], refs[1:5], refs[5]
-    gains_ref, small_ref, chosen_ref, hidden_ref, norm_ref, gate_ref, share_ref, turn_s = refs[6:]
-    mixed = jnp.concatenate([r[...] for r in mix_refs], axis=0)
-    both = mixed.astype(F32).T.astype(BF)
-    hidden = tok_ref[...].astype(F32) + dot(both, wout_ref[...], NT)
+    gains_ref, small_ref, chosen_ref = refs[6:9]
+    hidden_ref, norm_ref, gate_ref, share_ref, turn_s = refs[9 + skipped :]
+    mixed = jnp.concatenate([r[...] for r in mix_refs], axis=0).astype(F32).T.astype(BF)
+    hidden = tok_ref[...].astype(F32) + dot(mixed, wout_ref[...], NT)
     parts = router_parts(hidden, gains_ref[1:2, :], small_ref[...], to_column(chosen_ref[...]), experts)
     hidden_ref[...] = hidden
     norm_ref[...] = parts[2]
@@ -513,13 +525,6 @@
     turn_s[...] = hidden.T
     share = share_ref.shape[0]
     share_ref[...] = turn_s[pl.ds(pl.multiple_of(at[0] * share, share), share), :]
-
-
-def sort_kernel(owner, pos_row, rows_ref, out_ref):
-    i = pl.program_id(0)
-    place = lax.broadcasted_iota(jnp.int32, (TILE, pos_row.shape[1]), 0) + i * TILE
-    pick = jnp.where(pos_row[...] == place, 1.0, 0.0).astype(BF)
-    out_ref[...] = dot(pick, rows_ref[...]).astype(BF)
 
 
 def pick_back(pos_col, total):
@@ -559,7 +564,7 @@
         hit = pos_row[...] == place
         pick = jnp.where(hit, 1.0, 0.0).astype(BF)
         x = dot(pick, norm_ref[...]).astype(BF)
-        cot = cot_ref[...].astype(F32)
+        cot = dot(pick, cot_ref[...])
         gate = jnp.sum(jnp.where(hit, gate_ref[...], 0.0), axis=1, keepdims=True)
         d_e = (gate * cot).astype(BF)
         w_in = w_ref[:, 0:ff]
@@ -647,8 +652,8 @@
 
 def hidden_back_kernel(experts, at, *refs):
     back_refs, (hidden_ref, cot_ref, gains_ref, router_ref, chosen_ref) = refs[:4], refs[4:9]
-    wout_ref, mix_refs = refs[9], refs[10:14]
-    dmix_refs, dh_ref, small_ref, gout_ref = refs[14:18], refs[18], refs[19], refs[20]
+    wout_ref, mix_refs = refs[9], refs[10:18]
+    dmix_refs, dh_ref, small_ref, gout_ref = refs[18:22], refs[22], refs[23], refs[24]
     part, model = hidden_ref.shape
     back = sum(r[...].astype(F32) for r in back_refs)
     gain = gains_ref[1:2, :]
@@ -676,10 +681,10 @@
     d_mixed = dot(d_attn, wout_ref[...]).T.astype(BF)
     width = model // 4
     for s in range(4):
-        r = (4 - s) % 4
-        dmix_refs[r][...] = d_mixed[s * width : (s + 1) * width, :]
+        dmix_refs[(4 - s) % 4][...] = d_mixed[s * width : (s + 1) * width, :]
     dh_ref[...] = d_hidden
-    mixed = jnp.concatenate([r[...] for r in mix_refs], axis=0)
+    one, two = (jnp.concatenate([r[...] for r in mix_refs[n : n + 4]], axis=0) for n in (0, 4))
+    mixed = jnp.where(at[0] < 2, one, two)
     gout_ref[...] = dot(d_attn_t, mixed, NT).astype(BF)
 
 
@@ -745,24 +750,29 @@
         out[...] = (keep_ref[rows, :].astype(F32) + got_ref[rows, :].astype(F32)).astype(BF)
 
 
-def dense_sum_kernel(cols, count, *refs):
-    parts, (qkv_ref, late_ref, *outs) = refs[:count], refs[count:]
+def dense_sum_kernel(cols, count, table_at, *refs):
+    parts, (qkv_ref, table_ref, *outs) = refs[:count], refs[count:]
     total = sum(r[...].astype(F32) for r in parts)
     width = qkv_ref.shape[2]
     for c in range(3):
         qkv_ref[c] = total[:, c * width : (c + 1) * width]
     late = total[:, total.shape[1] - LANES :]
-    late_ref[...] = late.T
+    table_rows, heads = table_ref.shape
+    table_ref[...] = late[0:table_rows, table_at : table_at + heads]
     for s, out in enumerate(outs):
         piece = total[:, cols + s * width : cols + (s + 1) * width]
         gap = jnp.zeros((late.shape[0], out.shape[1] - LANES - width), F32)
         out[...] = jnp.concatenate([late, piece, gap], axis=1).astype(BF)
 
 
-def last_sum_kernel(p0, p1, p2, p3, out_ref, late_ref):
+def last_sum_kernel(p0, p1, p2, p3, out_ref, router_ref, two_ref, one_ref):
     total = sum(r[...].astype(F32) for r in (p0, p1, p2, p3))
     out_ref[...] = total[:, LANES : LANES + out_ref.shape[1]]
-    late_ref[...] = total[:, 0:LANES].T
+    late = total[:, 0:LANES].T
+    experts = router_ref.shape[0]
+    router_ref[...] = late[0:experts, :]
+    two_ref[...] = late[experts : experts + 1, :]
+    one_ref[...] = late[experts + 1 : experts + 2, :]
 
 def xor_step(x, axis, s):
     return lax.ppermute(x, axis, [(i, i ^ s) for i in range(lax.axis_size(axis))])
@@ -828,13 +838,12 @@
     at = jnp.stack([jnp.int32(v) for v in (tp_at, ctx_at, ctx_at * blocks, fsdp_at, *starts)])
 
     qkv_cols = 3 * width
-    first_col = model
-    cols = -(-(model + qkv_cols) // LANES) * LANES + LANES
+    first_col = 0
+    cols = -(-qkv_cols // LANES) * LANES + LANES
     small = call(
         pack_kernel,
         (1,),
         [
-            *[whole(own, width)] * 4,
             whole(3, own, width),
             whole(experts, own),
             whole(1, own),
@@ -844,12 +853,13 @@
         shaped((own, cols), BF),
         name="pack_small",
     )(
-        *gather_turns(w_attn_out),
         w_qkv.transpose(1, 0, 2),
         w_router.T,
         gain_attn[None, :],
         gain_ffn[None, :],
     )
+    out_line = jnp.concatenate(gather_turns(after(w_attn_out, small)), axis=1)
+    out_all = lax.all_gather(out_line, dense, axis=0, tiled=True)
     tokens_other = xor_step(tokens, "ctx", 1)
     half = model // ctx_n
     w_half = jnp.concatenate(
@@ -926,57 +936,59 @@
         prefetch=1,
         name="norm_qkv",
     )(at, tokens, tokens_other, *small_parts)
-    mixed, mixed_low, lse = attention_fwd(info, table, qkv_all, docs, docs, band, rows)
-    mixed_turns = gather_turns(mixed_low)
+    mixed, low_one, lse, *kept = attention_fwd(info, table, qkv_all, docs, band, rows)
+    turns_one = gather_turns(low_one)
+    mixed, low_two, lse = attention_fwd(info, table, qkv_all, docs, band, rows, (mixed, lse, *kept))
+    turns_one, low_two = lax.optimization_barrier((turns_one, low_two))
+    turns_two = gather_turns(low_two)
+
+    router_block = pl.BlockSpec((model, LANES), lambda i, at: (0, cols // LANES - 1))
+    out_block = whole(model, model)
+
+    def hidden_half(first, turns, before):
+        anywhere = pl.BlockSpec(memory_space=pl.ANY)
+        return call(
+            partial(hidden_kernel, experts, len(before)),
+            (blocks // 2,),
+            [
+                pl.BlockSpec((BQ, model), lambda i, at: (first + i, 0)),
+                *[pl.BlockSpec((width, BQ), lambda i, at: (0, i))] * 4,
+                out_block,
+                whole(8, model),
+                router_block,
+                pl.BlockSpec((1, BQ), lambda i, at: (0, first + i)),
+                *[anywhere] * len(before),
+            ],
+            [
+                pl.BlockSpec((BQ, model), lambda i, at: (first + i, 0)),
+                pl.BlockSpec((BQ, model), lambda i, at: (first + i, 0)),
+                pl.BlockSpec((1, BQ), lambda i, at: (0, first + i)),
+                pl.BlockSpec((share, BQ), lambda i, at: (0, first + i)),
+            ],
+            [
+                shaped((rows, model), F32),
+                shaped((rows, model), BF),
+                shaped((1, rows), F32),
+                shaped((share, rows), F32),
+            ],
+            scratch=[pltpu.VMEM((model, BQ), F32)],
+            prefetch=1,
+            aliases={10 + n: n for n in range(len(before))},
+            name="hidden_router",
+        )(at, tokens, *turns, out_all, gains, small_all, chosen, *before)
+
+    half_done = hidden_half(0, turns_one, ())
     sorted_rows = tiles * TILE
     sorted_spec = lambda cols: pl.BlockSpec((TILE, cols), lambda i, *_: (i, 0))
-    cot_sorted = call(
-        sort_kernel,
-        (tiles,),
-        [whole(1, rows), whole(rows, model)],
-        sorted_spec(model),
-        shaped((sorted_rows, model), BF),
-        prefetch=1,
-        name="sort_cotangents",
-    )(owner, pos, after(grad_out, mixed_low))
-    mixed_turns, cot_sorted = lax.optimization_barrier((mixed_turns, cot_sorted))
-
-    router_block = pl.BlockSpec((model, LANES), lambda i, at: (0, cols // LANES - 1))
-    out_block = pl.BlockSpec((model, model), lambda i, at: (0, 0))
-    hidden, normed_two, gate_row, hidden_share = call(
-        partial(hidden_kernel, experts),
-        (blocks,),
-        [
-            pl.BlockSpec((BQ, model), lambda i, at: (i, 0)),
-            *[pl.BlockSpec((width, BQ), lambda i, at: (0, i))] * 4,
-            out_block,
-            whole(8, model),
-            router_block,
-            pl.BlockSpec((1, BQ), lambda i, at: (0, i)),
-        ],
-        [
-            pl.BlockSpec((BQ, model), lambda i, at: (i, 0)),
-            pl.BlockSpec((BQ, model), lambda i, at: (i, 0)),
-            pl.BlockSpec((1, BQ), lambda i, at: (0, i)),
-            pl.BlockSpec((share, BQ), lambda i, at: (0, i)),
-        ],
-        [
-            shaped((rows, model), F32),
-            shaped((rows, model), BF),
-            shaped((1, rows), F32),
-            shaped((share, rows), F32),
-        ],
-        scratch=[pltpu.VMEM((model, BQ), F32)],
-        prefetch=1,
-        name="hidden_router",
-    )(at, tokens, *mixed_turns, small_all, gains, small_all, chosen)
+    turns_two, half_done = lax.optimization_barrier((turns_two, half_done))
+    hidden, normed_two, gate_row, hidden_share = hidden_half(blocks // 2, turns_two, half_done)
     *back, eo_sorted, x_sorted, d_expert, active, d_inner = call(
         expert_kernel,
         (tiles,),
         [
             whole(1, rows),
             whole(rows, model),
-            sorted_spec(model),
+            whole(rows, model),
             whole(1, rows),
             pl.BlockSpec((model, 2 * ff), lambda i, owner, at: (owner[0, i], 0)),
         ],
@@ -1002,7 +1014,7 @@
         ],
         prefetch=2,
         name="experts",
-    )(owner, at, pos, normed_two, cot_sorted, gate_row, w_experts)
+    )(owner, at, pos, normed_two, grad_out, gate_row, w_experts)
     back_mine = scatter_turns(back)
     back_got = back_mine[1:]
     grad_experts = call(
@@ -1025,12 +1037,14 @@
         prefetch=2,
         name="unsort_outputs",
     )(owner, at, pos, after(eo_sorted, grad_experts))
+    grad_experts = lax.psum_scatter(after(grad_experts, back_got, eo_out), dense, scatter_dimension=0, tiled=True)
+
     back_mine, eo_out = lax.optimization_barrier((back_mine, eo_out))
-    grad_experts = lax.psum_scatter(after(grad_experts, back_got), dense, scatter_dimension=0, tiled=True)
 
     small_rows = -(-(experts + 1) // 8) * 8
     row_block = pl.BlockSpec((part, model), lambda i, at: (at[0], 0))
-    col_block = pl.BlockSpec((width, part), lambda i, at: (0, at[0]))
+    col_one = pl.BlockSpec((width, part), lambda i, at: (0, jnp.minimum(at[0], 1)))
+    col_two = pl.BlockSpec((width, part), lambda i, at: (0, jnp.maximum(at[0] - 2, 0)))
     piece = whole(width, part)
     grad_rows = [model // 2] * 2 if square else [model]
     outs = call(
@@ -1044,7 +1058,8 @@
             router_block,
             pl.BlockSpec((1, part), lambda i, at: (0, at[0])),
             out_block,
-            *[col_block] * 4,
+            *[col_one] * 4,
+            *[col_two] * 4,
         ],
         [*[piece] * 4, whole(part, model), whole(small_rows, model), whole(model, model)],
         [
@@ -1055,14 +1070,14 @@
         ],
         prefetch=1,
         name="hidden_back",
-    )(at, *back_mine, hidden, grad_out, gains, small_all, chosen, small_all, *mixed_turns)
+    )(at, *back_mine, hidden, grad_out, gains, small_all, chosen, out_all, *turns_one, *turns_two)
     dmix_out, d_hidden, small_grads, grad_out_w = outs[0:4], outs[4], outs[5], outs[6]
     dmix = scatter_turns(dmix_out)
     dmix, eo_out = lax.optimization_barrier((dmix, eo_out))
     eo_mine = scatter_turns(eo_out)
 
     dq_t, dkv, skew, sides = attention_bwd(
-        info, table, qkv_all, docs, docs, band, mixed, lse, dmix, rows
+        info, table, qkv_all, docs, docs, band, mixed, lse, dmix, kept[0], rows
     )
     dkv, eo_mine = lax.optimization_barrier((dkv, eo_mine))
     other = lax.dynamic_slice_in_dim(dkv, (1 - ctx_at) * rows, rows)
@@ -1103,8 +1118,6 @@
         small_grads, skew, sides, diag, spread,
     )
     terms, grad_dense = outs[0], outs[1:]
-    terms, grad_experts = lax.optimization_barrier((terms, grad_experts))
-    grad_tokens = lax.psum_scatter(terms, "tp", scatter_dimension=0, tiled=True).astype(F32)
     dense_cols = late_at + LANES
     piece_cols = -(-(LANES + width) // LANES) * LANES
     if square:
@@ -1117,35 +1130,41 @@
             [shaped((own, dense_cols), BF)] * 4,
             name="dense_pair_sum",
         )(keep, xor_step(send, "ctx", 1))
+        first_pieces = pieces
         pieces = [pieces[0]] + [xor_step(pieces[s], "fsdp", s) for s in (1, 2, 3)]
     else:
+        first_pieces = []
         pieces = [lax.psum_scatter(grad_dense[0], dense, scatter_dimension=0, tiled=True)]
-    grad_qkv, grad_late, *pieces = call(
-        partial(dense_sum_kernel, wide_cols, len(pieces)),
+    terms = after(terms, grad_experts, first_pieces)
+    grad_tokens = lax.psum_scatter(terms, "tp", scatter_dimension=0, tiled=True).astype(F32)
+    grad_qkv, grad_table, *pieces = call(
+        partial(dense_sum_kernel, wide_cols, len(pieces), experts + 2),
         (1,),
         [whole(own, dense_cols)] * len(pieces),
-        [whole(3, own, width), whole(LANES, own), *[whole(own, piece_cols)] * 4],
+        [whole(3, own, width), whole(table_rows, heads), *[whole(own, piece_cols)] * 4],
         [
             shaped((3, own, width), F32),
-            shaped((LANES, own), F32),
+            shaped((table_rows, heads), F32),
             *[shaped((own, piece_cols), BF)] * 4,
         ],
         name="dense_sum",
     )(*pieces)
     pieces = [pieces[0]] + [turn(pieces[s], 4 - s) for s in (1, 2, 3)]
-    grad_out_mine, grad_small = call(
+    grad_in, grad_down = grad_experts[:, 0:ff].astype(F32), grad_experts[:, ff:].astype(F32)
+    pieces, grad_in, grad_down = lax.optimization_barrier((pieces, grad_in, grad_down))
+    grad_out_mine, grad_router, grad_gain_two, grad_gain_one = call(
         last_sum_kernel,
         (1,),
         [whole(own, piece_cols)] * 4,
-        [whole(own, width), whole(LANES, own)],
-        [shaped((own, width), F32), shaped((LANES, own), F32)],
+        [whole(own, width), whole(experts, own), whole(1, own), whole(1, own)],
+        [
+            shaped((own, width), F32),
+            shaped((experts, own), F32),
+            shaped((1, own), F32),
+            shaped((1, own), F32),
+        ],
         name="last_sum",
     )(*pieces)
-    grad_table = grad_late[experts + 2 : experts + 2 + heads, 0:table_rows].T
-    grad_router = grad_small[0:experts].T
-    grad_gain_two = grad_small[experts]
-    grad_gain_one = grad_small[experts + 1]
-
     hidden_share = after(hidden_share, grad_qkv)
     share_block = pl.BlockSpec((share, BQ), lambda i, *_: (0, i))
     out_share = call(
@@ -1162,11 +1181,11 @@
         grad_qkv.transpose(1, 0, 2),
         grad_out_mine,
         grad_table,
-        grad_gain_one,
-        grad_gain_two,
-        grad_router,
-        grad_experts[None, :, 0:ff].astype(F32),
-        grad_experts[None, :, ff:].astype(F32),
+        grad_gain_one.reshape(own),
+        grad_gain_two.reshape(own),
+        grad_router.T,
+        grad_in[None],
+        grad_down[None],
     )
 
 

time: 321 us -> 302 us (0.941)
  waiting for transfers between devices: 79.5 us -> 64.1 us
  local copies, waits for them, and re-layouts: 15.8 us -> 10.6 us
  starting transfers between devices: 52.2 us -> 47.7 us
    ppermute x18 -> x21, waiting for transfers between devices: 48.5 us -> 39 us  [turn(): return lax.ppermute(x, 'tp', [(i, (i + s) % 4) for i in range(4)])]
    pallas_call x6 -> x7, Pallas kernels: 64.9 us -> 69.6 us  [the longest x2 30.2 us: attention_fwd(): pl.pallas_call(partial(fwd_kernel, heads, first, blocks), grid_spec=pltpu...]
    ppermute x9, waiting for transfers between devices: 23.3 us -> 18.9 us  [xor_step(): lax.ppermute(x, axis, [(i, i ^ s) for i in range(lax.axis_size(axis))])]
    ppermute x9, starting transfers between devices: 10.9 us -> 7.42 us  [xor_step(): lax.ppermute(x, axis, [(i, i ^ s) for i in range(lax.axis_size(axis))])]
    unnamed x67 -> x68, local copies, waits for them, and re-layouts: 8.97 us -> 6.96 us
    ppermute x18 -> x21, starting transfers between devices: 41.1 us -> 40.1 us  [turn(): return lax.ppermute(x, 'tp', [(i, (i + s) % 4) for i in range(4)])]
  transfers between devices with their start and end apart: 31 -> 35, of which waited for: 19 -> 16; matrix products, arithmetic and copies ran while one was open for 4% -> 2% of each run, Pallas kernels for 41% -> 44%
where the time goes in v4:
time: 302 us; the launch traced here: 300 us
  Pallas kernels  157 us (52%)
  waiting for transfers between devices  64.1 us (21%)
  starting transfers between devices  47.7 us (16%)
  between operations  14.1 us (5%)
  local copies, waits for them, and re-layouts  10.6 us (4%)
  other arithmetic  6.25 us (2%)
    ppermute x21, starting transfers between devices, turn(): return lax.ppermute(x, 'tp', [(i, (i + s) % 4) for i in range(4)])  40.1 us
    ppermute x21, waiting for transfers between devices, turn(): return lax.ppermute(x, 'tp', [(i, (i + s) % 4) for i in range(4)])  39 us
    pallas_call x2, Pallas kernels, attention_fwd(): pl.pallas_call(partial(fwd_kernel, heads, first, blocks), grid_spec=pltpu...  30.2 us
    pallas_call x1, Pallas kernels, attention_bwd(): pl.pallas_call(partial(bwd_kernel, heads), grid_spec=pltpu.PrefetchScalar...  27.1 us
    pallas_call x1, Pallas kernels, shards(): call(expert_kernel, (tiles,), [whole(1, rows), whole(rows, model), whole(...  23.7 us
    ppermute x9, waiting for transfers between devices, xor_step(): lax.ppermute(x, axis, [(i, i ^ s) for i in range(lax.axis_size(axis))])  18.9 us
    pallas_call x1, Pallas kernels, shards(): call(partial(qkv_back_kernel, first_col, experts, heads), (blocks,), [pl....  12.4 us
    pallas_call x1, Pallas kernels, shards(): call(weight_grad_kernel, (tiles,), [sorted_spec(model), sorted_spec(ff),...  12.3 us
  transfers between devices with their start and end apart: 35, of which 16 were waited for; matrix products, arithmetic and copies ran while one was open for 2% of the time, Pallas kernels for 44%

profile of v4, /device:TPU:0, one launch (start us, length us, event | category | flops | bytes accessed | tf_op | source)
XLA Modules:
  0.0 300.0 jit_solution(4474498320286681297)
XLA Ops:
  7.2 1.7 pack_small.1
  8.9 5.0 %collective-permute-start.13 = (bf16[96,192]{1,0:T(8,128)(2,1)}, bf16[96,192]{1,0:T(8,128)(2,1)S(1)}, u32[]{:S(2)}, u32[]{:S(2)}) collective-permute-start(bf16[96,192]{1,0:T(8,128)(2,1)} %param.15), channel_id=1, source_target_pairs={{0,3},{1,0},{2,1},{3,2},{4,7},{5,4},{6,5},{7,6},{8,11},{9,8},{10,9... | collective-permute-start | bytes 110600 | tf_op jit(solution)/shard_map/ppermute | solution.py:782
  14.0 1.0 collective-permute-start.11
  15.0 1.4 collective-permute-done.13
  16.4 2.8 collective-permute-done.12
  19.2 0.9 collective-permute-done.11
  20.1 1.6 pad_maximum_fusion.2
  21.8 2.5 collective-permute-start.2
  25.4 0.7 stack.66.at
  26.0 4.2 %plan.1 = (s32[1,1024]{1,0:T(1,128)}, s32[1,128]{1,0:T(1,128)}, f32[1,1024]{1,0:T(1,128)}, f32[1,2048]{1,0:T(1,128)}, s32[1,128]{1,0:T(1,128)}, /*index=5*/f32[3...) custom-call(s32[12]{0:T(128)} %stack.66.at, s32[1,1024]{1,0:T(1,128)} %bitcast.53, ...), custom_call_target="tpu_custom_call" | custom-call | flops 10000000 | bytes 100000 | tf_op jit(solution)/shard_map/plan/pallas_call | solution.py:873
  30.3 1.3 dynamic-slice_bitcast_fusion
  31.6 1.1 pad_maximum_fusion
  32.7 1.1 collective-permute-done.1
  34.2 2.0 collective-permute-done.3.refs_1_
  36.3 0.7 copy-done.11
  37.5 9.7 %norm_qkv.1 = (bf16[2048,576]{1,0:T(8,128)(2,1)}, bf16[2048,768]{1,0:T(8,128)(2,1)}, f32[1,2048]{1,0:T(1,128)}, bf16[768,768]{1,0:T(8,128)(2,1)}, f32[8,768]{1,0:T(8,128)}) custom-call(s32[12]{0:T(128)} %stack.66.at, bf16[1024,768]{1,0:T(8,128)(2,1)} %tok_ref.1, bf16[1024,768]{1,0:T(8,128)(2,1)} %copy-done.1, bf16[4,96,768]{2,1,0:T(8,128)(2,1)} %copy-done, ...), custom_call_target="tpu_custom_call" | custom-call | flops 10000000 | bytes 100000 | tf_op jit(solution)/shard_map/norm_qkv/pallas_call | solution.py:914
  47.2 15.0 %attention_fwd.2 = (f32[192,1024]{1,0:T(8,128)}, bf16[192,512]{1,0:T(8,128)(2,1)}, f32[3,1024]{1,0:T(4,128)}, bf16[3,2048,128]{2,1,0:T(8,128)(2,1)}, bf16[3,80,2048]{2,1,0:T(8,128)(2,1)}) custom-call(s32[1,128]{1,0:T(1,128)} %get-tuple-element.135.info, f32[3,32]{1,0:T(4,128)} %bitcast.45, bf16[2048,576]{1,0:T(8,128)(2,1)} %get-tuple-element.145.qkv_ref.qkv_all, ...), custom_call_target="tpu_custom_call" | custom-call | flops 10000000 | bytes 100000 | tf_op jit(solution)/shard_map/attention_fwd/pallas_call | solution.py:226
  62.6 1.9 collective-permute-start.5
  64.5 15.2 %attention_fwd.3 = (f32[192,1024]{1,0:T(8,128)}, bf16[192,512]{1,0:T(8,128)(2,1)}, f32[3,1024]{1,0:T(4,128)}) custom-call(s32[1,128]{1,0:T(1,128)} %get-tuple-element.135.info, f32[3,32]{1,0:T(4,128)} %bitcast.46, bf16[2048,576]{1,0:T(8,128)(2,1)} %get-tuple-element.145.qkv_ref.qkv_all, ...), custom_call_target="tpu_custom_call", output_to_operand_aliasing={{0}: (8, {}), {2}: (9, {})} | custom-call | flops 10000000 | bytes 100000 | tf_op jit(solution)/shard_map/attention_fwd/pallas_call | solution.py:226
  79.8 2.1 collective-permute-start.10
  81.9 1.7 collective-permute-start.9
  83.7 2.0 collective-permute-start.8
  85.7 5.8 %hidden_router.2 = (f32[1024,768]{1,0:T(8,128)}, bf16[1024,768]{1,0:T(8,128)(2,1)}, f32[1,1024]{1,0:T(1,128)}, f32[192,1024]{1,0:T(8,128)}) custom-call(s32[12]{0:T(128)} %stack.66.at, bf16[1024,768]{1,0:T(8,128)(2,1)} %tok_ref.1, bf16[192,512]{1,0:T(8,128)(2,1)} %get-tuple-element.159.refs_1_.refs_10_, bf16[192,512]{1,0:T(8,128)(2,1)} %copy-done.7, ...), custom_call_target="tpu_custom_call" | custom-call | flops 10000000 | bytes 100000 | tf_op jit(solution)/shard_map/hidden_router/pallas_call | solution.py:950
  91.6 10.4 %collective-permute-done.9.refs_3_.refs_16_ = bf16[192,512]{1,0:T(8,128)(2,1)S(1)} collective-permute-done((bf16[192,512]{1,0:T(8,128)(2,1)}, bf16[192,512]{1,0:T(8,128)(2,1)S(1)}, u32[]{:S(2)}, u32[]{:S(2)}) %collective-permute-start.9) | collective-permute-done | bytes 196640 | tf_op jit(solution)/shard_map/ppermute | solution.py:782
  101.9 0.7 copy-done.9
  102.7 5.9 %hidden_router.3 = (f32[1024,768]{1,0:T(8,128)}, bf16[1024,768]{1,0:T(8,128)(2,1)}, f32[1,1024]{1,0:T(1,128)}, f32[192,1024]{1,0:T(8,128)}) custom-call(s32[12]{0:T(128)} %stack.66.at, bf16[1024,768]{1,0:T(8,128)(2,1)} %tok_ref.1, ...), custom_call_target="tpu_custom_call", output_to_operand_aliasing={{0}: (10, {}), {1}: (11, {}), {2}: (12, {}), {3}: (13, {})} | custom-call | flops 10000000 | bytes 100000 | tf_op jit(solution)/shard_map/hidden_router/pallas_call | solution.py:950
  108.6 23.7 %experts.1 = (bf16[272,768]{1,0:T(8,128)(2,1)}, bf16[272,768]{1,0:T(8,128)(2,1)}, bf16[272,768]{1,0:T(8,128)(2,1)}, bf16[272,768]{1,0:T(8,128)(2,1)}, bf16[1792,...) custom-call(s32[1,128]{1,0:T(1,128)} %get-tuple-element.154.owner, ...), custom_call_target="tpu_custom_call" | custom-call | flops 10000000 | bytes 100000 | tf_op jit(solution)/shard_map/experts/pallas_call | solution.py:985
  132.4 1.4 collective-permute-start.15
  133.8 2.5 collective-permute-start.16
  136.2 12.3 %expert_weight_grads.1 = bf16[3072,1536]{1,0:T(8,128)(2,1)} custom-call(s32[1,128]{1,0:T(1,128)} %get-tuple-element.154.owner, bf16[1792,768]{1,0:T(8,128)(2,1)} %get-tuple-element.187.x_ref, bf16[1792,768]{1,0:T(8,128)(2,1)} %get-tuple-element.188.di_ref, bf16[1792,768]{1,0:T(8,128)(2,1)} %get-tuple-element.189.de_ref, ...), custom_call_target="tpu_custom_call" | custom-call | flops 10000000 | bytes 100000 | tf_op jit(solution)/shard_map/expert_weight_grads/pallas_call | solution.py:1020
  148.5 7.1 %unsort_outputs.1 = (bf16[192,1024]{1,0:T(8,128)(2,1)}, bf16[192,1024]{1,0:T(8,128)(2,1)}, bf16[192,1024]{1,0:T(8,128)(2,1)}, bf16[192,1024]{1,0:T(8,128)(2,1)}) custom-call(s32[1,128]{1,0:T(1,128)} %get-tuple-element.154.owner, s32[12]{0:T(128)} %stack.66.at, s32[1,1024]{1,0:T(1,128)} %get-tuple-element.155.pos_row, ...), custom_call_target="tpu_custom_call" | custom-call | flops 10000000 | bytes 100000 | tf_op jit(solution)/shard_map/unsort_outputs/pallas_call | solution.py:1030
  155.7 8.2 %collective-permute-done.15.refs_2_ = bf16[272,768]{1,0:T(8,128)(2,1)S(1)} collective-permute-done((bf16[272,768]{1,0:T(8,128)(2,1)}, bf16[272,768]{1,0:T(8,128)(2,1)S(1)}, u32[]{:S(2)}, u32[]{:S(2)}) %collective-permute-start.15) | collective-permute-done | bytes 417824 | tf_op jit(solution)/shard_map/ppermute | solution.py:782
  163.9 0.7 copy-done.14
  164.8 6.9 %hidden_back.1 = (bf16[192,256]{1,0:T(8,128)(2,1)}, bf16[192,256]{1,0:T(8,128)(2,1)}, bf16[192,256]{1,0:T(8,128)(2,1)}, bf16[192,256]{1,0:T(8,128)(2,1)}, f32[25...) custom-call(s32[12]{0:T(128)} %stack.66.at, bf16[272,768]{1,0:T(8,128)(2,1)} %get-tuple-element.196.refs_0_, ...), custom_call_target="tpu_custom_call" | custom-call | flops 10000000 | bytes 100000 | tf_op jit(solution)/shard_map/hidden_back/pallas_call | solution.py:1050
  171.7 8.4 %collective-permute-start.17 = (bf16[192,256]{1,0:T(8,128)(2,1)}, bf16[192,256]{1,0:T(8,128)(2,1)S(1)}, u32[]{:S(2)}, u32[]{:S(2)}) collective-permute-start(bf16[192,256]{1,0:T(8,128)(2,1)} %get-tuple-element.202), channel_id=1, source_target_pairs={{0,1},{1,2},{2,3},{3,0},{4,5},{5,6},{6,7},{7,4},{8,9},{9,10},{10,1... | collective-permute-start | bytes 294920 | tf_op jit(solution)/shard_map/ppermute | solution.py:782
  180.5 2.0 collective-permute-start.19
  182.5 1.1 collective-permute-done.17.m1
  183.7 4.0 %collective-permute-done.18.m2 = bf16[192,256]{1,0:T(8,128)(2,1)S(1)} collective-permute-done((bf16[192,256]{1,0:T(8,128)(2,1)}, bf16[192,256]{1,0:T(8,128)(2,1)S(1)}, u32[]{:S(2)}, u32[]{:S(2)}) %collective-permute-start.18) | collective-permute-done | bytes 98336 | tf_op jit(solution)/shard_map/ppermute | solution.py:782
  187.7 1.9 collective-permute-start.20
  189.7 2.1 collective-permute-start.21
  192.1 27.1 %attention_bwd.1 = (bf16[192,1024]{1,0:T(8,128)(2,1)}, bf16[2048,384]{1,0:T(8,128)(2,1)}, f32[16,512]{1,0:T(8,128)}, f32[8,256]{1,0:T(8,128)}) custom-call(s32[1,128]{1,0:T(1,128)} %get-tuple-element.135.info, f32[3,32]{1,0:T(4,128)} %bitcast.47, bf16[2048,576]{1,0:T(8,128)(2,1)} %get-tuple-element.145.qkv_ref.qkv_all, ...), custom_call_target="tpu_custom_call" | custom-call | flops 10000000 | bytes 100000 | tf_op jit(solution)/shard_map/attention_bwd/pallas_call | solution.py:345
  219.3 1.6 constant_dynamic-slice_fusion
  221.0 2.3 collective-permute-done.23.got_ref
  223.3 0.9 copy-done.4
  224.2 12.4 %qkv_back.1 = (bf16[768,1024]{1,0:T(8,128)(2,1)}, bf16[384,1536]{1,0:T(8,128)(2,1)}, bf16[384,1536]{1,0:T(8,128)(2,1)}) custom-call(s32[12]{0:T(128)} %stack.66.at, bf16[192,1024]{1,0:T(8,128)(2,1)} %get-tuple-element.223.dq_ref, bf16[2048,384]{1,0:T(8,128)(2,1)} %get-tuple-element.224.dkv_ref, bf16[1024,384]{1,0:T(8,128)(2,1)} %copy-done.4, ...), custom_call_target="tpu_custom_call" | custom-call | flops 10000000 | bytes 100000 | tf_op jit(solution)/shard_map/qkv_back/pallas_call | solution.py:1085
  236.7 3.0 collective-permute-done.24.got_ref
  239.7 1.0 copy-done.3
  240.7 2.7 dense_pair_sum.1
  243.4 3.8 %reduce-scatter.3.cloned.1.call-done = bf16[384,1536]{1,0:T(8,128)(2,1)} async-done(((bf16[3072,1536]{1,0:T(8,128)(2,1)}), bf16[384,1536]{1,0:T(8,128)(2,1)}) %reduce-scatter.3.cloned.1.call-update) | async-done | bytes 1179664 | tf_op jit(solution)/shard_map/reduce_scatter | solution.py:1040
  247.3 1.4 collective-permute-start.25
  248.7 0.7 collective-permute-start.26
  249.4 1.5 collective-permute-start.27
  250.8 6.4 %collective-permute-done.25.refs_1_ = bf16[96,1536]{1,0:T(8,128)(2,1)S(1)} collective-permute-done((bf16[96,1536]{1,0:T(8,128)(2,1)S(1)}, bf16[96,1536]{1,0:T(8,128)(2,1)S(1)}, u32[]{:S(2)}, u32[]{:S(2)}) %collective-permute-start.25) | collective-permute-done | bytes 294944 | tf_op jit(solution)/shard_map/ppermute | solution.py:778
  257.2 6.3 %collective-permute-done.26.refs_2_ = bf16[96,1536]{1,0:T(8,128)(2,1)S(1)} collective-permute-done((bf16[96,1536]{1,0:T(8,128)(2,1)S(1)}, bf16[96,1536]{1,0:T(8,128)(2,1)S(1)}, u32[]{:S(2)}, u32[]{:S(2)}) %collective-permute-start.26) | collective-permute-done | bytes 294944 | tf_op jit(solution)/shard_map/ppermute | solution.py:778
  263.5 0.7 copy-done.20
  264.2 0.7 copy-done.21
  264.9 2.2 dense_sum.1
  267.1 6.0 %collective-permute-start.28 = (bf16[96,384]{1,0:T(8,128)(2,1)}, bf16[96,384]{1,0:T(8,128)(2,1)S(1)}, u32[]{:S(2)}, u32[]{:S(2)}) collective-permute-start(bf16[96,384]{1,0:T(8,128)(2,1)} %get-tuple-element.246), channel_id=1, source_target_pairs={{0,3},{1,0},{2,1},{3,2},{4,7},{5,4},{6,5},{7,6},{8,11},{9,8},{10,9... | collective-permute-start | bytes 221192 | tf_op jit(solution)/shard_map/ppermute | solution.py:782
  273.8 3.6 %layer_output.1 = bf16[192,1024]{1,0:T(8,128)(2,1)} custom-call(bf16[192,1024]{1,0:T(8,128)(2,1)} %get-tuple-element.218.e0, bf16[192,1024]{1,0:T(8,128)(2,1)} %copy-done.16, bf16[192,1024]{1,0:T(8,128)(2,1)} %copy-done.17, bf16[192,1024]{1,0:T(8,128)(2,1)} %copy-done.18, f32[192,1024]{1,0:T(8,128)} %get-tuple-element.241.hidden_ref, ...), custom_call_target="tpu_custom_call" | custom-call | flops 10000000 | bytes 100000 | tf_op jit(solution)/shard_map/layer_output/pallas_call | solution.py:1170
  277.4 1.6 slice_convert_fusion
  279.0 10.2 %collective-permute-done.29.p2 = bf16[96,384]{1,0:T(8,128)(2,1)S(1)} collective-permute-done((bf16[96,384]{1,0:T(8,128)(2,1)}, bf16[96,384]{1,0:T(8,128)(2,1)S(1)}, u32[]{:S(2)}, u32[]{:S(2)}) %collective-permute-start.29) | collective-permute-done | bytes 73760 | tf_op jit(solution)/shard_map/ppermute | solution.py:782
  289.2 0.6 copy-done.26
  289.8 1.7 last_sum.1
  291.5 2.0 convert_bitcast_fusion
  (103 shorter events, 4.7 us)
Async XLA Ops:
  7.2 78.5 %all-gather.3.cloned.1.call-start = ((), (), s32[]{:S(2)}) async-start(), calls=%async_computation.2 | async-start | bytes 1327104 | tf_op jit(solution)/shard_map/all_gather | solution.py:862
  8.9 7.4 %collective-permute-start.13 = (bf16[96,192]{1,0:T(8,128)(2,1)}, bf16[96,192]{1,0:T(8,128)(2,1)S(1)}, u32[]{:S(2)}, u32[]{:S(2)}) collective-permute-start(bf16[96,192]{1,0:T(8,128)(2,1)} %param.15), channel_id=1, source_target_pairs={{0,3},{1,0},{2,1},{3,2},{4,7},{5,4},{6,5},{7,6},{8,11},{9,8},{10,9... | collective-permute-start | bytes 110600 | tf_op jit(solution)/shard_map/ppermute | solution.py:782
  14.0 5.2 %collective-permute-start.12 = (bf16[96,192]{1,0:T(8,128)(2,1)}, bf16[96,192]{1,0:T(8,128)(2,1)S(1)}, u32[]{:S(2)}, u32[]{:S(2)}) collective-permute-start(bf16[96,192]{1,0:T(8,128)(2,1)} %param.15), channel_id=1, source_target_pairs={{0,2},{1,3},{2,0},{3,1},{4,6},{5,7},{6,4},{7,5},{8,10},{9,11},{10,... | collective-permute-start | bytes 110600 | tf_op jit(solution)/shard_map/ppermute | solution.py:782
  14.0 6.1 %collective-permute-start.11 = (bf16[96,192]{1,0:T(8,128)(2,1)}, bf16[96,192]{1,0:T(8,128)(2,1)S(1)}, u32[]{:S(2)}, u32[]{:S(2)}) collective-permute-start(bf16[96,192]{1,0:T(8,128)(2,1)} %param.15), channel_id=1, source_target_pairs={{0,1},{1,2},{2,3},{3,0},{4,5},{5,6},{6,7},{7,4},{8,9},{9,10},{10,1... | collective-permute-start | bytes 110600 | tf_op jit(solution)/shard_map/ppermute | solution.py:782
  21.7 86.9 %all-gather.5.cloned.1.call-start = ((), (), s32[]{:S(2)}) async-start(), calls=%async_computation.3 | async-start | bytes 10616832 | tf_op jit(solution)/shard_map/all_gather | solution.py:909
  21.7 14.5 %collective-permute-start.4 = (bf16[1024,768]{1,0:T(8,128)(2,1)}, bf16[1024,768]{1,0:T(8,128)(2,1)S(1)}, u32[]{:S(2)}, u32[]{:S(2)}) collective-permute-start(bf16[1024,768]{1,0:T(8,128)(2,1)} %tok_ref.1), channel_id=1, source_target_pairs={{0,4},{4,0},{1,5},{5,1},{2,6},{6,2},{3,7},{7,3},{8,12},{12,8},{9,1... | collective-permute-start | bytes 4718600 | tf_op jit(solution)/shard_map/ppermute | solution.py:778
  21.8 10.9 %collective-permute-start.2 = (bf16[96,768]{1,0:T(8,128)(2,1)}, bf16[96,768]{1,0:T(8,128)(2,1)S(1)}, u32[]{:S(2)}, u32[]{:S(2)}) collective-permute-start(bf16[96,768]{1,0:T(8,128)(2,1)} %pack_small.1), channel_id=1, source_target_pairs={{0,24},{8,16},{16,8},{24,0},{1,25},{9,17},{17,9},{25,1},{2,26},{10... | collective-permute-start | bytes 442376 | tf_op jit(solution)/shard_map/ppermute | solution.py:778
  24.3 9.5 %collective-permute-start.1 = (bf16[96,768]{1,0:T(8,128)(2,1)}, bf16[96,768]{1,0:T(8,128)(2,1)S(1)}, u32[]{:S(2)}, u32[]{:S(2)}) collective-permute-start(bf16[96,768]{1,0:T(8,128)(2,1)} %pack_small.1), channel_id=1, source_target_pairs={{0,16},{8,24},{16,0},{24,8},{1,17},{9,25},{17,1},{25,9},{2,18},{10... | collective-permute-start | bytes 442376 | tf_op jit(solution)/shard_map/ppermute | solution.py:778
  24.8 9.2 %collective-permute-start = (bf16[96,768]{1,0:T(8,128)(2,1)}, bf16[96,768]{1,0:T(8,128)(2,1)S(1)}, u32[]{:S(2)}, u32[]{:S(2)}) collective-permute-start(bf16[96,768]{1,0:T(8,128)(2,1)} %pack_small.1), channel_id=1, source_target_pairs={{0,8},{8,0},{16,24},{24,16},{1,9},{9,1},{17,25},{25,17},{2,10},{10... | collective-permute-start | bytes 442376 | tf_op jit(solution)/shard_map/ppermute | solution.py:778
  31.6 2.4 copy-start.12
  34.1 2.2 copy-start
  34.1 2.1 collective-permute-start.3
  36.2 0.8 copy-start.11
  36.2 1.3 copy-start.1
  36.2 211.0 %reduce-scatter.3.cloned.1.call-start = ((), (), s32[]{:S(2)}) async-start(), calls=%async_computation.4 | async-start | bytes 10616832 | tf_op jit(solution)/shard_map/reduce_scatter | solution.py:1040
  62.2 17.5 %collective-permute-start.7 = (bf16[192,512]{1,0:T(8,128)(2,1)}, bf16[192,512]{1,0:T(8,128)(2,1)S(1)}, u32[]{:S(2)}, u32[]{:S(2)}) collective-permute-start(bf16[192,512]{1,0:T(8,128)(2,1)} %get-tuple-element.159.refs_1_.refs_10_), channel_id=1, source_target_pairs={{0,3},{1,0},{2,1},{3,2},{4,7},{5,4},{6,5},{7,6},{8,11},{9,8},{10,9... | collective-permute-start | bytes 589832 | tf_op jit(solution)/shard_map/ppermute | solution.py:782
  62.3 17.5 %collective-permute-start.6 = (bf16[192,512]{1,0:T(8,128)(2,1)}, bf16[192,512]{1,0:T(8,128)(2,1)S(1)}, u32[]{:S(2)}, u32[]{:S(2)}) collective-permute-start(bf16[192,512]{1,0:T(8,128)(2,1)} %get-tuple-element.159.refs_1_.refs_10_), channel_id=1, source_target_pairs={{0,2},{1,3},{2,0},{3,1},{4,6},{5,7},{6,4},{7,5},{8,10},{9,11},{10,... | collective-permute-start | bytes 589832 | tf_op jit(solution)/shard_map/ppermute | solution.py:782
  62.6 17.2 %collective-permute-start.5 = (bf16[192,512]{1,0:T(8,128)(2,1)}, bf16[192,512]{1,0:T(8,128)(2,1)S(1)}, u32[]{:S(2)}, u32[]{:S(2)}) collective-permute-start(bf16[192,512]{1,0:T(8,128)(2,1)} %get-tuple-element.159.refs_1_.refs_10_), channel_id=1, source_target_pairs={{0,1},{1,2},{2,3},{3,0},{4,5},{5,6},{6,7},{7,4},{8,9},{9,10},{10,1... | collective-permute-start | bytes 589832 | tf_op jit(solution)/shard_map/ppermute | solution.py:782
  79.7 6.0 %copy-start.5 = (bf16[192,512]{1,0:T(8,128)(2,1)}, bf16[192,512]{1,0:T(8,128)(2,1)S(1)}, u32[]{:S(2)}) copy-start(bf16[192,512]{1,0:T(8,128)(2,1)S(1)} %collective-permute-done.7.refs_4_.refs_13_) | copy-start | bytes 589828
  79.8 6.0 %copy-start.6 = (bf16[192,512]{1,0:T(8,128)(2,1)}, bf16[192,512]{1,0:T(8,128)(2,1)S(1)}, u32[]{:S(2)}) copy-start(bf16[192,512]{1,0:T(8,128)(2,1)S(1)} %collective-permute-done.6.refs_3_.refs_12_) | copy-start | bytes 589828
  79.8 5.9 %copy-start.7 = (bf16[192,512]{1,0:T(8,128)(2,1)}, bf16[192,512]{1,0:T(8,128)(2,1)S(1)}, u32[]{:S(2)}) copy-start(bf16[192,512]{1,0:T(8,128)(2,1)S(1)} %collective-permute-done.5.refs_2_.refs_11_) | copy-start | bytes 589828
  79.8 11.7 %collective-permute-start.10 = (bf16[192,512]{1,0:T(8,128)(2,1)}, bf16[192,512]{1,0:T(8,128)(2,1)S(1)}, u32[]{:S(2)}, u32[]{:S(2)}) collective-permute-start(bf16[192,512]{1,0:T(8,128)(2,1)} %get-tuple-element.171.refs_1_.refs_14_), channel_id=1, source_target_pairs={{0,3},{1,0},{2,1},{3,2},{4,7},{5,4},{6,5},{7,6},{8,11},{9,8},{10,9... | collective-permute-start | bytes 589832 | tf_op jit(solution)/shard_map/ppermute | solution.py:782
  81.9 20.0 %collective-permute-start.9 = (bf16[192,512]{1,0:T(8,128)(2,1)}, bf16[192,512]{1,0:T(8,128)(2,1)S(1)}, u32[]{:S(2)}, u32[]{:S(2)}) collective-permute-start(bf16[192,512]{1,0:T(8,128)(2,1)} %get-tuple-element.171.refs_1_.refs_14_), channel_id=1, source_target_pairs={{0,2},{1,3},{2,0},{3,1},{4,6},{5,7},{6,4},{7,5},{8,10},{9,11},{10,... | collective-permute-start | bytes 589832 | tf_op jit(solution)/shard_map/ppermute | solution.py:782
  83.7 18.2 %collective-permute-start.8 = (bf16[192,512]{1,0:T(8,128)(2,1)}, bf16[192,512]{1,0:T(8,128)(2,1)S(1)}, u32[]{:S(2)}, u32[]{:S(2)}) collective-permute-start(bf16[192,512]{1,0:T(8,128)(2,1)} %get-tuple-element.171.refs_1_.refs_14_), channel_id=1, source_target_pairs={{0,1},{1,2},{2,3},{3,0},{4,5},{5,6},{6,7},{7,4},{8,9},{9,10},{10,1... | collective-permute-start | bytes 589832 | tf_op jit(solution)/shard_map/ppermute | solution.py:782
  91.5 10.4 %copy-start.8 = (bf16[192,512]{1,0:T(8,128)(2,1)}, bf16[192,512]{1,0:T(8,128)(2,1)S(1)}, u32[]{:S(2)}) copy-start(bf16[192,512]{1,0:T(8,128)(2,1)S(1)} %collective-permute-done.10.refs_4_.refs_17_) | copy-start | bytes 589828
  101.9 0.8 copy-start.10
  132.4 23.3 %collective-permute-start.14 = (bf16[272,768]{1,0:T(8,128)(2,1)}, bf16[272,768]{1,0:T(8,128)(2,1)S(1)}, u32[]{:S(2)}, u32[]{:S(2)}) collective-permute-start(bf16[272,768]{1,0:T(8,128)(2,1)} %get-tuple-element.183), channel_id=1, source_target_pairs={{0,1},{1,2},{2,3},{3,0},{4,5},{5,6},{6,7},{7,4},{8,9},{9,10},{10,1... | collective-permute-start | bytes 1253384 | tf_op jit(solution)/shard_map/ppermute | solution.py:782
  132.4 31.4 %collective-permute-start.15 = (bf16[272,768]{1,0:T(8,128)(2,1)}, bf16[272,768]{1,0:T(8,128)(2,1)S(1)}, u32[]{:S(2)}, u32[]{:S(2)}) collective-permute-start(bf16[272,768]{1,0:T(8,128)(2,1)} %get-tuple-element.184), channel_id=1, source_target_pairs={{0,2},{1,3},{2,0},{3,1},{4,6},{5,7},{6,4},{7,5},{8,10},{9,11},{10,... | collective-permute-start | bytes 1253384 | tf_op jit(solution)/shard_map/ppermute | solution.py:782
  133.8 30.1 %collective-permute-start.16 = (bf16[272,768]{1,0:T(8,128)(2,1)}, bf16[272,768]{1,0:T(8,128)(2,1)S(1)}, u32[]{:S(2)}, u32[]{:S(2)}) collective-permute-start(bf16[272,768]{1,0:T(8,128)(2,1)} %get-tuple-element.185), channel_id=1, source_target_pairs={{0,3},{1,0},{2,1},{3,2},{4,7},{5,4},{6,5},{7,6},{8,11},{9,8},{10,9... | collective-permute-start | bytes 1253384 | tf_op jit(solution)/shard_map/ppermute | solution.py:782
  155.7 8.2 %copy-start.13 = (bf16[272,768]{1,0:T(8,128)(2,1)}, bf16[272,768]{1,0:T(8,128)(2,1)S(1)}, u32[]{:S(2)}) copy-start(bf16[272,768]{1,0:T(8,128)(2,1)S(1)} %collective-permute-done.14.refs_1_) | copy-start | bytes 1253380
  163.9 0.7 copy-start.14
  163.9 0.9 copy-start.15
  164.8 126.8 %reduce-scatter.5.cloned.1.call-start = ((), (), s32[]{:S(2)}) async-start(), calls=%async_computation.5 | async-start | bytes 1966080 | tf_op jit(solution)/shard_map/reduce_scatter | solution.py:1139
  164.8 23.0 %copy-start.30 = (bf16[192,1024]{1,0:T(8,128)(2,1)S(1)}, bf16[192,1024]{1,0:T(8,128)(2,1)}, u32[]{:S(2)}) copy-start(bf16[192,1024]{1,0:T(8,128)(2,1)} %get-tuple-element.215) | copy-start | bytes 1179652
  164.8 24.9 %copy-start.29 = (bf16[192,1024]{1,0:T(8,128)(2,1)S(1)}, bf16[192,1024]{1,0:T(8,128)(2,1)}, u32[]{:S(2)}) copy-start(bf16[192,1024]{1,0:T(8,128)(2,1)} %get-tuple-element.216) | copy-start | bytes 1179652
  164.8 27.0 %copy-start.28 = (bf16[192,1024]{1,0:T(8,128)(2,1)S(1)}, bf16[192,1024]{1,0:T(8,128)(2,1)}, u32[]{:S(2)}) copy-start(bf16[192,1024]{1,0:T(8,128)(2,1)} %get-tuple-element.217) | copy-start | bytes 1179652
  171.7 12.0 %collective-permute-start.17 = (bf16[192,256]{1,0:T(8,128)(2,1)}, bf16[192,256]{1,0:T(8,128)(2,1)S(1)}, u32[]{:S(2)}, u32[]{:S(2)}) collective-permute-start(bf16[192,256]{1,0:T(8,128)(2,1)} %get-tuple-element.202), channel_id=1, source_target_pairs={{0,1},{1,2},{2,3},{3,0},{4,5},{5,6},{6,7},{7,4},{8,9},{9,10},{10,1... | collective-permute-start | bytes 294920 | tf_op jit(solution)/shard_map/ppermute | solution.py:782
  180.1 7.6 %collective-permute-start.18 = (bf16[192,256]{1,0:T(8,128)(2,1)}, bf16[192,256]{1,0:T(8,128)(2,1)S(1)}, u32[]{:S(2)}, u32[]{:S(2)}) collective-permute-start(bf16[192,256]{1,0:T(8,128)(2,1)} %get-tuple-element.203), channel_id=1, source_target_pairs={{0,2},{1,3},{2,0},{3,1},{4,6},{5,7},{6,4},{7,5},{8,10},{9,11},{10,... | collective-permute-start | bytes 294920 | tf_op jit(solution)/shard_map/ppermute | solution.py:782
  180.5 7.2 %collective-permute-start.19 = (bf16[192,256]{1,0:T(8,128)(2,1)}, bf16[192,256]{1,0:T(8,128)(2,1)S(1)}, u32[]{:S(2)}, u32[]{:S(2)}) collective-permute-start(bf16[192,256]{1,0:T(8,128)(2,1)} %get-tuple-element.204), channel_id=1, source_target_pairs={{0,3},{1,0},{2,1},{3,2},{4,7},{5,4},{6,5},{7,6},{8,11},{9,8},{10,9... | collective-permute-start | bytes 294920 | tf_op jit(solution)/shard_map/ppermute | solution.py:782
  183.7 8.4 %copy-start.22 = (bf16[192,256]{1,0:T(8,128)(2,1)}, bf16[192,256]{1,0:T(8,128)(2,1)S(1)}, u32[]{:S(2)}) copy-start(bf16[192,256]{1,0:T(8,128)(2,1)S(1)} %collective-permute-done.17.m1) | copy-start | bytes 294916
  187.7 4.4 %copy-start.23 = (bf16[192,256]{1,0:T(8,128)(2,1)}, bf16[192,256]{1,0:T(8,128)(2,1)S(1)}, u32[]{:S(2)}) copy-start(bf16[192,256]{1,0:T(8,128)(2,1)S(1)} %collective-permute-done.18.m2) | copy-start | bytes 294916
  187.7 4.4 %copy-start.24 = (bf16[192,256]{1,0:T(8,128)(2,1)}, bf16[192,256]{1,0:T(8,128)(2,1)S(1)}, u32[]{:S(2)}) copy-start(bf16[192,256]{1,0:T(8,128)(2,1)S(1)} %collective-permute-done.19.m3) | copy-start | bytes 294916
  187.7 31.5 %collective-permute-start.20 = (bf16[192,1024]{1,0:T(8,128)(2,1)S(1)}, bf16[192,1024]{1,0:T(8,128)(2,1)S(1)}, u32[]{:S(2)}, u32[]{:S(2)}) collective-permute-start(bf16[192,1024]{1,0:T(8,128)(2,1)S(1)} %copy-done.30), channel_id=1, source_target_pairs={{0,1},{1,2},{2,3},{3,0},{4,5},{5,6},{6,7},{7,4},{8,9},{9,10},{10,1... | collective-permute-start | bytes 1179656 | tf_op jit(solution)/shard_map/ppermute | solution.py:782
  189.7 29.6 %collective-permute-start.21 = (bf16[192,1024]{1,0:T(8,128)(2,1)S(1)}, bf16[192,1024]{1,0:T(8,128)(2,1)S(1)}, u32[]{:S(2)}, u32[]{:S(2)}) collective-permute-start(bf16[192,1024]{1,0:T(8,128)(2,1)S(1)} %copy-done.29), channel_id=1, source_target_pairs={{0,2},{1,3},{2,0},{3,1},{4,6},{5,7},{6,4},{7,5},{8,10},{9,11},{10,... | collective-permute-start | bytes 1179656 | tf_op jit(solution)/shard_map/ppermute | solution.py:782
  191.8 27.5 %collective-permute-start.22 = (bf16[192,1024]{1,0:T(8,128)(2,1)S(1)}, bf16[192,1024]{1,0:T(8,128)(2,1)S(1)}, u32[]{:S(2)}, u32[]{:S(2)}) collective-permute-start(bf16[192,1024]{1,0:T(8,128)(2,1)S(1)} %copy-done.28), channel_id=1, source_target_pairs={{0,3},{1,0},{2,1},{3,2},{4,7},{5,4},{6,5},{7,6},{8,11},{9,8},{10,9... | collective-permute-start | bytes 1179656 | tf_op jit(solution)/shard_map/ppermute | solution.py:782
  219.3 17.3 %copy-start.16 = (bf16[192,1024]{1,0:T(8,128)(2,1)}, bf16[192,1024]{1,0:T(8,128)(2,1)S(1)}, u32[]{:S(2)}) copy-start(bf16[192,1024]{1,0:T(8,128)(2,1)S(1)} %collective-permute-done.20.e1) | copy-start | bytes 1179652
  219.3 17.3 %copy-start.17 = (bf16[192,1024]{1,0:T(8,128)(2,1)}, bf16[192,1024]{1,0:T(8,128)(2,1)S(1)}, u32[]{:S(2)}) copy-start(bf16[192,1024]{1,0:T(8,128)(2,1)S(1)} %collective-permute-done.21.e2) | copy-start | bytes 1179652
  219.3 17.2 %copy-start.18 = (bf16[192,1024]{1,0:T(8,128)(2,1)}, bf16[192,1024]{1,0:T(8,128)(2,1)S(1)}, u32[]{:S(2)}) copy-start(bf16[192,1024]{1,0:T(8,128)(2,1)S(1)} %collective-permute-done.22.e3) | copy-start | bytes 1179652
  220.9 2.4 collective-permute-start.23
  223.3 0.9 copy-start.4
  236.6 3.1 %collective-permute-start.24 = (bf16[384,1536]{1,0:T(8,128)(2,1)}, bf16[384,1536]{1,0:T(8,128)(2,1)S(1)}, u32[]{:S(2)}, u32[]{:S(2)}) collective-permute-start(bf16[384,1536]{1,0:T(8,128)(2,1)} %get-tuple-element.235), channel_id=1, source_target_pairs={{0,4},{4,0},{1,5},{5,1},{2,6},{6,2},{3,7},{7,3},{8,12},{12,8},{9,1... | collective-permute-start | bytes 3538952 | tf_op jit(solution)/shard_map/ppermute | solution.py:778
  239.7 1.0 copy-start.3
  243.4 3.8 %copy-start.33 = (bf16[96,1536]{1,0:T(8,128)(2,1)S(1)}, bf16[96,1536]{1,0:T(8,128)(2,1)}, u32[]{:S(2)}) copy-start(bf16[96,1536]{1,0:T(8,128)(2,1)} %get-tuple-element.237) | copy-start | bytes 884740
  243.4 5.3 %copy-start.32 = (bf16[96,1536]{1,0:T(8,128)(2,1)S(1)}, bf16[96,1536]{1,0:T(8,128)(2,1)}, u32[]{:S(2)}) copy-start(bf16[96,1536]{1,0:T(8,128)(2,1)} %get-tuple-element.238) | copy-start | bytes 884740
  243.4 5.9 %copy-start.31 = (bf16[96,1536]{1,0:T(8,128)(2,1)S(1)}, bf16[96,1536]{1,0:T(8,128)(2,1)}, u32[]{:S(2)}) copy-start(bf16[96,1536]{1,0:T(8,128)(2,1)} %get-tuple-element.239) | copy-start | bytes 884740
  247.3 10.0 %collective-permute-start.25 = (bf16[96,1536]{1,0:T(8,128)(2,1)S(1)}, bf16[96,1536]{1,0:T(8,128)(2,1)S(1)}, u32[]{:S(2)}, u32[]{:S(2)}) collective-permute-start(bf16[96,1536]{1,0:T(8,128)(2,1)S(1)} %copy-done.33), channel_id=1, source_target_pairs={{0,8},{8,0},{16,24},{24,16},{1,9},{9,1},{17,25},{25,17},{2,10},{10... | collective-permute-start | bytes 884744 | tf_op jit(solution)/shard_map/ppermute | solution.py:778
  248.7 14.8 %collective-permute-start.26 = (bf16[96,1536]{1,0:T(8,128)(2,1)S(1)}, bf16[96,1536]{1,0:T(8,128)(2,1)S(1)}, u32[]{:S(2)}, u32[]{:S(2)}) collective-permute-start(bf16[96,1536]{1,0:T(8,128)(2,1)S(1)} %copy-done.32), channel_id=1, source_target_pairs={{0,16},{8,24},{16,0},{24,8},{1,17},{9,25},{17,1},{25,9},{2,18},{10... | collective-permute-start | bytes 884744 | tf_op jit(solution)/shard_map/ppermute | solution.py:778
  249.4 14.1 %collective-permute-start.27 = (bf16[96,1536]{1,0:T(8,128)(2,1)S(1)}, bf16[96,1536]{1,0:T(8,128)(2,1)S(1)}, u32[]{:S(2)}, u32[]{:S(2)}) collective-permute-start(bf16[96,1536]{1,0:T(8,128)(2,1)S(1)} %copy-done.31), channel_id=1, source_target_pairs={{0,24},{8,16},{16,8},{24,0},{1,25},{9,17},{17,9},{25,1},{2,26},{10... | collective-permute-start | bytes 884744 | tf_op jit(solution)/shard_map/ppermute | solution.py:778
  257.2 6.3 %copy-start.19 = (bf16[96,1536]{1,0:T(8,128)(2,1)}, bf16[96,1536]{1,0:T(8,128)(2,1)S(1)}, u32[]{:S(2)}) copy-start(bf16[96,1536]{1,0:T(8,128)(2,1)S(1)} %collective-permute-done.25.refs_1_) | copy-start | bytes 884740
  267.1 10.3 %copy-start.2 = (bf16[384,1536]{1,0:T(8,128)(2,1)S(1)}, bf16[384,1536]{1,0:T(8,128)(2,1)}, u32[]{:S(2)}) copy-start(bf16[384,1536]{1,0:T(8,128)(2,1)} %reduce-scatter.3.cloned.1.call-done) | copy-start | bytes 3538948
  267.1 11.8 %collective-permute-start.28 = (bf16[96,384]{1,0:T(8,128)(2,1)}, bf16[96,384]{1,0:T(8,128)(2,1)S(1)}, u32[]{:S(2)}, u32[]{:S(2)}) collective-permute-start(bf16[96,384]{1,0:T(8,128)(2,1)} %get-tuple-element.246), channel_id=1, source_target_pairs={{0,3},{1,0},{2,1},{3,2},{4,7},{5,4},{6,5},{7,6},{8,11},{9,8},{10,9... | collective-permute-start | bytes 221192 | tf_op jit(solution)/shard_map/ppermute | solution.py:782
  273.1 16.1 %collective-permute-start.29 = (bf16[96,384]{1,0:T(8,128)(2,1)}, bf16[96,384]{1,0:T(8,128)(2,1)S(1)}, u32[]{:S(2)}, u32[]{:S(2)}) collective-permute-start(bf16[96,384]{1,0:T(8,128)(2,1)} %get-tuple-element.247), channel_id=1, source_target_pairs={{0,2},{1,3},{2,0},{3,1},{4,6},{5,7},{6,4},{7,5},{8,10},{9,11},{10,... | collective-permute-start | bytes 221192 | tf_op jit(solution)/shard_map/ppermute | solution.py:782
  273.6 15.6 %collective-permute-start.30 = (bf16[96,384]{1,0:T(8,128)(2,1)}, bf16[96,384]{1,0:T(8,128)(2,1)S(1)}, u32[]{:S(2)}, u32[]{:S(2)}) collective-permute-start(bf16[96,384]{1,0:T(8,128)(2,1)} %get-tuple-element.248), channel_id=1, source_target_pairs={{0,1},{1,2},{2,3},{3,0},{4,5},{5,6},{6,7},{7,4},{8,9},{9,10},{10,1... | collective-permute-start | bytes 221192 | tf_op jit(solution)/shard_map/ppermute | solution.py:782
  279.0 10.2 %copy-start.25 = (bf16[96,384]{1,0:T(8,128)(2,1)}, bf16[96,384]{1,0:T(8,128)(2,1)S(1)}, u32[]{:S(2)}) copy-start(bf16[96,384]{1,0:T(8,128)(2,1)S(1)} %collective-permute-done.28.p1) | copy-start | bytes 221188
  (5 other events, 3.4 us)
Sparse Core Ops, SparseCore 0:
  21.8 22.9 all-gather.2
  47.2 58.8 all-gather.4
  164.0 83.1 reduce-scatter.2
  249.4 40.0 reduce-scatter.4

commit v5 on v4

--- a/solution.py
+++ b/solution.py
@@ -652,8 +652,8 @@
 
 def hidden_back_kernel(experts, at, *refs):
     back_refs, (hidden_ref, cot_ref, gains_ref, router_ref, chosen_ref) = refs[:4], refs[4:9]
-    wout_ref, mix_refs = refs[9], refs[10:18]
-    dmix_refs, dh_ref, small_ref, gout_ref = refs[18:22], refs[22], refs[23], refs[24]
+    wout_ref = refs[9]
+    dmix_refs, dh_ref, small_ref = refs[10:14], refs[14], refs[15]
     part, model = hidden_ref.shape
     back = sum(r[...].astype(F32) for r in back_refs)
     gain = gains_ref[1:2, :]
@@ -677,15 +677,18 @@
         d_hat - hat * jnp.mean(d_hat * hat, axis=-1, keepdims=True)
     )
     d_attn = d_hidden.astype(BF)
-    d_attn_t = d_hidden.T.astype(BF)
     d_mixed = dot(d_attn, wout_ref[...]).T.astype(BF)
     width = model // 4
     for s in range(4):
         dmix_refs[(4 - s) % 4][...] = d_mixed[s * width : (s + 1) * width, :]
     dh_ref[...] = d_hidden
+
+
+def out_grad_kernel(at, dh_ref, *refs):
+    mix_refs, gout_ref = refs[:8], refs[8]
     one, two = (jnp.concatenate([r[...] for r in mix_refs[n : n + 4]], axis=0) for n in (0, 4))
     mixed = jnp.where(at[0] < 2, one, two)
-    gout_ref[...] = dot(d_attn_t, mixed, NT).astype(BF)
+    gout_ref[...] = dot(dh_ref[...].T.astype(BF), mixed, NT).astype(BF)
 
 
 def qkv_back_kernel(
@@ -1058,22 +1061,28 @@
             router_block,
             pl.BlockSpec((1, part), lambda i, at: (0, at[0])),
             out_block,
-            *[col_one] * 4,
-            *[col_two] * 4,
-        ],
-        [*[piece] * 4, whole(part, model), whole(small_rows, model), whole(model, model)],
+        ],
+        [*[piece] * 4, whole(part, model), whole(small_rows, model)],
         [
             *[shaped((width, part), BF)] * 4,
             shaped((part, model), F32),
             shaped((small_rows, model), F32),
-            shaped((model, model), BF),
         ],
         prefetch=1,
         name="hidden_back",
-    )(at, *back_mine, hidden, grad_out, gains, small_all, chosen, out_all, *turns_one, *turns_two)
-    dmix_out, d_hidden, small_grads, grad_out_w = outs[0:4], outs[4], outs[5], outs[6]
+    )(at, *back_mine, hidden, grad_out, gains, small_all, chosen, out_all)
+    dmix_out, d_hidden, small_grads = outs[0:4], outs[4], outs[5]
+    grad_out_w = call(
+        out_grad_kernel,
+        (1,),
+        [whole(part, model), *[col_one] * 4, *[col_two] * 4],
+        whole(model, model),
+        shaped((model, model), BF),
+        prefetch=1,
+        name="out_projection_grad",
+    )(at, d_hidden, *turns_one, *turns_two)
     dmix = scatter_turns(dmix_out)
-    dmix, eo_out = lax.optimization_barrier((dmix, eo_out))
+    dmix, eo_out, grad_out_w = lax.optimization_barrier((dmix, eo_out, grad_out_w))
     eo_mine = scatter_turns(eo_out)
 
     dq_t, dkv, skew, sides = attention_bwd(

time: 302 us -> 302 us (level)
    pallas_call x0 -> x1, Pallas kernels: none -> 4.18 us  [shards(): call(out_grad_kernel, (1,), [whole(part, model), *[col_one] * 4, *[col_tw...]
    reduce_scatter x1, waiting for transfers between devices: 3.8 us -> 7.09 us  [shards(): lax.psum_scatter(after(grad_experts, back_got, eo_out), dense, scatter_di...]
  transfers between devices with their start and end apart: 35 -> 35, of which waited for: 16 -> 18; matrix products, arithmetic and copies ran while one was open for 2% -> 2% of each run, Pallas kernels for 44% -> 43%
where the time goes in v5:
time: 302 us; the launch traced here: 301 us
  Pallas kernels  156 us (52%)
  waiting for transfers between devices  66.1 us (22%)
  starting transfers between devices  48.8 us (16%)
  between operations  14 us (5%)
  local copies, waits for them, and re-layouts  9.75 us (3%)
  other arithmetic  6.25 us (2%)
    ppermute x21, starting transfers between devices, turn(): return lax.ppermute(x, 'tp', [(i, (i + s) % 4) for i in range(4)])  41.2 us
    ppermute x21, waiting for transfers between devices, turn(): return lax.ppermute(x, 'tp', [(i, (i + s) % 4) for i in range(4)])  37.2 us
    pallas_call x2, Pallas kernels, attention_fwd(): pl.pallas_call(partial(fwd_kernel, heads, first, blocks), grid_spec=pltpu...  27.5 us
    pallas_call x1, Pallas kernels, attention_bwd(): pl.pallas_call(partial(bwd_kernel, heads), grid_spec=pltpu.PrefetchScalar...  24.7 us
    pallas_call x1, Pallas kernels, shards(): call(expert_kernel, (tiles,), [whole(1, rows), whole(rows, model), whole(...  23.7 us
    ppermute x9, waiting for transfers between devices, xor_step(): lax.ppermute(x, axis, [(i, i ^ s) for i in range(lax.axis_size(axis))])  19.4 us
    pallas_call x1, Pallas kernels, shards(): call(partial(qkv_back_kernel, first_col, experts, heads), (blocks,), [pl....  12.4 us
    pallas_call x1, Pallas kernels, shards(): call(weight_grad_kernel, (tiles,), [sorted_spec(model), sorted_spec(ff),...  12.3 us
  transfers between devices with their start and end apart: 35, of which 18 were waited for; matrix products, arithmetic and copies ran while one was open for 2% of the time, Pallas kernels for 43%

profile of v5, /device:TPU:0, one launch (start us, length us, event | category | flops | bytes accessed | tf_op | source)
XLA Modules:
  0.0 300.7 jit_solution(1162906195275577038)
XLA Ops:
  7.2 1.7 pack_small.1
  8.9 5.0 %collective-permute-start.13 = (bf16[96,192]{1,0:T(8,128)(2,1)}, bf16[96,192]{1,0:T(8,128)(2,1)S(1)}, u32[]{:S(2)}, u32[]{:S(2)}) collective-permute-start(bf16[96,192]{1,0:T(8,128)(2,1)} %param.15), channel_id=1, source_target_pairs={{0,3},{1,0},{2,1},{3,2},{4,7},{5,4},{6,5},{7,6},{8,11},{9,8},{10,9... | collective-permute-start | bytes 110600 | tf_op jit(solution)/shard_map/ppermute | solution.py:785
  14.0 1.0 collective-permute-start.11
  15.0 1.4 collective-permute-done.13
  16.4 2.8 collective-permute-done.12
  19.2 0.9 collective-permute-done.11
  20.1 1.6 pad_maximum_fusion.2
  21.8 2.5 collective-permute-start.2
  25.4 0.7 stack.66.at
  26.0 4.2 %plan.1 = (s32[1,1024]{1,0:T(1,128)}, s32[1,128]{1,0:T(1,128)}, f32[1,1024]{1,0:T(1,128)}, f32[1,2048]{1,0:T(1,128)}, s32[1,128]{1,0:T(1,128)}, /*index=5*/f32[3...) custom-call(s32[12]{0:T(128)} %stack.66.at, s32[1,1024]{1,0:T(1,128)} %bitcast.53, ...), custom_call_target="tpu_custom_call" | custom-call | flops 10000000 | bytes 100000 | tf_op jit(solution)/shard_map/plan/pallas_call | solution.py:876
  30.3 1.3 dynamic-slice_bitcast_fusion
  31.6 1.1 pad_maximum_fusion
  32.7 1.1 collective-permute-done.1
  34.2 2.0 collective-permute-done.3.refs_1_
  36.3 0.7 copy-done.11
  37.5 9.7 %norm_qkv.1 = (bf16[2048,576]{1,0:T(8,128)(2,1)}, bf16[2048,768]{1,0:T(8,128)(2,1)}, f32[1,2048]{1,0:T(1,128)}, bf16[768,768]{1,0:T(8,128)(2,1)}, f32[8,768]{1,0:T(8,128)}) custom-call(s32[12]{0:T(128)} %stack.66.at, bf16[1024,768]{1,0:T(8,128)(2,1)} %tok_ref.1, bf16[1024,768]{1,0:T(8,128)(2,1)} %copy-done.1, bf16[4,96,768]{2,1,0:T(8,128)(2,1)} %copy-done, ...), custom_call_target="tpu_custom_call" | custom-call | flops 10000000 | bytes 100000 | tf_op jit(solution)/shard_map/norm_qkv/pallas_call | solution.py:917
  47.2 14.1 %attention_fwd.2 = (f32[192,1024]{1,0:T(8,128)}, bf16[192,512]{1,0:T(8,128)(2,1)}, f32[3,1024]{1,0:T(4,128)}, bf16[3,2048,128]{2,1,0:T(8,128)(2,1)}, bf16[3,80,2048]{2,1,0:T(8,128)(2,1)}) custom-call(s32[1,128]{1,0:T(1,128)} %get-tuple-element.135.info, f32[3,32]{1,0:T(4,128)} %bitcast.45, bf16[2048,576]{1,0:T(8,128)(2,1)} %get-tuple-element.145.qkv_ref.qkv_all, ...), custom_call_target="tpu_custom_call" | custom-call | flops 10000000 | bytes 100000 | tf_op jit(solution)/shard_map/attention_fwd/pallas_call | solution.py:226
  61.7 1.9 collective-permute-start.5
  63.6 13.4 %attention_fwd.3 = (f32[192,1024]{1,0:T(8,128)}, bf16[192,512]{1,0:T(8,128)(2,1)}, f32[3,1024]{1,0:T(4,128)}) custom-call(s32[1,128]{1,0:T(1,128)} %get-tuple-element.135.info, f32[3,32]{1,0:T(4,128)} %bitcast.46, bf16[2048,576]{1,0:T(8,128)(2,1)} %get-tuple-element.145.qkv_ref.qkv_all, ...), custom_call_target="tpu_custom_call", output_to_operand_aliasing={{0}: (8, {}), {2}: (9, {})} | custom-call | flops 10000000 | bytes 100000 | tf_op jit(solution)/shard_map/attention_fwd/pallas_call | solution.py:226
  77.1 1.3 collective-permute-done.6.refs_3_.refs_2_
  78.4 1.3 collective-permute-start.10
  79.7 3.2 %collective-permute-start.9 = (bf16[192,512]{1,0:T(8,128)(2,1)}, bf16[192,512]{1,0:T(8,128)(2,1)S(1)}, u32[]{:S(2)}, u32[]{:S(2)}) collective-permute-start(bf16[192,512]{1,0:T(8,128)(2,1)} %get-tuple-element.171.refs_1_.refs_4_), channel_id=1, source_target_pairs={{0,2},{1,3},{2,0},{3,1},{4,6},{5,7},{6,4},{7,5},{8,10},{9,11},{10,... | collective-permute-start | bytes 589832 | tf_op jit(solution)/shard_map/ppermute | solution.py:785
  82.9 2.0 collective-permute-start.8
  84.9 6.0 %hidden_router.2 = (f32[1024,768]{1,0:T(8,128)}, bf16[1024,768]{1,0:T(8,128)(2,1)}, f32[1,1024]{1,0:T(1,128)}, f32[192,1024]{1,0:T(8,128)}) custom-call(s32[12]{0:T(128)} %stack.66.at, bf16[1024,768]{1,0:T(8,128)(2,1)} %tok_ref.1, bf16[192,512]{1,0:T(8,128)(2,1)} %get-tuple-element.159.refs_1_.refs_0_, bf16[192,512]{1,0:T(8,128)(2,1)} %copy-done.7, ...), custom_call_target="tpu_custom_call" | custom-call | flops 10000000 | bytes 100000 | tf_op jit(solution)/shard_map/hidden_router/pallas_call | solution.py:953
  90.9 10.2 %collective-permute-done.9.refs_3_.refs_6_ = bf16[192,512]{1,0:T(8,128)(2,1)S(1)} collective-permute-done((bf16[192,512]{1,0:T(8,128)(2,1)}, bf16[192,512]{1,0:T(8,128)(2,1)S(1)}, u32[]{:S(2)}, u32[]{:S(2)}) %collective-permute-start.9) | collective-permute-done | bytes 196640 | tf_op jit(solution)/shard_map/ppermute | solution.py:785
  101.9 5.9 %hidden_router.3 = (f32[1024,768]{1,0:T(8,128)}, bf16[1024,768]{1,0:T(8,128)(2,1)}, f32[1,1024]{1,0:T(1,128)}, f32[192,1024]{1,0:T(8,128)}) custom-call(s32[12]{0:T(128)} %stack.66.at, bf16[1024,768]{1,0:T(8,128)(2,1)} %tok_ref.1, ...), custom_call_target="tpu_custom_call", output_to_operand_aliasing={{0}: (10, {}), {1}: (11, {}), {2}: (12, {}), {3}: (13, {})} | custom-call | flops 10000000 | bytes 100000 | tf_op jit(solution)/shard_map/hidden_router/pallas_call | solution.py:953
  107.8 23.7 %experts.1 = (bf16[272,768]{1,0:T(8,128)(2,1)}, bf16[272,768]{1,0:T(8,128)(2,1)}, bf16[272,768]{1,0:T(8,128)(2,1)}, bf16[272,768]{1,0:T(8,128)(2,1)}, bf16[1792,...) custom-call(s32[1,128]{1,0:T(1,128)} %get-tuple-element.154.owner, ...), custom_call_target="tpu_custom_call" | custom-call | flops 10000000 | bytes 100000 | tf_op jit(solution)/shard_map/experts/pallas_call | solution.py:988
  131.6 2.2 collective-permute-start.15
  133.8 1.6 collective-permute-start.16
  135.4 12.3 %expert_weight_grads.1 = bf16[3072,1536]{1,0:T(8,128)(2,1)} custom-call(s32[1,128]{1,0:T(1,128)} %get-tuple-element.154.owner, bf16[1792,768]{1,0:T(8,128)(2,1)} %get-tuple-element.187.x_ref, bf16[1792,768]{1,0:T(8,128)(2,1)} %get-tuple-element.188.di_ref, bf16[1792,768]{1,0:T(8,128)(2,1)} %get-tuple-element.189.de_ref, ...), custom_call_target="tpu_custom_call" | custom-call | flops 10000000 | bytes 100000 | tf_op jit(solution)/shard_map/expert_weight_grads/pallas_call | solution.py:1023
  147.7 7.1 %unsort_outputs.1 = (bf16[192,1024]{1,0:T(8,128)(2,1)}, bf16[192,1024]{1,0:T(8,128)(2,1)}, bf16[192,1024]{1,0:T(8,128)(2,1)}, bf16[192,1024]{1,0:T(8,128)(2,1)}) custom-call(s32[1,128]{1,0:T(1,128)} %get-tuple-element.154.owner, s32[12]{0:T(128)} %stack.66.at, s32[1,1024]{1,0:T(1,128)} %get-tuple-element.155.pos_row, ...), custom_call_target="tpu_custom_call" | custom-call | flops 10000000 | bytes 100000 | tf_op jit(solution)/shard_map/unsort_outputs/pallas_call | solution.py:1033
  154.9 8.2 %collective-permute-done.15.refs_2_ = bf16[272,768]{1,0:T(8,128)(2,1)S(1)} collective-permute-done((bf16[272,768]{1,0:T(8,128)(2,1)}, bf16[272,768]{1,0:T(8,128)(2,1)S(1)}, u32[]{:S(2)}, u32[]{:S(2)}) %collective-permute-start.15) | collective-permute-done | bytes 417824 | tf_op jit(solution)/shard_map/ppermute | solution.py:785
  163.1 0.7 copy-done.14
  164.0 6.0 %hidden_back.1 = (bf16[192,256]{1,0:T(8,128)(2,1)}, bf16[192,256]{1,0:T(8,128)(2,1)}, bf16[192,256]{1,0:T(8,128)(2,1)}, bf16[192,256]{1,0:T(8,128)(2,1)}, f32[256,768]{1,0:T(8,128)}, /*index=5*/f32[8,768]{1,0:T(8,128)}) custom-call(s32[12]{0:T(128)} %stack.66.at, bf16[272,768]{1,0:T(8,128)(2,1)} %get-tuple-element.196.refs_0_, bf16[272,768]{1,0:T(8,128)(2,1)} %copy-done.13, ...), custom_call_target="tpu_custom_call" | custom-call | flops 10000000 | bytes 100000 | tf_op jit(solution)/shard_map/hidden_back/pallas_call | solution.py:1053
  170.0 9.4 %collective-permute-start.17 = (bf16[192,256]{1,0:T(8,128)(2,1)}, bf16[192,256]{1,0:T(8,128)(2,1)S(1)}, u32[]{:S(2)}, u32[]{:S(2)}) collective-permute-start(bf16[192,256]{1,0:T(8,128)(2,1)} %get-tuple-element.202), channel_id=1, source_target_pairs={{0,1},{1,2},{2,3},{3,0},{4,5},{5,6},{6,7},{7,4},{8,9},{9,10},{10,1... | collective-permute-start | bytes 294920 | tf_op jit(solution)/shard_map/ppermute | solution.py:785
  179.8 2.1 collective-permute-start.19
  181.8 4.2 %out_projection_grad.1.gout_ref = bf16[768,768]{1,0:T(8,128)(2,1)} custom-call(s32[12]{0:T(128)} %stack.66.at, f32[256,768]{1,0:T(8,128)} %get-tuple-element.209.dh_ref, bf16[192,512]{1,0:T(8,128)(2,1)} %get-tuple-element.159.refs_1_.refs_0_, bf16[192,512]{1,0:T(8,128)(2,1)} %copy-done.7, bf16[192,512]{1,0:T(8,128)(2,1)} %copy-done.6, ...), custom_call_target="tpu_custom_call" | custom-call | flops 10000000 | bytes 100000 | tf_op jit(solution)/shard_map/out_projection_grad/pallas_call | solution.py:1075
  186.0 1.1 collective-permute-done.18.m2
  187.1 2.6 collective-permute-start.20
  189.7 2.3 collective-permute-start.21
  192.1 24.7 %attention_bwd.1 = (bf16[192,1024]{1,0:T(8,128)(2,1)}, bf16[2048,384]{1,0:T(8,128)(2,1)}, f32[16,512]{1,0:T(8,128)}, f32[8,256]{1,0:T(8,128)}) custom-call(s32[1,128]{1,0:T(1,128)} %get-tuple-element.135.info, f32[3,32]{1,0:T(4,128)} %bitcast.47, bf16[2048,576]{1,0:T(8,128)(2,1)} %get-tuple-element.145.qkv_ref.qkv_all, ...), custom_call_target="tpu_custom_call" | custom-call | flops 10000000 | bytes 100000 | tf_op jit(solution)/shard_map/attention_bwd/pallas_call | solution.py:345
  217.3 1.5 constant_dynamic-slice_fusion
  218.9 2.3 collective-permute-done.23.got_ref
  221.1 0.9 copy-done.4
  222.0 12.4 %qkv_back.1 = (bf16[768,1024]{1,0:T(8,128)(2,1)}, bf16[384,1536]{1,0:T(8,128)(2,1)}, bf16[384,1536]{1,0:T(8,128)(2,1)}) custom-call(s32[12]{0:T(128)} %stack.66.at, bf16[192,1024]{1,0:T(8,128)(2,1)} %get-tuple-element.224.dq_ref, bf16[2048,384]{1,0:T(8,128)(2,1)} %get-tuple-element.225.dkv_ref, bf16[1024,384]{1,0:T(8,128)(2,1)} %copy-done.4, ...), custom_call_target="tpu_custom_call" | custom-call | flops 10000000 | bytes 100000 | tf_op jit(solution)/shard_map/qkv_back/pallas_call | solution.py:1094
  234.6 3.0 collective-permute-done.24.got_ref
  237.6 1.0 copy-done.3
  238.6 2.7 dense_pair_sum.1
  241.4 7.1 %reduce-scatter.3.cloned.1.call-done = bf16[384,1536]{1,0:T(8,128)(2,1)} async-done(((bf16[3072,1536]{1,0:T(8,128)(2,1)}), bf16[384,1536]{1,0:T(8,128)(2,1)}) %reduce-scatter.3.cloned.1.call-update) | async-done | bytes 1179664 | tf_op jit(solution)/shard_map/reduce_scatter | solution.py:1043
  248.5 1.4 collective-permute-start.25
  249.9 0.7 collective-permute-start.26
  250.6 1.4 collective-permute-start.27
  252.0 6.4 %collective-permute-done.25.refs_1_ = bf16[96,1536]{1,0:T(8,128)(2,1)S(1)} collective-permute-done((bf16[96,1536]{1,0:T(8,128)(2,1)S(1)}, bf16[96,1536]{1,0:T(8,128)(2,1)S(1)}, u32[]{:S(2)}, u32[]{:S(2)}) %collective-permute-start.25) | collective-permute-done | bytes 294944 | tf_op jit(solution)/shard_map/ppermute | solution.py:781
  258.5 4.9 %collective-permute-done.26.refs_2_ = bf16[96,1536]{1,0:T(8,128)(2,1)S(1)} collective-permute-done((bf16[96,1536]{1,0:T(8,128)(2,1)S(1)}, bf16[96,1536]{1,0:T(8,128)(2,1)S(1)}, u32[]{:S(2)}, u32[]{:S(2)}) %collective-permute-start.26) | collective-permute-done | bytes 294944 | tf_op jit(solution)/shard_map/ppermute | solution.py:781
  263.3 1.8 collective-permute-done.27.refs_3_
  265.1 0.7 copy-done.21
  265.9 2.2 dense_sum.1
  268.0 4.9 %collective-permute-start.28 = (bf16[96,384]{1,0:T(8,128)(2,1)}, bf16[96,384]{1,0:T(8,128)(2,1)S(1)}, u32[]{:S(2)}, u32[]{:S(2)}) collective-permute-start(bf16[96,384]{1,0:T(8,128)(2,1)} %get-tuple-element.246), channel_id=1, source_target_pairs={{0,3},{1,0},{2,1},{3,2},{4,7},{5,4},{6,5},{7,6},{8,11},{9,8},{10,9... | collective-permute-start | bytes 221192 | tf_op jit(solution)/shard_map/ppermute | solution.py:785
  273.0 0.7 collective-permute-start.29
  273.7 3.7 %layer_output.1 = bf16[192,1024]{1,0:T(8,128)(2,1)} custom-call(bf16[192,1024]{1,0:T(8,128)(2,1)} %get-tuple-element.219.e0, bf16[192,1024]{1,0:T(8,128)(2,1)} %copy-done.16, bf16[192,1024]{1,0:T(8,128)(2,1)} %copy-done.17, bf16[192,1024]{1,0:T(8,128)(2,1)} %copy-done.18, f32[192,1024]{1,0:T(8,128)} %get-tuple-element.241.hidden_ref, ...), custom_call_target="tpu_custom_call" | custom-call | flops 10000000 | bytes 100000 | tf_op jit(solution)/shard_map/layer_output/pallas_call | solution.py:1179
  277.3 1.6 slice_convert_fusion
  278.9 10.9 %collective-permute-done.29.p2 = bf16[96,384]{1,0:T(8,128)(2,1)S(1)} collective-permute-done((bf16[96,384]{1,0:T(8,128)(2,1)}, bf16[96,384]{1,0:T(8,128)(2,1)S(1)}, u32[]{:S(2)}, u32[]{:S(2)}) %collective-permute-start.29) | collective-permute-done | bytes 73760 | tf_op jit(solution)/shard_map/ppermute | solution.py:785
  290.5 1.7 last_sum.1
  292.2 2.0 convert_bitcast_fusion
  (104 shorter events, 5.5 us)
Async XLA Ops:
  7.2 77.7 %all-gather.3.cloned.1.call-start = ((), (), s32[]{:S(2)}) async-start(), calls=%async_computation.2 | async-start | bytes 1327104 | tf_op jit(solution)/shard_map/all_gather | solution.py:865
  8.9 7.4 %collective-permute-start.13 = (bf16[96,192]{1,0:T(8,128)(2,1)}, bf16[96,192]{1,0:T(8,128)(2,1)S(1)}, u32[]{:S(2)}, u32[]{:S(2)}) collective-permute-start(bf16[96,192]{1,0:T(8,128)(2,1)} %param.15), channel_id=1, source_target_pairs={{0,3},{1,0},{2,1},{3,2},{4,7},{5,4},{6,5},{7,6},{8,11},{9,8},{10,9... | collective-permute-start | bytes 110600 | tf_op jit(solution)/shard_map/ppermute | solution.py:785
  14.0 5.2 %collective-permute-start.12 = (bf16[96,192]{1,0:T(8,128)(2,1)}, bf16[96,192]{1,0:T(8,128)(2,1)S(1)}, u32[]{:S(2)}, u32[]{:S(2)}) collective-permute-start(bf16[96,192]{1,0:T(8,128)(2,1)} %param.15), channel_id=1, source_target_pairs={{0,2},{1,3},{2,0},{3,1},{4,6},{5,7},{6,4},{7,5},{8,10},{9,11},{10,... | collective-permute-start | bytes 110600 | tf_op jit(solution)/shard_map/ppermute | solution.py:785
  14.0 6.1 %collective-permute-start.11 = (bf16[96,192]{1,0:T(8,128)(2,1)}, bf16[96,192]{1,0:T(8,128)(2,1)S(1)}, u32[]{:S(2)}, u32[]{:S(2)}) collective-permute-start(bf16[96,192]{1,0:T(8,128)(2,1)} %param.15), channel_id=1, source_target_pairs={{0,1},{1,2},{2,3},{3,0},{4,5},{5,6},{6,7},{7,4},{8,9},{9,10},{10,1... | collective-permute-start | bytes 110600 | tf_op jit(solution)/shard_map/ppermute | solution.py:785
  21.7 86.1 %all-gather.5.cloned.1.call-start = ((), (), s32[]{:S(2)}) async-start(), calls=%async_computation.3 | async-start | bytes 10616832 | tf_op jit(solution)/shard_map/all_gather | solution.py:912
  21.7 14.5 %collective-permute-start.4 = (bf16[1024,768]{1,0:T(8,128)(2,1)}, bf16[1024,768]{1,0:T(8,128)(2,1)S(1)}, u32[]{:S(2)}, u32[]{:S(2)}) collective-permute-start(bf16[1024,768]{1,0:T(8,128)(2,1)} %tok_ref.1), channel_id=1, source_target_pairs={{0,4},{4,0},{1,5},{5,1},{2,6},{6,2},{3,7},{7,3},{8,12},{12,8},{9,1... | collective-permute-start | bytes 4718600 | tf_op jit(solution)/shard_map/ppermute | solution.py:781
  21.8 10.9 %collective-permute-start.2 = (bf16[96,768]{1,0:T(8,128)(2,1)}, bf16[96,768]{1,0:T(8,128)(2,1)S(1)}, u32[]{:S(2)}, u32[]{:S(2)}) collective-permute-start(bf16[96,768]{1,0:T(8,128)(2,1)} %pack_small.1), channel_id=1, source_target_pairs={{0,24},{8,16},{16,8},{24,0},{1,25},{9,17},{17,9},{25,1},{2,26},{10... | collective-permute-start | bytes 442376 | tf_op jit(solution)/shard_map/ppermute | solution.py:781
  24.3 9.5 %collective-permute-start.1 = (bf16[96,768]{1,0:T(8,128)(2,1)}, bf16[96,768]{1,0:T(8,128)(2,1)S(1)}, u32[]{:S(2)}, u32[]{:S(2)}) collective-permute-start(bf16[96,768]{1,0:T(8,128)(2,1)} %pack_small.1), channel_id=1, source_target_pairs={{0,16},{8,24},{16,0},{24,8},{1,17},{9,25},{17,1},{25,9},{2,18},{10... | collective-permute-start | bytes 442376 | tf_op jit(solution)/shard_map/ppermute | solution.py:781
  24.8 9.2 %collective-permute-start = (bf16[96,768]{1,0:T(8,128)(2,1)}, bf16[96,768]{1,0:T(8,128)(2,1)S(1)}, u32[]{:S(2)}, u32[]{:S(2)}) collective-permute-start(bf16[96,768]{1,0:T(8,128)(2,1)} %pack_small.1), channel_id=1, source_target_pairs={{0,8},{8,0},{16,24},{24,16},{1,9},{9,1},{17,25},{25,17},{2,10},{10... | collective-permute-start | bytes 442376 | tf_op jit(solution)/shard_map/ppermute | solution.py:781
  31.6 2.4 copy-start.12
  34.1 2.2 copy-start
  34.1 2.1 collective-permute-start.3
  36.2 0.8 copy-start.11
  36.2 1.3 copy-start.1
  36.2 212.2 %reduce-scatter.3.cloned.1.call-start = ((), (), s32[]{:S(2)}) async-start(), calls=%async_computation.4 | async-start | bytes 10616832 | tf_op jit(solution)/shard_map/reduce_scatter | solution.py:1043
  61.3 15.7 %collective-permute-start.7 = (bf16[192,512]{1,0:T(8,128)(2,1)}, bf16[192,512]{1,0:T(8,128)(2,1)S(1)}, u32[]{:S(2)}, u32[]{:S(2)}) collective-permute-start(bf16[192,512]{1,0:T(8,128)(2,1)} %get-tuple-element.159.refs_1_.refs_0_), channel_id=1, source_target_pairs={{0,3},{1,0},{2,1},{3,2},{4,7},{5,4},{6,5},{7,6},{8,11},{9,8},{10,9... | collective-permute-start | bytes 589832 | tf_op jit(solution)/shard_map/ppermute | solution.py:785
  61.4 17.0 %collective-permute-start.6 = (bf16[192,512]{1,0:T(8,128)(2,1)}, bf16[192,512]{1,0:T(8,128)(2,1)S(1)}, u32[]{:S(2)}, u32[]{:S(2)}) collective-permute-start(bf16[192,512]{1,0:T(8,128)(2,1)} %get-tuple-element.159.refs_1_.refs_0_), channel_id=1, source_target_pairs={{0,2},{1,3},{2,0},{3,1},{4,6},{5,7},{6,4},{7,5},{8,10},{9,11},{10,... | collective-permute-start | bytes 589832 | tf_op jit(solution)/shard_map/ppermute | solution.py:785
  61.7 16.7 %collective-permute-start.5 = (bf16[192,512]{1,0:T(8,128)(2,1)}, bf16[192,512]{1,0:T(8,128)(2,1)S(1)}, u32[]{:S(2)}, u32[]{:S(2)}) collective-permute-start(bf16[192,512]{1,0:T(8,128)(2,1)} %get-tuple-element.159.refs_1_.refs_0_), channel_id=1, source_target_pairs={{0,1},{1,2},{2,3},{3,0},{4,5},{5,6},{6,7},{7,4},{8,9},{9,10},{10,1... | collective-permute-start | bytes 589832 | tf_op jit(solution)/shard_map/ppermute | solution.py:785
  77.1 7.8 %copy-start.5 = (bf16[192,512]{1,0:T(8,128)(2,1)}, bf16[192,512]{1,0:T(8,128)(2,1)S(1)}, u32[]{:S(2)}) copy-start(bf16[192,512]{1,0:T(8,128)(2,1)S(1)} %collective-permute-done.7.refs_4_.refs_3_) | copy-start | bytes 589828
  78.4 6.5 %copy-start.6 = (bf16[192,512]{1,0:T(8,128)(2,1)}, bf16[192,512]{1,0:T(8,128)(2,1)S(1)}, u32[]{:S(2)}) copy-start(bf16[192,512]{1,0:T(8,128)(2,1)S(1)} %collective-permute-done.6.refs_3_.refs_2_) | copy-start | bytes 589828
  78.4 6.5 %copy-start.7 = (bf16[192,512]{1,0:T(8,128)(2,1)}, bf16[192,512]{1,0:T(8,128)(2,1)S(1)}, u32[]{:S(2)}) copy-start(bf16[192,512]{1,0:T(8,128)(2,1)S(1)} %collective-permute-done.5.refs_2_.refs_1_) | copy-start | bytes 589828
  78.4 12.5 %collective-permute-start.10 = (bf16[192,512]{1,0:T(8,128)(2,1)}, bf16[192,512]{1,0:T(8,128)(2,1)S(1)}, u32[]{:S(2)}, u32[]{:S(2)}) collective-permute-start(bf16[192,512]{1,0:T(8,128)(2,1)} %get-tuple-element.171.refs_1_.refs_4_), channel_id=1, source_target_pairs={{0,3},{1,0},{2,1},{3,2},{4,7},{5,4},{6,5},{7,6},{8,11},{9,8},{10,9... | collective-permute-start | bytes 589832 | tf_op jit(solution)/shard_map/ppermute | solution.py:785
  79.7 21.4 %collective-permute-start.9 = (bf16[192,512]{1,0:T(8,128)(2,1)}, bf16[192,512]{1,0:T(8,128)(2,1)S(1)}, u32[]{:S(2)}, u32[]{:S(2)}) collective-permute-start(bf16[192,512]{1,0:T(8,128)(2,1)} %get-tuple-element.171.refs_1_.refs_4_), channel_id=1, source_target_pairs={{0,2},{1,3},{2,0},{3,1},{4,6},{5,7},{6,4},{7,5},{8,10},{9,11},{10,... | collective-permute-start | bytes 589832 | tf_op jit(solution)/shard_map/ppermute | solution.py:785
  82.9 18.2 %collective-permute-start.8 = (bf16[192,512]{1,0:T(8,128)(2,1)}, bf16[192,512]{1,0:T(8,128)(2,1)S(1)}, u32[]{:S(2)}, u32[]{:S(2)}) collective-permute-start(bf16[192,512]{1,0:T(8,128)(2,1)} %get-tuple-element.171.refs_1_.refs_4_), channel_id=1, source_target_pairs={{0,1},{1,2},{2,3},{3,0},{4,5},{5,6},{6,7},{7,4},{8,9},{9,10},{10,1... | collective-permute-start | bytes 589832 | tf_op jit(solution)/shard_map/ppermute | solution.py:785
  90.9 10.2 %copy-start.8 = (bf16[192,512]{1,0:T(8,128)(2,1)}, bf16[192,512]{1,0:T(8,128)(2,1)S(1)}, u32[]{:S(2)}) copy-start(bf16[192,512]{1,0:T(8,128)(2,1)S(1)} %collective-permute-done.10.refs_4_.refs_7_) | copy-start | bytes 589828
  101.1 0.8 copy-start.10
  131.6 23.3 %collective-permute-start.14 = (bf16[272,768]{1,0:T(8,128)(2,1)}, bf16[272,768]{1,0:T(8,128)(2,1)S(1)}, u32[]{:S(2)}, u32[]{:S(2)}) collective-permute-start(bf16[272,768]{1,0:T(8,128)(2,1)} %get-tuple-element.183), channel_id=1, source_target_pairs={{0,1},{1,2},{2,3},{3,0},{4,5},{5,6},{6,7},{7,4},{8,9},{9,10},{10,1... | collective-permute-start | bytes 1253384 | tf_op jit(solution)/shard_map/ppermute | solution.py:785
  131.6 31.4 %collective-permute-start.15 = (bf16[272,768]{1,0:T(8,128)(2,1)}, bf16[272,768]{1,0:T(8,128)(2,1)S(1)}, u32[]{:S(2)}, u32[]{:S(2)}) collective-permute-start(bf16[272,768]{1,0:T(8,128)(2,1)} %get-tuple-element.184), channel_id=1, source_target_pairs={{0,2},{1,3},{2,0},{3,1},{4,6},{5,7},{6,4},{7,5},{8,10},{9,11},{10,... | collective-permute-start | bytes 1253384 | tf_op jit(solution)/shard_map/ppermute | solution.py:785
  133.8 29.2 %collective-permute-start.16 = (bf16[272,768]{1,0:T(8,128)(2,1)}, bf16[272,768]{1,0:T(8,128)(2,1)S(1)}, u32[]{:S(2)}, u32[]{:S(2)}) collective-permute-start(bf16[272,768]{1,0:T(8,128)(2,1)} %get-tuple-element.185), channel_id=1, source_target_pairs={{0,3},{1,0},{2,1},{3,2},{4,7},{5,4},{6,5},{7,6},{8,11},{9,8},{10,9... | collective-permute-start | bytes 1253384 | tf_op jit(solution)/shard_map/ppermute | solution.py:785
  154.9 8.2 %copy-start.13 = (bf16[272,768]{1,0:T(8,128)(2,1)}, bf16[272,768]{1,0:T(8,128)(2,1)S(1)}, u32[]{:S(2)}) copy-start(bf16[272,768]{1,0:T(8,128)(2,1)S(1)} %collective-permute-done.14.refs_1_) | copy-start | bytes 1253380
  163.1 0.9 copy-start.15
  164.0 128.2 %reduce-scatter.5.cloned.1.call-start = ((), (), s32[]{:S(2)}) async-start(), calls=%async_computation.5 | async-start | bytes 1966080 | tf_op jit(solution)/shard_map/reduce_scatter | solution.py:1148
  170.0 16.0 %collective-permute-start.17 = (bf16[192,256]{1,0:T(8,128)(2,1)}, bf16[192,256]{1,0:T(8,128)(2,1)S(1)}, u32[]{:S(2)}, u32[]{:S(2)}) collective-permute-start(bf16[192,256]{1,0:T(8,128)(2,1)} %get-tuple-element.202), channel_id=1, source_target_pairs={{0,1},{1,2},{2,3},{3,0},{4,5},{5,6},{6,7},{7,4},{8,9},{9,10},{10,1... | collective-permute-start | bytes 294920 | tf_op jit(solution)/shard_map/ppermute | solution.py:785
  179.4 7.7 %collective-permute-start.18 = (bf16[192,256]{1,0:T(8,128)(2,1)}, bf16[192,256]{1,0:T(8,128)(2,1)S(1)}, u32[]{:S(2)}, u32[]{:S(2)}) collective-permute-start(bf16[192,256]{1,0:T(8,128)(2,1)} %get-tuple-element.203), channel_id=1, source_target_pairs={{0,2},{1,3},{2,0},{3,1},{4,6},{5,7},{6,4},{7,5},{8,10},{9,11},{10,... | collective-permute-start | bytes 294920 | tf_op jit(solution)/shard_map/ppermute | solution.py:785
  179.8 7.3 %collective-permute-start.19 = (bf16[192,256]{1,0:T(8,128)(2,1)}, bf16[192,256]{1,0:T(8,128)(2,1)S(1)}, u32[]{:S(2)}, u32[]{:S(2)}) collective-permute-start(bf16[192,256]{1,0:T(8,128)(2,1)} %get-tuple-element.204), channel_id=1, source_target_pairs={{0,3},{1,0},{2,1},{3,2},{4,7},{5,4},{6,5},{7,6},{8,11},{9,8},{10,9... | collective-permute-start | bytes 294920 | tf_op jit(solution)/shard_map/ppermute | solution.py:785
  181.8 5.3 %copy-start.30 = (bf16[192,1024]{1,0:T(8,128)(2,1)S(1)}, bf16[192,1024]{1,0:T(8,128)(2,1)}, u32[]{:S(2)}) copy-start(bf16[192,1024]{1,0:T(8,128)(2,1)} %get-tuple-element.216) | copy-start | bytes 1179652
  181.8 7.8 %copy-start.29 = (bf16[192,1024]{1,0:T(8,128)(2,1)S(1)}, bf16[192,1024]{1,0:T(8,128)(2,1)}, u32[]{:S(2)}) copy-start(bf16[192,1024]{1,0:T(8,128)(2,1)} %get-tuple-element.217) | copy-start | bytes 1179652
  181.8 10.2 %copy-start.28 = (bf16[192,1024]{1,0:T(8,128)(2,1)S(1)}, bf16[192,1024]{1,0:T(8,128)(2,1)}, u32[]{:S(2)}) copy-start(bf16[192,1024]{1,0:T(8,128)(2,1)} %get-tuple-element.218) | copy-start | bytes 1179652
  186.0 6.1 %copy-start.22 = (bf16[192,256]{1,0:T(8,128)(2,1)}, bf16[192,256]{1,0:T(8,128)(2,1)S(1)}, u32[]{:S(2)}) copy-start(bf16[192,256]{1,0:T(8,128)(2,1)S(1)} %collective-permute-done.17.m1) | copy-start | bytes 294916
  187.1 5.0 %copy-start.23 = (bf16[192,256]{1,0:T(8,128)(2,1)}, bf16[192,256]{1,0:T(8,128)(2,1)S(1)}, u32[]{:S(2)}) copy-start(bf16[192,256]{1,0:T(8,128)(2,1)S(1)} %collective-permute-done.18.m2) | copy-start | bytes 294916
  187.1 5.0 %copy-start.24 = (bf16[192,256]{1,0:T(8,128)(2,1)}, bf16[192,256]{1,0:T(8,128)(2,1)S(1)}, u32[]{:S(2)}) copy-start(bf16[192,256]{1,0:T(8,128)(2,1)S(1)} %collective-permute-done.19.m3) | copy-start | bytes 294916
  187.1 29.8 %collective-permute-start.20 = (bf16[192,1024]{1,0:T(8,128)(2,1)S(1)}, bf16[192,1024]{1,0:T(8,128)(2,1)S(1)}, u32[]{:S(2)}, u32[]{:S(2)}) collective-permute-start(bf16[192,1024]{1,0:T(8,128)(2,1)S(1)} %copy-done.30), channel_id=1, source_target_pairs={{0,1},{1,2},{2,3},{3,0},{4,5},{5,6},{6,7},{7,4},{8,9},{9,10},{10,1... | collective-permute-start | bytes 1179656 | tf_op jit(solution)/shard_map/ppermute | solution.py:785
  189.7 27.6 %collective-permute-start.21 = (bf16[192,1024]{1,0:T(8,128)(2,1)S(1)}, bf16[192,1024]{1,0:T(8,128)(2,1)S(1)}, u32[]{:S(2)}, u32[]{:S(2)}) collective-permute-start(bf16[192,1024]{1,0:T(8,128)(2,1)S(1)} %copy-done.29), channel_id=1, source_target_pairs={{0,2},{1,3},{2,0},{3,1},{4,6},{5,7},{6,4},{7,5},{8,10},{9,11},{10,... | collective-permute-start | bytes 1179656 | tf_op jit(solution)/shard_map/ppermute | solution.py:785
  192.0 25.3 %collective-permute-start.22 = (bf16[192,1024]{1,0:T(8,128)(2,1)S(1)}, bf16[192,1024]{1,0:T(8,128)(2,1)S(1)}, u32[]{:S(2)}, u32[]{:S(2)}) collective-permute-start(bf16[192,1024]{1,0:T(8,128)(2,1)S(1)} %copy-done.28), channel_id=1, source_target_pairs={{0,3},{1,0},{2,1},{3,2},{4,7},{5,4},{6,5},{7,6},{8,11},{9,8},{10,9... | collective-permute-start | bytes 1179656 | tf_op jit(solution)/shard_map/ppermute | solution.py:785
  216.9 17.6 %copy-start.16 = (bf16[192,1024]{1,0:T(8,128)(2,1)}, bf16[192,1024]{1,0:T(8,128)(2,1)S(1)}, u32[]{:S(2)}) copy-start(bf16[192,1024]{1,0:T(8,128)(2,1)S(1)} %collective-permute-done.20.e1) | copy-start | bytes 1179652
  217.3 17.2 %copy-start.17 = (bf16[192,1024]{1,0:T(8,128)(2,1)}, bf16[192,1024]{1,0:T(8,128)(2,1)S(1)}, u32[]{:S(2)}) copy-start(bf16[192,1024]{1,0:T(8,128)(2,1)S(1)} %collective-permute-done.21.e2) | copy-start | bytes 1179652
  217.3 17.2 %copy-start.18 = (bf16[192,1024]{1,0:T(8,128)(2,1)}, bf16[192,1024]{1,0:T(8,128)(2,1)S(1)}, u32[]{:S(2)}) copy-start(bf16[192,1024]{1,0:T(8,128)(2,1)S(1)} %collective-permute-done.22.e3) | copy-start | bytes 1179652
  218.8 2.4 collective-permute-start.23
  221.1 0.9 copy-start.4
  234.5 3.1 %collective-permute-start.24 = (bf16[384,1536]{1,0:T(8,128)(2,1)}, bf16[384,1536]{1,0:T(8,128)(2,1)S(1)}, u32[]{:S(2)}, u32[]{:S(2)}) collective-permute-start(bf16[384,1536]{1,0:T(8,128)(2,1)} %get-tuple-element.235), channel_id=1, source_target_pairs={{0,4},{4,0},{1,5},{5,1},{2,6},{6,2},{3,7},{7,3},{8,12},{12,8},{9,1... | collective-permute-start | bytes 3538952 | tf_op jit(solution)/shard_map/ppermute | solution.py:781
  237.6 1.0 copy-start.3
  241.4 7.1 %copy-start.33 = (bf16[96,1536]{1,0:T(8,128)(2,1)S(1)}, bf16[96,1536]{1,0:T(8,128)(2,1)}, u32[]{:S(2)}) copy-start(bf16[96,1536]{1,0:T(8,128)(2,1)} %get-tuple-element.237) | copy-start | bytes 884740
  241.4 8.6 %copy-start.32 = (bf16[96,1536]{1,0:T(8,128)(2,1)S(1)}, bf16[96,1536]{1,0:T(8,128)(2,1)}, u32[]{:S(2)}) copy-start(bf16[96,1536]{1,0:T(8,128)(2,1)} %get-tuple-element.238) | copy-start | bytes 884740
  241.4 9.2 %copy-start.31 = (bf16[96,1536]{1,0:T(8,128)(2,1)S(1)}, bf16[96,1536]{1,0:T(8,128)(2,1)}, u32[]{:S(2)}) copy-start(bf16[96,1536]{1,0:T(8,128)(2,1)} %get-tuple-element.239) | copy-start | bytes 884740
  248.5 10.0 %collective-permute-start.25 = (bf16[96,1536]{1,0:T(8,128)(2,1)S(1)}, bf16[96,1536]{1,0:T(8,128)(2,1)S(1)}, u32[]{:S(2)}, u32[]{:S(2)}) collective-permute-start(bf16[96,1536]{1,0:T(8,128)(2,1)S(1)} %copy-done.33), channel_id=1, source_target_pairs={{0,8},{8,0},{16,24},{24,16},{1,9},{9,1},{17,25},{25,17},{2,10},{10... | collective-permute-start | bytes 884744 | tf_op jit(solution)/shard_map/ppermute | solution.py:781
  249.9 13.4 %collective-permute-start.26 = (bf16[96,1536]{1,0:T(8,128)(2,1)S(1)}, bf16[96,1536]{1,0:T(8,128)(2,1)S(1)}, u32[]{:S(2)}, u32[]{:S(2)}) collective-permute-start(bf16[96,1536]{1,0:T(8,128)(2,1)S(1)} %copy-done.32), channel_id=1, source_target_pairs={{0,16},{8,24},{16,0},{24,8},{1,17},{9,25},{17,1},{25,9},{2,18},{10... | collective-permute-start | bytes 884744 | tf_op jit(solution)/shard_map/ppermute | solution.py:781
  250.6 14.5 %collective-permute-start.27 = (bf16[96,1536]{1,0:T(8,128)(2,1)S(1)}, bf16[96,1536]{1,0:T(8,128)(2,1)S(1)}, u32[]{:S(2)}, u32[]{:S(2)}) collective-permute-start(bf16[96,1536]{1,0:T(8,128)(2,1)S(1)} %copy-done.31), channel_id=1, source_target_pairs={{0,24},{8,16},{16,8},{24,0},{1,25},{9,17},{17,9},{25,1},{2,26},{10... | collective-permute-start | bytes 884744 | tf_op jit(solution)/shard_map/ppermute | solution.py:781
  258.4 6.7 %copy-start.19 = (bf16[96,1536]{1,0:T(8,128)(2,1)}, bf16[96,1536]{1,0:T(8,128)(2,1)S(1)}, u32[]{:S(2)}) copy-start(bf16[96,1536]{1,0:T(8,128)(2,1)S(1)} %collective-permute-done.25.refs_1_) | copy-start | bytes 884740
  263.3 1.8 copy-start.20
  268.0 9.3 %copy-start.2 = (bf16[384,1536]{1,0:T(8,128)(2,1)S(1)}, bf16[384,1536]{1,0:T(8,128)(2,1)}, u32[]{:S(2)}) copy-start(bf16[384,1536]{1,0:T(8,128)(2,1)} %reduce-scatter.3.cloned.1.call-done) | copy-start | bytes 3538948
  268.0 10.8 %collective-permute-start.28 = (bf16[96,384]{1,0:T(8,128)(2,1)}, bf16[96,384]{1,0:T(8,128)(2,1)S(1)}, u32[]{:S(2)}, u32[]{:S(2)}) collective-permute-start(bf16[96,384]{1,0:T(8,128)(2,1)} %get-tuple-element.246), channel_id=1, source_target_pairs={{0,3},{1,0},{2,1},{3,2},{4,7},{5,4},{6,5},{7,6},{8,11},{9,8},{10,9... | collective-permute-start | bytes 221192 | tf_op jit(solution)/shard_map/ppermute | solution.py:785
  273.0 16.8 %collective-permute-start.29 = (bf16[96,384]{1,0:T(8,128)(2,1)}, bf16[96,384]{1,0:T(8,128)(2,1)S(1)}, u32[]{:S(2)}, u32[]{:S(2)}) collective-permute-start(bf16[96,384]{1,0:T(8,128)(2,1)} %get-tuple-element.247), channel_id=1, source_target_pairs={{0,2},{1,3},{2,0},{3,1},{4,6},{5,7},{6,4},{7,5},{8,10},{9,11},{10,... | collective-permute-start | bytes 221192 | tf_op jit(solution)/shard_map/ppermute | solution.py:785
  273.7 16.2 %collective-permute-start.30 = (bf16[96,384]{1,0:T(8,128)(2,1)}, bf16[96,384]{1,0:T(8,128)(2,1)S(1)}, u32[]{:S(2)}, u32[]{:S(2)}) collective-permute-start(bf16[96,384]{1,0:T(8,128)(2,1)} %get-tuple-element.248), channel_id=1, source_target_pairs={{0,1},{1,2},{2,3},{3,0},{4,5},{5,6},{6,7},{7,4},{8,9},{9,10},{10,1... | collective-permute-start | bytes 221192 | tf_op jit(solution)/shard_map/ppermute | solution.py:785
  278.9 11.0 %copy-start.25 = (bf16[96,384]{1,0:T(8,128)(2,1)}, bf16[96,384]{1,0:T(8,128)(2,1)S(1)}, u32[]{:S(2)}) copy-start(bf16[96,384]{1,0:T(8,128)(2,1)S(1)} %collective-permute-done.28.p1) | copy-start | bytes 221188
  (5 other events, 3.5 us)
Sparse Core Ops, SparseCore 0:
  21.8 22.9 all-gather.2
  47.2 58.8 all-gather.4
  163.2 85.1 reduce-scatter.2
  250.6 40.0 reduce-scatter.4
